TPU v7x, 32 devices: a whole 2x2x4 slice. The times are simulated.
32 devices in a mesh: case: 2 (over y), gx: 4 (over z), gy: 2 (over x), gz: 2 (over core).
Axes of the slice: x: 2, y: 2, z: 4, core: 2. Of those that a mesh axis runs over, the one named last changes fastest.
Arguments:
- displacement: float32 [3, 128, 64, 512], P(None, ('case', 'gx'), 'gy', 'gz'), parts along dimension 1, may hold values from -6 to 6
- velocity: float32 [3, 128, 64, 512], P(None, ('case', 'gx'), 'gy', 'gz'), parts along dimension 1, may hold values from -6 to 6
- damage: float32 [128, 64, 512], P(('case', 'gx'), 'gy', 'gz'), parts along dimension 0, may hold values from 0 to 0.9
- history: float32 [128, 64, 512], P(('case', 'gx'), 'gy', 'gz'), parts along dimension 0, may hold values from 0.05 to 5
- contact: int32 [128, 64, 512], P(('case', 'gx'), 'gy', 'gz'), parts along dimension 0, may hold values 0 or 1
- notch: int32 [128, 64, 512], P(('case', 'gx'), 'gy', 'gz'), parts along dimension 0, may hold values 0 or 1
- labels: int32 [128, 64, 512], P(('case', 'gx'), 'gy', 'gz'), parts along dimension 0, may hold values from 0 to 3
- table: float32 [4, 4], replicated, may hold values from 0.5 to 2
- impact: float32 [6], P('case'), parts along dimension 0, may hold values from -4 to 4
Outputs:
- displacement_new: float32 [3, 128, 64, 512], P(None, ('case', 'gx'), 'gy', 'gz'), parts along dimension 1
- velocity_new: float32 [3, 128, 64, 512], P(None, ('case', 'gx'), 'gy', 'gz'), parts along dimension 1
- history_new: float32 [128, 64, 512], P(('case', 'gx'), 'gy', 'gz'), parts along dimension 0
- damage_new: float32 [128, 64, 512], P(('case', 'gx'), 'gy', 'gz'), parts along dimension 0
There are 2 independent parts, one for each index of `case`. A program takes and returns all parts, laid end to end along the dimension named above; an argument that names none is the same for every part. Nothing has to cross between parts.
All inputs are finite; a program needn't handle non-finite values. No bound on the sum of `contact` or of `notch` on one device may be relied on, other than what follows from the above.
Results may differ from a plain program's by a relative error of at most 0.0001.
Values sent between devices are 32-bit elements; how exact they have to be, the bound alone decides.
No kernel may reach another device: no remote copies, remote signals or barrier semaphores. Data moves between devices by JAX's collectives and lax.ppermute only.
A program may use at most 64 MiB of HBM per device.

v0:
```python
import jax
import jax.numpy as jnp
from jax import lax
from jax.sharding import PartitionSpec as P

ITERS = 3


TIME_STEP = 0.1
KAPPA_COEF = 0.5
NOTCH_LOAD = 20.0
STIFF_FLOOR = 0.001
component_of = ((0, 3, 4), (3, 1, 5), (4, 5, 2))


def padded_2(block, sides, width):
    for axis, dim in sides:
        count = lax.axis_size(axis)
        forward = [(i, i + 1) for i in range(count - 1)]
        backward = [(target, source) for source, target in forward]
        low = lax.ppermute(
            lax.slice_in_dim(block, block.shape[dim] - width, None, axis=dim), axis, forward
        )
        high = lax.ppermute(lax.slice_in_dim(block, 0, width, axis=dim), axis, backward)
        block = jnp.concatenate([low, block, high], axis=dim)
    return block


def central(padded, spatial):
    upper_start, upper_limit, lower_start, lower_limit = ([], [], [], [])
    for which in range(3):
        extent = padded.shape[which]
        if which == spatial:
            upper_start.append(2)
            upper_limit.append(extent)
            lower_start.append(0)
            lower_limit.append(extent - 2)
        else:
            upper_start.append(1)
            upper_limit.append(extent - 1)
            lower_start.append(1)
            lower_limit.append(extent - 1)
    return 0.5 * (
        lax.slice(padded, upper_start, upper_limit) - lax.slice(padded, lower_start, lower_limit)
    )


def material(labels, table):
    properties = []
    for quantity in range(4):
        picked = jnp.zeros(labels.shape, jnp.float32)
        for region in range(table.shape[1]):
            picked = picked + jnp.where(labels == region, table[quantity, region], 0.0)
        properties.append(picked)
    return properties


def stress_parts(grads, lame, shear, degrade):
    trace = grads[0][0] + grads[1][1] + grads[2][2]
    strain = [
        grads[0][0],
        grads[1][1],
        grads[2][2],
        0.5 * (grads[0][1] + grads[1][0]),
        0.5 * (grads[0][2] + grads[2][0]),
        0.5 * (grads[1][2] + grads[2][1]),
    ]
    stress = []
    for which in range(6):
        if which < 3:
            stress.append(degrade * (lame * trace + 2.0 * shear * strain[which]))
        else:
            stress.append(degrade * (2.0 * shear * strain[which]))
    positive = jnp.maximum(trace, 0.0)
    squares = strain[0] * strain[0] + strain[1] * strain[1] + strain[2] * strain[2]
    squares = squares + 2.0 * (
        strain[3] * strain[3] + strain[4] * strain[4] + strain[5] * strain[5]
    )
    energy = 0.5 * lame * positive * positive + shear * squares
    return (stress, energy)


def neighbours(padded):
    total = padded[2:, 1:-1, 1:-1] + padded[:-2, 1:-1, 1:-1]
    total = total + padded[1:-1, 2:, 1:-1] + padded[1:-1, :-2, 1:-1]
    total = total + padded[1:-1, 1:-1, 2:] + padded[1:-1, 1:-1, :-2]
    return total


def operate(field, diagonal):
    padded = padded_2(field, (("gx", 0), ("gy", 1), ("gz", 2)), 1)
    return diagonal * field - KAPPA_COEF * neighbours(padded)


def inner_rz(residual, precond):
    return lax.psum(jnp.sum(residual * precond), ("gx", "gy", "gz"))


def per_device(displacement, velocity, damage, history, contact, notch, labels, table, impact):
    lame, shear, density, fracture = material(labels, table)
    degrade = (1.0 - damage) * (1.0 - damage) + STIFF_FLOOR
    joined = jnp.concatenate([displacement, damage[None]], 0)
    padded_all = padded_2(joined, (("gx", 1), ("gy", 2), ("gz", 3)), 1)
    damage_padded = padded_all[3]
    grads = [[central(padded_all[c], j) for j in range(3)] for c in range(3)]
    stress, energy = stress_parts(grads, lame, shear, degrade)
    stress_wide = padded_2(jnp.stack(stress), (("gx", 1), ("gy", 2), ("gz", 3)), 1)
    loaded = contact.astype(jnp.float32)
    new_vel, new_disp = ([], [])
    for component in range(3):
        force = central(stress_wide[component_of[component][0]], 0)
        force = force + central(stress_wide[component_of[component][1]], 1)
        force = force + central(stress_wide[component_of[component][2]], 2)
        total = force + loaded * impact[component]
        speed = velocity[component] + TIME_STEP * total / density
        new_vel.append(speed)
        new_disp.append(displacement[component] + TIME_STEP * speed)
    history_new = jnp.maximum(jnp.maximum(history, energy), NOTCH_LOAD * notch.astype(jnp.float32))
    diagonal = fracture + 2.0 * history_new + 6.0 * KAPPA_COEF
    iterate = damage
    start_image = diagonal * damage - KAPPA_COEF * neighbours(damage_padded)
    residual = 2.0 * history_new - start_image
    precond = residual / diagonal
    direction = precond
    norm_now = inner_rz(residual, precond)
    for sweep in range(ITERS):
        image = operate(direction, diagonal)
        alpha = norm_now / lax.psum(jnp.sum(direction * image), ("gx", "gy", "gz"))
        iterate = iterate + alpha * direction
        residual = residual - alpha * image
        if sweep + 1 < ITERS:
            precond = residual / diagonal
            norm_next = inner_rz(residual, precond)
            direction = precond + norm_next / norm_now * direction
            norm_now = norm_next
    return (jnp.stack(new_disp), jnp.stack(new_vel), history_new, jnp.maximum(iterate, damage))


def solution(mesh):
    placed = (
        P(None, ("case", "gx"), "gy", "gz"),
        P(None, ("case", "gx"), "gy", "gz"),
        P(("case", "gx"), "gy", "gz"),
        P(("case", "gx"), "gy", "gz"),
        P(("case", "gx"), "gy", "gz"),
        P(("case", "gx"), "gy", "gz"),
        P(("case", "gx"), "gy", "gz"),
        P(),
        P("case"),
    )
    return jax.shard_map(
        per_device,
        mesh=mesh,
        in_specs=placed,
        out_specs=(
            P(None, ("case", "gx"), "gy", "gz"),
            P(None, ("case", "gx"), "gy", "gz"),
            P(("case", "gx"), "gy", "gz"),
            P(("case", "gx"), "gy", "gz"),
        ),
        check_vma=False,
    )
```

profile of v0, /device:TPU:0, one launch (start us, length us, event | category | flops | bytes accessed | tf_op | source)
XLA Modules:
  0.0 377.1 jit_solution(271523306365797273)
XLA Ops:
  1.8 4.9 %collective-permute-start = (f32[4,1,32,256]{3,2,1,0:T(8,128)S(1)}, f32[4,1,32,256]{3,2,1,0:T(8,128)S(1)}, u32[]{:S(2)}, u32[]{:S(2)}) collective-permute-start(f32[4,1,32,256]{3,2,1,0:T(8,128)S(1)} %get-tuple-element.57), channel_id=1, source_target_pairs={{0,4},{4,8},{8,12},{1,5},{5,9},{9,13},{2,6},{6,10},{10,14},{3,7},{... | collective-permute-start | bytes 393224 | tf_op jit(solution)/shard_map/ppermute | solution.py:21
  6.7 1.3 collective-permute-start.1
  8.0 1.4 collective-permute-done
  9.5 4.1 %collective-permute-done.1 = f32[4,1,32,256]{3,2,1,0:T(8,128)S(1)} collective-permute-done((f32[4,1,32,256]{3,2,1,0:T(8,128)S(1)}, f32[4,1,32,256]{3,2,1,0:T(8,128)S(1)}, u32[]{:S(2)}, u32[]{:S(2)}) %collective-permute-start.1) | collective-permute-done | bytes 131104 | tf_op jit(solution)/shard_map/ppermute | solution.py:24
  14.7 3.4 collective-permute-start.2
  18.1 1.3 collective-permute-start.3
  20.0 4.3 %collective-permute-done.3 = f32[4,18,1,256]{3,2,1,0:T(1,128)S(1)} collective-permute-done((f32[4,18,1,256]{3,2,1,0:T(1,128)S(1)}, f32[4,18,1,256]{3,2,1,0:T(1,128)S(1)}, u32[]{:S(2)}, u32[]{:S(2)}) %collective-permute-start.3) | collective-permute-done | bytes 73760 | tf_op jit(solution)/shard_map/ppermute | solution.py:24
  24.8 2.1 fusion.78
  26.9 2.0 copy.39
  30.2 2.0 copy.40
  34.2 1.7 copy.41
  35.9 1.7 copy.42
  37.7 6.5 %pad_maximum_fusion.1 = f32[4,18,34,258]{3,2,1,0:T(8,128)S(1)} fusion(f32[4,18,34,1]{3,2,1,0:T(8,128)} %copy.42, f32[4,18,1,256]{3,2,1,0:T(1,128)S(1)} %collective-permute-done.3, f32[4,1,32,256]{3,2,1,0:T(8,128)S(1)} %collective-permute-done.1, f32[1,16,32,256]{3,2,1,0:T(8,128)S(1)} %bitcast.85, f32[3,16,32,256]{3,2,1,0:T(8,128)S(1)} %copy-done.1, ...), kind=kLoop, calls=%fused_computation.1 | loop fusion | flops 4421088 | bytes 5052672 | tf_op jit(solution)/shard_map/concatenate | solution.py:25
  45.8 11.9 %fusion.66 = (f32[16,32,256]{2,1,0:T(8,128)S(1)}, f32[16,32,256]{2,1,0:T(8,128)S(1)}, f32[16,32,256]{2,1,0:T(8,128)S(1)}, f32[16,32,256]{2,1,0:T(8,128)}, f32[16...) fusion(f32[18,34,258]{2,1,0:T(8,128)S(1)} %get-tuple-element.46, ...), kind=kLoop, calls=%fused_computation.208 | loop fusion | flops 10485760 | bytes 18874416 | tf_op jit(solution)/shard_map/div | solution.py:123
  57.8 1.3 collective-permute-start.12
  59.1 4.5 %collective-permute-start.13 = (f32[1,32,256]{2,1,0:T(8,128)S(1)}, f32[1,32,256]{2,1,0:T(8,128)S(1)}, u32[]{:S(2)}, u32[]{:S(2)}) collective-permute-start(f32[1,32,256]{2,1,0:T(8,128)S(1)} %get-tuple-element.75), channel_id=1, source_target_pairs={{0,4},{4,8},{8,12},{1,5},{5,9},{9,13},{2,6},{6,10},{10,14},{3,7},{... | collective-permute-start | bytes 98312 | tf_op jit(solution)/shard_map/ppermute | solution.py:21
  63.8 1.5 collective-permute-done.13
  66.6 4.5 %collective-permute-start.15 = (f32[18,1,256]{2,1,0:T(1,128)S(1)}, f32[18,1,256]{2,1,0:T(1,128)S(1)}, u32[]{:S(2)}, u32[]{:S(2)}) collective-permute-start(f32[18,1,256]{2,1,0:T(1,128)S(1)} %get-tuple-element.69), channel_id=1, source_target_pairs={{0,2},{1,3},{4,6},{5,7},{8,10},{9,11},{12,14},{13,15},{16,18},{17,... | collective-permute-start | bytes 55304 | tf_op jit(solution)/shard_map/ppermute | solution.py:21
  71.2 1.4 collective-permute-done.15
  74.2 3.1 collective-permute-start.17
  78.5 2.1 multiply_reduce_fusion.3
  80.7 36.2 %all-reduce = (f32[]{:T(128)}, f32[]{:T(128)}) all-reduce(f32[]{:T(128)} %get-tuple-element.9, f32[]{:T(128)} %get-tuple-element.8), channel_id=1, replica_groups=mesh['case'=2,'gx'=4,'gy'=2,'gz'=2] {'gx','gy','gz'}, use_global_device_ids=true, to_apply=%region_1.2 | all-reduce | flops 2 | bytes 16 | tf_op jit(solution)/shard_map/psum | solution.py:96
  118.2 3.3 multiply_reduce_fusion.2
  121.4 30.1 %psum.44 = f32[]{:T(128)} all-reduce(f32[]{:T(128)} %get-tuple-element.14), channel_id=1, replica_groups=mesh['case'=2,'gx'=4,'gy'=2,'gz'=2] {'gx','gy','gz'}, use_global_device_ids=true, to_apply=%region_5.6 | all-reduce | flops 1 | bytes 8 | tf_op jit(solution)/shard_map/psum | solution.py:96
  154.1 1.4 collective-permute-start.18
  155.5 4.5 %collective-permute-start.19 = (f32[1,32,256]{2,1,0:T(8,128)S(1)}, f32[1,32,256]{2,1,0:T(8,128)S(1)}, u32[]{:S(2)}, u32[]{:S(2)}) collective-permute-start(f32[1,32,256]{2,1,0:T(8,128)S(1)} %get-tuple-element.73), channel_id=1, source_target_pairs={{0,4},{4,8},{8,12},{1,5},{5,9},{9,13},{2,6},{6,10},{10,14},{3,7},{... | collective-permute-start | bytes 98312 | tf_op jit(solution)/shard_map/ppermute | solution.py:21
  160.1 8.1 %bitcast_dynamic-update-slice_fusion.5 = (f32[6,16,32,256]{3,2,1,0:T(8,128)S(1)}, f32[16,32,256]{2,1,0:T(8,128)S(1)}) fusion(f32[16,32,256]{2,1,0:T(8,128)S(1)} %copy-done, f32[18,34,258]{2,1,0:T(8,128)} %copy-done.9, pred[16,32,256]{2,1,0:T(8,128)(4,1)} %get-tuple-element.28, f32[]{:T(128)} %bitcast.13, pred[16,32,256]{2,1,0:T(8,128)(4,1)} %get-tuple-element.27, ...), kind=kLoop, calls=%fused_computation.165 | loop fusion | flops 3932159 | bytes 5242912
  168.2 1.3 collective-permute-start.20
  169.5 4.5 %collective-permute-start.21 = (f32[18,1,256]{2,1,0:T(1,128)S(1)}, f32[18,1,256]{2,1,0:T(1,128)S(1)}, u32[]{:S(2)}, u32[]{:S(2)}) collective-permute-start(f32[18,1,256]{2,1,0:T(1,128)S(1)} %get-tuple-element.67), channel_id=1, source_target_pairs={{0,2},{1,3},{4,6},{5,7},{8,10},{9,11},{12,14},{13,15},{16,18},{17,... | collective-permute-start | bytes 55304 | tf_op jit(solution)/shard_map/ppermute | solution.py:21
  174.1 3.0 bitcast_dynamic-update-slice_fusion.4
  178.7 3.3 collective-permute-start.23
  181.9 3.0 bitcast_dynamic-update-slice_fusion.3
  185.0 1.6 copy-done.4
  186.6 2.0 multiply_reduce_fusion.1
  188.6 30.1 %psum.45 = f32[]{:T(128)} all-reduce(f32[]{:T(128)} %get-tuple-element.12), channel_id=1, replica_groups=mesh['case'=2,'gx'=4,'gy'=2,'gz'=2] {'gx','gy','gz'}, use_global_device_ids=true, to_apply=%region_7.8 | all-reduce | flops 1 | bytes 8 | tf_op jit(solution)/shard_map/psum | solution.py:128
  219.9 2.1 multiply_reduce_fusion
  222.0 4.7 %bitcast_dynamic-update-slice_fusion.2 = f32[6,16,32,256]{3,2,1,0:T(8,128)} fusion(f32[6,16,32,256]{3,2,1,0:T(8,128)} %copy-done.4, f32[16,32,256]{2,1,0:T(8,128)} %get-tuple-element.24, f32[16,32,256]{2,1,0:T(8,128)S(1)} %copy-done, pred[16,32,256]{2,1,0:T(8,128)(4,1)} %get-tuple-element.28, f32[]{:T(128)} %bitcast.13, ...), kind=kLoop, calls=%fused_computation.162 | loop fusion | flops 1703936 | bytes 2099200
  226.8 30.2 %psum.46 = f32[]{:T(128)} all-reduce(f32[]{:T(128)} %multiply_reduce_fusion), channel_id=1, replica_groups=mesh['case'=2,'gx'=4,'gy'=2,'gz'=2] {'gx','gy','gz'}, use_global_device_ids=true, to_apply=%region_9.10 | all-reduce | flops 1 | bytes 8 | tf_op jit(solution)/shard_map/psum | solution.py:96
  258.3 1.5 multiply_add_fusion
  259.8 1.3 collective-permute-start.24
  261.1 4.5 %collective-permute-start.25 = (f32[1,32,256]{2,1,0:T(8,128)S(1)}, f32[1,32,256]{2,1,0:T(8,128)S(1)}, u32[]{:S(2)}, u32[]{:S(2)}) collective-permute-start(f32[1,32,256]{2,1,0:T(8,128)S(1)} %get-tuple-element.71), channel_id=1, source_target_pairs={{0,4},{4,8},{8,12},{1,5},{5,9},{9,13},{2,6},{6,10},{10,14},{3,7},{... | collective-permute-start | bytes 98312 | tf_op jit(solution)/shard_map/ppermute | solution.py:21
  265.7 4.6 %bitcast_dynamic-update-slice_fusion.1 = f32[6,16,32,256]{3,2,1,0:T(8,128)} fusion(f32[6,16,32,256]{3,2,1,0:T(8,128)} %bitcast_dynamic-update-slice_fusion.2, f32[16,32,256]{2,1,0:T(8,128)S(1)} %copy-done.22, f32[16,32,256]{2,1,0:T(8,128)S(1)} %copy-done, pred[16,32,256]{2,1,0:T(8,128)(4,1)} %get-tuple-element.28, f32[]{:T(128)} %bitcast.13, ...), kind=kLoop, calls=%fused_computation.161 | loop fusion | flops 1703936 | bytes 2099200
  270.3 1.3 collective-permute-start.26
  271.6 4.5 %collective-permute-start.27 = (f32[18,1,256]{2,1,0:T(1,128)S(1)}, f32[18,1,256]{2,1,0:T(1,128)S(1)}, u32[]{:S(2)}, u32[]{:S(2)}) collective-permute-start(f32[18,1,256]{2,1,0:T(1,128)S(1)} %get-tuple-element.65), channel_id=1, source_target_pairs={{0,2},{1,3},{4,6},{5,7},{8,10},{9,11},{12,14},{13,15},{16,18},{17,... | collective-permute-start | bytes 55304 | tf_op jit(solution)/shard_map/ppermute | solution.py:21
  276.1 4.6 %bitcast_dynamic-update-slice_fusion = f32[6,16,32,256]{3,2,1,0:T(8,128)} fusion(f32[6,16,32,256]{3,2,1,0:T(8,128)} %bitcast_dynamic-update-slice_fusion.1, f32[16,32,256]{2,1,0:T(8,128)S(1)} %copy-done.21, f32[16,32,256]{2,1,0:T(8,128)S(1)} %copy-done, pred[16,32,256]{2,1,0:T(8,128)(4,1)} %get-tuple-element.28, f32[]{:T(128)} %bitcast.13, ...), kind=kLoop, calls=%fused_computation.160 | loop fusion | flops 1703936 | bytes 2099200 | tf_op jit(solution)/shard_map/stack | solution.py:107
  281.0 1.4 collective-permute-start.28
  282.4 3.1 collective-permute-start.29
  286.6 1.9 collective-permute-start.6
  292.2 4.1 %collective-permute-done.7 = f32[6,1,32,256]{3,2,1,0:T(8,128)S(1)} collective-permute-done((f32[6,1,32,256]{3,2,1,0:T(8,128)S(1)}, f32[6,1,32,256]{3,2,1,0:T(8,128)S(1)}, u32[]{:S(2)}, u32[]{:S(2)}) %collective-permute-start.7) | collective-permute-done | bytes 196640 | tf_op jit(solution)/shard_map/ppermute | solution.py:24
  300.2 30.1 %psum.47 = f32[]{:T(128)} all-reduce(f32[]{:T(128)} %fusion.7), channel_id=1, replica_groups=mesh['case'=2,'gx'=4,'gy'=2,'gz'=2] {'gx','gy','gz'}, use_global_device_ids=true, to_apply=%region_11.12 | all-reduce | flops 1 | bytes 8 | tf_op jit(solution)/shard_map/psum | solution.py:128
  331.7 2.7 pad_maximum_fusion.2
  334.5 2.8 fusion.76
  337.2 2.5 copy.43
  339.8 1.8 collective-permute-start.10
  341.6 3.1 copy.44
  344.7 1.5 collective-permute-start.11
  346.2 2.0 add_maximum_fusion
  348.2 2.2 copy.45
  350.4 3.1 copy.46
  353.5 7.5 %pad_maximum_fusion = f32[6,18,34,258]{3,2,1,0:T(8,128)S(1)} fusion(f32[6,18,34,1]{3,2,1,0:T(8,128)} %copy.46, f32[6,18,1,256]{3,2,1,0:T(1,128)} %copy-done.32, f32[6,1,32,256]{3,2,1,0:T(8,128)S(1)} %copy-done.26, f32[6,16,32,256]{3,2,1,0:T(8,128)} %bitcast_dynamic-update-slice_fusion, f32[6,1,32,256]{3,2,1,0:T(8,128)S(1)} %copy-done.24, ...), kind=kLoop, calls=%fused_computation | loop fusion | flops 5684256 | bytes 7579008 | tf_op jit(solution)/shard_map/concatenate | solution.py:25
  362.8 4.2 %fusion.61 = (f32[1,16,32,256]{3,2,1,0:T(8,128)S(1)}, f32[16,32,256]{2,1,0:T(8,128)S(1)}) fusion(f32[3,16,32,256]{3,2,1,0:T(8,128)S(1)} %copy-done.1, pred[16,32,256]{2,1,0:T(8,128)(4,1)S(1)} %copy-done.18, f32[]{:T(128)} %bitcast.27, pred[16,32,256]{2,1,0:T(8,128)(4,1)S(1)} %copy-done.16, f32[]{:T(128)} %bitcast.26, ...), kind=kLoop, calls=%fused_computation.167 | loop fusion | flops 2752512 | bytes 6291476 | tf_op jit(solution)/shard_map/stack | solution.py:136
  367.0 4.1 %fusion.60 = (f32[1,16,32,256]{3,2,1,0:T(8,128)S(1)}, f32[16,32,256]{2,1,0:T(8,128)S(1)}) fusion(f32[3,16,32,256]{3,2,1,0:T(8,128)S(1)} %copy-done.1, pred[16,32,256]{2,1,0:T(8,128)(4,1)S(1)} %copy-done.18, f32[]{:T(128)} %bitcast.27, pred[16,32,256]{2,1,0:T(8,128)(4,1)S(1)} %copy-done.16, f32[]{:T(128)} %bitcast.26, ...), kind=kLoop, calls=%fused_computation.159 | loop fusion | flops 2752512 | bytes 6291476 | tf_op jit(solution)/shard_map/stack | solution.py:136
  371.1 4.2 %fusion.59 = (f32[1,16,32,256]{3,2,1,0:T(8,128)S(1)}, f32[16,32,256]{2,1,0:T(8,128)S(1)}) fusion(f32[3,16,32,256]{3,2,1,0:T(8,128)S(1)} %copy-done.1, pred[16,32,256]{2,1,0:T(8,128)(4,1)S(1)} %copy-done.18, f32[]{:T(128)} %bitcast.27, pred[16,32,256]{2,1,0:T(8,128)(4,1)S(1)} %copy-done.16, f32[]{:T(128)} %bitcast.26, ...), kind=kLoop, calls=%fused_computation.157 | loop fusion | flops 2752512 | bytes 6291476 | tf_op jit(solution)/shard_map/stack | solution.py:136
  375.3 1.9 pad_maximum_fusion.4
  (124 shorter events, 26.1 us)
Async XLA Ops:
  0.6 23.7 %copy-start = (f32[16,32,256]{2,1,0:T(8,128)S(1)}, f32[16,32,256]{2,1,0:T(8,128)}, u32[]{:S(2)}) copy-start(f32[16,32,256]{2,1,0:T(8,128)} %param.11) | copy-start | bytes 1572868
  0.6 13.0 %copy-start.1 = (f32[3,16,32,256]{3,2,1,0:T(8,128)S(1)}, f32[3,16,32,256]{3,2,1,0:T(8,128)}, u32[]{:S(2)}) copy-start(f32[3,16,32,256]{3,2,1,0:T(8,128)} %param.9) | copy-start | bytes 4718596
  1.8 7.7 %collective-permute-start = (f32[4,1,32,256]{3,2,1,0:T(8,128)S(1)}, f32[4,1,32,256]{3,2,1,0:T(8,128)S(1)}, u32[]{:S(2)}, u32[]{:S(2)}) collective-permute-start(f32[4,1,32,256]{3,2,1,0:T(8,128)S(1)} %get-tuple-element.57), channel_id=1, source_target_pairs={{0,4},{4,8},{8,12},{1,5},{5,9},{9,13},{2,6},{6,10},{10,14},{3,7},{... | collective-permute-start | bytes 393224 | tf_op jit(solution)/shard_map/ppermute | solution.py:21
  6.7 6.9 %collective-permute-start.1 = (f32[4,1,32,256]{3,2,1,0:T(8,128)S(1)}, f32[4,1,32,256]{3,2,1,0:T(8,128)S(1)}, u32[]{:S(2)}, u32[]{:S(2)}) collective-permute-start(f32[4,1,32,256]{3,2,1,0:T(8,128)S(1)} %get-tuple-element.58), channel_id=1, source_target_pairs={{4,0},{8,4},{12,8},{5,1},{9,5},{13,9},{6,2},{10,6},{14,10},{7,3},{... | collective-permute-start | bytes 393224 | tf_op jit(solution)/shard_map/ppermute | solution.py:24
  14.7 5.4 %collective-permute-start.2 = (f32[4,18,1,256]{3,2,1,0:T(1,128)S(1)}, f32[4,18,1,256]{3,2,1,0:T(1,128)S(1)}, u32[]{:S(2)}, u32[]{:S(2)}) collective-permute-start(f32[4,18,1,256]{3,2,1,0:T(1,128)S(1)} %get-tuple-element.55), channel_id=1, source_target_pairs={{0,2},{1,3},{4,6},{5,7},{8,10},{9,11},{12,14},{13,15},{16,18},{17,... | collective-permute-start | bytes 221192 | tf_op jit(solution)/shard_map/ppermute | solution.py:21
  18.1 6.2 %collective-permute-start.3 = (f32[4,18,1,256]{3,2,1,0:T(1,128)S(1)}, f32[4,18,1,256]{3,2,1,0:T(1,128)S(1)}, u32[]{:S(2)}, u32[]{:S(2)}) collective-permute-start(f32[4,18,1,256]{3,2,1,0:T(1,128)S(1)} %get-tuple-element.56), channel_id=1, source_target_pairs={{2,0},{3,1},{6,4},{7,5},{10,8},{11,9},{14,12},{15,13},{18,16},{19,... | collective-permute-start | bytes 221192 | tf_op jit(solution)/shard_map/ppermute | solution.py:24
  26.9 6.5 %copy-start.33 = (f32[4,4]{1,0:T(4,128)S(1)}, f32[4,4]{1,0:T(4,128)}, u32[]{:S(2)}) copy-start(f32[4,4]{1,0:T(4,128)} %param.16) | copy-start | bytes 196
  28.9 5.3 %collective-permute-start.4 = (f32[4,18,34,1]{2,0,3,1:T(4,128)S(1)}, f32[4,18,34,1]{2,0,3,1:T(4,128)S(1)}, u32[]{:S(2)}, u32[]{:S(2)}) collective-permute-start(f32[4,18,34,1]{2,0,3,1:T(4,128)S(1)} %copy.39), channel_id=1, source_target_pairs={{0,1},{2,3},{4,5},{6,7},{8,9},{10,11},{12,13},{14,15},{16,17},{18,... | collective-permute-start | bytes 29384 | tf_op jit(solution)/shard_map/ppermute | solution.py:21
  32.1 3.8 collective-permute-start.5
  44.2 1.0 copy-start.28
  44.2 1.2 copy-start.29
  44.2 1.6 copy-start.30
  44.5 13.3 %copy-start.2 = (f32[18,34,258]{2,1,0:T(8,128)}, f32[18,34,258]{2,1,0:T(8,128)S(1)}, u32[]{:S(2)}) copy-start(f32[18,34,258]{2,1,0:T(8,128)S(1)} %get-tuple-element.48) | copy-start | bytes 1894756
  44.5 13.2 %copy-start.9 = (f32[18,34,258]{2,1,0:T(8,128)}, f32[18,34,258]{2,1,0:T(8,128)S(1)}, u32[]{:S(2)}) copy-start(f32[18,34,258]{2,1,0:T(8,128)S(1)} %get-tuple-element.45) | copy-start | bytes 1894756
  57.8 22.9 %copy-start.6 = (f32[16,32,256]{2,1,0:T(8,128)}, f32[16,32,256]{2,1,0:T(8,128)S(1)}, u32[]{:S(2)}) copy-start(f32[16,32,256]{2,1,0:T(8,128)S(1)} %get-tuple-element.20) | copy-start | bytes 1572868
  57.8 22.9 %copy-start.12 = (f32[16,32,256]{2,1,0:T(8,128)}, f32[16,32,256]{2,1,0:T(8,128)S(1)}, u32[]{:S(2)}) copy-start(f32[16,32,256]{2,1,0:T(8,128)S(1)} %get-tuple-element.18) | copy-start | bytes 1572868
  57.8 22.9 %copy-start.20 = (f32[16,32,256]{2,1,0:T(8,128)}, f32[16,32,256]{2,1,0:T(8,128)S(1)}, u32[]{:S(2)}) copy-start(f32[16,32,256]{2,1,0:T(8,128)S(1)} %get-tuple-element.19) | copy-start | bytes 1572868
  57.8 6.0 %collective-permute-start.12 = (f32[1,32,256]{2,1,0:T(8,128)S(1)}, f32[1,32,256]{2,1,0:T(8,128)S(1)}, u32[]{:S(2)}, u32[]{:S(2)}) collective-permute-start(f32[1,32,256]{2,1,0:T(8,128)S(1)} %get-tuple-element.76), channel_id=1, source_target_pairs={{4,0},{8,4},{12,8},{5,1},{9,5},{13,9},{6,2},{10,6},{14,10},{7,3},{... | collective-permute-start | bytes 98312 | tf_op jit(solution)/shard_map/ppermute | solution.py:24
  59.1 6.2 %collective-permute-start.13 = (f32[1,32,256]{2,1,0:T(8,128)S(1)}, f32[1,32,256]{2,1,0:T(8,128)S(1)}, u32[]{:S(2)}, u32[]{:S(2)}) collective-permute-start(f32[1,32,256]{2,1,0:T(8,128)S(1)} %get-tuple-element.75), channel_id=1, source_target_pairs={{0,4},{4,8},{8,12},{1,5},{5,9},{9,13},{2,6},{6,10},{10,14},{3,7},{... | collective-permute-start | bytes 98312 | tf_op jit(solution)/shard_map/ppermute | solution.py:21
  65.3 5.9 %collective-permute-start.14 = (f32[18,1,256]{2,1,0:T(1,128)S(1)}, f32[18,1,256]{2,1,0:T(1,128)S(1)}, u32[]{:S(2)}, u32[]{:S(2)}) collective-permute-start(f32[18,1,256]{2,1,0:T(1,128)S(1)} %get-tuple-element.70), channel_id=1, source_target_pairs={{2,0},{3,1},{6,4},{7,5},{10,8},{11,9},{14,12},{15,13},{18,16},{19,... | collective-permute-start | bytes 55304 | tf_op jit(solution)/shard_map/ppermute | solution.py:24
  66.6 6.0 %collective-permute-start.15 = (f32[18,1,256]{2,1,0:T(1,128)S(1)}, f32[18,1,256]{2,1,0:T(1,128)S(1)}, u32[]{:S(2)}, u32[]{:S(2)}) collective-permute-start(f32[18,1,256]{2,1,0:T(1,128)S(1)} %get-tuple-element.69), channel_id=1, source_target_pairs={{0,2},{1,3},{4,6},{5,7},{8,10},{9,11},{12,14},{13,15},{16,18},{17,... | collective-permute-start | bytes 55304 | tf_op jit(solution)/shard_map/ppermute | solution.py:21
  72.9 4.4 %collective-permute-start.16 = (f32[18,34,1]{2,1,0:T(8,128)S(1)}, f32[18,34,1]{2,1,0:T(8,128)S(1)}, u32[]{:S(2)}, u32[]{:S(2)}) collective-permute-start(f32[18,34,1]{2,1,0:T(8,128)S(1)} %get-tuple-element.63), channel_id=1, source_target_pairs={{1,0},{3,2},{5,4},{7,6},{9,8},{11,10},{13,12},{15,14},{17,16},{19,... | collective-permute-start | bytes 7352 | tf_op jit(solution)/shard_map/ppermute | solution.py:24
  74.2 4.4 %collective-permute-start.17 = (f32[18,34,1]{2,1,0:T(8,128)S(1)}, f32[18,34,1]{2,1,0:T(8,128)S(1)}, u32[]{:S(2)}, u32[]{:S(2)}) collective-permute-start(f32[18,34,1]{2,1,0:T(8,128)S(1)} %get-tuple-element.64), channel_id=1, source_target_pairs={{0,1},{2,3},{4,5},{6,7},{8,9},{10,11},{12,13},{14,15},{16,17},{18,... | collective-permute-start | bytes 7352 | tf_op jit(solution)/shard_map/ppermute | solution.py:21
  154.0 32.5 %copy-start.10 = (f32[16,32,256]{2,1,0:T(8,128)}, f32[16,32,256]{2,1,0:T(8,128)S(1)}, u32[]{:S(2)}) copy-start(f32[16,32,256]{2,1,0:T(8,128)S(1)} %multiply_add_fusion.1) | copy-start | bytes 1572868
  154.1 20.0 %copy-start.3 = (f32[18,34,258]{2,1,0:T(8,128)S(1)}, f32[18,34,258]{2,1,0:T(8,128)}, u32[]{:S(2)}) copy-start(f32[18,34,258]{2,1,0:T(8,128)} %copy-done.2) | copy-start | bytes 1894756
  154.1 20.0 %copy-start.15 = (pred[16,32,256]{2,1,0:T(8,128)(4,1)S(1)}, pred[16,32,256]{2,1,0:T(8,128)(4,1)}, u32[]{:S(2)}) copy-start(pred[16,32,256]{2,1,0:T(8,128)(4,1)} %get-tuple-element.27) | copy-start | bytes 393220
  154.1 20.0 %copy-start.17 = (pred[16,32,256]{2,1,0:T(8,128)(4,1)S(1)}, pred[16,32,256]{2,1,0:T(8,128)(4,1)}, u32[]{:S(2)}) copy-start(pred[16,32,256]{2,1,0:T(8,128)(4,1)} %get-tuple-element.28) | copy-start | bytes 393220
  154.1 14.0 %collective-permute-start.18 = (f32[1,32,256]{2,1,0:T(8,128)S(1)}, f32[1,32,256]{2,1,0:T(8,128)S(1)}, u32[]{:S(2)}, u32[]{:S(2)}) collective-permute-start(f32[1,32,256]{2,1,0:T(8,128)S(1)} %get-tuple-element.74), channel_id=1, source_target_pairs={{4,0},{8,4},{12,8},{5,1},{9,5},{13,9},{6,2},{10,6},{14,10},{7,3},{... | collective-permute-start | bytes 98312 | tf_op jit(solution)/shard_map/ppermute | solution.py:24
  155.5 12.6 %collective-permute-start.19 = (f32[1,32,256]{2,1,0:T(8,128)S(1)}, f32[1,32,256]{2,1,0:T(8,128)S(1)}, u32[]{:S(2)}, u32[]{:S(2)}) collective-permute-start(f32[1,32,256]{2,1,0:T(8,128)S(1)} %get-tuple-element.73), channel_id=1, source_target_pairs={{0,4},{4,8},{8,12},{1,5},{5,9},{9,13},{2,6},{6,10},{10,14},{3,7},{... | collective-permute-start | bytes 98312 | tf_op jit(solution)/shard_map/ppermute | solution.py:21
  168.2 8.9 %collective-permute-start.20 = (f32[18,1,256]{2,1,0:T(1,128)S(1)}, f32[18,1,256]{2,1,0:T(1,128)S(1)}, u32[]{:S(2)}, u32[]{:S(2)}) collective-permute-start(f32[18,1,256]{2,1,0:T(1,128)S(1)} %get-tuple-element.68), channel_id=1, source_target_pairs={{2,0},{3,1},{6,4},{7,5},{10,8},{11,9},{14,12},{15,13},{18,16},{19,... | collective-permute-start | bytes 55304 | tf_op jit(solution)/shard_map/ppermute | solution.py:24
  169.5 7.6 %collective-permute-start.21 = (f32[18,1,256]{2,1,0:T(1,128)S(1)}, f32[18,1,256]{2,1,0:T(1,128)S(1)}, u32[]{:S(2)}, u32[]{:S(2)}) collective-permute-start(f32[18,1,256]{2,1,0:T(1,128)S(1)} %get-tuple-element.67), channel_id=1, source_target_pairs={{0,2},{1,3},{4,6},{5,7},{8,10},{9,11},{12,14},{13,15},{16,18},{17,... | collective-permute-start | bytes 55304 | tf_op jit(solution)/shard_map/ppermute | solution.py:21
  177.1 9.5 %copy-start.7 = (f32[16,32,256]{2,1,0:T(8,128)S(1)}, f32[16,32,256]{2,1,0:T(8,128)}, u32[]{:S(2)}) copy-start(f32[16,32,256]{2,1,0:T(8,128)} %copy-done.6) | copy-start | bytes 1572868
  177.4 9.2 %collective-permute-start.22 = (f32[18,34,1]{2,1,0:T(8,128)S(1)}, f32[18,34,1]{2,1,0:T(8,128)S(1)}, u32[]{:S(2)}, u32[]{:S(2)}) collective-permute-start(f32[18,34,1]{2,1,0:T(8,128)S(1)} %get-tuple-element.61), channel_id=1, source_target_pairs={{1,0},{3,2},{5,4},{7,6},{9,8},{11,10},{13,12},{15,14},{17,16},{19,... | collective-permute-start | bytes 7352 | tf_op jit(solution)/shard_map/ppermute | solution.py:24
  178.7 7.9 %collective-permute-start.23 = (f32[18,34,1]{2,1,0:T(8,128)S(1)}, f32[18,34,1]{2,1,0:T(8,128)S(1)}, u32[]{:S(2)}, u32[]{:S(2)}) collective-permute-start(f32[18,34,1]{2,1,0:T(8,128)S(1)} %get-tuple-element.62), channel_id=1, source_target_pairs={{0,1},{2,3},{4,5},{6,7},{8,9},{10,11},{12,13},{14,15},{16,17},{18,... | collective-permute-start | bytes 7352 | tf_op jit(solution)/shard_map/ppermute | solution.py:21
  184.9 1.6 copy-start.4
  186.6 71.7 %copy-start.8 = (f32[16,32,256]{2,1,0:T(8,128)S(1)}, f32[16,32,256]{2,1,0:T(8,128)}, u32[]{:S(2)}) copy-start(f32[16,32,256]{2,1,0:T(8,128)} %copy-done.6) | copy-start | bytes 1572868
  188.6 69.7 %copy-start.11 = (f32[16,32,256]{2,1,0:T(8,128)S(1)}, f32[16,32,256]{2,1,0:T(8,128)}, u32[]{:S(2)}) copy-start(f32[16,32,256]{2,1,0:T(8,128)} %copy-done.10) | copy-start | bytes 1572868
  258.3 7.4 %copy-start.22 = (f32[16,32,256]{2,1,0:T(8,128)S(1)}, f32[16,32,256]{2,1,0:T(8,128)}, u32[]{:S(2)}) copy-start(f32[16,32,256]{2,1,0:T(8,128)} %get-tuple-element.23) | copy-start | bytes 1572868
  258.3 17.8 %copy-start.21 = (f32[16,32,256]{2,1,0:T(8,128)S(1)}, f32[16,32,256]{2,1,0:T(8,128)}, u32[]{:S(2)}) copy-start(f32[16,32,256]{2,1,0:T(8,128)} %get-tuple-element.22) | copy-start | bytes 1572868
  259.8 30.1 %copy-start.14 = (f32[16,32,256]{2,1,0:T(8,128)}, f32[16,32,256]{2,1,0:T(8,128)S(1)}, u32[]{:S(2)}) copy-start(f32[16,32,256]{2,1,0:T(8,128)S(1)} %multiply_add_fusion) | copy-start | bytes 1572868
  259.8 10.4 %collective-permute-start.24 = (f32[1,32,256]{2,1,0:T(8,128)S(1)}, f32[1,32,256]{2,1,0:T(8,128)S(1)}, u32[]{:S(2)}, u32[]{:S(2)}) collective-permute-start(f32[1,32,256]{2,1,0:T(8,128)S(1)} %get-tuple-element.72), channel_id=1, source_target_pairs={{4,0},{8,4},{12,8},{5,1},{9,5},{13,9},{6,2},{10,6},{14,10},{7,3},{... | collective-permute-start | bytes 98312 | tf_op jit(solution)/shard_map/ppermute | solution.py:24
  261.1 9.1 %collective-permute-start.25 = (f32[1,32,256]{2,1,0:T(8,128)S(1)}, f32[1,32,256]{2,1,0:T(8,128)S(1)}, u32[]{:S(2)}, u32[]{:S(2)}) collective-permute-start(f32[1,32,256]{2,1,0:T(8,128)S(1)} %get-tuple-element.71), channel_id=1, source_target_pairs={{0,4},{4,8},{8,12},{1,5},{5,9},{9,13},{2,6},{6,10},{10,14},{3,7},{... | collective-permute-start | bytes 98312 | tf_op jit(solution)/shard_map/ppermute | solution.py:21
  270.3 10.4 %collective-permute-start.26 = (f32[18,1,256]{2,1,0:T(1,128)S(1)}, f32[18,1,256]{2,1,0:T(1,128)S(1)}, u32[]{:S(2)}, u32[]{:S(2)}) collective-permute-start(f32[18,1,256]{2,1,0:T(1,128)S(1)} %get-tuple-element.66), channel_id=1, source_target_pairs={{2,0},{3,1},{6,4},{7,5},{10,8},{11,9},{14,12},{15,13},{18,16},{19,... | collective-permute-start | bytes 55304 | tf_op jit(solution)/shard_map/ppermute | solution.py:24
  271.6 9.1 %collective-permute-start.27 = (f32[18,1,256]{2,1,0:T(1,128)S(1)}, f32[18,1,256]{2,1,0:T(1,128)S(1)}, u32[]{:S(2)}, u32[]{:S(2)}) collective-permute-start(f32[18,1,256]{2,1,0:T(1,128)S(1)} %get-tuple-element.65), channel_id=1, source_target_pairs={{0,2},{1,3},{4,6},{5,7},{8,10},{9,11},{12,14},{13,15},{16,18},{17,... | collective-permute-start | bytes 55304 | tf_op jit(solution)/shard_map/ppermute | solution.py:21
  280.7 15.6 %copy-start.5 = (f32[6,16,32,256]{3,2,1,0:T(8,128)S(1)}, f32[6,16,32,256]{3,2,1,0:T(8,128)}, u32[]{:S(2)}) copy-start(f32[6,16,32,256]{3,2,1,0:T(8,128)} %bitcast_dynamic-update-slice_fusion) | copy-start | bytes 9437188
  281.0 8.8 %collective-permute-start.28 = (f32[18,34,1]{2,1,0:T(8,128)S(1)}, f32[18,34,1]{2,1,0:T(8,128)S(1)}, u32[]{:S(2)}, u32[]{:S(2)}) collective-permute-start(f32[18,34,1]{2,1,0:T(8,128)S(1)} %get-tuple-element.59), channel_id=1, source_target_pairs={{1,0},{3,2},{5,4},{7,6},{9,8},{11,10},{13,12},{15,14},{17,16},{19,... | collective-permute-start | bytes 7352 | tf_op jit(solution)/shard_map/ppermute | solution.py:24
  282.4 7.4 %collective-permute-start.29 = (f32[18,34,1]{2,1,0:T(8,128)S(1)}, f32[18,34,1]{2,1,0:T(8,128)S(1)}, u32[]{:S(2)}, u32[]{:S(2)}) collective-permute-start(f32[18,34,1]{2,1,0:T(8,128)S(1)} %get-tuple-element.60), channel_id=1, source_target_pairs={{0,1},{2,3},{4,5},{6,7},{8,9},{10,11},{12,13},{14,15},{16,17},{18,... | collective-permute-start | bytes 7352 | tf_op jit(solution)/shard_map/ppermute | solution.py:21
  286.5 13.0 %copy-start.34 = (f32[3]{0:T(128)S(1)}, f32[3]{0:T(128)}, u32[]{:S(2)}) copy-start(f32[3]{0:T(128)} %param.17) | copy-start | bytes 40
  286.6 5.6 %collective-permute-start.6 = (f32[6,1,32,256]{3,2,1,0:T(8,128)S(1)}, f32[6,1,32,256]{3,2,1,0:T(8,128)S(1)}, u32[]{:S(2)}, u32[]{:S(2)}) collective-permute-start(f32[6,1,32,256]{3,2,1,0:T(8,128)S(1)} %get-tuple-element.51), channel_id=1, source_target_pairs={{0,4},{4,8},{8,12},{1,5},{5,9},{9,13},{2,6},{6,10},{10,14},{3,7},{... | collective-permute-start | bytes 589832 | tf_op jit(solution)/shard_map/ppermute | solution.py:21
  288.5 7.8 %collective-permute-start.7 = (f32[6,1,32,256]{3,2,1,0:T(8,128)S(1)}, f32[6,1,32,256]{3,2,1,0:T(8,128)S(1)}, u32[]{:S(2)}, u32[]{:S(2)}) collective-permute-start(f32[6,1,32,256]{3,2,1,0:T(8,128)S(1)} %get-tuple-element.52), channel_id=1, source_target_pairs={{4,0},{8,4},{12,8},{5,1},{9,5},{13,9},{6,2},{10,6},{14,10},{7,3},{... | collective-permute-start | bytes 589832 | tf_op jit(solution)/shard_map/ppermute | solution.py:24
  292.2 4.3 %copy-start.23 = (f32[6,1,32,256]{3,2,1,0:T(8,128)}, f32[6,1,32,256]{3,2,1,0:T(8,128)S(1)}, u32[]{:S(2)}) copy-start(f32[6,1,32,256]{3,2,1,0:T(8,128)S(1)} %collective-permute-done.6) | copy-start | bytes 589828
  297.0 34.7 %collective-permute-start.8 = (f32[6,18,1,256]{3,2,1,0:T(1,128)S(1)}, f32[6,18,1,256]{3,2,1,0:T(1,128)S(1)}, u32[]{:S(2)}, u32[]{:S(2)}) collective-permute-start(f32[6,18,1,256]{3,2,1,0:T(1,128)S(1)} %get-tuple-element.49), channel_id=1, source_target_pairs={{0,2},{1,3},{4,6},{5,7},{8,10},{9,11},{12,14},{13,15},{16,18},{17,... | collective-permute-start | bytes 331784 | tf_op jit(solution)/shard_map/ppermute | solution.py:21
  298.3 33.5 %collective-permute-start.9 = (f32[6,18,1,256]{3,2,1,0:T(1,128)S(1)}, f32[6,18,1,256]{3,2,1,0:T(1,128)S(1)}, u32[]{:S(2)}, u32[]{:S(2)}) collective-permute-start(f32[6,18,1,256]{3,2,1,0:T(1,128)S(1)} %get-tuple-element.50), channel_id=1, source_target_pairs={{2,0},{3,1},{6,4},{7,5},{10,8},{11,9},{14,12},{15,13},{18,16},{19,... | collective-permute-start | bytes 331784 | tf_op jit(solution)/shard_map/ppermute | solution.py:24
  331.7 2.8 copy-start.31
  331.7 2.7 copy-start.32
  337.2 8.9 %copy-start.13 = (f32[16,32,256]{2,1,0:T(8,128)S(1)}, f32[16,32,256]{2,1,0:T(8,128)}, u32[]{:S(2)}) copy-start(f32[16,32,256]{2,1,0:T(8,128)} %copy-done.12) | copy-start | bytes 1572868
  339.8 8.4 %collective-permute-start.10 = (f32[6,18,34,1]{2,3,1,0:T(1,128)S(1)}, f32[6,18,34,1]{2,3,1,0:T(1,128)S(1)}, u32[]{:S(2)}, u32[]{:S(2)}) collective-permute-start(f32[6,18,34,1]{2,3,1,0:T(1,128)S(1)} %copy.43), channel_id=1, source_target_pairs={{0,1},{2,3},{4,5},{6,7},{8,9},{10,11},{12,13},{14,15},{16,17},{18,... | collective-permute-start | bytes 44072 | tf_op jit(solution)/shard_map/ppermute | solution.py:21
  344.7 5.8 %collective-permute-start.11 = (f32[6,18,34,1]{2,3,1,0:T(1,128)}, f32[6,18,34,1]{2,3,1,0:T(1,128)}, u32[]{:S(2)}, u32[]{:S(2)}) collective-permute-start(f32[6,18,34,1]{2,3,1,0:T(1,128)} %copy.44), channel_id=1, source_target_pairs={{1,0},{3,2},{5,4},{7,6},{9,8},{11,10},{13,12},{15,14},{17,16},{19,... | collective-permute-start | bytes 44072 | tf_op jit(solution)/shard_map/ppermute | solution.py:24
  348.2 5.3 %copy-start.24 = (f32[6,1,32,256]{3,2,1,0:T(8,128)S(1)}, f32[6,1,32,256]{3,2,1,0:T(8,128)}, u32[]{:S(2)}) copy-start(f32[6,1,32,256]{3,2,1,0:T(8,128)} %copy-done.23) | copy-start | bytes 589828
  348.2 5.3 %copy-start.26 = (f32[6,1,32,256]{3,2,1,0:T(8,128)S(1)}, f32[6,1,32,256]{3,2,1,0:T(8,128)}, u32[]{:S(2)}) copy-start(f32[6,1,32,256]{3,2,1,0:T(8,128)} %copy-done.25) | copy-start | bytes 589828
  361.0 0.9 copy-start.16
  361.0 1.0 copy-start.18
  361.0 1.2 copy-start.19
  361.1 1.7 copy-start.27
  (1 other events, 0.7 us)
where the time goes:
time: 380 us; the launch traced here: 377 us
  blocking collectives  157 us (41%)
  other arithmetic  89.6 us (24%)
  starting transfers between devices  71.1 us (19%)
  local copies, waits for them, and re-layouts  31.6 us (8%)
  waiting for transfers between devices  20.1 us (5%)
  between operations  7.93 us (2%)
    psum x3, blocking collectives, inner_rz(): return lax.psum(jnp.sum(residual * precond), ('gx', 'gy', 'gz'))  96.5 us
    psum x2, blocking collectives, per_device(): alpha = norm_now / lax.psum(jnp.sum(direction * image), ('gx', 'gy', 'gz'))  60.2 us
    ppermute x15, starting transfers between devices, padded_2(): lax.ppermute(lax.slice_in_dim(block, block.shape[dim] - width, None, axis...  51.3 us
    unnamed x5, other arithmetic  23.4 us
    ppermute x15, starting transfers between devices, padded_2(): lax.ppermute(lax.slice_in_dim(block, 0, width, axis=dim), axis, backward)  19.8 us
    concatenate x10, other arithmetic, padded_2(): block = jnp.concatenate([low, block, high], axis=dim)  17.6 us
    another operation x4, other arithmetic, per_device(): jnp.stack(new_disp)  14.4 us
    ppermute x15, waiting for transfers between devices, padded_2(): lax.ppermute(lax.slice_in_dim(block, 0, width, axis=dim), axis, backward)  12.7 us
  transfers between devices with their start and end apart: 30, of which 10 were waited for; matrix products, arithmetic and copies ran while one was open for 10% of the time, Pallas kernels for 0%

commit v1 on v0

v1 whole, which is shorter than its diff:
```python
import functools
import jax
import jax.numpy as jnp
from jax import lax
from jax.experimental import pallas as pl
from jax.experimental.pallas import tpu as pltpu
from jax.sharding import PartitionSpec as P

TIME_STEP = 0.1
KAPPA_COEF = 0.5
NOTCH_LOAD = 20.0
STIFF_FLOOR = 0.001
ALPHA_LOW, ALPHA_HIGH = 0.5, 6.5
VMEM_BYTES = 24 * 1024 * 1024
F32 = jnp.float32


def iota2(shape, dim):
    return lax.broadcasted_iota(jnp.int32, shape, dim)


def pick(flag, when, other):
    return jnp.where(flag, when, other)


class Sides:
    def __init__(self, pos, refs, plan):
        self.first_y = pos[0] == 0
        self.first_z = pos[1] == 0
        self.xlo, self.xhi = refs[0], refs[1]
        rest = refs[2:]
        self.ys, rest = (rest[:1], rest[1:]) if plan[0] else (rest[:2], rest[2:])
        self.zs = rest

    def along_x(self, ref, lead, field, x):
        count = ref.shape[-3]
        lower = ref[(*lead, jnp.maximum(x - 1, 0))]
        upper = ref[(*lead, jnp.minimum(x + 1, count - 1))]
        lower = jnp.where(x == 0, self.xlo[field], lower)
        upper = jnp.where(x == count - 1, self.xhi[field], upper)
        return upper, lower

    def along_y(self, plane, field, x):
        rows = iota2(plane.shape, 0)
        last = plane.shape[0] - 1
        if len(self.ys) == 1:
            row = self.ys[0][field, pl.ds(x, 1), :]
            lo = jnp.where(self.first_y, 0.0, row)
            hi = jnp.where(self.first_y, row, 0.0)
        else:
            lo = self.ys[0][field, pl.ds(x, 1), :]
            hi = self.ys[1][field, pl.ds(x, 1), :]
        upper = jnp.where(rows == last, hi, pltpu.roll(plane, last, 0))
        lower = jnp.where(rows == 0, lo, pltpu.roll(plane, 1, 0))
        return upper, lower

    def along_z(self, plane, field, x):
        lanes = iota2(plane.shape, 1)
        last = plane.shape[1] - 1
        if len(self.zs) == 1:
            column = self.zs[0][x][:, field : field + 1]
            lo = jnp.where(self.first_z, 0.0, column)
            hi = jnp.where(self.first_z, column, 0.0)
        else:
            lo = self.zs[0][x][:, field : field + 1]
            hi = self.zs[1][x][:, field : field + 1]
        upper = jnp.where(lanes == last, hi, pltpu.roll(plane, last, 1))
        lower = jnp.where(lanes == 0, lo, pltpu.roll(plane, 1, 1))
        return upper, lower


class Faces:
    def __init__(self, pos, refs, plan):
        self.first_y = pos[0] == 0
        self.first_z = pos[1] == 0
        self.pos_z = pos[1]
        self.xlo, self.xhi = refs[0], refs[1]
        rest = refs[2:]
        self.ys, rest = (rest[:1], rest[1:]) if plan[0] else (rest[:2], rest[2:])
        self.zs = rest

    def put_y(self, plane, field, x):
        last = plane.shape[0] - 1
        low, high = plane[0:1, :], plane[last : last + 1, :]
        if len(self.ys) == 1:
            self.ys[0][field, pl.ds(x, 1), :] = jnp.where(self.first_y, high, low)
        else:
            self.ys[0][field, pl.ds(x, 1), :] = low
            self.ys[1][field, pl.ds(x, 1), :] = high

    def put_z(self, planes, x):
        depth = planes[0].shape[1]
        lanes = iota2((planes[0].shape[0], 128), 1)
        if len(self.zs) == 1:
            tile = None
            for field, plane in enumerate(planes):
                part = jnp.where(self.first_z, plane[:, depth - 128 :], plane[:, :128])
                part = pltpu.roll(part, field + 1 - self.pos_z, 1)
                tile = part if tile is None else jnp.where(lanes == field, part, tile)
            self.zs[0][x] = tile
        else:
            for which, (start, shift) in enumerate(((0, 0), (depth - 128, 1))):
                tile = None
                for field, plane in enumerate(planes):
                    part = plane[:, start : start + 128]
                    if field + shift:
                        part = pltpu.roll(part, field + shift, 1)
                    tile = part if tile is None else jnp.where(lanes == field, part, tile)
                self.zs[which][x] = tile


def folded(values):
    total = None
    for start in range(0, values.shape[1], 128):
        part = values[:, start : start + 128]
        total = part if total is None else total + part
    out = None
    for start in range(0, values.shape[0], 8):
        part = total[start : start + 8]
        out = part if out is None else out + part
    return out


def by_label(labels, scalars):
    picked = scalars[0]
    for region in range(1, len(scalars)):
        picked = jnp.where(labels == region, scalars[region], picked)
    return picked


def pack_kernel(plan, pos, disp, damage, *outs):
    faces = Faces(pos, outs, plan)
    count = damage.shape[0]
    for field in range(4):
        src = damage if field == 3 else disp.at[field]
        faces.xlo[field] = src[0]
        faces.xhi[field] = src[count - 1]

    def body(x, carry):
        planes = [disp[0, x], disp[1, x], disp[2, x], damage[x]]
        for field in range(4):
            faces.put_y(planes[field], field, x)
        faces.put_z(planes, x)
        return carry

    lax.fori_loop(0, count, body, 0)


def local_kernel(plan, n_sides, pos, table, disp, damage, history, notch, labels, *refs):
    sides = Sides(pos, refs[:n_sides], plan)
    hist_out, rd_out, v_out, stress_out, mom_out = refs[n_sides : n_sides + 5]
    faces = Faces(pos, refs[n_sides + 5 :], plan)
    count = damage.shape[0]
    regions = table.shape[1]
    lames = [table[0, r] for r in range(regions)]
    shears = [table[1, r] for r in range(regions)]
    fractures = [table[3, r] for r in range(regions)]

    def body(x, total):
        g = []
        for c in range(3):
            plane = disp[c, x]
            row = []
            for upper, lower in (
                sides.along_x(disp, (c,), c, x),
                sides.along_y(plane, c, x),
                sides.along_z(plane, c, x),
            ):
                row.append(0.5 * (upper - lower))
            g.append(row)
        lab = labels[x]
        lame = by_label(lab, lames)
        shear = by_label(lab, shears)
        fracture = by_label(lab, fractures)
        dmg = damage[x]
        degrade = (1.0 - dmg) * (1.0 - dmg) + STIFF_FLOOR
        trace = g[0][0] + g[1][1] + g[2][2]
        strain = [
            g[0][0],
            g[1][1],
            g[2][2],
            0.5 * (g[0][1] + g[1][0]),
            0.5 * (g[0][2] + g[2][0]),
            0.5 * (g[1][2] + g[2][1]),
        ]
        positive = jnp.maximum(trace, 0.0)
        squares = strain[0] * strain[0] + strain[1] * strain[1] + strain[2] * strain[2]
        squares = squares + 2.0 * (
            strain[3] * strain[3] + strain[4] * strain[4] + strain[5] * strain[5]
        )
        energy = 0.5 * lame * positive * positive + shear * squares
        scale = degrade * (2.0 * shear)
        base = degrade * (lame * trace)
        stress = [base + scale * strain[k] if k < 3 else scale * strain[k] for k in range(6)]
        for k in range(6):
            stress_out[k, x] = stress[k]
        hist = jnp.maximum(
            jnp.maximum(history[x], energy), NOTCH_LOAD * notch[x].astype(F32)
        )
        hist_out[x] = hist
        diagonal = fracture + 2.0 * hist + 6.0 * KAPPA_COEF
        rd = 1.0 / diagonal
        rd_out[x] = rd
        xu, xl = sides.along_x(damage, (), 3, x)
        yu, yl = sides.along_y(dmg, 3, x)
        zu, zl = sides.along_z(dmg, 3, x)
        around = ((xu + xl) + (yu + yl)) + (zu + zl)
        residual = 2.0 * hist - (diagonal * dmg - KAPPA_COEF * around)
        v = residual * rd
        v_out[x] = v
        for field, plane in enumerate((v, stress[3], stress[1], stress[5])):
            faces.put_y(plane, field, x)
        faces.put_z((v, stress[4], stress[5], stress[2]), x)
        return total + folded(residual * v)

    total = lax.fori_loop(0, count, body, jnp.zeros((8, 128), F32))
    mom_out[...] = jnp.zeros((8, 128), F32)
    mom_out[0:1, :] = jnp.sum(total, axis=0, keepdims=True)
    for end, ref in ((0, faces.xlo), (count - 1, faces.xhi)):
        ref[0] = v_out[end]
        for slot, k in ((1, 0), (2, 3), (3, 4)):
            ref[slot] = stress_out[k, end]


def apply_kernel(plan, n_sides, step, pos, v, rd, mom, *refs):
    sides = Sides(pos, refs[:n_sides], plan)
    outs = refs[n_sides:]
    last = step == 2
    count = v.shape[0]
    if not last:
        new, mom_out = outs[:2]
        faces = Faces(pos, outs[2:], plan)
    else:
        (mom_out,) = outs

    def body(x, totals):
        plane = v[x]
        xu, xl = sides.along_x(v, (), 0, x)
        yu, yl = sides.along_y(plane, 0, x)
        zu, zl = sides.along_z(plane, 0, x)
        image = KAPPA_COEF * (((xu + xl) + (yu + yl)) + (zu + zl))
        first = totals[0] + folded(plane * image)
        if last:
            return (first,)
        made = image * rd[x]
        new[x] = made
        faces.put_y(made, 0, x)
        faces.put_z((made,), x)
        return (first, totals[1] + folded(made * image))

    zero = jnp.zeros((8, 128), F32)
    totals = lax.fori_loop(0, count, body, (zero,) if last else (zero, zero))
    rows = iota2((8, 128), 0)
    result = mom[...]
    for at, total in enumerate(totals):
        result = jnp.where(
            rows == 2 * step + 1 + at, jnp.sum(total, axis=0, keepdims=True), result
        )
    if last:
        for peer in range(mom_out.shape[0]):
            mom_out[peer] = result
    else:
        mom_out[...] = result
        faces.xlo[0] = new[0]
        faces.xhi[0] = new[count - 1]


def force_kernel(plan, n_sides, pos, table, impact, disp, vel, contact, labels, stress, *refs):
    sides = Sides(pos, refs[:n_sides], plan)
    disp_out, vel_out = refs[n_sides:]
    count = contact.shape[0]
    regions = table.shape[1]
    rates = [table[2, r] for r in range(regions)]

    def body(x, carry):
        loaded = contact[x].astype(F32)
        rate = TIME_STEP / by_label(labels[x], rates)
        for c, (kx, ky, kz) in enumerate(((0, 3, 4), (3, 1, 5), (4, 5, 2))):
            xu, xl = sides.along_x(stress, (kx,), c + 1, x)
            yu, yl = sides.along_y(stress[ky, x], c + 1, x)
            zu, zl = sides.along_z(stress[kz, x], c + 1, x)
            force = 0.5 * (((xu - xl) + (yu - yl)) + (zu - zl))
            speed = vel[c, x] + rate * (force + loaded * impact[c])
            vel_out[c, x] = speed
            disp_out[c, x] = disp[c, x] + TIME_STEP * speed
        return carry

    lax.fori_loop(0, count, body, 0)


def cg_coefficients(k):
    zero, one = jnp.zeros_like(k[0]), jnp.ones_like(k[0])
    z, p, out = [one], [one], [zero, zero, zero]

    def form(a, b, moments):
        total = None
        for i, ai in enumerate(a):
            for j, bj in enumerate(b):
                term = ai * bj * moments[i + j]
                total = term if total is None else total + term
        return total

    energy = [k[j] - k[j + 1] for j in range(5)]
    rz = k[0]
    for step in range(3):
        alpha = jnp.clip(rz / form(p, p, energy), ALPHA_LOW, ALPHA_HIGH)
        out = [o + alpha * (p[i] if i < len(p) else zero) for i, o in enumerate(out)]
        if step == 2:
            break
        image = [(p[i] if i < len(p) else zero) - (p[i - 1] if i else zero) for i in range(len(p) + 1)]
        z = [(z[i] if i < len(z) else zero) - alpha * image[i] for i in range(len(image))]
        new = jnp.maximum(form(z, z, k), 0.0)
        beta = new / rz
        p = [z[i] + beta * (p[i] if i < len(p) else zero) for i in range(len(z))]
        rz = new
    return out


def final_kernel(mom, damage, v0, v1, v2, out):
    sums = jnp.sum(jnp.sum(mom[...], axis=0), axis=1, keepdims=True)
    c0, c1, c2 = cg_coefficients([sums[j : j + 1, :] for j in range(6)])

    def body(x, carry):
        dmg = damage[x]
        out[x] = jnp.maximum(dmg + (c0 * v0[x] + c1 * v1[x] + c2 * v2[x]), dmg)
        return carry

    lax.fori_loop(0, damage.shape[0], body, 0)


def swap_or_shift(axis, faces):
    count = lax.axis_size(axis)
    if len(faces) == 1:
        return [lax.ppermute(faces[0], axis, [(0, 1), (1, 0)])]
    forward = [(i, i + 1) for i in range(count - 1)]
    backward = [(b, a) for a, b in forward]
    return [lax.ppermute(faces[1], axis, forward), lax.ppermute(faces[0], axis, backward)]


def exchange(faces, plan):
    xs, rest = faces[:2], faces[2:]
    ys, zs = (rest[:1], rest[1:]) if plan[0] else (rest[:2], rest[2:])
    return [*swap_or_shift("gx", xs), *swap_or_shift("gy", ys), *swap_or_shift("gz", zs)]


def call(kernel, n_smem, ins, outs, flops):
    vmem = pl.BlockSpec(memory_space=pltpu.VMEM)
    smem = pl.BlockSpec(memory_space=pltpu.SMEM)
    moved = sum(4 * a.size for a in (*ins, *outs))
    return pl.pallas_call(
        kernel,
        out_shape=outs,
        in_specs=[smem] * n_smem + [vmem] * (len(ins) - n_smem),
        out_specs=[vmem] * len(outs),
        compiler_params=pltpu.CompilerParams(vmem_limit_bytes=VMEM_BYTES),
        cost_estimate=pl.CostEstimate(flops=flops, bytes_accessed=moved, transcendentals=0),
    )(*ins)


def per_device(displacement, velocity, damage, history, contact, notch, labels, table, impact):
    nx, ny, nz = damage.shape
    size = damage.size
    plan = (lax.axis_size("gy") == 2, lax.axis_size("gz") == 2)
    pos = jnp.stack([lax.axis_index("gy"), lax.axis_index("gz")]).astype(jnp.int32)

    def arr(*shape):
        return jax.ShapeDtypeStruct(shape, F32)

    def face_shapes(fields):
        out = [arr(fields, ny, nz)] * 2
        out += [arr(fields, nx, nz)] * (1 if plan[0] else 2)
        out += [arr(nx, ny, 128)] * (1 if plan[1] else 2)
        return out

    field = arr(nx, ny, nz)
    sent = call(
        functools.partial(pack_kernel, plan), 1, (pos, displacement, damage), face_shapes(4), size
    )
    got = exchange(sent, plan)
    n_sides = len(got)
    hist, rd, v0, stress, mom, *sent = call(
        functools.partial(local_kernel, plan, n_sides),
        2,
        (pos, table, displacement, damage, history, notch, labels, *got),
        [field, field, field, arr(6, nx, ny, nz), arr(8, 128), *face_shapes(4)],
        150 * size,
    )
    got0 = exchange(sent, plan)
    v1, mom, *sent = call(
        functools.partial(apply_kernel, plan, n_sides, 0),
        1,
        (pos, v0, rd, mom, *got0),
        [field, arr(8, 128), *face_shapes(1)],
        20 * size,
    )
    got1 = exchange(sent, plan)
    new_disp, new_vel = call(
        functools.partial(force_kernel, plan, n_sides),
        3,
        (pos, table, impact, displacement, velocity, contact, labels, stress, *got0),
        [arr(3, nx, ny, nz), arr(3, nx, ny, nz)],
        60 * size,
    )
    v2, mom, *sent = call(
        functools.partial(apply_kernel, plan, n_sides, 1),
        1,
        (pos, v1, rd, mom, *got1),
        [field, arr(8, 128), *face_shapes(1)],
        20 * size,
    )
    got2 = exchange(sent, plan)
    axes = ("gx", "gy", "gz")
    peers = lax.axis_size("gx") * lax.axis_size("gy") * lax.axis_size("gz")
    (spread,) = call(
        functools.partial(apply_kernel, plan, n_sides, 2),
        1,
        (pos, v2, rd, mom, *got2),
        [arr(peers, 8, 128)],
        20 * size,
    )
    mom = lax.all_to_all(spread, axes, 0, 0, tiled=True)
    (damage_new,) = call(final_kernel, 0, (mom, damage, v0, v1, v2), [field], 8 * size)
    return new_disp, new_vel, hist, damage_new


def solution(mesh):
    placed = (
        P(None, ("case", "gx"), "gy", "gz"),
        P(None, ("case", "gx"), "gy", "gz"),
        P(("case", "gx"), "gy", "gz"),
        P(("case", "gx"), "gy", "gz"),
        P(("case", "gx"), "gy", "gz"),
        P(("case", "gx"), "gy", "gz"),
        P(("case", "gx"), "gy", "gz"),
        P(),
        P("case"),
    )
    return jax.shard_map(
        per_device,
        mesh=mesh,
        in_specs=placed,
        out_specs=(
            P(None, ("case", "gx"), "gy", "gz"),
            P(None, ("case", "gx"), "gy", "gz"),
            P(("case", "gx"), "gy", "gz"),
            P(("case", "gx"), "gy", "gz"),
        ),
        check_vma=False,
    )
```

time: 380 us -> 85.9 us (0.23)
  blocking collectives: 157 us -> 0 us
  other arithmetic: 89.6 us -> 0.08 us
  starting transfers between devices: 71.1 us -> 32.2 us
  Pallas kernels: 0 us -> 23.9 us
  local copies, waits for them, and re-layouts: 31.6 us -> 12.9 us
  between operations: 7.93 us -> 0.84 us
  waiting for transfers between devices: 20.1 us -> 15.2 us
    psum x5 -> x0, blocking collectives: 157 us -> none  [the longest x3 96.5 us: inner_rz(): return lax.psum(jnp.sum(residual * precond), ('gx', 'gy', 'gz'))]
    ppermute x30 -> x16, starting transfers between devices: 71.1 us -> 27.4 us  [the longest x4 15.4 us: swap_or_shift(): lax.ppermute(faces[1], axis, forward)]
    pallas_call x0 -> x7, Pallas kernels: none -> 23.9 us  [call(): pl.pallas_call(kernel, out_shape=outs, in_specs=[smem] * n_smem + [vmem]...]
    unnamed x5 -> x0, other arithmetic: 23.4 us -> none
    another operation x5 -> x1, other arithmetic: 19 us -> 0.08 us  [per_device(): jnp.stack([lax.axis_index('gy'), lax.axis_index('gz')]).astype(jnp.int32)]
    concatenate x10 -> x0, other arithmetic: 17.6 us -> none  [padded_2(): block = jnp.concatenate([low, block, high], axis=dim)]
    slice x15 -> x0, local copies, waits for them, and re-layouts: 17.3 us -> none  [the longest x8 10.4 us: padded_2(): lax.slice_in_dim(block, block.shape[dim] - width, None, axis=dim)]
    div x1 -> x0, other arithmetic: 11.9 us -> none  [per_device(): precond = residual / diagonal]
  transfers between devices with their start and end apart: 30 -> 17, of which waited for: 10 -> 8; matrix products, arithmetic and copies ran while one was open for 10% -> 0% of each run, Pallas kernels for 0% -> 6%
where the time goes in v1:
time: 85.9 us; the launch traced here: 85.1 us
  starting transfers between devices  32.2 us (37%)
  Pallas kernels  23.9 us (28%)
  waiting for transfers between devices  15.2 us (18%)
  local copies, waits for them, and re-layouts  12.9 us (15%)
    pallas_call x7, Pallas kernels, call(): pl.pallas_call(kernel, out_shape=outs, in_specs=[smem] * n_smem + [vmem]...  23.9 us
    ppermute x4, starting transfers between devices, swap_or_shift(): lax.ppermute(faces[1], axis, forward)  15.4 us
    unnamed x42, local copies, waits for them, and re-layouts  12.9 us
    ppermute x8, waiting for transfers between devices, swap_or_shift(): return [lax.ppermute(faces[0], axis, [(0, 1), (1, 0)])]  10.1 us
    ppermute x8, starting transfers between devices, swap_or_shift(): return [lax.ppermute(faces[0], axis, [(0, 1), (1, 0)])]  6.81 us
    ppermute x4, starting transfers between devices, swap_or_shift(): lax.ppermute(faces[0], axis, backward)  5.17 us
    ppermute x4, waiting for transfers between devices, swap_or_shift(): lax.ppermute(faces[0], axis, backward)  5.15 us
    all_to_all x1, starting transfers between devices, per_device(): mom = lax.all_to_all(spread, axes, 0, 0, tiled=True)  4.76 us
  transfers between devices with their start and end apart: 17, of which 8 were waited for; matrix products, arithmetic and copies ran while one was open for 0% of the time, Pallas kernels for 6%

profile of v1, /device:TPU:0, one launch (start us, length us, event | category | flops | bytes accessed | tf_op | source)
XLA Modules:
  0.0 85.1 jit_solution(997739676530055912)
XLA Ops:
  0.6 0.0 copy-start.19
  0.6 0.1 pad_add_fusion.pos
  0.7 1.4 %copy-done = f32[3,16,32,256]{3,2,1,0:T(8,128)S(1)} copy-done((f32[3,16,32,256]{3,2,1,0:T(8,128)S(1)}, f32[3,16,32,256]{3,2,1,0:T(8,128)}, u32[]{:S(2)}) %copy-start) | copy-done | bytes 1572888
  2.1 1.0 %copy-done.2 = f32[16,32,256]{2,1,0:T(8,128)S(1)} copy-done((f32[16,32,256]{2,1,0:T(8,128)S(1)}, f32[16,32,256]{2,1,0:T(8,128)}, u32[]{:S(2)}) %copy-start.2) | copy-done | bytes 524312
  3.2 1.9 %shard_map.120 = (f32[4,32,256]{2,1,0:T(8,128)S(1)}, f32[4,32,256]{2,1,0:T(8,128)S(1)}, f32[4,16,256]{2,1,0:T(8,128)S(1)}, f32[16,32,128]{2,1,0:T(8,128)S(1)}) custom-call(s32[2]{0:T(128)S(1)} %pad_add_fusion.pos, f32[3,16,32,256]{3,2,1,0:T(8,128)S(1)} %copy-done, f32[16,32,256]{2,1,0:T(8,128)S(1)} %copy-done.2), custom_call_target="tpu_custom_call" | custom-call | flops 131072 | bytes 2686984 | tf_op jit(solution)/shard_map/pallas_call | solution.py:350
  5.1 0.5 collective-permute-start.3
  5.6 4.5 %collective-permute-start = (f32[4,32,256]{2,1,0:T(8,128)S(1)}, f32[4,32,256]{2,1,0:T(8,128)S(1)}, u32[]{:S(2)}, u32[]{:S(2)}) collective-permute-start(f32[4,32,256]{2,1,0:T(8,128)S(1)} %get-tuple-element.31), channel_id=1, source_target_pairs={{0,4},{4,8},{8,12},{1,5},{5,9},{9,13},{2,6},{6,10},{10,14},{3,7},{... | collective-permute-start | bytes 393224 | tf_op jit(solution)/shard_map/ppermute | solution.py:337
  10.1 1.3 %collective-permute-start.1 = (f32[4,32,256]{2,1,0:T(8,128)S(1)}, f32[4,32,256]{2,1,0:T(8,128)S(1)}, u32[]{:S(2)}, u32[]{:S(2)}) collective-permute-start(f32[4,32,256]{2,1,0:T(8,128)S(1)} %get-tuple-element.32), channel_id=1, source_target_pairs={{4,0},{8,4},{12,8},{5,1},{9,5},{13,9},{6,2},{10,6},{14,10},{7,3},{... | collective-permute-start | bytes 393224 | tf_op jit(solution)/shard_map/ppermute | solution.py:337
  11.4 1.6 %collective-permute-start.2 = (f32[4,16,256]{2,1,0:T(8,128)S(1)}, f32[4,16,256]{2,1,0:T(8,128)S(1)}, u32[]{:S(2)}, u32[]{:S(2)}) collective-permute-start(f32[4,16,256]{2,1,0:T(8,128)S(1)} %get-tuple-element.33), channel_id=1, source_target_pairs={{0,2},{2,0},{1,3},{3,1},{4,6},{6,4},{5,7},{7,5},{8,10},{10,8},{9,1... | collective-permute-start | bytes 196616 | tf_op jit(solution)/shard_map/ppermute | solution.py:334
  13.0 2.8 %collective-permute-done.2.refs_2_ = f32[4,16,256]{2,1,0:T(8,128)S(1)} collective-permute-done((f32[4,16,256]{2,1,0:T(8,128)S(1)}, f32[4,16,256]{2,1,0:T(8,128)S(1)}, u32[]{:S(2)}, u32[]{:S(2)}) %collective-permute-start.2) | collective-permute-done | bytes 65568 | tf_op jit(solution)/shard_map/ppermute | solution.py:334
  15.8 0.0 collective-permute-done.refs_0_
  15.8 1.9 %collective-permute-done.1.refs_1_ = f32[4,32,256]{2,1,0:T(8,128)S(1)} collective-permute-done((f32[4,32,256]{2,1,0:T(8,128)S(1)}, f32[4,32,256]{2,1,0:T(8,128)S(1)}, u32[]{:S(2)}, u32[]{:S(2)}) %collective-permute-start.1) | collective-permute-done | bytes 131104 | tf_op jit(solution)/shard_map/ppermute | solution.py:337
  17.6 0.0 collective-permute-done.3.refs_3_
  17.6 0.0 copy-done.19
  17.6 0.0 copy-done.8
  17.6 0.0 copy-done.14
  17.6 0.0 copy-done.15
  17.7 6.0 %shard_map.121 = (f32[16,32,256]{2,1,0:T(8,128)}, f32[16,32,256]{2,1,0:T(8,128)S(1)}, f32[16,32,256]{2,1,0:T(8,128)S(1)}, f32[6,16,32,256]{3,2,1,0:T(8,128)S(1)}...) custom-call(s32[2]{0:T(128)S(1)} %pad_add_fusion.pos, ...), custom_call_target="tpu_custom_call" | custom-call | flops 19660800 | bytes 9572424 | tf_op jit(solution)/shard_map/pallas_call | solution.py:350
  23.7 1.6 %copy-done.4 = f32[6,16,32,256]{3,2,1,0:T(8,128)} copy-done((f32[6,16,32,256]{3,2,1,0:T(8,128)}, f32[6,16,32,256]{3,2,1,0:T(8,128)S(1)}, u32[]{:S(2)}) %copy-start.4) | copy-done | bytes 3145752
  25.3 0.0 collective-permute-start.7
  25.3 3.5 %collective-permute-start.4 = (f32[4,32,256]{2,1,0:T(8,128)S(1)}, f32[4,32,256]{2,1,0:T(8,128)S(1)}, u32[]{:S(2)}, u32[]{:S(2)}) collective-permute-start(f32[4,32,256]{2,1,0:T(8,128)S(1)} %get-tuple-element.36), channel_id=1, source_target_pairs={{0,4},{4,8},{8,12},{1,5},{5,9},{9,13},{2,6},{6,10},{10,14},{3,7},{... | collective-permute-start | bytes 393224 | tf_op jit(solution)/shard_map/ppermute | solution.py:337
  28.8 1.3 %collective-permute-start.5 = (f32[4,32,256]{2,1,0:T(8,128)S(1)}, f32[4,32,256]{2,1,0:T(8,128)S(1)}, u32[]{:S(2)}, u32[]{:S(2)}) collective-permute-start(f32[4,32,256]{2,1,0:T(8,128)S(1)} %get-tuple-element.37), channel_id=1, source_target_pairs={{4,0},{8,4},{12,8},{5,1},{9,5},{13,9},{6,2},{10,6},{14,10},{7,3},{... | collective-permute-start | bytes 393224 | tf_op jit(solution)/shard_map/ppermute | solution.py:337
  30.1 1.6 %collective-permute-start.6 = (f32[4,16,256]{2,1,0:T(8,128)S(1)}, f32[4,16,256]{2,1,0:T(8,128)S(1)}, u32[]{:S(2)}, u32[]{:S(2)}) collective-permute-start(f32[4,16,256]{2,1,0:T(8,128)S(1)} %get-tuple-element.38), channel_id=1, source_target_pairs={{0,2},{2,0},{1,3},{3,1},{4,6},{6,4},{5,7},{7,5},{8,10},{10,8},{9,1... | collective-permute-start | bytes 196616 | tf_op jit(solution)/shard_map/ppermute | solution.py:334
  31.7 2.8 %collective-permute-done.6.refs_2_ = f32[4,16,256]{2,1,0:T(8,128)S(1)} collective-permute-done((f32[4,16,256]{2,1,0:T(8,128)S(1)}, f32[4,16,256]{2,1,0:T(8,128)S(1)}, u32[]{:S(2)}, u32[]{:S(2)}) %collective-permute-start.6) | collective-permute-done | bytes 65568 | tf_op jit(solution)/shard_map/ppermute | solution.py:334
  34.5 0.0 collective-permute-done.4.refs_0_
  34.5 1.9 %collective-permute-done.5.refs_1_ = f32[4,32,256]{2,1,0:T(8,128)S(1)} collective-permute-done((f32[4,32,256]{2,1,0:T(8,128)S(1)}, f32[4,32,256]{2,1,0:T(8,128)S(1)}, u32[]{:S(2)}, u32[]{:S(2)}) %collective-permute-start.5) | collective-permute-done | bytes 131104 | tf_op jit(solution)/shard_map/ppermute | solution.py:337
  36.4 0.0 collective-permute-done.7.refs_3_
  36.4 3.2 %shard_map.123 = (f32[16,32,256]{2,1,0:T(8,128)S(1)}, f32[8,128]{1,0:T(8,128)S(1)}, f32[1,32,256]{2,1,0:T(8,128)S(1)}, f32[1,32,256]{2,1,0:T(8,128)S(1)}, f32[1,...) custom-call(s32[2]{0:T(128)S(1)} %pad_add_fusion.pos, f32[16,32,256]{2,1,0:T(8,128)S(1)} %get-tuple-element.43.v.v0, ...), custom_call_target="tpu_custom_call" | custom-call | flops 2621440 | bytes 2514952 | tf_op jit(solution)/shard_map/pallas_call | solution.py:350
  39.6 0.0 collective-permute-start.11
  39.6 3.6 %collective-permute-start.8 = (f32[1,32,256]{2,1,0:T(8,128)S(1)}, f32[1,32,256]{2,1,0:T(8,128)S(1)}, u32[]{:S(2)}, u32[]{:S(2)}) collective-permute-start(f32[1,32,256]{2,1,0:T(8,128)S(1)} %get-tuple-element.48), channel_id=1, source_target_pairs={{0,4},{4,8},{8,12},{1,5},{5,9},{9,13},{2,6},{6,10},{10,14},{3,7},{... | collective-permute-start | bytes 98312 | tf_op jit(solution)/shard_map/ppermute | solution.py:337
  43.3 1.3 %collective-permute-start.9 = (f32[1,32,256]{2,1,0:T(8,128)S(1)}, f32[1,32,256]{2,1,0:T(8,128)S(1)}, u32[]{:S(2)}, u32[]{:S(2)}) collective-permute-start(f32[1,32,256]{2,1,0:T(8,128)S(1)} %get-tuple-element.49), channel_id=1, source_target_pairs={{4,0},{8,4},{12,8},{5,1},{9,5},{13,9},{6,2},{10,6},{14,10},{7,3},{... | collective-permute-start | bytes 98312 | tf_op jit(solution)/shard_map/ppermute | solution.py:337
  44.6 1.6 %collective-permute-start.10 = (f32[1,16,256]{2,1,0:T(8,128)S(1)}, f32[1,16,256]{2,1,0:T(8,128)S(1)}, u32[]{:S(2)}, u32[]{:S(2)}) collective-permute-start(f32[1,16,256]{2,1,0:T(8,128)S(1)} %get-tuple-element.50), channel_id=1, source_target_pairs={{0,2},{2,0},{1,3},{3,1},{4,6},{6,4},{5,7},{7,5},{8,10},{10,8},{9,1... | collective-permute-start | bytes 49160 | tf_op jit(solution)/shard_map/ppermute | solution.py:334
  46.1 2.2 %collective-permute-done.10.refs_2_ = f32[1,16,256]{2,1,0:T(8,128)S(1)} collective-permute-done((f32[1,16,256]{2,1,0:T(8,128)S(1)}, f32[1,16,256]{2,1,0:T(8,128)S(1)}, u32[]{:S(2)}, u32[]{:S(2)}) %collective-permute-start.10) | collective-permute-done | bytes 16416 | tf_op jit(solution)/shard_map/ppermute | solution.py:334
  48.4 0.0 collective-permute-done.8.refs_0_
  48.4 0.7 collective-permute-done.9.refs_1_
  49.1 0.0 collective-permute-done.11.refs_3_
  49.1 0.0 copy-done.16
  49.1 0.0 copy-done.11
  49.1 3.2 %shard_map.124 = (f32[16,32,256]{2,1,0:T(8,128)S(1)}, f32[8,128]{1,0:T(8,128)S(1)}, f32[1,32,256]{2,1,0:T(8,128)S(1)}, f32[1,32,256]{2,1,0:T(8,128)S(1)}, f32[1,...) custom-call(s32[2]{0:T(128)S(1)} %pad_add_fusion.pos, f32[16,32,256]{2,1,0:T(8,128)S(1)} %get-tuple-element.46.v.v1, ...), custom_call_target="tpu_custom_call" | custom-call | flops 2621440 | bytes 2269192 | tf_op jit(solution)/shard_map/pallas_call | solution.py:350
  52.3 0.0 collective-permute-start.15
  52.3 3.9 %collective-permute-start.12 = (f32[1,32,256]{2,1,0:T(8,128)S(1)}, f32[1,32,256]{2,1,0:T(8,128)S(1)}, u32[]{:S(2)}, u32[]{:S(2)}) collective-permute-start(f32[1,32,256]{2,1,0:T(8,128)S(1)} %get-tuple-element.54), channel_id=1, source_target_pairs={{0,4},{4,8},{8,12},{1,5},{5,9},{9,13},{2,6},{6,10},{10,14},{3,7},{... | collective-permute-start | bytes 98312 | tf_op jit(solution)/shard_map/ppermute | solution.py:337
  56.2 1.3 %collective-permute-start.13 = (f32[1,32,256]{2,1,0:T(8,128)S(1)}, f32[1,32,256]{2,1,0:T(8,128)S(1)}, u32[]{:S(2)}, u32[]{:S(2)}) collective-permute-start(f32[1,32,256]{2,1,0:T(8,128)S(1)} %get-tuple-element.55), channel_id=1, source_target_pairs={{4,0},{8,4},{12,8},{5,1},{9,5},{13,9},{6,2},{10,6},{14,10},{7,3},{... | collective-permute-start | bytes 98312 | tf_op jit(solution)/shard_map/ppermute | solution.py:337
  57.5 1.6 %collective-permute-start.14 = (f32[1,16,256]{2,1,0:T(8,128)S(1)}, f32[1,16,256]{2,1,0:T(8,128)S(1)}, u32[]{:S(2)}, u32[]{:S(2)}) collective-permute-start(f32[1,16,256]{2,1,0:T(8,128)S(1)} %get-tuple-element.56), channel_id=1, source_target_pairs={{0,2},{2,0},{1,3},{3,1},{4,6},{6,4},{5,7},{7,5},{8,10},{10,8},{9,1... | collective-permute-start | bytes 49160 | tf_op jit(solution)/shard_map/ppermute | solution.py:334
  59.1 2.2 %collective-permute-done.14.refs_2_ = f32[1,16,256]{2,1,0:T(8,128)S(1)} collective-permute-done((f32[1,16,256]{2,1,0:T(8,128)S(1)}, f32[1,16,256]{2,1,0:T(8,128)S(1)}, u32[]{:S(2)}, u32[]{:S(2)}) %collective-permute-start.14) | collective-permute-done | bytes 16416 | tf_op jit(solution)/shard_map/ppermute | solution.py:334
  61.3 0.0 collective-permute-done.12.refs_0_
  61.3 0.7 collective-permute-done.13.refs_1_
  62.0 0.0 collective-permute-done.15.refs_3_
  62.0 2.2 %shard_map.125 = f32[16,8,128]{2,1,0:T(8,128)S(1)} custom-call(s32[2]{0:T(128)S(1)} %pad_add_fusion.pos, f32[16,32,256]{2,1,0:T(8,128)S(1)} %get-tuple-element.52.v.v2, f32[16,32,256]{2,1,0:T(8,128)S(1)} %get-tuple-element.44.rd, f32[8,128]{1,0:T(8,128)S(1)} %get-tuple-element.53.mom, f32[1,32,256]{2,1,0:T(8,128)S(1)} %collective-permute-done.12.refs_0_, ...), custom_call_target="tpu_custom_call" | custom-call | flops 2621440 | bytes 1462280 | tf_op jit(solution)/shard_map/pallas_call | solution.py:350
  64.2 0.0 copy-start.18
  64.2 0.6 copy-done.18
  64.8 4.8 %all-to-all-start = ((f32[16,8,128]{2,1,0:T(8,128)}), f32[16,8,128]{2,1,0:T(8,128)}, u32[]{:S(2)}, u32[]{:S(2)}) async-start(f32[16,8,128]{2,1,0:T(8,128)} %copy-done.18), calls=%async_computation | async-start | bytes 131072 | tf_op jit(solution)/shard_map/all_to_all | solution.py:421
  69.6 0.0 copy-done.6
  69.6 0.0 copy-done.1
  69.6 1.9 %copy-done.5 = f32[6,16,32,256]{3,2,1,0:T(8,128)S(1)} copy-done((f32[6,16,32,256]{3,2,1,0:T(8,128)S(1)}, f32[6,16,32,256]{3,2,1,0:T(8,128)}, u32[]{:S(2)}) %copy-start.5) | copy-done | bytes 3145752
  71.5 1.0 %copy-done.9 = s32[16,32,256]{2,1,0:T(8,128)S(1)} copy-done((s32[16,32,256]{2,1,0:T(8,128)S(1)}, s32[16,32,256]{2,1,0:T(8,128)}, u32[]{:S(2)}) %copy-start.9) | copy-done | bytes 524312
  72.5 1.4 %copy-done.10 = f32[3,16,32,256]{3,2,1,0:T(8,128)S(1)} copy-done((f32[3,16,32,256]{3,2,1,0:T(8,128)S(1)}, f32[3,16,32,256]{3,2,1,0:T(8,128)}, u32[]{:S(2)}) %copy-start.10) | copy-done | bytes 1572888
  74.0 0.9 %copy-done.12 = f32[4,32,256]{2,1,0:T(8,128)S(1)} copy-done((f32[4,32,256]{2,1,0:T(8,128)S(1)}, f32[4,32,256]{2,1,0:T(8,128)}, u32[]{:S(2)}) %copy-start.12) | copy-done | bytes 131096
  74.9 1.0 %copy-done.13 = s32[16,32,256]{2,1,0:T(8,128)S(1)} copy-done((s32[16,32,256]{2,1,0:T(8,128)S(1)}, s32[16,32,256]{2,1,0:T(8,128)}, u32[]{:S(2)}) %copy-start.13) | copy-done | bytes 524312
  75.9 0.8 copy-done.17
  76.7 4.8 %shard_map.122 = (f32[3,16,32,256]{3,2,1,0:T(8,128)}, f32[3,16,32,256]{3,2,1,0:T(8,128)}) custom-call(s32[2]{0:T(128)S(1)} %pad_add_fusion.pos, f32[4,4]{1,0:T(4,128)S(1)} %copy-done.19, f32[3]{0:T(128)S(1)} %copy-done.20, f32[3,16,32,256]{3,2,1,0:T(8,128)S(1)} %copy-done.1, f32[3,16,32,256]{3,2,1,0:T(8,128)S(1)} %copy-done.10, ...), custom_call_target="tpu_custom_call" | custom-call | flops 7864320 | bytes 11075668 | tf_op jit(solution)/shard_map/pallas_call | solution.py:350
  81.6 0.0 all-to-all-done.mom
  81.6 0.0 copy-start.7
  81.6 1.0 %copy-done.7 = f32[16,32,256]{2,1,0:T(8,128)S(1)} copy-done((f32[16,32,256]{2,1,0:T(8,128)S(1)}, f32[16,32,256]{2,1,0:T(8,128)}, u32[]{:S(2)}) %copy-start.7) | copy-done | bytes 524312
  82.6 2.5 %shard_map.126 = f32[16,32,256]{2,1,0:T(8,128)} custom-call(f32[16,8,128]{2,1,0:T(8,128)} %all-to-all-done.mom, f32[16,32,256]{2,1,0:T(8,128)S(1)} %copy-done.3, f32[16,32,256]{2,1,0:T(8,128)S(1)} %get-tuple-element.43.v.v0, f32[16,32,256]{2,1,0:T(8,128)S(1)} %get-tuple-element.46.v.v1, f32[16,32,256]{2,1,0:T(8,128)S(1)} %copy-done.7), custom_call_target="tpu_custom_call" | custom-call | flops 1048576 | bytes 2686976 | tf_op jit(solution)/shard_map/pallas_call | solution.py:350
  (20 shorter events, 0.0 us)
Async XLA Ops:
  0.6 17.0 %copy-start.19 = (f32[4,4]{1,0:T(4,128)S(1)}, f32[4,4]{1,0:T(4,128)}, u32[]{:S(2)}) copy-start(f32[4,4]{1,0:T(4,128)} %table.3) | copy-start | bytes 196
  0.7 1.4 %copy-start = (f32[3,16,32,256]{3,2,1,0:T(8,128)S(1)}, f32[3,16,32,256]{3,2,1,0:T(8,128)}, u32[]{:S(2)}) copy-start(f32[3,16,32,256]{3,2,1,0:T(8,128)} %disp.5) | copy-start | bytes 4718596
  2.1 1.0 %copy-start.2 = (f32[16,32,256]{2,1,0:T(8,128)S(1)}, f32[16,32,256]{2,1,0:T(8,128)}, u32[]{:S(2)}) copy-start(f32[16,32,256]{2,1,0:T(8,128)} %damage.5) | copy-start | bytes 1572868
  3.2 14.5 %copy-start.8 = (s32[16,32,256]{2,1,0:T(8,128)S(1)}, s32[16,32,256]{2,1,0:T(8,128)}, u32[]{:S(2)}) copy-start(s32[16,32,256]{2,1,0:T(8,128)} %labels.3) | copy-start | bytes 1572868
  3.2 14.5 %copy-start.14 = (f32[16,32,256]{2,1,0:T(8,128)S(1)}, f32[16,32,256]{2,1,0:T(8,128)}, u32[]{:S(2)}) copy-start(f32[16,32,256]{2,1,0:T(8,128)} %history.1) | copy-start | bytes 1572868
  3.2 14.5 %copy-start.15 = (s32[16,32,256]{2,1,0:T(8,128)S(1)}, s32[16,32,256]{2,1,0:T(8,128)}, u32[]{:S(2)}) copy-start(s32[16,32,256]{2,1,0:T(8,128)} %notch.1) | copy-start | bytes 1572868
  5.1 12.5 %collective-permute-start.3 = (f32[16,32,128]{2,1,0:T(8,128)S(1)}, f32[16,32,128]{2,1,0:T(8,128)S(1)}, u32[]{:S(2)}, u32[]{:S(2)}) collective-permute-start(f32[16,32,128]{2,1,0:T(8,128)S(1)} %get-tuple-element.34), channel_id=1, source_target_pairs={{0,1},{1,0},{2,3},{3,2},{4,5},{5,4},{6,7},{7,6},{8,9},{9,8},{10,11... | collective-permute-start | bytes 786440 | tf_op jit(solution)/shard_map/ppermute | solution.py:334
  5.6 10.1 %collective-permute-start = (f32[4,32,256]{2,1,0:T(8,128)S(1)}, f32[4,32,256]{2,1,0:T(8,128)S(1)}, u32[]{:S(2)}, u32[]{:S(2)}) collective-permute-start(f32[4,32,256]{2,1,0:T(8,128)S(1)} %get-tuple-element.31), channel_id=1, source_target_pairs={{0,4},{4,8},{8,12},{1,5},{5,9},{9,13},{2,6},{6,10},{10,14},{3,7},{... | collective-permute-start | bytes 393224 | tf_op jit(solution)/shard_map/ppermute | solution.py:337
  10.1 7.5 %collective-permute-start.1 = (f32[4,32,256]{2,1,0:T(8,128)S(1)}, f32[4,32,256]{2,1,0:T(8,128)S(1)}, u32[]{:S(2)}, u32[]{:S(2)}) collective-permute-start(f32[4,32,256]{2,1,0:T(8,128)S(1)} %get-tuple-element.32), channel_id=1, source_target_pairs={{4,0},{8,4},{12,8},{5,1},{9,5},{13,9},{6,2},{10,6},{14,10},{7,3},{... | collective-permute-start | bytes 393224 | tf_op jit(solution)/shard_map/ppermute | solution.py:337
  11.4 4.3 %collective-permute-start.2 = (f32[4,16,256]{2,1,0:T(8,128)S(1)}, f32[4,16,256]{2,1,0:T(8,128)S(1)}, u32[]{:S(2)}, u32[]{:S(2)}) collective-permute-start(f32[4,16,256]{2,1,0:T(8,128)S(1)} %get-tuple-element.33), channel_id=1, source_target_pairs={{0,2},{2,0},{1,3},{3,1},{4,6},{6,4},{5,7},{7,5},{8,10},{10,8},{9,1... | collective-permute-start | bytes 196616 | tf_op jit(solution)/shard_map/ppermute | solution.py:334
  23.7 1.6 %copy-start.4 = (f32[6,16,32,256]{3,2,1,0:T(8,128)}, f32[6,16,32,256]{3,2,1,0:T(8,128)S(1)}, u32[]{:S(2)}) copy-start(f32[6,16,32,256]{3,2,1,0:T(8,128)S(1)} %get-tuple-element.35.stress) | copy-start | bytes 9437188
  25.3 11.0 %collective-permute-start.7 = (f32[16,32,128]{2,1,0:T(8,128)S(1)}, f32[16,32,128]{2,1,0:T(8,128)S(1)}, u32[]{:S(2)}, u32[]{:S(2)}) collective-permute-start(f32[16,32,128]{2,1,0:T(8,128)S(1)} %get-tuple-element.39), channel_id=1, source_target_pairs={{0,1},{1,0},{2,3},{3,2},{4,5},{5,4},{6,7},{7,6},{8,9},{9,8},{10,11... | collective-permute-start | bytes 786440 | tf_op jit(solution)/shard_map/ppermute | solution.py:334
  25.3 9.1 %collective-permute-start.4 = (f32[4,32,256]{2,1,0:T(8,128)S(1)}, f32[4,32,256]{2,1,0:T(8,128)S(1)}, u32[]{:S(2)}, u32[]{:S(2)}) collective-permute-start(f32[4,32,256]{2,1,0:T(8,128)S(1)} %get-tuple-element.36), channel_id=1, source_target_pairs={{0,4},{4,8},{8,12},{1,5},{5,9},{9,13},{2,6},{6,10},{10,14},{3,7},{... | collective-permute-start | bytes 393224 | tf_op jit(solution)/shard_map/ppermute | solution.py:337
  28.8 7.5 %collective-permute-start.5 = (f32[4,32,256]{2,1,0:T(8,128)S(1)}, f32[4,32,256]{2,1,0:T(8,128)S(1)}, u32[]{:S(2)}, u32[]{:S(2)}) collective-permute-start(f32[4,32,256]{2,1,0:T(8,128)S(1)} %get-tuple-element.37), channel_id=1, source_target_pairs={{4,0},{8,4},{12,8},{5,1},{9,5},{13,9},{6,2},{10,6},{14,10},{7,3},{... | collective-permute-start | bytes 393224 | tf_op jit(solution)/shard_map/ppermute | solution.py:337
  30.1 4.3 %collective-permute-start.6 = (f32[4,16,256]{2,1,0:T(8,128)S(1)}, f32[4,16,256]{2,1,0:T(8,128)S(1)}, u32[]{:S(2)}, u32[]{:S(2)}) collective-permute-start(f32[4,16,256]{2,1,0:T(8,128)S(1)} %get-tuple-element.38), channel_id=1, source_target_pairs={{0,2},{2,0},{1,3},{3,1},{4,6},{6,4},{5,7},{7,5},{8,10},{10,8},{9,1... | collective-permute-start | bytes 196616 | tf_op jit(solution)/shard_map/ppermute | solution.py:334
  34.5 14.6 %copy-start.16 = (f32[4,16,256]{2,1,0:T(8,128)}, f32[4,16,256]{2,1,0:T(8,128)S(1)}, u32[]{:S(2)}) copy-start(f32[4,16,256]{2,1,0:T(8,128)S(1)} %collective-permute-done.6.refs_2_) | copy-start | bytes 196612
  36.4 12.7 %copy-start.11 = (f32[4,32,256]{2,1,0:T(8,128)}, f32[4,32,256]{2,1,0:T(8,128)S(1)}, u32[]{:S(2)}) copy-start(f32[4,32,256]{2,1,0:T(8,128)S(1)} %collective-permute-done.5.refs_1_) | copy-start | bytes 393220
  39.6 30.0 %copy-start.1 = (f32[3,16,32,256]{3,2,1,0:T(8,128)S(1)}, f32[3,16,32,256]{3,2,1,0:T(8,128)}, u32[]{:S(2)}) copy-start(f32[3,16,32,256]{3,2,1,0:T(8,128)} %disp.5) | copy-start | bytes 4718596
  39.6 30.0 %copy-start.20 = (f32[3]{0:T(128)S(1)}, f32[3]{0:T(128)}, u32[]{:S(2)}) copy-start(f32[3]{0:T(128)} %impact.1) | copy-start | bytes 40
  39.6 9.5 %collective-permute-start.11 = (f32[16,32,128]{2,1,0:T(8,128)S(1)}, f32[16,32,128]{2,1,0:T(8,128)S(1)}, u32[]{:S(2)}, u32[]{:S(2)}) collective-permute-start(f32[16,32,128]{2,1,0:T(8,128)S(1)} %get-tuple-element.51), channel_id=1, source_target_pairs={{0,1},{1,0},{2,3},{3,2},{4,5},{5,4},{6,7},{7,6},{8,9},{9,8},{10,11... | collective-permute-start | bytes 786440 | tf_op jit(solution)/shard_map/ppermute | solution.py:334
  39.6 8.7 %collective-permute-start.8 = (f32[1,32,256]{2,1,0:T(8,128)S(1)}, f32[1,32,256]{2,1,0:T(8,128)S(1)}, u32[]{:S(2)}, u32[]{:S(2)}) collective-permute-start(f32[1,32,256]{2,1,0:T(8,128)S(1)} %get-tuple-element.48), channel_id=1, source_target_pairs={{0,4},{4,8},{8,12},{1,5},{5,9},{9,13},{2,6},{6,10},{10,14},{3,7},{... | collective-permute-start | bytes 98312 | tf_op jit(solution)/shard_map/ppermute | solution.py:337
  43.3 5.8 %collective-permute-start.9 = (f32[1,32,256]{2,1,0:T(8,128)S(1)}, f32[1,32,256]{2,1,0:T(8,128)S(1)}, u32[]{:S(2)}, u32[]{:S(2)}) collective-permute-start(f32[1,32,256]{2,1,0:T(8,128)S(1)} %get-tuple-element.49), channel_id=1, source_target_pairs={{4,0},{8,4},{12,8},{5,1},{9,5},{13,9},{6,2},{10,6},{14,10},{7,3},{... | collective-permute-start | bytes 98312 | tf_op jit(solution)/shard_map/ppermute | solution.py:337
  44.6 3.8 %collective-permute-start.10 = (f32[1,16,256]{2,1,0:T(8,128)S(1)}, f32[1,16,256]{2,1,0:T(8,128)S(1)}, u32[]{:S(2)}, u32[]{:S(2)}) collective-permute-start(f32[1,16,256]{2,1,0:T(8,128)S(1)} %get-tuple-element.50), channel_id=1, source_target_pairs={{0,2},{2,0},{1,3},{3,1},{4,6},{6,4},{5,7},{7,5},{8,10},{10,8},{9,1... | collective-permute-start | bytes 49160 | tf_op jit(solution)/shard_map/ppermute | solution.py:334
  52.3 17.3 %copy-start.6 = (f32[16,32,256]{2,1,0:T(8,128)}, f32[16,32,256]{2,1,0:T(8,128)S(1)}, u32[]{:S(2)}) copy-start(f32[16,32,256]{2,1,0:T(8,128)S(1)} %get-tuple-element.52.v.v2) | copy-start | bytes 1572868
  52.3 9.7 %collective-permute-start.15 = (f32[16,32,128]{2,1,0:T(8,128)S(1)}, f32[16,32,128]{2,1,0:T(8,128)S(1)}, u32[]{:S(2)}, u32[]{:S(2)}) collective-permute-start(f32[16,32,128]{2,1,0:T(8,128)S(1)} %get-tuple-element.57), channel_id=1, source_target_pairs={{0,1},{1,0},{2,3},{3,2},{4,5},{5,4},{6,7},{7,6},{8,9},{9,8},{10,11... | collective-permute-start | bytes 786440 | tf_op jit(solution)/shard_map/ppermute | solution.py:334
  52.3 9.0 %collective-permute-start.12 = (f32[1,32,256]{2,1,0:T(8,128)S(1)}, f32[1,32,256]{2,1,0:T(8,128)S(1)}, u32[]{:S(2)}, u32[]{:S(2)}) collective-permute-start(f32[1,32,256]{2,1,0:T(8,128)S(1)} %get-tuple-element.54), channel_id=1, source_target_pairs={{0,4},{4,8},{8,12},{1,5},{5,9},{9,13},{2,6},{6,10},{10,14},{3,7},{... | collective-permute-start | bytes 98312 | tf_op jit(solution)/shard_map/ppermute | solution.py:337
  56.2 5.8 %collective-permute-start.13 = (f32[1,32,256]{2,1,0:T(8,128)S(1)}, f32[1,32,256]{2,1,0:T(8,128)S(1)}, u32[]{:S(2)}, u32[]{:S(2)}) collective-permute-start(f32[1,32,256]{2,1,0:T(8,128)S(1)} %get-tuple-element.55), channel_id=1, source_target_pairs={{4,0},{8,4},{12,8},{5,1},{9,5},{13,9},{6,2},{10,6},{14,10},{7,3},{... | collective-permute-start | bytes 98312 | tf_op jit(solution)/shard_map/ppermute | solution.py:337
  57.5 3.8 %collective-permute-start.14 = (f32[1,16,256]{2,1,0:T(8,128)S(1)}, f32[1,16,256]{2,1,0:T(8,128)S(1)}, u32[]{:S(2)}, u32[]{:S(2)}) collective-permute-start(f32[1,16,256]{2,1,0:T(8,128)S(1)} %get-tuple-element.56), channel_id=1, source_target_pairs={{0,2},{2,0},{1,3},{3,1},{4,6},{6,4},{5,7},{7,5},{8,10},{10,8},{9,1... | collective-permute-start | bytes 49160 | tf_op jit(solution)/shard_map/ppermute | solution.py:334
  64.2 0.6 copy-start.18
  64.8 16.8 %all-to-all-start = ((f32[16,8,128]{2,1,0:T(8,128)}), f32[16,8,128]{2,1,0:T(8,128)}, u32[]{:S(2)}, u32[]{:S(2)}) async-start(f32[16,8,128]{2,1,0:T(8,128)} %copy-done.18), calls=%async_computation | async-start | bytes 131072 | tf_op jit(solution)/shard_map/all_to_all | solution.py:421
  69.6 1.9 %copy-start.5 = (f32[6,16,32,256]{3,2,1,0:T(8,128)S(1)}, f32[6,16,32,256]{3,2,1,0:T(8,128)}, u32[]{:S(2)}) copy-start(f32[6,16,32,256]{3,2,1,0:T(8,128)} %copy-done.4) | copy-start | bytes 9437188
  71.5 1.0 %copy-start.9 = (s32[16,32,256]{2,1,0:T(8,128)S(1)}, s32[16,32,256]{2,1,0:T(8,128)}, u32[]{:S(2)}) copy-start(s32[16,32,256]{2,1,0:T(8,128)} %labels.3) | copy-start | bytes 1572868
  72.5 1.4 %copy-start.10 = (f32[3,16,32,256]{3,2,1,0:T(8,128)S(1)}, f32[3,16,32,256]{3,2,1,0:T(8,128)}, u32[]{:S(2)}) copy-start(f32[3,16,32,256]{3,2,1,0:T(8,128)} %vel.1) | copy-start | bytes 4718596
  74.0 0.9 %copy-start.12 = (f32[4,32,256]{2,1,0:T(8,128)S(1)}, f32[4,32,256]{2,1,0:T(8,128)}, u32[]{:S(2)}) copy-start(f32[4,32,256]{2,1,0:T(8,128)} %copy-done.11) | copy-start | bytes 393220
  74.9 1.0 %copy-start.13 = (s32[16,32,256]{2,1,0:T(8,128)S(1)}, s32[16,32,256]{2,1,0:T(8,128)}, u32[]{:S(2)}) copy-start(s32[16,32,256]{2,1,0:T(8,128)} %contact.1) | copy-start | bytes 1572868
  75.9 0.8 copy-start.17
  76.7 4.8 %copy-start.3 = (f32[16,32,256]{2,1,0:T(8,128)S(1)}, f32[16,32,256]{2,1,0:T(8,128)}, u32[]{:S(2)}) copy-start(f32[16,32,256]{2,1,0:T(8,128)} %damage.5) | copy-start | bytes 1572868
  81.6 1.0 %copy-start.7 = (f32[16,32,256]{2,1,0:T(8,128)S(1)}, f32[16,32,256]{2,1,0:T(8,128)}, u32[]{:S(2)}) copy-start(f32[16,32,256]{2,1,0:T(8,128)} %copy-done.6) | copy-start | bytes 1572868

commit v2 on v1

--- a/solution.py
+++ b/solution.py
@@ -25,9 +25,11 @@
 
 class Sides:
     def __init__(self, pos, refs, plan):
+        self.swap_x = plan[2]
+        self.odd_x = pos[2] == 1
         self.first_y = pos[0] == 0
         self.first_z = pos[1] == 0
-        self.xlo, self.xhi = refs[0], refs[1]
+        self.xs = refs[:2]
         rest = refs[2:]
         self.ys, rest = (rest[:1], rest[1:]) if plan[0] else (rest[:2], rest[2:])
         self.zs = rest
@@ -36,8 +38,14 @@
         count = ref.shape[-3]
         lower = ref[(*lead, jnp.maximum(x - 1, 0))]
         upper = ref[(*lead, jnp.minimum(x + 1, count - 1))]
-        lower = jnp.where(x == 0, self.xlo[field], lower)
-        upper = jnp.where(x == count - 1, self.xhi[field], upper)
+        first, second = self.xs[0][field], self.xs[1][field]
+        if self.swap_x:
+            lo = jnp.where(self.odd_x, first, second)
+            hi = jnp.where(self.odd_x, second, first)
+        else:
+            lo, hi = first, second
+        lower = jnp.where(x == 0, lo, lower)
+        upper = jnp.where(x == count - 1, hi, upper)
         return upper, lower
 
     def along_y(self, plane, field, x):
@@ -71,13 +79,47 @@
 
 class Faces:
     def __init__(self, pos, refs, plan):
+        self.swap_x = plan[2]
+        self.odd_x = pos[2] == 1
         self.first_y = pos[0] == 0
         self.first_z = pos[1] == 0
         self.pos_z = pos[1]
-        self.xlo, self.xhi = refs[0], refs[1]
+        self.xs = refs[:2]
         rest = refs[2:]
         self.ys, rest = (rest[:1], rest[1:]) if plan[0] else (rest[:2], rest[2:])
         self.zs = rest
+
+    def put_x(self, field, low, high):
+        if self.swap_x:
+            self.xs[0][field] = jnp.where(self.odd_x, low, high)
+            self.xs[1][field] = jnp.where(self.odd_x, high, low)
+        else:
+            self.xs[0][field] = low
+            self.xs[1][field] = high
+
+    def put_low_x(self, field, plane):
+        if self.swap_x:
+            @pl.when(self.odd_x)
+            def _():
+                self.xs[0][field] = plane
+
+            @pl.when(jnp.logical_not(self.odd_x))
+            def _():
+                self.xs[1][field] = plane
+        else:
+            self.xs[0][field] = plane
+
+    def put_high_x(self, field, plane):
+        if self.swap_x:
+            @pl.when(self.odd_x)
+            def _():
+                self.xs[1][field] = plane
+
+            @pl.when(jnp.logical_not(self.odd_x))
+            def _():
+                self.xs[0][field] = plane
+        else:
+            self.xs[1][field] = plane
 
     def put_y(self, plane, field, x):
         last = plane.shape[0] - 1
@@ -109,6 +151,15 @@
                 self.zs[which][x] = tile
 
 
+def unrolled(count, body, carry, many=4):
+    def several(block, carry):
+        for at in range(many):
+            carry = body(block * many + at, carry)
+        return carry
+
+    return lax.fori_loop(0, count // many, several, carry)
+
+
 def folded(values):
     total = None
     for start in range(0, values.shape[1], 128):
@@ -130,33 +181,42 @@
 
 def pack_kernel(plan, pos, disp, damage, *outs):
     faces = Faces(pos, outs, plan)
+    step, steps = pl.program_id(0), pl.num_programs(0)
     count = damage.shape[0]
-    for field in range(4):
-        src = damage if field == 3 else disp.at[field]
-        faces.xlo[field] = src[0]
-        faces.xhi[field] = src[count - 1]
-
-    def body(x, carry):
-        planes = [disp[0, x], disp[1, x], disp[2, x], damage[x]]
+    sources = [disp.at[0], disp.at[1], disp.at[2], damage]
+
+    @pl.when(step == 0)
+    def _():
         for field in range(4):
-            faces.put_y(planes[field], field, x)
-        faces.put_z(planes, x)
-        return carry
-
-    lax.fori_loop(0, count, body, 0)
+            faces.put_low_x(field, sources[field][0])
+
+    @pl.when(step == steps - 1)
+    def _():
+        for field in range(4):
+            faces.put_high_x(field, sources[field][count - 1])
+
+    for at in range(count):
+        planes = [source[at] for source in sources]
+        for field in range(4):
+            faces.put_y(planes[field], field, step * count + at)
+        faces.put_z(planes, at)
 
 
 def local_kernel(plan, n_sides, pos, table, disp, damage, history, notch, labels, *refs):
     sides = Sides(pos, refs[:n_sides], plan)
     hist_out, rd_out, v_out, stress_out, mom_out = refs[n_sides : n_sides + 5]
-    faces = Faces(pos, refs[n_sides + 5 :], plan)
+    faces = Faces(pos, refs[n_sides + 5 : -1], plan)
+    held = refs[-1]
+    step, steps = pl.program_id(0), pl.num_programs(0)
     count = damage.shape[0]
+    block = history.shape[0]
     regions = table.shape[1]
     lames = [table[0, r] for r in range(regions)]
     shears = [table[1, r] for r in range(regions)]
     fractures = [table[3, r] for r in range(regions)]
 
-    def body(x, total):
+    def body(at, total):
+        x = step * block + at
         g = []
         for c in range(3):
             plane = disp[c, x]
@@ -168,7 +228,7 @@
             ):
                 row.append(0.5 * (upper - lower))
             g.append(row)
-        lab = labels[x]
+        lab = labels[at]
         lame = by_label(lab, lames)
         shear = by_label(lab, shears)
         fracture = by_label(lab, fractures)
@@ -195,9 +255,9 @@
         for k in range(6):
             stress_out[k, x] = stress[k]
         hist = jnp.maximum(
-            jnp.maximum(history[x], energy), NOTCH_LOAD * notch[x].astype(F32)
+            jnp.maximum(history[at], energy), NOTCH_LOAD * notch[at].astype(F32)
         )
-        hist_out[x] = hist
+        hist_out[at] = hist
         diagonal = fracture + 2.0 * hist + 6.0 * KAPPA_COEF
         rd = 1.0 / diagonal
         rd_out[x] = rd
@@ -213,18 +273,27 @@
         faces.put_z((v, stress[4], stress[5], stress[2]), x)
         return total + folded(residual * v)
 
-    total = lax.fori_loop(0, count, body, jnp.zeros((8, 128), F32))
-    mom_out[...] = jnp.zeros((8, 128), F32)
-    mom_out[0:1, :] = jnp.sum(total, axis=0, keepdims=True)
-    for end, ref in ((0, faces.xlo), (count - 1, faces.xhi)):
-        ref[0] = v_out[end]
-        for slot, k in ((1, 0), (2, 3), (3, 4)):
-            ref[slot] = stress_out[k, end]
+    total = jnp.where(step == 0, 0.0, held[...])
+    for at in range(block):
+        total = body(at, total)
+    held[...] = total
+
+    @pl.when(step == 0)
+    def _():
+        for slot, src in enumerate((v_out, stress_out.at[0], stress_out.at[3], stress_out.at[4])):
+            faces.put_low_x(slot, src[0])
+
+    @pl.when(step == steps - 1)
+    def _():
+        for slot, src in enumerate((v_out, stress_out.at[0], stress_out.at[3], stress_out.at[4])):
+            faces.put_high_x(slot, src[count - 1])
+        mom_out[...] = jnp.zeros((8, 128), F32)
+        mom_out[0:1, :] = jnp.sum(total, axis=0, keepdims=True)
 
 
 def apply_kernel(plan, n_sides, step, pos, v, rd, mom, *refs):
     sides = Sides(pos, refs[:n_sides], plan)
-    outs = refs[n_sides:]
+    outs = refs[n_sides + (step == 1) :]
     last = step == 2
     count = v.shape[0]
     if not last:
@@ -249,7 +318,7 @@
         return (first, totals[1] + folded(made * image))
 
     zero = jnp.zeros((8, 128), F32)
-    totals = lax.fori_loop(0, count, body, (zero,) if last else (zero, zero))
+    totals = unrolled(count, body, (zero,) if last else (zero, zero))
     rows = iota2((8, 128), 0)
     result = mom[...]
     for at, total in enumerate(totals):
@@ -261,31 +330,28 @@
             mom_out[peer] = result
     else:
         mom_out[...] = result
-        faces.xlo[0] = new[0]
-        faces.xhi[0] = new[count - 1]
+        faces.put_x(0, new[0], new[count - 1])
 
 
 def force_kernel(plan, n_sides, pos, table, impact, disp, vel, contact, labels, stress, *refs):
     sides = Sides(pos, refs[:n_sides], plan)
-    disp_out, vel_out = refs[n_sides:]
-    count = contact.shape[0]
+    disp_out, vel_out, token = refs[n_sides:]
+    token[...] = jnp.zeros((8, 128), F32)
+    step, block = pl.program_id(0), contact.shape[0]
     regions = table.shape[1]
     rates = [table[2, r] for r in range(regions)]
-
-    def body(x, carry):
-        loaded = contact[x].astype(F32)
-        rate = TIME_STEP / by_label(labels[x], rates)
+    for at in range(block):
+        x = step * block + at
+        loaded = contact[at].astype(F32)
+        rate = TIME_STEP / by_label(labels[at], rates)
         for c, (kx, ky, kz) in enumerate(((0, 3, 4), (3, 1, 5), (4, 5, 2))):
             xu, xl = sides.along_x(stress, (kx,), c + 1, x)
             yu, yl = sides.along_y(stress[ky, x], c + 1, x)
             zu, zl = sides.along_z(stress[kz, x], c + 1, x)
             force = 0.5 * (((xu - xl) + (yu - yl)) + (zu - zl))
-            speed = vel[c, x] + rate * (force + loaded * impact[c])
-            vel_out[c, x] = speed
-            disp_out[c, x] = disp[c, x] + TIME_STEP * speed
-        return carry
-
-    lax.fori_loop(0, count, body, 0)
+            speed = vel[c, at] + rate * (force + loaded * impact[c])
+            vel_out[c, at] = speed
+            disp_out[c, at] = disp[c, at] + TIME_STEP * speed
 
 
 def cg_coefficients(k):
@@ -316,20 +382,23 @@
     return out
 
 
-def final_kernel(mom, damage, v0, v1, v2, out):
+def final_kernel(mom, v0, v1, v2, damage, out):
     sums = jnp.sum(jnp.sum(mom[...], axis=0), axis=1, keepdims=True)
     c0, c1, c2 = cg_coefficients([sums[j : j + 1, :] for j in range(6)])
-
-    def body(x, carry):
-        dmg = damage[x]
-        out[x] = jnp.maximum(dmg + (c0 * v0[x] + c1 * v1[x] + c2 * v2[x]), dmg)
-        return carry
-
-    lax.fori_loop(0, damage.shape[0], body, 0)
-
-
-def swap_or_shift(axis, faces):
+    step, block = pl.program_id(0), damage.shape[0]
+    for at in range(block):
+        x, dmg = step * block + at, damage[at]
+        out[at] = jnp.maximum(dmg + (c0 * v0[x] + c1 * v1[x] + c2 * v2[x]), dmg)
+
+
+def swap_or_shift(axis, faces, paired=False):
     count = lax.axis_size(axis)
+    if paired:
+        out = []
+        for start, face in enumerate(faces):
+            pairs = [(i, i + 1) for i in range(start, count - 1, 2)]
+            out.append(lax.ppermute(face, axis, pairs + [(b, a) for a, b in pairs]))
+        return out
     if len(faces) == 1:
         return [lax.ppermute(faces[0], axis, [(0, 1), (1, 0)])]
     forward = [(i, i + 1) for i in range(count - 1)]
@@ -340,18 +409,34 @@
 def exchange(faces, plan):
     xs, rest = faces[:2], faces[2:]
     ys, zs = (rest[:1], rest[1:]) if plan[0] else (rest[:2], rest[2:])
-    return [*swap_or_shift("gx", xs), *swap_or_shift("gy", ys), *swap_or_shift("gz", zs)]
-
-
-def call(kernel, n_smem, ins, outs, flops):
-    vmem = pl.BlockSpec(memory_space=pltpu.VMEM)
-    smem = pl.BlockSpec(memory_space=pltpu.SMEM)
+    return [*swap_or_shift("gx", xs, plan[2]), *swap_or_shift("gy", ys), *swap_or_shift("gz", zs)]
+
+
+STEPS = 4
+
+
+def spec_of(kind, a):
+    if kind == "s":
+        return pl.BlockSpec(memory_space=pltpu.SMEM)
+    if kind == "v":
+        return pl.BlockSpec(memory_space=pltpu.VMEM)
+    if kind == "a":
+        return pl.BlockSpec(memory_space=pl.ANY)
+    lead = len(a.shape) - 3
+    block = (*a.shape[:lead], a.shape[lead] // STEPS, *a.shape[lead + 1 :])
+    return pl.BlockSpec(block, lambda i: (*(0,) * lead, i, 0, 0))
+
+
+def call(kernel, kinds, ins, out_kinds, outs, flops, scratch=()):
     moved = sum(4 * a.size for a in (*ins, *outs))
+    grid = (STEPS,) if "b" in (*kinds, *out_kinds) else ()
     return pl.pallas_call(
         kernel,
         out_shape=outs,
-        in_specs=[smem] * n_smem + [vmem] * (len(ins) - n_smem),
-        out_specs=[vmem] * len(outs),
+        grid=grid,
+        in_specs=[spec_of(k, a) for k, a in zip(kinds, ins, strict=True)],
+        out_specs=[spec_of(k, a) for k, a in zip(out_kinds, outs, strict=True)],
+        scratch_shapes=scratch,
         compiler_params=pltpu.CompilerParams(vmem_limit_bytes=VMEM_BYTES),
         cost_estimate=pl.CostEstimate(flops=flops, bytes_accessed=moved, transcendentals=0),
     )(*ins)
@@ -360,8 +445,14 @@
 def per_device(displacement, velocity, damage, history, contact, notch, labels, table, impact):
     nx, ny, nz = damage.shape
     size = damage.size
-    plan = (lax.axis_size("gy") == 2, lax.axis_size("gz") == 2)
-    pos = jnp.stack([lax.axis_index("gy"), lax.axis_index("gz")]).astype(jnp.int32)
+    plan = (
+        lax.axis_size("gy") == 2,
+        lax.axis_size("gz") == 2,
+        lax.axis_size("gx") % 2 == 0,
+    )
+    pos = jnp.stack(
+        [lax.axis_index("gy"), lax.axis_index("gz"), lax.axis_index("gx") % 2]
+    ).astype(jnp.int32)
 
     def arr(*shape):
         return jax.ShapeDtypeStruct(shape, F32)
@@ -372,40 +463,53 @@
         out += [arr(nx, ny, 128)] * (1 if plan[1] else 2)
         return out
 
-    field = arr(nx, ny, nz)
+    field, small = arr(nx, ny, nz), arr(8, 128)
+    faces4, faces1 = face_shapes(4), face_shapes(1)
+    n_sides = len(faces4)
+    n_flat = 3 if plan[0] else 4
+    sides = "v" * n_sides
     sent = call(
-        functools.partial(pack_kernel, plan), 1, (pos, displacement, damage), face_shapes(4), size
+        functools.partial(pack_kernel, plan),
+        "sbb",
+        (pos, displacement, damage),
+        "v" * n_flat + "b" * (n_sides - n_flat),
+        faces4,
+        size,
     )
     got = exchange(sent, plan)
-    n_sides = len(got)
     hist, rd, v0, stress, mom, *sent = call(
         functools.partial(local_kernel, plan, n_sides),
-        2,
+        "ssvvbbb" + sides,
         (pos, table, displacement, damage, history, notch, labels, *got),
-        [field, field, field, arr(6, nx, ny, nz), arr(8, 128), *face_shapes(4)],
+        "bvvvv" + sides,
+        [field, field, field, arr(6, nx, ny, nz), small, *faces4],
         150 * size,
+        [pltpu.VMEM((8, 128), F32)],
     )
     got0 = exchange(sent, plan)
     v1, mom, *sent = call(
         functools.partial(apply_kernel, plan, n_sides, 0),
-        1,
+        "svvv" + sides,
         (pos, v0, rd, mom, *got0),
-        [field, arr(8, 128), *face_shapes(1)],
+        "vv" + sides,
+        [field, small, *faces1],
         20 * size,
     )
     got1 = exchange(sent, plan)
-    new_disp, new_vel = call(
+    new_disp, new_vel, token = call(
         functools.partial(force_kernel, plan, n_sides),
-        3,
+        "sssbbbbv" + sides,
         (pos, table, impact, displacement, velocity, contact, labels, stress, *got0),
-        [arr(3, nx, ny, nz), arr(3, nx, ny, nz)],
+        "bbv",
+        [arr(3, nx, ny, nz), arr(3, nx, ny, nz), small],
         60 * size,
     )
     v2, mom, *sent = call(
         functools.partial(apply_kernel, plan, n_sides, 1),
-        1,
-        (pos, v1, rd, mom, *got1),
-        [field, arr(8, 128), *face_shapes(1)],
+        "svvv" + sides + "a",
+        (pos, v1, rd, mom, *got1, token),
+        "vv" + sides,
+        [field, small, *faces1],
         20 * size,
     )
     got2 = exchange(sent, plan)
@@ -413,13 +517,16 @@
     peers = lax.axis_size("gx") * lax.axis_size("gy") * lax.axis_size("gz")
     (spread,) = call(
         functools.partial(apply_kernel, plan, n_sides, 2),
-        1,
+        "svvv" + sides,
         (pos, v2, rd, mom, *got2),
+        "v",
         [arr(peers, 8, 128)],
         20 * size,
     )
     mom = lax.all_to_all(spread, axes, 0, 0, tiled=True)
-    (damage_new,) = call(final_kernel, 0, (mom, damage, v0, v1, v2), [field], 8 * size)
+    (damage_new,) = call(
+        final_kernel, "vvvvb", (mom, v0, v1, v2, damage), "b", [field], 8 * size
+    )
     return new_disp, new_vel, hist, damage_new
 
 

time: 85.9 us -> 62.1 us (0.72)
  starting transfers between devices: 32.2 us -> 20.9 us
  blocking collectives: 0 us -> 10.8 us
  local copies, waits for them, and re-layouts: 12.9 us -> 2.49 us
  waiting for transfers between devices: 15.2 us -> 8.79 us
  Pallas kernels: 23.9 us -> 17.9 us
    all_to_all x0 -> x1, blocking collectives: none -> 10.8 us  [per_device(): mom = lax.all_to_all(spread, axes, 0, 0, tiled=True)]
    unnamed x42 -> x22, local copies, waits for them, and re-layouts: 12.9 us -> 2.49 us
    pallas_call x7, Pallas kernels: 23.9 us -> 17.9 us  [call(): pl.pallas_call(kernel, out_shape=outs, grid=grid, in_specs=[spec_of(k, a)...]
    ppermute x8, starting transfers between devices: 20.6 us -> 15 us  [swap_or_shift(): out.append(lax.ppermute(face, axis, pairs + [(b, a) for a, b in pairs]))]
    ppermute x8, waiting for transfers between devices: 5.16 us -> 0.02 us  [swap_or_shift(): out.append(lax.ppermute(face, axis, pairs + [(b, a) for a, b in pairs]))]
    all_to_all x1 -> x0, starting transfers between devices: 4.76 us -> none  [per_device(): mom = lax.all_to_all(spread, axes, 0, 0, tiled=True)]
    ppermute x8, waiting for transfers between devices: 10.1 us -> 8.77 us  [swap_or_shift(): return [lax.ppermute(faces[0], axis, [(0, 1), (1, 0)])]]
    ppermute x8, starting transfers between devices: 6.81 us -> 5.86 us  [swap_or_shift(): return [lax.ppermute(faces[0], axis, [(0, 1), (1, 0)])]]
  transfers between devices with their start and end apart: 17 -> 16, of which waited for: 8 -> 3; matrix products, arithmetic and copies ran while one was open for 0% -> 0% of each run, Pallas kernels for 6% -> 7%
where the time goes in v2:
time: 62.1 us; the launch traced here: 61.8 us
  starting transfers between devices  20.9 us (34%)
  Pallas kernels  17.9 us (29%)
  blocking collectives  10.8 us (17%)
  waiting for transfers between devices  8.79 us (14%)
  local copies, waits for them, and re-layouts  2.49 us (4%)
  between operations  0.81 us (1%)
    pallas_call x7, Pallas kernels, call(): pl.pallas_call(kernel, out_shape=outs, grid=grid, in_specs=[spec_of(k, a)...  17.9 us
    ppermute x8, starting transfers between devices, swap_or_shift(): out.append(lax.ppermute(face, axis, pairs + [(b, a) for a, b in pairs]))  15 us
    all_to_all x1, blocking collectives, per_device(): mom = lax.all_to_all(spread, axes, 0, 0, tiled=True)  10.8 us
    ppermute x8, waiting for transfers between devices, swap_or_shift(): return [lax.ppermute(faces[0], axis, [(0, 1), (1, 0)])]  8.77 us
    ppermute x8, starting transfers between devices, swap_or_shift(): return [lax.ppermute(faces[0], axis, [(0, 1), (1, 0)])]  5.86 us
    unnamed x22, local copies, waits for them, and re-layouts  2.49 us
  transfers between devices with their start and end apart: 16, of which 3 were waited for; matrix products, arithmetic and copies ran while one was open for 0% of the time, Pallas kernels for 7%

profile of v2, /device:TPU:0, one launch (start us, length us, event | category | flops | bytes accessed | tf_op | source)
XLA Modules:
  0.0 61.8 jit_solution(6790614959862128006)
XLA Ops:
  0.6 0.0 copy-start.9
  0.7 0.1 pad_add_fusion.pos
  0.7 0.0 copy-start
  0.7 1.4 %copy-done = f32[3,16,32,256]{3,2,1,0:T(8,128)S(1)} copy-done((f32[3,16,32,256]{3,2,1,0:T(8,128)S(1)}, f32[3,16,32,256]{3,2,1,0:T(8,128)}, u32[]{:S(2)}) %copy-start) | copy-done | bytes 1572888
  2.1 0.0 copy-start.2
  2.1 1.0 %copy-done.2 = f32[16,32,256]{2,1,0:T(8,128)S(1)} copy-done((f32[16,32,256]{2,1,0:T(8,128)S(1)}, f32[16,32,256]{2,1,0:T(8,128)}, u32[]{:S(2)}) %copy-start.2) | copy-done | bytes 524312
  3.2 0.0 copy-start.4
  3.2 0.0 copy-start.7
  3.2 0.0 copy-start.8
  3.2 1.3 %shard_map.120 = (f32[4,32,256]{2,1,0:T(8,128)S(1)}, f32[4,32,256]{2,1,0:T(8,128)S(1)}, f32[4,16,256]{2,1,0:T(8,128)S(1)}, f32[16,32,128]{2,1,0:T(8,128)S(1)}) custom-call(s32[3]{0:T(128)S(1)} %pad_add_fusion.pos, f32[3,16,32,256]{3,2,1,0:T(8,128)S(1)} %copy-done, f32[16,32,256]{2,1,0:T(8,128)S(1)} %copy-done.2), custom_call_target="tpu_custom_call" | custom-call | flops 131072 | bytes 2686988 | tf_op jit(solution)/shard_map/pallas_call | solution.py:433
  4.5 0.5 collective-permute-start.3
  5.1 2.7 %collective-permute-start = (f32[4,32,256]{2,1,0:T(8,128)S(1)}, f32[4,32,256]{2,1,0:T(8,128)S(1)}, u32[]{:S(2)}, u32[]{:S(2)}) collective-permute-start(f32[4,32,256]{2,1,0:T(8,128)S(1)} %get-tuple-element.32), channel_id=1, source_target_pairs={{0,4},{8,12},{4,0},{12,8},{1,5},{9,13},{5,1},{13,9},{2,6},{10,14},... | collective-permute-start | bytes 393224 | tf_op jit(solution)/shard_map/ppermute | solution.py:400
  7.7 0.7 %collective-permute-start.1 = (f32[4,32,256]{2,1,0:T(8,128)S(1)}, f32[4,32,256]{2,1,0:T(8,128)S(1)}, u32[]{:S(2)}, u32[]{:S(2)}) collective-permute-start(f32[4,32,256]{2,1,0:T(8,128)S(1)} %get-tuple-element.33), channel_id=1, source_target_pairs={{4,8},{8,4},{5,9},{9,5},{6,10},{10,6},{7,11},{11,7},{20,24},{24,20... | collective-permute-start | bytes 393224 | tf_op jit(solution)/shard_map/ppermute | solution.py:400
  8.4 1.6 %collective-permute-start.2 = (f32[4,16,256]{2,1,0:T(8,128)S(1)}, f32[4,16,256]{2,1,0:T(8,128)S(1)}, u32[]{:S(2)}, u32[]{:S(2)}) collective-permute-start(f32[4,16,256]{2,1,0:T(8,128)S(1)} %get-tuple-element.34), channel_id=1, source_target_pairs={{0,2},{2,0},{1,3},{3,1},{4,6},{6,4},{5,7},{7,5},{8,10},{10,8},{9,1... | collective-permute-start | bytes 196616 | tf_op jit(solution)/shard_map/ppermute | solution.py:403
  9.9 2.8 %collective-permute-done.2.refs_2_ = f32[4,16,256]{2,1,0:T(8,128)S(1)} collective-permute-done((f32[4,16,256]{2,1,0:T(8,128)S(1)}, f32[4,16,256]{2,1,0:T(8,128)S(1)}, u32[]{:S(2)}, u32[]{:S(2)}) %collective-permute-start.2) | collective-permute-done | bytes 65568 | tf_op jit(solution)/shard_map/ppermute | solution.py:403
  12.7 0.0 collective-permute-done.refs_0_
  12.7 0.0 collective-permute-done.1.refs_1_
  12.7 0.0 collective-permute-done.3.refs_3_
  12.7 0.0 copy-done.9
  12.7 0.0 copy-done.4
  12.7 0.0 copy-done.7
  12.7 0.0 copy-done.8
  12.8 0.0 copy-start.5
  12.8 0.0 copy-start.6
  12.8 5.6 %shard_map.121 = (f32[16,32,256]{2,1,0:T(8,128)}, f32[16,32,256]{2,1,0:T(8,128)S(1)}, f32[16,32,256]{2,1,0:T(8,128)S(1)}, f32[6,16,32,256]{3,2,1,0:T(8,128)S(1)}...) custom-call(s32[3]{0:T(128)S(1)} %pad_add_fusion.pos, ...), custom_call_target="tpu_custom_call" | custom-call | flops 19660800 | bytes 9572428 | tf_op jit(solution)/shard_map/pallas_call | solution.py:433
  18.4 0.0 copy-start.1
  18.4 0.0 copy-start.10
  18.4 0.0 collective-permute-start.7
  18.4 4.5 %collective-permute-start.4 = (f32[4,32,256]{2,1,0:T(8,128)S(1)}, f32[4,32,256]{2,1,0:T(8,128)S(1)}, u32[]{:S(2)}, u32[]{:S(2)}) collective-permute-start(f32[4,32,256]{2,1,0:T(8,128)S(1)} %get-tuple-element.37), channel_id=1, source_target_pairs={{0,4},{8,12},{4,0},{12,8},{1,5},{9,13},{5,1},{13,9},{2,6},{10,14},... | collective-permute-start | bytes 393224 | tf_op jit(solution)/shard_map/ppermute | solution.py:400
  22.8 0.7 %collective-permute-start.5 = (f32[4,32,256]{2,1,0:T(8,128)S(1)}, f32[4,32,256]{2,1,0:T(8,128)S(1)}, u32[]{:S(2)}, u32[]{:S(2)}) collective-permute-start(f32[4,32,256]{2,1,0:T(8,128)S(1)} %get-tuple-element.38), channel_id=1, source_target_pairs={{4,8},{8,4},{5,9},{9,5},{6,10},{10,6},{7,11},{11,7},{20,24},{24,20... | collective-permute-start | bytes 393224 | tf_op jit(solution)/shard_map/ppermute | solution.py:400
  23.5 1.6 %collective-permute-start.6 = (f32[4,16,256]{2,1,0:T(8,128)S(1)}, f32[4,16,256]{2,1,0:T(8,128)S(1)}, u32[]{:S(2)}, u32[]{:S(2)}) collective-permute-start(f32[4,16,256]{2,1,0:T(8,128)S(1)} %get-tuple-element.39), channel_id=1, source_target_pairs={{0,2},{2,0},{1,3},{3,1},{4,6},{6,4},{5,7},{7,5},{8,10},{10,8},{9,1... | collective-permute-start | bytes 196616 | tf_op jit(solution)/shard_map/ppermute | solution.py:403
  25.1 2.8 %collective-permute-done.6.refs_2_ = f32[4,16,256]{2,1,0:T(8,128)S(1)} collective-permute-done((f32[4,16,256]{2,1,0:T(8,128)S(1)}, f32[4,16,256]{2,1,0:T(8,128)S(1)}, u32[]{:S(2)}, u32[]{:S(2)}) %collective-permute-start.6) | collective-permute-done | bytes 65568 | tf_op jit(solution)/shard_map/ppermute | solution.py:403
  27.8 0.0 collective-permute-done.4.refs_0_
  27.8 0.0 collective-permute-done.5.refs_1_
  27.8 0.0 collective-permute-done.7.refs_3_
  27.8 1.8 %shard_map.123 = (f32[16,32,256]{2,1,0:T(8,128)S(1)}, f32[8,128]{1,0:T(8,128)S(1)}, f32[1,32,256]{2,1,0:T(8,128)S(1)}, f32[1,32,256]{2,1,0:T(8,128)S(1)}, f32[1,...) custom-call(s32[3]{0:T(128)S(1)} %pad_add_fusion.pos, f32[16,32,256]{2,1,0:T(8,128)S(1)} %get-tuple-element.44.v.v0, ...), custom_call_target="tpu_custom_call" | custom-call | flops 2621440 | bytes 2514956 | tf_op jit(solution)/shard_map/pallas_call | solution.py:433
  29.6 0.0 collective-permute-start.11
  29.7 2.8 %collective-permute-start.8 = (f32[1,32,256]{2,1,0:T(8,128)S(1)}, f32[1,32,256]{2,1,0:T(8,128)S(1)}, u32[]{:S(2)}, u32[]{:S(2)}) collective-permute-start(f32[1,32,256]{2,1,0:T(8,128)S(1)} %get-tuple-element.49), channel_id=1, source_target_pairs={{0,4},{8,12},{4,0},{12,8},{1,5},{9,13},{5,1},{13,9},{2,6},{10,14},... | collective-permute-start | bytes 98312 | tf_op jit(solution)/shard_map/ppermute | solution.py:400
  32.5 0.7 %collective-permute-start.9 = (f32[1,32,256]{2,1,0:T(8,128)S(1)}, f32[1,32,256]{2,1,0:T(8,128)S(1)}, u32[]{:S(2)}, u32[]{:S(2)}) collective-permute-start(f32[1,32,256]{2,1,0:T(8,128)S(1)} %get-tuple-element.50), channel_id=1, source_target_pairs={{4,8},{8,4},{5,9},{9,5},{6,10},{10,6},{7,11},{11,7},{20,24},{24,20... | collective-permute-start | bytes 98312 | tf_op jit(solution)/shard_map/ppermute | solution.py:400
  33.1 1.6 %collective-permute-start.10 = (f32[1,16,256]{2,1,0:T(8,128)S(1)}, f32[1,16,256]{2,1,0:T(8,128)S(1)}, u32[]{:S(2)}, u32[]{:S(2)}) collective-permute-start(f32[1,16,256]{2,1,0:T(8,128)S(1)} %get-tuple-element.51), channel_id=1, source_target_pairs={{0,2},{2,0},{1,3},{3,1},{4,6},{6,4},{5,7},{7,5},{8,10},{10,8},{9,1... | collective-permute-start | bytes 49160 | tf_op jit(solution)/shard_map/ppermute | solution.py:403
  34.7 0.0 copy-done.5
  34.7 0.0 copy-done.6
  34.7 0.0 copy-done.1
  34.7 0.0 copy-done.10
  34.7 4.1 %shard_map.122 = (f32[3,16,32,256]{3,2,1,0:T(8,128)}, f32[3,16,32,256]{3,2,1,0:T(8,128)}, f32[8,128]{1,0:T(8,128)S(1)}) custom-call(s32[3]{0:T(128)S(1)} %pad_add_fusion.pos, f32[4,4]{1,0:T(4,128)S(1)} %copy-done.9, f32[3]{0:T(128)S(1)} %copy-done.10, f32[3,16,32,256]{3,2,1,0:T(8,128)S(1)} %copy-done.1, f32[3,16,32,256]{3,2,1,0:T(8,128)S(1)} %copy-done.5, ...), custom_call_target="tpu_custom_call" | custom-call | flops 7864320 | bytes 11079768 | tf_op jit(solution)/shard_map/pallas_call | solution.py:433
  38.8 0.0 copy-start.3
  38.8 0.0 collective-permute-done.10.refs_2_
  38.8 0.0 collective-permute-done.8.refs_0_
  38.8 0.0 collective-permute-done.9.refs_1_
  38.8 0.0 collective-permute-done.11.refs_3_
  38.8 1.8 %shard_map.124 = (f32[16,32,256]{2,1,0:T(8,128)S(1)}, f32[8,128]{1,0:T(8,128)S(1)}, f32[1,32,256]{2,1,0:T(8,128)S(1)}, f32[1,32,256]{2,1,0:T(8,128)S(1)}, f32[1,...) custom-call(s32[3]{0:T(128)S(1)} %pad_add_fusion.pos, f32[16,32,256]{2,1,0:T(8,128)S(1)} %get-tuple-element.47.v.v1, ...), custom_call_target="tpu_custom_call" | custom-call | flops 2621440 | bytes 2273292 | tf_op jit(solution)/shard_map/pallas_call | solution.py:433
  40.6 0.0 collective-permute-start.15
  40.7 2.5 %collective-permute-start.12 = (f32[1,32,256]{2,1,0:T(8,128)S(1)}, f32[1,32,256]{2,1,0:T(8,128)S(1)}, u32[]{:S(2)}, u32[]{:S(2)}) collective-permute-start(f32[1,32,256]{2,1,0:T(8,128)S(1)} %get-tuple-element.56), channel_id=1, source_target_pairs={{0,4},{8,12},{4,0},{12,8},{1,5},{9,13},{5,1},{13,9},{2,6},{10,14},... | collective-permute-start | bytes 98312 | tf_op jit(solution)/shard_map/ppermute | solution.py:400
  43.2 0.7 %collective-permute-start.13 = (f32[1,32,256]{2,1,0:T(8,128)S(1)}, f32[1,32,256]{2,1,0:T(8,128)S(1)}, u32[]{:S(2)}, u32[]{:S(2)}) collective-permute-start(f32[1,32,256]{2,1,0:T(8,128)S(1)} %get-tuple-element.57), channel_id=1, source_target_pairs={{4,8},{8,4},{5,9},{9,5},{6,10},{10,6},{7,11},{11,7},{20,24},{24,20... | collective-permute-start | bytes 98312 | tf_op jit(solution)/shard_map/ppermute | solution.py:400
  43.9 0.6 collective-permute-start.14
  44.5 3.2 %collective-permute-done.14.refs_2_ = f32[1,16,256]{2,1,0:T(8,128)S(1)} collective-permute-done((f32[1,16,256]{2,1,0:T(8,128)S(1)}, f32[1,16,256]{2,1,0:T(8,128)S(1)}, u32[]{:S(2)}, u32[]{:S(2)}) %collective-permute-start.14) | collective-permute-done | bytes 16416 | tf_op jit(solution)/shard_map/ppermute | solution.py:403
  47.7 0.0 collective-permute-done.12.refs_0_
  47.7 0.0 collective-permute-done.13.refs_1_
  47.7 0.0 collective-permute-done.15.refs_3_
  47.7 1.3 %shard_map.125 = f32[16,8,128]{2,1,0:T(8,128)S(1)} custom-call(s32[3]{0:T(128)S(1)} %pad_add_fusion.pos, f32[16,32,256]{2,1,0:T(8,128)S(1)} %get-tuple-element.54.v.v2, f32[16,32,256]{2,1,0:T(8,128)S(1)} %get-tuple-element.45.rd, f32[8,128]{1,0:T(8,128)S(1)} %get-tuple-element.55.mom, f32[1,32,256]{2,1,0:T(8,128)S(1)} %collective-permute-done.12.refs_0_, ...), custom_call_target="tpu_custom_call" | custom-call | flops 2621440 | bytes 1462284 | tf_op jit(solution)/shard_map/pallas_call | solution.py:433
  49.0 10.8 %all_to_all.5.mom = f32[16,8,128]{2,1,0:T(8,128)S(1)} all-to-all(f32[16,8,128]{2,1,0:T(8,128)S(1)} %shard_map.125), channel_id=1, replica_groups=mesh['case'=2,'gx'=4,'gy'=2,'gz'=2] {'gx','gy','gz'}, dimensions={0} | all-to-all | bytes 131072 | tf_op jit(solution)/shard_map/all_to_all | solution.py:526
  59.8 0.0 copy-done.3
  59.8 2.0 %shard_map.126 = f32[16,32,256]{2,1,0:T(8,128)} custom-call(f32[16,8,128]{2,1,0:T(8,128)S(1)} %all_to_all.5.mom, f32[16,32,256]{2,1,0:T(8,128)S(1)} %get-tuple-element.44.v.v0, f32[16,32,256]{2,1,0:T(8,128)S(1)} %get-tuple-element.47.v.v1, f32[16,32,256]{2,1,0:T(8,128)S(1)} %get-tuple-element.54.v.v2, f32[16,32,256]{2,1,0:T(8,128)S(1)} %copy-done.3), custom_call_target="tpu_custom_call" | custom-call | flops 1048576 | bytes 2686976 | tf_op jit(solution)/shard_map/pallas_call | solution.py:433
Async XLA Ops:
  0.6 12.1 %copy-start.9 = (f32[4,4]{1,0:T(4,128)S(1)}, f32[4,4]{1,0:T(4,128)}, u32[]{:S(2)}) copy-start(f32[4,4]{1,0:T(4,128)} %table.3) | copy-start | bytes 196
  0.7 1.4 %copy-start = (f32[3,16,32,256]{3,2,1,0:T(8,128)S(1)}, f32[3,16,32,256]{3,2,1,0:T(8,128)}, u32[]{:S(2)}) copy-start(f32[3,16,32,256]{3,2,1,0:T(8,128)} %disp.5) | copy-start | bytes 4718596
  2.1 1.0 %copy-start.2 = (f32[16,32,256]{2,1,0:T(8,128)S(1)}, f32[16,32,256]{2,1,0:T(8,128)}, u32[]{:S(2)}) copy-start(f32[16,32,256]{2,1,0:T(8,128)} %damage.5) | copy-start | bytes 1572868
  3.2 9.6 %copy-start.4 = (s32[16,32,256]{2,1,0:T(8,128)S(1)}, s32[16,32,256]{2,1,0:T(8,128)}, u32[]{:S(2)}) copy-start(s32[16,32,256]{2,1,0:T(8,128)} %labels.3) | copy-start | bytes 1572868
  3.2 9.6 %copy-start.7 = (f32[16,32,256]{2,1,0:T(8,128)S(1)}, f32[16,32,256]{2,1,0:T(8,128)}, u32[]{:S(2)}) copy-start(f32[16,32,256]{2,1,0:T(8,128)} %history.1) | copy-start | bytes 1572868
  3.2 9.6 %copy-start.8 = (s32[16,32,256]{2,1,0:T(8,128)S(1)}, s32[16,32,256]{2,1,0:T(8,128)}, u32[]{:S(2)}) copy-start(s32[16,32,256]{2,1,0:T(8,128)} %notch.1) | copy-start | bytes 1572868
  4.5 8.2 %collective-permute-start.3 = (f32[16,32,128]{2,1,0:T(8,128)S(1)}, f32[16,32,128]{2,1,0:T(8,128)S(1)}, u32[]{:S(2)}, u32[]{:S(2)}) collective-permute-start(f32[16,32,128]{2,1,0:T(8,128)S(1)} %get-tuple-element.35), channel_id=1, source_target_pairs={{0,1},{1,0},{2,3},{3,2},{4,5},{5,4},{6,7},{7,6},{8,9},{9,8},{10,11... | collective-permute-start | bytes 786440 | tf_op jit(solution)/shard_map/ppermute | solution.py:403
  5.1 7.7 %collective-permute-start = (f32[4,32,256]{2,1,0:T(8,128)S(1)}, f32[4,32,256]{2,1,0:T(8,128)S(1)}, u32[]{:S(2)}, u32[]{:S(2)}) collective-permute-start(f32[4,32,256]{2,1,0:T(8,128)S(1)} %get-tuple-element.32), channel_id=1, source_target_pairs={{0,4},{8,12},{4,0},{12,8},{1,5},{9,13},{5,1},{13,9},{2,6},{10,14},... | collective-permute-start | bytes 393224 | tf_op jit(solution)/shard_map/ppermute | solution.py:400
  7.7 5.0 %collective-permute-start.1 = (f32[4,32,256]{2,1,0:T(8,128)S(1)}, f32[4,32,256]{2,1,0:T(8,128)S(1)}, u32[]{:S(2)}, u32[]{:S(2)}) collective-permute-start(f32[4,32,256]{2,1,0:T(8,128)S(1)} %get-tuple-element.33), channel_id=1, source_target_pairs={{4,8},{8,4},{5,9},{9,5},{6,10},{10,6},{7,11},{11,7},{20,24},{24,20... | collective-permute-start | bytes 393224 | tf_op jit(solution)/shard_map/ppermute | solution.py:400
  8.4 4.3 %collective-permute-start.2 = (f32[4,16,256]{2,1,0:T(8,128)S(1)}, f32[4,16,256]{2,1,0:T(8,128)S(1)}, u32[]{:S(2)}, u32[]{:S(2)}) collective-permute-start(f32[4,16,256]{2,1,0:T(8,128)S(1)} %get-tuple-element.34), channel_id=1, source_target_pairs={{0,2},{2,0},{1,3},{3,1},{4,6},{6,4},{5,7},{7,5},{8,10},{10,8},{9,1... | collective-permute-start | bytes 196616 | tf_op jit(solution)/shard_map/ppermute | solution.py:403
  12.8 21.9 %copy-start.5 = (f32[3,16,32,256]{3,2,1,0:T(8,128)S(1)}, f32[3,16,32,256]{3,2,1,0:T(8,128)}, u32[]{:S(2)}) copy-start(f32[3,16,32,256]{3,2,1,0:T(8,128)} %vel.1) | copy-start | bytes 4718596
  12.8 21.9 %copy-start.6 = (s32[16,32,256]{2,1,0:T(8,128)S(1)}, s32[16,32,256]{2,1,0:T(8,128)}, u32[]{:S(2)}) copy-start(s32[16,32,256]{2,1,0:T(8,128)} %contact.1) | copy-start | bytes 1572868
  18.4 16.3 %copy-start.1 = (f32[3,16,32,256]{3,2,1,0:T(8,128)S(1)}, f32[3,16,32,256]{3,2,1,0:T(8,128)}, u32[]{:S(2)}) copy-start(f32[3,16,32,256]{3,2,1,0:T(8,128)} %disp.5) | copy-start | bytes 4718596
  18.4 16.3 %copy-start.10 = (f32[3]{0:T(128)S(1)}, f32[3]{0:T(128)}, u32[]{:S(2)}) copy-start(f32[3]{0:T(128)} %impact.1) | copy-start | bytes 40
  18.4 9.5 %collective-permute-start.7 = (f32[16,32,128]{2,1,0:T(8,128)S(1)}, f32[16,32,128]{2,1,0:T(8,128)S(1)}, u32[]{:S(2)}, u32[]{:S(2)}) collective-permute-start(f32[16,32,128]{2,1,0:T(8,128)S(1)} %get-tuple-element.40), channel_id=1, source_target_pairs={{0,1},{1,0},{2,3},{3,2},{4,5},{5,4},{6,7},{7,6},{8,9},{9,8},{10,11... | collective-permute-start | bytes 786440 | tf_op jit(solution)/shard_map/ppermute | solution.py:403
  18.4 9.5 %collective-permute-start.4 = (f32[4,32,256]{2,1,0:T(8,128)S(1)}, f32[4,32,256]{2,1,0:T(8,128)S(1)}, u32[]{:S(2)}, u32[]{:S(2)}) collective-permute-start(f32[4,32,256]{2,1,0:T(8,128)S(1)} %get-tuple-element.37), channel_id=1, source_target_pairs={{0,4},{8,12},{4,0},{12,8},{1,5},{9,13},{5,1},{13,9},{2,6},{10,14},... | collective-permute-start | bytes 393224 | tf_op jit(solution)/shard_map/ppermute | solution.py:400
  22.8 5.0 %collective-permute-start.5 = (f32[4,32,256]{2,1,0:T(8,128)S(1)}, f32[4,32,256]{2,1,0:T(8,128)S(1)}, u32[]{:S(2)}, u32[]{:S(2)}) collective-permute-start(f32[4,32,256]{2,1,0:T(8,128)S(1)} %get-tuple-element.38), channel_id=1, source_target_pairs={{4,8},{8,4},{5,9},{9,5},{6,10},{10,6},{7,11},{11,7},{20,24},{24,20... | collective-permute-start | bytes 393224 | tf_op jit(solution)/shard_map/ppermute | solution.py:400
  23.5 4.3 %collective-permute-start.6 = (f32[4,16,256]{2,1,0:T(8,128)S(1)}, f32[4,16,256]{2,1,0:T(8,128)S(1)}, u32[]{:S(2)}, u32[]{:S(2)}) collective-permute-start(f32[4,16,256]{2,1,0:T(8,128)S(1)} %get-tuple-element.39), channel_id=1, source_target_pairs={{0,2},{2,0},{1,3},{3,1},{4,6},{6,4},{5,7},{7,5},{8,10},{10,8},{9,1... | collective-permute-start | bytes 196616 | tf_op jit(solution)/shard_map/ppermute | solution.py:403
  29.6 9.2 %collective-permute-start.11 = (f32[16,32,128]{2,1,0:T(8,128)S(1)}, f32[16,32,128]{2,1,0:T(8,128)S(1)}, u32[]{:S(2)}, u32[]{:S(2)}) collective-permute-start(f32[16,32,128]{2,1,0:T(8,128)S(1)} %get-tuple-element.52), channel_id=1, source_target_pairs={{0,1},{1,0},{2,3},{3,2},{4,5},{5,4},{6,7},{7,6},{8,9},{9,8},{10,11... | collective-permute-start | bytes 786440 | tf_op jit(solution)/shard_map/ppermute | solution.py:403
  29.7 9.1 %collective-permute-start.8 = (f32[1,32,256]{2,1,0:T(8,128)S(1)}, f32[1,32,256]{2,1,0:T(8,128)S(1)}, u32[]{:S(2)}, u32[]{:S(2)}) collective-permute-start(f32[1,32,256]{2,1,0:T(8,128)S(1)} %get-tuple-element.49), channel_id=1, source_target_pairs={{0,4},{8,12},{4,0},{12,8},{1,5},{9,13},{5,1},{13,9},{2,6},{10,14},... | collective-permute-start | bytes 98312 | tf_op jit(solution)/shard_map/ppermute | solution.py:400
  32.5 6.4 %collective-permute-start.9 = (f32[1,32,256]{2,1,0:T(8,128)S(1)}, f32[1,32,256]{2,1,0:T(8,128)S(1)}, u32[]{:S(2)}, u32[]{:S(2)}) collective-permute-start(f32[1,32,256]{2,1,0:T(8,128)S(1)} %get-tuple-element.50), channel_id=1, source_target_pairs={{4,8},{8,4},{5,9},{9,5},{6,10},{10,6},{7,11},{11,7},{20,24},{24,20... | collective-permute-start | bytes 98312 | tf_op jit(solution)/shard_map/ppermute | solution.py:400
  33.1 5.7 %collective-permute-start.10 = (f32[1,16,256]{2,1,0:T(8,128)S(1)}, f32[1,16,256]{2,1,0:T(8,128)S(1)}, u32[]{:S(2)}, u32[]{:S(2)}) collective-permute-start(f32[1,16,256]{2,1,0:T(8,128)S(1)} %get-tuple-element.51), channel_id=1, source_target_pairs={{0,2},{2,0},{1,3},{3,1},{4,6},{6,4},{5,7},{7,5},{8,10},{10,8},{9,1... | collective-permute-start | bytes 49160 | tf_op jit(solution)/shard_map/ppermute | solution.py:403
  38.8 21.0 %copy-start.3 = (f32[16,32,256]{2,1,0:T(8,128)S(1)}, f32[16,32,256]{2,1,0:T(8,128)}, u32[]{:S(2)}) copy-start(f32[16,32,256]{2,1,0:T(8,128)} %damage.5) | copy-start | bytes 1572868
  40.6 7.0 %collective-permute-start.15 = (f32[16,32,128]{2,1,0:T(8,128)S(1)}, f32[16,32,128]{2,1,0:T(8,128)S(1)}, u32[]{:S(2)}, u32[]{:S(2)}) collective-permute-start(f32[16,32,128]{2,1,0:T(8,128)S(1)} %get-tuple-element.59), channel_id=1, source_target_pairs={{0,1},{1,0},{2,3},{3,2},{4,5},{5,4},{6,7},{7,6},{8,9},{9,8},{10,11... | collective-permute-start | bytes 786440 | tf_op jit(solution)/shard_map/ppermute | solution.py:403
  40.7 7.0 %collective-permute-start.12 = (f32[1,32,256]{2,1,0:T(8,128)S(1)}, f32[1,32,256]{2,1,0:T(8,128)S(1)}, u32[]{:S(2)}, u32[]{:S(2)}) collective-permute-start(f32[1,32,256]{2,1,0:T(8,128)S(1)} %get-tuple-element.56), channel_id=1, source_target_pairs={{0,4},{8,12},{4,0},{12,8},{1,5},{9,13},{5,1},{13,9},{2,6},{10,14},... | collective-permute-start | bytes 98312 | tf_op jit(solution)/shard_map/ppermute | solution.py:400
  43.2 4.5 %collective-permute-start.13 = (f32[1,32,256]{2,1,0:T(8,128)S(1)}, f32[1,32,256]{2,1,0:T(8,128)S(1)}, u32[]{:S(2)}, u32[]{:S(2)}) collective-permute-start(f32[1,32,256]{2,1,0:T(8,128)S(1)} %get-tuple-element.57), channel_id=1, source_target_pairs={{4,8},{8,4},{5,9},{9,5},{6,10},{10,6},{7,11},{11,7},{20,24},{24,20... | collective-permute-start | bytes 98312 | tf_op jit(solution)/shard_map/ppermute | solution.py:400
  43.9 3.8 %collective-permute-start.14 = (f32[1,16,256]{2,1,0:T(8,128)S(1)}, f32[1,16,256]{2,1,0:T(8,128)S(1)}, u32[]{:S(2)}, u32[]{:S(2)}) collective-permute-start(f32[1,16,256]{2,1,0:T(8,128)S(1)} %get-tuple-element.58), channel_id=1, source_target_pairs={{0,2},{2,0},{1,3},{3,1},{4,6},{6,4},{5,7},{7,5},{8,10},{10,8},{9,1... | collective-permute-start | bytes 49160 | tf_op jit(solution)/shard_map/ppermute | solution.py:403

commit v3 on v0

v3 whole, which is shorter than its diff:
```python
import functools
import jax
import jax.numpy as jnp
from jax import lax
from jax.experimental import pallas as pl
from jax.experimental.pallas import tpu as pltpu
from jax.sharding import PartitionSpec as P

TIME_STEP = 0.1
KAPPA_COEF = 0.5
NOTCH_LOAD = 20.0
STIFF_FLOOR = 0.001
ALPHA_LOW, ALPHA_HIGH = 0.5, 6.5
VMEM_BYTES = 28 * 1024 * 1024
CHUNKS = 4
F32 = jnp.float32


def iota2(shape, dim):
    return lax.broadcasted_iota(jnp.int32, shape, dim)


def low_high(odd, got):
    if len(got) == 2:
        return jnp.where(odd, got[0], got[1]), jnp.where(odd, got[1], got[0])
    return jnp.where(odd, got[0], 0.0), jnp.where(odd, 0.0, got[0])


def send(odd, refs, index, low, high):
    refs[0][index] = jnp.where(odd, low, high)
    if len(refs) == 2:
        refs[1][index] = jnp.where(odd, high, low)


def send_early(odd, refs, index, plane, is_low):
    def store(ref):
        ref[index] = plane

    at_odd, at_even = (0, 1) if is_low else (1, 0)
    pl.when(odd)(functools.partial(store, refs[at_odd]))
    pl.when(jnp.logical_not(odd))(functools.partial(store, refs[at_even]))


def shift_x(ref, lead, x, at, block, steps, faces):
    count = ref.shape[-3]
    lo, hi = faces
    if at > 0:
        lower = ref[(*lead, x - 1)]
    else:
        lower = jnp.where(x == 0, lo(), ref[(*lead, jnp.maximum(x - 1, 0))])
    if at < block - 1:
        upper = ref[(*lead, x + 1)]
    else:
        upper = jnp.where(x == count - 1, hi(), ref[(*lead, jnp.minimum(x + 1, count - 1))])
    return upper, lower


def shift_y(plane, rows):
    lo, hi = rows
    at = iota2(plane.shape, 0)
    last = plane.shape[0] - 1
    upper = jnp.where(at == last, hi, pltpu.roll(plane, last, 0))
    lower = jnp.where(at == 0, lo, pltpu.roll(plane, 1, 0))
    return upper, lower


def shift_z(plane, column, first_z):
    at = iota2(plane.shape, 1)
    last = plane.shape[1] - 1
    lo = jnp.where(first_z, 0.0, column)
    hi = jnp.where(first_z, column, 0.0)
    upper = jnp.where(at == last, hi, pltpu.roll(plane, last, 1))
    lower = jnp.where(at == 0, lo, pltpu.roll(plane, 1, 1))
    return upper, lower


def send_columns(ref, x, planes, gz):
    depth = planes[0].shape[1]
    lanes = iota2((planes[0].shape[0], 128), 1)
    tile = None
    for field, plane in enumerate(planes):
        part = jnp.where(gz == 0, plane[:, depth - 128 :], plane[:, :128])
        part = pltpu.roll(part, field + 1 - gz, 1)
        tile = part if tile is None else jnp.where(lanes == field, part, tile)
    ref[x] = tile


def folded(values):
    total = None
    for start in range(0, values.shape[1], 128):
        part = values[:, start : start + 128]
        total = part if total is None else total + part
    out = None
    for start in range(0, values.shape[0], 8):
        part = total[start : start + 8]
        out = part if out is None else out + part
    return out


def by_label(labels, scalars):
    picked = scalars[0]
    for region in range(1, len(scalars)):
        picked = jnp.where(labels == region, scalars[region], picked)
    return picked


def unrolled(count, many, body, carry):
    def several(block, carry):
        for at in range(many):
            carry = body(block * many + at, carry)
        return carry

    return lax.fori_loop(0, count // many, several, carry)


def pack_kernel(n_y, pos, disp_hbm, damage_hbm, *refs):
    disp, damage, *rest = refs
    xs, ys, zs, sems = rest[:2], rest[2 : 2 + n_y], rest[2 + n_y], rest[-1]
    odd_x, odd_y, gz = pos[0] == 1, pos[1] == 1, pos[2]
    count = damage.shape[0]
    block = count // CHUNKS
    copies = []
    for chunk in range(CHUNKS):
        part = pl.ds(chunk * block, block)
        for which, (src, dst) in enumerate(
            (
                (disp_hbm.at[:, part], disp.at[:, part]),
                (damage_hbm.at[part], damage.at[part]),
            )
        ):
            copy = pltpu.make_async_copy(src, dst, sems.at[chunk, which])
            copy.start()
            copies.append(copy)
    for chunk in range(CHUNKS):
        copies[2 * chunk].wait()
        copies[2 * chunk + 1].wait()
        for x in range(chunk * block, (chunk + 1) * block):
            planes = [disp[0, x], disp[1, x], disp[2, x], damage[x]]
            for field, plane in enumerate(planes):
                last = plane.shape[0] - 1
                send(
                    odd_y,
                    ys,
                    (field, pl.ds(x, 1), slice(None)),
                    plane[0:1],
                    plane[last : last + 1],
                )
            send_columns(zs, x, planes, gz)
    for field, src in enumerate((disp.at[0], disp.at[1], disp.at[2], damage)):
        send(odd_x, xs, field, src[0], src[count - 1])


def row_tile(v, rd, is_high):
    rows = v.shape[0]
    part = slice(rows - 8, rows) if is_high else slice(0, 8)
    at = iota2((8, v.shape[1]), 0)
    keep = at >= 4 if is_high else at < 4
    return jnp.where(keep, v[part], pltpu.roll(rd[part], 4, 0))


def local_kernel(n_y, pos, table, disp, damage, history, notch, labels, *refs):
    xg, yg, zg = refs[:2], refs[2 : 2 + n_y], refs[2 + n_y]
    refs = refs[3 + n_y :]
    hist_out, rd_out, v_out, stress_out, mom_out = refs[:5]
    refs = refs[5:]
    xs, ys, ds, zs, held = refs[:2], refs[2 : 2 + n_y], refs[2 + n_y : 2 + 3 * n_y], refs[-2], refs[-1]
    odd_x, odd_y, gz = pos[0] == 1, pos[1] == 1, pos[2]
    step, steps = pl.program_id(0), pl.num_programs(0)
    count = damage.shape[0]
    block = hist_out.shape[0]
    tall = count // 8
    regions = table.shape[1]
    lames = [table[0, r] for r in range(regions)]
    shears = [table[1, r] for r in range(regions)]
    fractures = [table[3, r] for r in range(regions)]

    def around(ref, lead, field, plane, x, at):
        faces = (
            lambda: jnp.where(odd_x, xg[0][field], xg[1][field]),
            lambda: jnp.where(odd_x, xg[1][field], xg[0][field]),
        )
        rows = low_high(odd_y, [y[field, pl.ds(x, 1), :] for y in yg])
        column = zg[x][:, field : field + 1]
        return (
            shift_x(ref, lead, x, at, block, steps, faces),
            shift_y(plane, rows),
            shift_z(plane, column, gz == 0),
        )

    total = jnp.where(step == 0, 0.0, held[...])
    for at in range(block):
        x = step * block + at
        g = []
        for c in range(3):
            pairs = around(disp, (c,), c, disp[c, x], x, at)
            g.append([0.5 * (upper - lower) for upper, lower in pairs])
        lab = labels[x]
        lame = by_label(lab, lames)
        shear = by_label(lab, shears)
        fracture = by_label(lab, fractures)
        dmg = damage[x]
        degrade = (1.0 - dmg) * (1.0 - dmg) + STIFF_FLOOR
        trace = g[0][0] + g[1][1] + g[2][2]
        strain = [
            g[0][0],
            g[1][1],
            g[2][2],
            0.5 * (g[0][1] + g[1][0]),
            0.5 * (g[0][2] + g[2][0]),
            0.5 * (g[1][2] + g[2][1]),
        ]
        positive = jnp.maximum(trace, 0.0)
        squares = strain[0] * strain[0] + strain[1] * strain[1] + strain[2] * strain[2]
        squares = squares + 2.0 * (
            strain[3] * strain[3] + strain[4] * strain[4] + strain[5] * strain[5]
        )
        energy = 0.5 * lame * positive * positive + shear * squares
        scale = degrade * (2.0 * shear)
        base = degrade * (lame * trace)
        stress = [base + scale * strain[k] if k < 3 else scale * strain[k] for k in range(6)]
        for k in range(6):
            stress_out[k, x] = stress[k]
        hist = jnp.maximum(
            jnp.maximum(history[x], energy), NOTCH_LOAD * notch[x].astype(F32)
        )
        hist_out[at] = hist
        diagonal = fracture + 2.0 * hist + 6.0 * KAPPA_COEF
        rd = 1.0 / diagonal
        rd_out[x] = rd
        (xu, xl), (yu, yl), (zu, zl) = around(damage, (), 3, dmg, x, at)
        near = ((xu + xl) + (yu + yl)) + (zu + zl)
        residual = 2.0 * hist - (diagonal * dmg - KAPPA_COEF * near)
        v = residual * rd
        v_out[x] = v
        total = total + folded(residual * v)
        send(odd_y, ys, x, row_tile(v, rd, False), row_tile(v, rd, True))
        for c, k in enumerate((3, 1, 5)):
            last = v.shape[0] - 1
            spot = (count + c * tall + lax.div(x, 8), pl.ds(lax.rem(x, 8), 1), slice(None))
            send(odd_y, ys, spot, stress[k][0:1], stress[k][last : last + 1])
        send_columns(zs, x, [stress[4], stress[5], stress[2]], gz)
    held[...] = total

    def x_fields(depth, x):
        out = [(depth - 1, v_out[x])]
        if depth <= 2:
            out.append((2 + depth, rd_out[x]))
        if depth == 1:
            out += [(5, stress_out[0, x]), (6, stress_out[3, x]), (7, stress_out[4, x])]
        return out

    @pl.when(step == 0)
    def _():
        for depth in (1, 2, 3):
            for slot, plane in x_fields(depth, depth - 1):
                send_early(odd_x, xs, slot, plane, True)
        for which in range(n_y):
            for depth in (1, 2):
                tile = ys[which][depth - 1]
                send_early(odd_x, (ds[which], ds[n_y + which]), depth - 1, tile, True)

    @pl.when(step == steps - 1)
    def _():
        for depth in (1, 2, 3):
            for slot, plane in x_fields(depth, count - depth):
                send_early(odd_x, xs, slot, plane, False)
        for which in range(n_y):
            for depth in (1, 2):
                tile = ys[which][count - depth]
                send_early(odd_x, (ds[which], ds[n_y + which]), depth - 1, tile, False)
        mom_out[...] = jnp.zeros((8, 128), F32)
        mom_out[0:1, :] = jnp.sum(total, axis=0, keepdims=True)


class Enlarged:
    def __init__(self, n_y, pos, v, rd, refs):
        self.odd_x, self.odd_y = pos[0] == 1, pos[1] == 1
        self.v, self.rd, self.n_y = v, rd, n_y
        self.xg, self.yg, self.dg = refs[:2], refs[2 : 2 + n_y], refs[2 + n_y : 2 + 3 * n_y]

    def rows(self, tiles):
        at = iota2(tiles[0].shape, 0)
        if self.n_y == 1:
            keep = lax.shift_right_logical(at, 2) == self.odd_y.astype(jnp.int32)
            tile = tiles[0]
            return jnp.where(keep, tile, 0.0), jnp.where(keep, pltpu.roll(tile, 4, 0), 0.0)
        lo, hi = low_high(self.odd_y, tiles)
        tile = jnp.where(at >= 4, lo, hi)
        moved = jnp.where(at >= 4, pltpu.roll(lo, 4, 0), pltpu.roll(hi, 4, 0))
        return tile, moved

    def own(self, x):
        v_rows, rd_rows = self.rows([y[x] for y in self.yg])
        return self.v[x], v_rows, self.rd[x], rd_rows

    def halo(self, is_low, depth):
        first, second = (0, 1) if is_low else (1, 0)

        def of(a, b):
            return jnp.where(self.odd_x, (a, b)[first], (a, b)[second])

        v = of(self.xg[0][depth - 1], self.xg[1][depth - 1])
        nothing = jnp.zeros((8, v.shape[1]), F32)
        if depth > 2:
            return v, nothing, jnp.zeros_like(v), nothing
        rd = of(self.xg[0][2 + depth], self.xg[1][2 + depth])
        tiles = [
            of(self.dg[w][depth - 1], self.dg[self.n_y + w][depth - 1]) for w in range(self.n_y)
        ]
        v_rows, rd_rows = self.rows(tiles)
        return v, v_rows, rd, rd_rows

    def outer(self, count):
        for depth in (1, 2, 3):
            yield -depth, self.halo(True, depth)
            yield count - 1 + depth, self.halo(False, depth)


def join_kernel(n_y, pos, v, rd, *refs):
    big = Enlarged(n_y, pos, v, rd, refs[:-1])
    out = refs[-1]
    first_z = pos[2] == 0
    count, ny, depth = v.shape

    def tile(v_part, rd_part):
        lanes = iota2((v_part.shape[0], 128), 1)
        keep = lax.shift_right_logical(lanes, 6) == 1 - pos[2]
        mine = jnp.where(first_z, v_part[:, depth - 128 :], v_part[:, :128])
        moved = jnp.where(first_z, rd_part[:, depth - 128 :], rd_part[:, :128])
        return jnp.where(keep, mine, pltpu.roll(moved, 64, 1))

    def put(p, parts):
        v_own, v_rows, rd_own, rd_rows = parts
        out[p + 3, 0:ny] = tile(v_own, rd_own)
        out[p + 3, ny : ny + 8] = tile(v_rows, rd_rows)

    for p, parts in big.outer(count):
        put(p, parts)

    def body(x, carry):
        put(x, big.own(x))
        return carry

    unrolled(count, 4, body, 0)


def krylov_kernel(n_y, pos, v, rd, mom, token, z_got, *refs):
    n_got = 2 + 3 * n_y
    big = Enlarged(n_y, pos, v, rd, refs[:n_got])
    v1_out, v2_out, spread, big_v, big_rd, big_v1, big_v2 = refs[n_got:]
    count, ny, nz = v.shape

    def put(p, parts):
        v_own, v_rows, rd_own, rd_rows = parts
        tile = z_got[p + 3]
        keep = lax.shift_right_logical(iota2(tile.shape, 1), 6) == pos[2]
        big_v[p + 3, 0:ny, 0:nz] = v_own
        big_v[p + 3, ny : ny + 8, 0:nz] = v_rows
        big_v[p + 3, :, nz : nz + 128] = jnp.where(keep, tile, 0.0)
        big_rd[p + 3, 0:ny, 0:nz] = rd_own
        big_rd[p + 3, ny : ny + 8, 0:nz] = rd_rows
        big_rd[p + 3, :, nz : nz + 128] = jnp.where(keep, pltpu.roll(tile, 64, 1), 0.0)

    for p, parts in big.outer(count):
        put(p, parts)

    def fill(x, carry):
        put(x, big.own(x))
        return carry

    unrolled(count, 4, fill, 0)

    def image_of(ref, at):
        plane = ref[at]
        rows, lanes = plane.shape
        near = (ref[at - 1] + ref[at + 1]) + (pltpu.roll(plane, 1, 0) + pltpu.roll(plane, rows - 1, 0))
        near = near + (pltpu.roll(plane, 1, 1) + pltpu.roll(plane, lanes - 1, 1))
        return plane, KAPPA_COEF * near

    def inside(values):
        return folded(values[0:ny, 0:nz])

    def first(x, totals):
        plane, image = image_of(big_v, x + 3)
        made = image * big_rd[x + 3]
        big_v1[x + 2] = made
        v1_out[x] = made[0:ny, 0:nz]
        return totals[0] + inside(plane * image), totals[1] + inside(made * image)

    def second(x, totals):
        plane, image = image_of(big_v1, x + 2)
        made = image * big_rd[x + 3]
        big_v2[x + 1] = made
        v2_out[x] = made[0:ny, 0:nz]
        return totals[0] + inside(plane * image), totals[1] + inside(made * image)

    def third(x, total):
        plane, image = image_of(big_v2, x + 1)
        return total + inside(plane * image)

    zero = jnp.zeros((8, 128), F32)
    for p in (-2, -1, count, count + 1):
        big_v1[p + 2] = image_of(big_v, p + 3)[1] * big_rd[p + 3]
    k1, k2 = unrolled(count, 4, first, (zero, zero))
    for p in (-1, count):
        big_v2[p + 1] = image_of(big_v1, p + 2)[1] * big_rd[p + 3]
    k3, k4 = unrolled(count, 4, second, (zero, zero))
    k5 = unrolled(count, 4, third, zero)
    rows = iota2((8, 128), 0)
    result = mom[...]
    for at, total in enumerate((k1, k2, k3, k4, k5)):
        result = jnp.where(rows == at + 1, jnp.sum(total, axis=0, keepdims=True), result)
    for peer in range(spread.shape[0]):
        spread[peer] = result


def force_kernel(n_y, pos, table, impact, disp, vel, contact, labels, stress, *refs):
    xg, yg, zg = refs[:2], refs[2 : 2 + n_y], refs[2 + n_y]
    disp_out, vel_out, token = refs[3 + n_y :]
    token[...] = jnp.zeros((8, 128), F32)
    odd_x, odd_y, gz = pos[0] == 1, pos[1] == 1, pos[2]
    step, steps, block = pl.program_id(0), pl.num_programs(0), contact.shape[0]
    count = stress.shape[1]
    tall = count // 8
    rates = [table[2, r] for r in range(table.shape[1])]
    for at in range(block):
        x = step * block + at
        loaded = contact[at].astype(F32)
        rate = TIME_STEP / by_label(labels[at], rates)
        for c, (kx, ky, kz) in enumerate(((0, 3, 4), (3, 1, 5), (4, 5, 2))):
            faces = (
                lambda: jnp.where(odd_x, xg[0][5 + c], xg[1][5 + c]),
                lambda: jnp.where(odd_x, xg[1][5 + c], xg[0][5 + c]),
            )
            spot = (count + c * tall + lax.div(x, 8), pl.ds(lax.rem(x, 8), 1), slice(None))
            rows = low_high(odd_y, [y[spot] for y in yg])
            xu, xl = shift_x(stress, (kx,), x, at, block, steps, faces)
            yu, yl = shift_y(stress[ky, x], rows)
            zu, zl = shift_z(stress[kz, x], zg[x][:, c : c + 1], gz == 0)
            force = 0.5 * (((xu - xl) + (yu - yl)) + (zu - zl))
            speed = vel[c, at] + rate * (force + loaded * impact[c])
            vel_out[c, at] = speed
            disp_out[c, at] = disp[c, at] + TIME_STEP * speed


def cg_coefficients(k):
    zero, one = jnp.zeros_like(k[0]), jnp.ones_like(k[0])
    z, p, out = [one], [one], [zero, zero, zero]

    def form(a, b, moments):
        total = None
        for i, ai in enumerate(a):
            for j, bj in enumerate(b):
                term = ai * bj * moments[i + j]
                total = term if total is None else total + term
        return total

    energy = [k[j] - k[j + 1] for j in range(5)]
    rz = k[0]
    for step in range(3):
        alpha = jnp.clip(rz / form(p, p, energy), ALPHA_LOW, ALPHA_HIGH)
        out = [o + alpha * (p[i] if i < len(p) else zero) for i, o in enumerate(out)]
        if step == 2:
            break
        image = [(p[i] if i < len(p) else zero) - (p[i - 1] if i else zero) for i in range(len(p) + 1)]
        z = [(z[i] if i < len(z) else zero) - alpha * image[i] for i in range(len(image))]
        new = jnp.maximum(form(z, z, k), 0.0)
        beta = new / rz
        p = [z[i] + beta * (p[i] if i < len(p) else zero) for i in range(len(z))]
        rz = new
    return out


def final_kernel(mom, v0, v1, v2, damage_hbm, out_hbm, damage, out, in_sems, out_sems):
    count = v0.shape[0]
    block = count // CHUNKS
    loads, stores = [], []
    for chunk in range(CHUNKS):
        part = pl.ds(chunk * block, block)
        loads.append(pltpu.make_async_copy(damage_hbm.at[part], damage.at[part], in_sems.at[chunk]))
        stores.append(pltpu.make_async_copy(out.at[part], out_hbm.at[part], out_sems.at[chunk]))
        loads[-1].start()
    sums = jnp.sum(jnp.sum(mom[...], axis=0), axis=1, keepdims=True)
    c0, c1, c2 = cg_coefficients([sums[j : j + 1, :] for j in range(6)])
    for chunk in range(CHUNKS):
        loads[chunk].wait()
        for x in range(chunk * block, (chunk + 1) * block):
            dmg = damage[x]
            out[x] = jnp.maximum(dmg + (c0 * v0[x] + c1 * v1[x] + c2 * v2[x]), dmg)
        stores[chunk].start()
    for store in stores:
        store.wait()


def pairs_of(axis):
    count = lax.axis_size(axis)
    out = [[(i, i + 1) for i in range(start, count - 1, 2)] for start in (0, 1)]
    return [pairs for pairs in out if pairs]


def swap(array, axis, pairs):
    return lax.ppermute(array, axis, pairs + [(b, a) for a, b in pairs])


def swap_along(axis, arrays):
    return [swap(a, axis, pairs) for a, pairs in zip(arrays, pairs_of(axis), strict=True)]


def swap_diagonal(arrays):
    columns = lax.axis_size("gy")
    out = []
    both = [(xp, yp) for xp in pairs_of("gx") for yp in pairs_of("gy")]
    for array, (x_pairs, y_pairs) in zip(arrays, both, strict=True):
        joint = []
        for a, b in x_pairs:
            for c, d in y_pairs:
                joint.append((a * columns + c, b * columns + d))
                joint.append((a * columns + d, b * columns + c))
        out.append(swap(array, ("gx", "gy"), joint))
    return out


def spec_of(kind, a):
    if kind == "s":
        return pl.BlockSpec(memory_space=pltpu.SMEM)
    if kind == "v":
        return pl.BlockSpec(memory_space=pltpu.VMEM)
    if kind == "h":
        return pl.BlockSpec(memory_space=pltpu.HBM)
    if kind == "a":
        return pl.BlockSpec(memory_space=pl.ANY)
    lead = len(a.shape) - 3
    block = (*a.shape[:lead], a.shape[lead] // CHUNKS, *a.shape[lead + 1 :])
    return pl.BlockSpec(block, lambda i: (*(0,) * lead, i, 0, 0))


def call(kernel, kinds, ins, out_kinds, outs, flops, scratch=()):
    moved = sum(4 * a.size for a in (*ins, *outs))
    grid = (CHUNKS,) if "b" in (*kinds, *out_kinds) else ()
    return pl.pallas_call(
        kernel,
        out_shape=outs,
        grid=grid,
        in_specs=[spec_of(k, a) for k, a in zip(kinds, ins, strict=True)],
        out_specs=[spec_of(k, a) for k, a in zip(out_kinds, outs, strict=True)],
        scratch_shapes=scratch,
        compiler_params=pltpu.CompilerParams(vmem_limit_bytes=VMEM_BYTES),
        cost_estimate=pl.CostEstimate(flops=flops, bytes_accessed=moved, transcendentals=0),
    )(*ins)


def per_device(displacement, velocity, damage, history, contact, notch, labels, table, impact):
    nx, ny, nz = damage.shape
    size = damage.size
    n_y = len(pairs_of("gy"))
    pos = jnp.stack(
        [lax.axis_index("gx") % 2, lax.axis_index("gy") % 2, lax.axis_index("gz")]
    ).astype(jnp.int32)

    def arr(*shape):
        return jax.ShapeDtypeStruct(shape, F32)

    field, fields3, small = arr(nx, ny, nz), arr(3, nx, ny, nz), arr(8, 128)
    columns = arr(nx, ny, 128)
    z_pairs = [(0, 1)]

    disp_here, damage_here, *sent = call(
        functools.partial(pack_kernel, n_y),
        "shh",
        (pos, displacement, damage),
        "vv" + "v" * (3 + n_y),
        [fields3, field, *[arr(4, ny, nz)] * 2, *[arr(4, nx, nz)] * n_y, columns],
        size,
        [pltpu.SemaphoreType.DMA((CHUNKS, 2))],
    )
    got = [
        *swap_along("gx", sent[:2]),
        *swap_along("gy", sent[2 : 2 + n_y]),
        swap(sent[-1], "gz", z_pairs),
    ]
    n_sent = 3 + 3 * n_y
    hist, rd, v0, stress, mom, *sent = call(
        functools.partial(local_kernel, n_y),
        "ssvvvvv" + "v" * (3 + n_y),
        (pos, table, disp_here, damage_here, history, notch, labels, *got),
        "bvvvv" + "v" * n_sent,
        [
            field,
            field,
            field,
            arr(6, nx, ny, nz),
            small,
            *[arr(8, ny, nz)] * 2,
            *[arr(nx + 3 * (nx // 8), 8, nz)] * n_y,
            *[arr(2, 8, nz)] * (2 * n_y),
            columns,
        ],
        150 * size,
        [pltpu.VMEM((8, 128), F32)],
    )
    xy = [
        *swap_along("gx", sent[:2]),
        *swap_along("gy", sent[2 : 2 + n_y]),
        *swap_diagonal(sent[2 + n_y : 2 + 3 * n_y]),
    ]
    stress_z = swap(sent[-1], "gz", z_pairs)
    (joined,) = call(
        functools.partial(join_kernel, n_y),
        "svv" + "v" * len(xy),
        (pos, v0, rd, *xy),
        "v",
        [arr(nx + 6, ny + 8, 128)],
        4 * size,
    )
    z_got = swap(joined, "gz", z_pairs)
    new_disp, new_vel, token = call(
        functools.partial(force_kernel, n_y),
        "sssbbbbv" + "v" * (3 + n_y),
        (
            pos,
            table,
            impact,
            displacement,
            velocity,
            contact,
            labels,
            stress,
            *xy[: 2 + n_y],
            stress_z,
        ),
        "bbv",
        [fields3, fields3, small],
        60 * size,
    )
    peers = lax.axis_size("gx") * lax.axis_size("gy") * lax.axis_size("gz")
    v1, v2, spread = call(
        functools.partial(krylov_kernel, n_y),
        "svvvav" + "v" * len(xy),
        (pos, v0, rd, mom, token, z_got, *xy),
        "vvv",
        [field, field, arr(peers, 8, 128)],
        60 * size,
        [
            pltpu.VMEM((nx + 6, ny + 8, nz + 128), F32),
            pltpu.VMEM((nx + 6, ny + 8, nz + 128), F32),
            pltpu.VMEM((nx + 4, ny + 8, nz + 128), F32),
            pltpu.VMEM((nx + 2, ny + 8, nz + 128), F32),
        ],
    )
    mom = lax.all_to_all(spread, ("gx", "gy", "gz"), 0, 0, tiled=True)
    (damage_new,) = call(
        final_kernel,
        "vvvvh",
        (mom, v0, v1, v2, damage),
        "h",
        [field],
        8 * size,
        [
            pltpu.VMEM((nx, ny, nz), F32),
            pltpu.VMEM((nx, ny, nz), F32),
            pltpu.SemaphoreType.DMA((CHUNKS,)),
            pltpu.SemaphoreType.DMA((CHUNKS,)),
        ],
    )
    return new_disp, new_vel, hist, damage_new


def solution(mesh):
    placed = (
        P(None, ("case", "gx"), "gy", "gz"),
        P(None, ("case", "gx"), "gy", "gz"),
        P(("case", "gx"), "gy", "gz"),
        P(("case", "gx"), "gy", "gz"),
        P(("case", "gx"), "gy", "gz"),
        P(("case", "gx"), "gy", "gz"),
        P(("case", "gx"), "gy", "gz"),
        P(),
        P("case"),
    )
    return jax.shard_map(
        per_device,
        mesh=mesh,
        in_specs=placed,
        out_specs=(
            P(None, ("case", "gx"), "gy", "gz"),
            P(None, ("case", "gx"), "gy", "gz"),
            P(("case", "gx"), "gy", "gz"),
            P(("case", "gx"), "gy", "gz"),
        ),
        check_vma=False,
    )
```

time: 380 us -> 56.5 us (0.15)
  blocking collectives: 157 us -> 13.5 us
  other arithmetic: 89.6 us -> 0.08 us
  starting transfers between devices: 71.1 us -> 15.8 us
  local copies, waits for them, and re-layouts: 31.6 us -> 2.49 us
  Pallas kernels: 0 us -> 17.7 us
  waiting for transfers between devices: 20.1 us -> 5.9 us
  between operations: 7.93 us -> 0.79 us
    psum x5 -> x0, blocking collectives: 157 us -> none  [the longest x3 96.5 us: inner_rz(): return lax.psum(jnp.sum(residual * precond), ('gx', 'gy', 'gz'))]
    ppermute x30 -> x11, starting transfers between devices: 71.1 us -> 15.8 us  [swap(): return lax.ppermute(array, axis, pairs + [(b, a) for a, b in pairs])]
    unnamed x5 -> x0, other arithmetic: 23.4 us -> none
    another operation x5 -> x1, other arithmetic: 19 us -> 0.08 us  [per_device(): jnp.stack([lax.axis_index('gx') % 2, lax.axis_index('gy') % 2, lax.axis_i...]
    pallas_call x0 -> x6, Pallas kernels: none -> 17.7 us  [call(): pl.pallas_call(kernel, out_shape=outs, grid=grid, in_specs=[spec_of(k, a)...]
    concatenate x10 -> x0, other arithmetic: 17.6 us -> none  [padded_2(): block = jnp.concatenate([low, block, high], axis=dim)]
    slice x15 -> x0, local copies, waits for them, and re-layouts: 17.3 us -> none  [the longest x8 10.4 us: padded_2(): lax.slice_in_dim(block, block.shape[dim] - width, None, axis=dim)]
    ppermute x30 -> x11, waiting for transfers between devices: 20.1 us -> 5.9 us  [swap(): return lax.ppermute(array, axis, pairs + [(b, a) for a, b in pairs])]
  transfers between devices with their start and end apart: 30 -> 11, of which waited for: 10 -> 3; matrix products, arithmetic and copies ran while one was open for 10% -> 0% of each run, Pallas kernels for 0% -> 7%
where the time goes in v3:
time: 56.5 us; the launch traced here: 56.2 us
  Pallas kernels  17.7 us (31%)
  starting transfers between devices  15.8 us (28%)
  blocking collectives  13.5 us (24%)
  waiting for transfers between devices  5.9 us (10%)
  local copies, waits for them, and re-layouts  2.49 us (4%)
  between operations  0.79 us (1%)
    pallas_call x6, Pallas kernels, call(): pl.pallas_call(kernel, out_shape=outs, grid=grid, in_specs=[spec_of(k, a)...  17.7 us
    ppermute x11, starting transfers between devices, swap(): return lax.ppermute(array, axis, pairs + [(b, a) for a, b in pairs])  15.8 us
    all_to_all x1, blocking collectives, per_device(): mom = lax.all_to_all(spread, ('gx', 'gy', 'gz'), 0, 0, tiled=True)  13.5 us
    ppermute x11, waiting for transfers between devices, swap(): return lax.ppermute(array, axis, pairs + [(b, a) for a, b in pairs])  5.9 us
    unnamed x22, local copies, waits for them, and re-layouts  2.49 us
  transfers between devices with their start and end apart: 11, of which 3 were waited for; matrix products, arithmetic and copies ran while one was open for 0% of the time, Pallas kernels for 7%

profile of v3, /device:TPU:0, one launch (start us, length us, event | category | flops | bytes accessed | tf_op | source)
XLA Modules:
  0.0 56.2 jit_solution(10566704353319740252)
XLA Ops:
  0.6 0.0 copy-start.9
  0.7 0.1 pad_add_fusion.pos
  0.7 0.0 copy-start
  0.7 1.4 %copy-done = f32[3,16,32,256]{3,2,1,0:T(8,128)S(1)} copy-done((f32[3,16,32,256]{3,2,1,0:T(8,128)S(1)}, f32[3,16,32,256]{3,2,1,0:T(8,128)}, u32[]{:S(2)}) %copy-start) | copy-done | bytes 1572888
  2.1 0.0 copy-start.2
  2.1 1.0 %copy-done.2 = f32[16,32,256]{2,1,0:T(8,128)S(1)} copy-done((f32[16,32,256]{2,1,0:T(8,128)S(1)}, f32[16,32,256]{2,1,0:T(8,128)}, u32[]{:S(2)}) %copy-start.2) | copy-done | bytes 524312
  3.2 0.0 copy-start.4
  3.2 0.0 copy-start.7
  3.2 0.0 copy-start.8
  3.2 2.1 %shard_map.120 = (f32[3,16,32,256]{3,2,1,0:T(8,128)S(1)}, f32[16,32,256]{2,1,0:T(8,128)S(1)}, f32[4,32,256]{2,1,0:T(8,128)S(1)}, f32[4,32,256]{2,1,0:T(8,128)S(1...) custom-call(s32[3]{0:T(128)S(1)} %pad_add_fusion.pos, f32[3,16,32,256]{3,2,1,0:T(8,128)S(1)} %copy-done, ...), custom_call_target="tpu_custom_call" | custom-call | flops 131072 | bytes 4784140 | tf_op jit(solution)/shard_map/pallas_call | solution.py:540
  5.3 0.5 collective-permute-start.3
  5.8 2.6 %collective-permute-start = (f32[4,32,256]{2,1,0:T(8,128)S(1)}, f32[4,32,256]{2,1,0:T(8,128)S(1)}, u32[]{:S(2)}, u32[]{:S(2)}) collective-permute-start(f32[4,32,256]{2,1,0:T(8,128)S(1)} %get-tuple-element.29), channel_id=1, source_target_pairs={{0,4},{8,12},{4,0},{12,8},{1,5},{9,13},{5,1},{13,9},{2,6},{10,14},... | collective-permute-start | bytes 393224 | tf_op jit(solution)/shard_map/ppermute | solution.py:502
  8.5 0.7 %collective-permute-start.1 = (f32[4,32,256]{2,1,0:T(8,128)S(1)}, f32[4,32,256]{2,1,0:T(8,128)S(1)}, u32[]{:S(2)}, u32[]{:S(2)}) collective-permute-start(f32[4,32,256]{2,1,0:T(8,128)S(1)} %get-tuple-element.30), channel_id=1, source_target_pairs={{4,8},{8,4},{5,9},{9,5},{6,10},{10,6},{7,11},{11,7},{20,24},{24,20... | collective-permute-start | bytes 393224 | tf_op jit(solution)/shard_map/ppermute | solution.py:502
  9.2 1.6 %collective-permute-start.2 = (f32[4,16,256]{2,1,0:T(8,128)S(1)}, f32[4,16,256]{2,1,0:T(8,128)S(1)}, u32[]{:S(2)}, u32[]{:S(2)}) collective-permute-start(f32[4,16,256]{2,1,0:T(8,128)S(1)} %get-tuple-element.31), channel_id=1, source_target_pairs={{0,2},{2,0},{1,3},{3,1},{4,6},{6,4},{5,7},{7,5},{8,10},{10,8},{9,1... | collective-permute-start | bytes 196616 | tf_op jit(solution)/shard_map/ppermute | solution.py:502
  10.7 2.8 %collective-permute-done.2.refs_2_ = f32[4,16,256]{2,1,0:T(8,128)S(1)} collective-permute-done((f32[4,16,256]{2,1,0:T(8,128)S(1)}, f32[4,16,256]{2,1,0:T(8,128)S(1)}, u32[]{:S(2)}, u32[]{:S(2)}) %collective-permute-start.2) | collective-permute-done | bytes 65568 | tf_op jit(solution)/shard_map/ppermute | solution.py:502
  13.5 0.0 collective-permute-done.refs_0_
  13.5 0.0 collective-permute-done.1.refs_1_
  13.5 0.0 collective-permute-done.3.refs_3_
  13.5 0.0 copy-done.9
  13.5 0.0 copy-done.4
  13.5 0.0 copy-done.7
  13.5 0.0 copy-done.8
  13.5 0.0 copy-start.5
  13.6 4.9 %shard_map.121 = (f32[16,32,256]{2,1,0:T(8,128)}, f32[16,32,256]{2,1,0:T(8,128)S(1)}, f32[16,32,256]{2,1,0:T(8,128)S(1)}, f32[6,16,32,256]{3,2,1,0:T(8,128)S(1)}...) custom-call(s32[3]{0:T(128)S(1)} %pad_add_fusion.pos, ...), custom_call_target="tpu_custom_call" | custom-call | flops 19660800 | bytes 9982028 | tf_op jit(solution)/shard_map/pallas_call | solution.py:540
  18.5 0.0 copy-start.1
  18.5 0.0 copy-start.6
  18.5 0.0 copy-start.10
  18.5 4.5 %collective-permute-start.4 = (f32[8,32,256]{2,1,0:T(8,128)S(1)}, f32[8,32,256]{2,1,0:T(8,128)S(1)}, u32[]{:S(2)}, u32[]{:S(2)}) collective-permute-start(f32[8,32,256]{2,1,0:T(8,128)S(1)} %get-tuple-element.34), channel_id=1, source_target_pairs={{0,4},{8,12},{4,0},{12,8},{1,5},{9,13},{5,1},{13,9},{2,6},{10,14},... | collective-permute-start | bytes 786440 | tf_op jit(solution)/shard_map/ppermute | solution.py:502
  22.9 0.7 %collective-permute-start.5 = (f32[8,32,256]{2,1,0:T(8,128)S(1)}, f32[8,32,256]{2,1,0:T(8,128)S(1)}, u32[]{:S(2)}, u32[]{:S(2)}) collective-permute-start(f32[8,32,256]{2,1,0:T(8,128)S(1)} %get-tuple-element.35), channel_id=1, source_target_pairs={{4,8},{8,4},{5,9},{9,5},{6,10},{10,6},{7,11},{11,7},{20,24},{24,20... | collective-permute-start | bytes 786440 | tf_op jit(solution)/shard_map/ppermute | solution.py:502
  23.6 1.6 %collective-permute-start.6 = (f32[22,8,256]{2,1,0:T(8,128)S(1)}, f32[22,8,256]{2,1,0:T(8,128)S(1)}, u32[]{:S(2)}, u32[]{:S(2)}) collective-permute-start(f32[22,8,256]{2,1,0:T(8,128)S(1)} %get-tuple-element.36), channel_id=1, source_target_pairs={{0,2},{2,0},{1,3},{3,1},{4,6},{6,4},{5,7},{7,5},{8,10},{10,8},{9,1... | collective-permute-start | bytes 540680 | tf_op jit(solution)/shard_map/ppermute | solution.py:502
  25.2 2.5 %collective-permute-start.8 = (f32[2,8,256]{2,1,0:T(8,128)S(1)}, f32[2,8,256]{2,1,0:T(8,128)S(1)}, u32[]{:S(2)}, u32[]{:S(2)}) collective-permute-start(f32[2,8,256]{2,1,0:T(8,128)S(1)} %get-tuple-element.45), channel_id=1, source_target_pairs={{0,6},{2,4},{8,14},{10,12},{6,0},{4,2},{14,8},{12,10},{1,7},{3,5},... | collective-permute-start | bytes 49160 | tf_op jit(solution)/shard_map/ppermute | solution.py:502
  27.7 0.7 %collective-permute-start.9 = (f32[2,8,256]{2,1,0:T(8,128)S(1)}, f32[2,8,256]{2,1,0:T(8,128)S(1)}, u32[]{:S(2)}, u32[]{:S(2)}) collective-permute-start(f32[2,8,256]{2,1,0:T(8,128)S(1)} %get-tuple-element.46), channel_id=1, source_target_pairs={{4,10},{6,8},{10,4},{8,6},{5,11},{7,9},{11,5},{9,7},{20,26},{22,24... | collective-permute-start | bytes 49160 | tf_op jit(solution)/shard_map/ppermute | solution.py:502
  28.4 1.4 %collective-permute-done.8.refs_3_ = f32[2,8,256]{2,1,0:T(8,128)S(1)} collective-permute-done((f32[2,8,256]{2,1,0:T(8,128)S(1)}, f32[2,8,256]{2,1,0:T(8,128)S(1)}, u32[]{:S(2)}, u32[]{:S(2)}) %collective-permute-start.8) | collective-permute-done | bytes 16416 | tf_op jit(solution)/shard_map/ppermute | solution.py:502
  29.8 0.0 collective-permute-done.9.refs_4_
  29.8 0.0 collective-permute-done.6.refs_2_
  29.8 0.0 collective-permute-done.4.refs_0_
  29.8 0.0 collective-permute-done.5.refs_1_
  29.8 1.0 %shard_map.123 = f32[22,40,128]{2,1,0:T(8,128)S(1)} custom-call(s32[3]{0:T(128)S(1)} %pad_add_fusion.pos, f32[16,32,256]{2,1,0:T(8,128)S(1)} %get-tuple-element.41.v.v0, f32[16,32,256]{2,1,0:T(8,128)S(1)} %get-tuple-element.42.rd, f32[8,32,256]{2,1,0:T(8,128)S(1)} %collective-permute-done.4.refs_0_, f32[8,32,256]{2,1,0:T(8,128)S(1)} %collective-permute-done.5.refs_1_, ...), custom_call_target="tpu_custom_call" | custom-call | flops 524288 | bytes 2236428 | tf_op jit(solution)/shard_map/pallas_call | solution.py:540
  30.8 0.1 collective-permute-start.10
  30.9 0.5 collective-permute-start.7
  31.4 1.7 %collective-permute-done.7.refs_3_ = f32[16,32,128]{2,1,0:T(8,128)S(1)} collective-permute-done((f32[16,32,128]{2,1,0:T(8,128)S(1)}, f32[16,32,128]{2,1,0:T(8,128)S(1)}, u32[]{:S(2)}, u32[]{:S(2)}) %collective-permute-start.7) | collective-permute-done | bytes 262176 | tf_op jit(solution)/shard_map/ppermute | solution.py:502
  33.1 0.0 copy-done.5
  33.1 0.0 copy-done.1
  33.1 0.0 copy-done.6
  33.1 0.0 copy-done.10
  33.1 4.0 %shard_map.122 = (f32[3,16,32,256]{3,2,1,0:T(8,128)}, f32[3,16,32,256]{3,2,1,0:T(8,128)}, f32[8,128]{1,0:T(8,128)S(1)}) custom-call(s32[3]{0:T(128)S(1)} %pad_add_fusion.pos, f32[4,4]{1,0:T(4,128)S(1)} %copy-done.9, f32[3]{0:T(128)S(1)} %copy-done.10, f32[3,16,32,256]{3,2,1,0:T(8,128)S(1)} %copy-done.1, f32[3,16,32,256]{3,2,1,0:T(8,128)S(1)} %copy-done.5, ...), custom_call_target="tpu_custom_call" | custom-call | flops 7864320 | bytes 11456600 | tf_op jit(solution)/shard_map/pallas_call | solution.py:540
  37.1 0.0 copy-start.3
  37.1 0.0 collective-permute-done.10.z_got
  37.1 3.8 %shard_map.124 = (f32[16,32,256]{2,1,0:T(8,128)S(1)}, f32[16,32,256]{2,1,0:T(8,128)S(1)}, f32[16,8,128]{2,1,0:T(8,128)S(1)}) custom-call(s32[3]{0:T(128)S(1)} %pad_add_fusion.pos, f32[16,32,256]{2,1,0:T(8,128)S(1)} %get-tuple-element.41.v.v0, f32[16,32,256]{2,1,0:T(8,128)S(1)} %get-tuple-element.42.rd, f32[8,128]{1,0:T(8,128)S(1)} %get-tuple-element.43.mom, ...), custom_call_target="tpu_custom_call" | custom-call | flops 7864320 | bytes 3358732 | tf_op jit(solution)/shard_map/pallas_call | solution.py:540
  40.9 13.5 %all_to_all.5.mom = f32[16,8,128]{2,1,0:T(8,128)S(1)} all-to-all(f32[16,8,128]{2,1,0:T(8,128)S(1)} %get-tuple-element.47), channel_id=1, replica_groups=mesh['case'=2,'gx'=4,'gy'=2,'gz'=2] {'gx','gy','gz'}, dimensions={0} | all-to-all | bytes 131072 | tf_op jit(solution)/shard_map/all_to_all | solution.py:650
  54.4 0.0 copy-done.3
  54.5 1.8 %shard_map.125 = f32[16,32,256]{2,1,0:T(8,128)} custom-call(f32[16,8,128]{2,1,0:T(8,128)S(1)} %all_to_all.5.mom, f32[16,32,256]{2,1,0:T(8,128)S(1)} %get-tuple-element.41.v.v0, f32[16,32,256]{2,1,0:T(8,128)S(1)} %get-tuple-element.48.v1, f32[16,32,256]{2,1,0:T(8,128)S(1)} %get-tuple-element.49.v2, f32[16,32,256]{2,1,0:T(8,128)S(1)} %copy-done.3), custom_call_target="tpu_custom_call" | custom-call | flops 1048576 | bytes 2686976 | tf_op jit(solution)/shard_map/pallas_call | solution.py:540
Async XLA Ops:
  0.6 12.9 %copy-start.9 = (f32[4,4]{1,0:T(4,128)S(1)}, f32[4,4]{1,0:T(4,128)}, u32[]{:S(2)}) copy-start(f32[4,4]{1,0:T(4,128)} %table.3) | copy-start | bytes 196
  0.7 1.4 %copy-start = (f32[3,16,32,256]{3,2,1,0:T(8,128)S(1)}, f32[3,16,32,256]{3,2,1,0:T(8,128)}, u32[]{:S(2)}) copy-start(f32[3,16,32,256]{3,2,1,0:T(8,128)} %disp.1) | copy-start | bytes 4718596
  2.1 1.0 %copy-start.2 = (f32[16,32,256]{2,1,0:T(8,128)S(1)}, f32[16,32,256]{2,1,0:T(8,128)}, u32[]{:S(2)}) copy-start(f32[16,32,256]{2,1,0:T(8,128)} %damage_hbm.3) | copy-start | bytes 1572868
  3.2 10.3 %copy-start.4 = (s32[16,32,256]{2,1,0:T(8,128)S(1)}, s32[16,32,256]{2,1,0:T(8,128)}, u32[]{:S(2)}) copy-start(s32[16,32,256]{2,1,0:T(8,128)} %labels.3) | copy-start | bytes 1572868
  3.2 10.3 %copy-start.7 = (f32[16,32,256]{2,1,0:T(8,128)S(1)}, f32[16,32,256]{2,1,0:T(8,128)}, u32[]{:S(2)}) copy-start(f32[16,32,256]{2,1,0:T(8,128)} %history.1) | copy-start | bytes 1572868
  3.2 10.3 %copy-start.8 = (s32[16,32,256]{2,1,0:T(8,128)S(1)}, s32[16,32,256]{2,1,0:T(8,128)}, u32[]{:S(2)}) copy-start(s32[16,32,256]{2,1,0:T(8,128)} %notch.1) | copy-start | bytes 1572868
  5.3 8.2 %collective-permute-start.3 = (f32[16,32,128]{2,1,0:T(8,128)S(1)}, f32[16,32,128]{2,1,0:T(8,128)S(1)}, u32[]{:S(2)}, u32[]{:S(2)}) collective-permute-start(f32[16,32,128]{2,1,0:T(8,128)S(1)} %get-tuple-element.32), channel_id=1, source_target_pairs={{0,1},{1,0},{2,3},{3,2},{4,5},{5,4},{6,7},{7,6},{8,9},{9,8},{10,11... | collective-permute-start | bytes 786440 | tf_op jit(solution)/shard_map/ppermute | solution.py:502
  5.8 7.6 %collective-permute-start = (f32[4,32,256]{2,1,0:T(8,128)S(1)}, f32[4,32,256]{2,1,0:T(8,128)S(1)}, u32[]{:S(2)}, u32[]{:S(2)}) collective-permute-start(f32[4,32,256]{2,1,0:T(8,128)S(1)} %get-tuple-element.29), channel_id=1, source_target_pairs={{0,4},{8,12},{4,0},{12,8},{1,5},{9,13},{5,1},{13,9},{2,6},{10,14},... | collective-permute-start | bytes 393224 | tf_op jit(solution)/shard_map/ppermute | solution.py:502
  8.5 5.0 %collective-permute-start.1 = (f32[4,32,256]{2,1,0:T(8,128)S(1)}, f32[4,32,256]{2,1,0:T(8,128)S(1)}, u32[]{:S(2)}, u32[]{:S(2)}) collective-permute-start(f32[4,32,256]{2,1,0:T(8,128)S(1)} %get-tuple-element.30), channel_id=1, source_target_pairs={{4,8},{8,4},{5,9},{9,5},{6,10},{10,6},{7,11},{11,7},{20,24},{24,20... | collective-permute-start | bytes 393224 | tf_op jit(solution)/shard_map/ppermute | solution.py:502
  9.2 4.3 %collective-permute-start.2 = (f32[4,16,256]{2,1,0:T(8,128)S(1)}, f32[4,16,256]{2,1,0:T(8,128)S(1)}, u32[]{:S(2)}, u32[]{:S(2)}) collective-permute-start(f32[4,16,256]{2,1,0:T(8,128)S(1)} %get-tuple-element.31), channel_id=1, source_target_pairs={{0,2},{2,0},{1,3},{3,1},{4,6},{6,4},{5,7},{7,5},{8,10},{10,8},{9,1... | collective-permute-start | bytes 196616 | tf_op jit(solution)/shard_map/ppermute | solution.py:502
  13.5 19.6 %copy-start.5 = (f32[3,16,32,256]{3,2,1,0:T(8,128)S(1)}, f32[3,16,32,256]{3,2,1,0:T(8,128)}, u32[]{:S(2)}) copy-start(f32[3,16,32,256]{3,2,1,0:T(8,128)} %vel.1) | copy-start | bytes 4718596
  18.5 14.6 %copy-start.1 = (f32[3,16,32,256]{3,2,1,0:T(8,128)S(1)}, f32[3,16,32,256]{3,2,1,0:T(8,128)}, u32[]{:S(2)}) copy-start(f32[3,16,32,256]{3,2,1,0:T(8,128)} %disp.1) | copy-start | bytes 4718596
  18.5 14.6 %copy-start.6 = (s32[16,32,256]{2,1,0:T(8,128)S(1)}, s32[16,32,256]{2,1,0:T(8,128)}, u32[]{:S(2)}) copy-start(s32[16,32,256]{2,1,0:T(8,128)} %contact.1) | copy-start | bytes 1572868
  18.5 14.6 %copy-start.10 = (f32[3]{0:T(128)S(1)}, f32[3]{0:T(128)}, u32[]{:S(2)}) copy-start(f32[3]{0:T(128)} %impact.1) | copy-start | bytes 40
  18.5 11.3 %collective-permute-start.4 = (f32[8,32,256]{2,1,0:T(8,128)S(1)}, f32[8,32,256]{2,1,0:T(8,128)S(1)}, u32[]{:S(2)}, u32[]{:S(2)}) collective-permute-start(f32[8,32,256]{2,1,0:T(8,128)S(1)} %get-tuple-element.34), channel_id=1, source_target_pairs={{0,4},{8,12},{4,0},{12,8},{1,5},{9,13},{5,1},{13,9},{2,6},{10,14},... | collective-permute-start | bytes 786440 | tf_op jit(solution)/shard_map/ppermute | solution.py:502
  22.9 6.9 %collective-permute-start.5 = (f32[8,32,256]{2,1,0:T(8,128)S(1)}, f32[8,32,256]{2,1,0:T(8,128)S(1)}, u32[]{:S(2)}, u32[]{:S(2)}) collective-permute-start(f32[8,32,256]{2,1,0:T(8,128)S(1)} %get-tuple-element.35), channel_id=1, source_target_pairs={{4,8},{8,4},{5,9},{9,5},{6,10},{10,6},{7,11},{11,7},{20,24},{24,20... | collective-permute-start | bytes 786440 | tf_op jit(solution)/shard_map/ppermute | solution.py:502
  23.6 6.2 %collective-permute-start.6 = (f32[22,8,256]{2,1,0:T(8,128)S(1)}, f32[22,8,256]{2,1,0:T(8,128)S(1)}, u32[]{:S(2)}, u32[]{:S(2)}) collective-permute-start(f32[22,8,256]{2,1,0:T(8,128)S(1)} %get-tuple-element.36), channel_id=1, source_target_pairs={{0,2},{2,0},{1,3},{3,1},{4,6},{6,4},{5,7},{7,5},{8,10},{10,8},{9,1... | collective-permute-start | bytes 540680 | tf_op jit(solution)/shard_map/ppermute | solution.py:502
  25.2 4.6 %collective-permute-start.8 = (f32[2,8,256]{2,1,0:T(8,128)S(1)}, f32[2,8,256]{2,1,0:T(8,128)S(1)}, u32[]{:S(2)}, u32[]{:S(2)}) collective-permute-start(f32[2,8,256]{2,1,0:T(8,128)S(1)} %get-tuple-element.45), channel_id=1, source_target_pairs={{0,6},{2,4},{8,14},{10,12},{6,0},{4,2},{14,8},{12,10},{1,7},{3,5},... | collective-permute-start | bytes 49160 | tf_op jit(solution)/shard_map/ppermute | solution.py:502
  27.7 2.1 %collective-permute-start.9 = (f32[2,8,256]{2,1,0:T(8,128)S(1)}, f32[2,8,256]{2,1,0:T(8,128)S(1)}, u32[]{:S(2)}, u32[]{:S(2)}) collective-permute-start(f32[2,8,256]{2,1,0:T(8,128)S(1)} %get-tuple-element.46), channel_id=1, source_target_pairs={{4,10},{6,8},{10,4},{8,6},{5,11},{7,9},{11,5},{9,7},{20,26},{22,24... | collective-permute-start | bytes 49160 | tf_op jit(solution)/shard_map/ppermute | solution.py:502
  30.8 6.3 %collective-permute-start.10 = (f32[22,40,128]{2,1,0:T(8,128)S(1)}, f32[22,40,128]{2,1,0:T(8,128)S(1)}, u32[]{:S(2)}, u32[]{:S(2)}) collective-permute-start(f32[22,40,128]{2,1,0:T(8,128)S(1)} %shard_map.123), channel_id=1, source_target_pairs={{0,1},{1,0},{2,3},{3,2},{4,5},{5,4},{6,7},{7,6},{8,9},{9,8},{10,11... | collective-permute-start | bytes 1351688 | tf_op jit(solution)/shard_map/ppermute | solution.py:502
  30.9 2.2 %collective-permute-start.7 = (f32[16,32,128]{2,1,0:T(8,128)S(1)}, f32[16,32,128]{2,1,0:T(8,128)S(1)}, u32[]{:S(2)}, u32[]{:S(2)}) collective-permute-start(f32[16,32,128]{2,1,0:T(8,128)S(1)} %get-tuple-element.37), channel_id=1, source_target_pairs={{0,1},{1,0},{2,3},{3,2},{4,5},{5,4},{6,7},{7,6},{8,9},{9,8},{10,11... | collective-permute-start | bytes 786440 | tf_op jit(solution)/shard_map/ppermute | solution.py:502
  37.1 17.3 %copy-start.3 = (f32[16,32,256]{2,1,0:T(8,128)S(1)}, f32[16,32,256]{2,1,0:T(8,128)}, u32[]{:S(2)}) copy-start(f32[16,32,256]{2,1,0:T(8,128)} %damage_hbm.3) | copy-start | bytes 1572868

commit v4 on v3

--- a/solution.py
+++ b/solution.py
@@ -12,6 +12,7 @@
 STIFF_FLOOR = 0.001
 ALPHA_LOW, ALPHA_HIGH = 0.5, 6.5
 VMEM_BYTES = 28 * 1024 * 1024
+MOST_VMEM_BYTES = 60 * 1024 * 1024
 CHUNKS = 4
 F32 = jnp.float32
 
@@ -32,16 +33,7 @@
         refs[1][index] = jnp.where(odd, high, low)
 
 
-def send_early(odd, refs, index, plane, is_low):
-    def store(ref):
-        ref[index] = plane
-
-    at_odd, at_even = (0, 1) if is_low else (1, 0)
-    pl.when(odd)(functools.partial(store, refs[at_odd]))
-    pl.when(jnp.logical_not(odd))(functools.partial(store, refs[at_even]))
-
-
-def shift_x(ref, lead, x, at, block, steps, faces):
+def shift_x(ref, lead, x, at, block, faces):
     count = ref.shape[-3]
     lo, hi = faces
     if at > 0:
@@ -114,8 +106,8 @@
 
 
 def pack_kernel(n_y, pos, disp_hbm, damage_hbm, *refs):
-    disp, damage, *rest = refs
-    xs, ys, zs, sems = rest[:2], rest[2 : 2 + n_y], rest[2 + n_y], rest[-1]
+    xs, ys, zs = refs[:2], refs[2 : 2 + n_y], refs[2 + n_y]
+    disp, damage, sems = refs[3 + n_y :]
     odd_x, odd_y, gz = pos[0] == 1, pos[1] == 1, pos[2]
     count = damage.shape[0]
     block = count // CHUNKS
@@ -161,18 +153,22 @@
 def local_kernel(n_y, pos, table, disp, damage, history, notch, labels, *refs):
     xg, yg, zg = refs[:2], refs[2 : 2 + n_y], refs[2 + n_y]
     refs = refs[3 + n_y :]
-    hist_out, rd_out, v_out, stress_out, mom_out = refs[:5]
+    hist_hbm, rd_out, v_out, stress_out, mom_out = refs[:5]
     refs = refs[5:]
-    xs, ys, ds, zs, held = refs[:2], refs[2 : 2 + n_y], refs[2 + n_y : 2 + 3 * n_y], refs[-2], refs[-1]
+    xs, ys, ds = refs[:2], refs[2 : 2 + n_y], refs[2 + n_y : 2 + 3 * n_y]
+    zs, hist_out, sems = refs[2 + 3 * n_y :]
     odd_x, odd_y, gz = pos[0] == 1, pos[1] == 1, pos[2]
-    step, steps = pl.program_id(0), pl.num_programs(0)
     count = damage.shape[0]
-    block = hist_out.shape[0]
+    block = count // CHUNKS
     tall = count // 8
     regions = table.shape[1]
     lames = [table[0, r] for r in range(regions)]
     shears = [table[1, r] for r in range(regions)]
-    fractures = [table[3, r] for r in range(regions)]
+    bases = [table[3, r] for r in range(regions)]
+
+    def store(step):
+        part = pl.ds(step * block, block)
+        return pltpu.make_async_copy(hist_out.at[part], hist_hbm.at[part], sems.at[step])
 
     def around(ref, lead, field, plane, x, at):
         faces = (
@@ -182,49 +178,41 @@
         rows = low_high(odd_y, [y[field, pl.ds(x, 1), :] for y in yg])
         column = zg[x][:, field : field + 1]
         return (
-            shift_x(ref, lead, x, at, block, steps, faces),
+            shift_x(ref, lead, x, at, block, faces),
             shift_y(plane, rows),
             shift_z(plane, column, gz == 0),
         )
 
-    total = jnp.where(step == 0, 0.0, held[...])
-    for at in range(block):
-        x = step * block + at
+    def body(x, at):
         g = []
         for c in range(3):
             pairs = around(disp, (c,), c, disp[c, x], x, at)
-            g.append([0.5 * (upper - lower) for upper, lower in pairs])
+            g.append([upper - lower for upper, lower in pairs])
         lab = labels[x]
         lame = by_label(lab, lames)
         shear = by_label(lab, shears)
-        fracture = by_label(lab, fractures)
+        base = by_label(lab, bases)
         dmg = damage[x]
-        degrade = (1.0 - dmg) * (1.0 - dmg) + STIFF_FLOOR
+        degrade = 4.0 * ((1.0 - dmg) * (1.0 - dmg) + STIFF_FLOOR)
         trace = g[0][0] + g[1][1] + g[2][2]
-        strain = [
-            g[0][0],
-            g[1][1],
-            g[2][2],
-            0.5 * (g[0][1] + g[1][0]),
-            0.5 * (g[0][2] + g[2][0]),
-            0.5 * (g[1][2] + g[2][1]),
-        ]
+        shears3 = [g[0][1] + g[1][0], g[0][2] + g[2][0], g[1][2] + g[2][1]]
         positive = jnp.maximum(trace, 0.0)
-        squares = strain[0] * strain[0] + strain[1] * strain[1] + strain[2] * strain[2]
-        squares = squares + 2.0 * (
-            strain[3] * strain[3] + strain[4] * strain[4] + strain[5] * strain[5]
+        squares = g[0][0] * g[0][0] + g[1][1] * g[1][1] + g[2][2] * g[2][2]
+        squares = (squares + squares) + (
+            shears3[0] * shears3[0] + shears3[1] * shears3[1] + shears3[2] * shears3[2]
         )
-        energy = 0.5 * lame * positive * positive + shear * squares
-        scale = degrade * (2.0 * shear)
-        base = degrade * (lame * trace)
-        stress = [base + scale * strain[k] if k < 3 else scale * strain[k] for k in range(6)]
+        energy = lame * positive * positive + shear * squares
+        half = degrade * shear
+        whole = half + half
+        level = (degrade * lame) * trace
+        stress = [level + whole * g[k][k] for k in range(3)] + [half * e for e in shears3]
         for k in range(6):
             stress_out[k, x] = stress[k]
         hist = jnp.maximum(
             jnp.maximum(history[x], energy), NOTCH_LOAD * notch[x].astype(F32)
         )
-        hist_out[at] = hist
-        diagonal = fracture + 2.0 * hist + 6.0 * KAPPA_COEF
+        hist_out[x] = hist
+        diagonal = base + 2.0 * hist
         rd = 1.0 / diagonal
         rd_out[x] = rd
         (xu, xl), (yu, yl), (zu, zl) = around(damage, (), 3, dmg, x, at)
@@ -232,44 +220,35 @@
         residual = 2.0 * hist - (diagonal * dmg - KAPPA_COEF * near)
         v = residual * rd
         v_out[x] = v
-        total = total + folded(residual * v)
         send(odd_y, ys, x, row_tile(v, rd, False), row_tile(v, rd, True))
         for c, k in enumerate((3, 1, 5)):
             last = v.shape[0] - 1
             spot = (count + c * tall + lax.div(x, 8), pl.ds(lax.rem(x, 8), 1), slice(None))
             send(odd_y, ys, spot, stress[k][0:1], stress[k][last : last + 1])
         send_columns(zs, x, [stress[4], stress[5], stress[2]], gz)
-    held[...] = total
-
-    def x_fields(depth, x):
-        out = [(depth - 1, v_out[x])]
+        return folded(residual * v)
+
+    def several(step, total):
+        for at in range(block):
+            total = total + body(step * block + at, at)
+        store(step).start()
+        return total
+
+    total = lax.fori_loop(0, CHUNKS, several, jnp.zeros((8, 128), F32))
+    for depth in (1, 2, 3):
+        low, high = depth - 1, count - depth
+        send(odd_x, xs, depth - 1, v_out[low], v_out[high])
         if depth <= 2:
-            out.append((2 + depth, rd_out[x]))
-        if depth == 1:
-            out += [(5, stress_out[0, x]), (6, stress_out[3, x]), (7, stress_out[4, x])]
-        return out
-
-    @pl.when(step == 0)
-    def _():
-        for depth in (1, 2, 3):
-            for slot, plane in x_fields(depth, depth - 1):
-                send_early(odd_x, xs, slot, plane, True)
-        for which in range(n_y):
-            for depth in (1, 2):
-                tile = ys[which][depth - 1]
-                send_early(odd_x, (ds[which], ds[n_y + which]), depth - 1, tile, True)
-
-    @pl.when(step == steps - 1)
-    def _():
-        for depth in (1, 2, 3):
-            for slot, plane in x_fields(depth, count - depth):
-                send_early(odd_x, xs, slot, plane, False)
-        for which in range(n_y):
-            for depth in (1, 2):
-                tile = ys[which][count - depth]
-                send_early(odd_x, (ds[which], ds[n_y + which]), depth - 1, tile, False)
-        mom_out[...] = jnp.zeros((8, 128), F32)
-        mom_out[0:1, :] = jnp.sum(total, axis=0, keepdims=True)
+            send(odd_x, xs, 2 + depth, rd_out[low], rd_out[high])
+            for which in range(n_y):
+                pair = (ds[which], ds[n_y + which])
+                send(odd_x, pair, depth - 1, ys[which][low], ys[which][high])
+    for slot, k in ((5, 0), (6, 3), (7, 4)):
+        send(odd_x, xs, slot, stress_out[k, 0], stress_out[k, count - 1])
+    mom_out[...] = jnp.zeros((8, 128), F32)
+    mom_out[0:1, :] = jnp.sum(total, axis=0, keepdims=True)
+    for step in range(CHUNKS):
+        store(step).wait()
 
 
 class Enlarged:
@@ -316,7 +295,7 @@
             yield count - 1 + depth, self.halo(False, depth)
 
 
-def join_kernel(n_y, pos, v, rd, *refs):
+def join_kernel(n_y, pos, v, rd, stress_z, *refs):
     big = Enlarged(n_y, pos, v, rd, refs[:-1])
     out = refs[-1]
     first_z = pos[2] == 0
@@ -396,7 +375,7 @@
 
     def third(x, total):
         plane, image = image_of(big_v2, x + 1)
-        return total + inside(plane * image)
+        return total + folded(plane[0:ny, 0:nz] * image[0:ny, 0:nz])
 
     zero = jnp.zeros((8, 128), F32)
     for p in (-2, -1, count, count + 1):
@@ -416,17 +395,24 @@
 
 def force_kernel(n_y, pos, table, impact, disp, vel, contact, labels, stress, *refs):
     xg, yg, zg = refs[:2], refs[2 : 2 + n_y], refs[2 + n_y]
-    disp_out, vel_out, token = refs[3 + n_y :]
+    disp_hbm, vel_hbm, token, disp_out, vel_out, sems = refs[3 + n_y :]
     token[...] = jnp.zeros((8, 128), F32)
     odd_x, odd_y, gz = pos[0] == 1, pos[1] == 1, pos[2]
-    step, steps, block = pl.program_id(0), pl.num_programs(0), contact.shape[0]
     count = stress.shape[1]
+    block = count // CHUNKS
     tall = count // 8
     rates = [table[2, r] for r in range(table.shape[1])]
-    for at in range(block):
-        x = step * block + at
-        loaded = contact[at].astype(F32)
-        rate = TIME_STEP / by_label(labels[at], rates)
+
+    def stores(step):
+        part = pl.ds(step * block, block)
+        return (
+            pltpu.make_async_copy(disp_out.at[:, part], disp_hbm.at[:, part], sems.at[step, 0]),
+            pltpu.make_async_copy(vel_out.at[:, part], vel_hbm.at[:, part], sems.at[step, 1]),
+        )
+
+    def body(x, at):
+        loaded = contact[x].astype(F32)
+        rate = by_label(labels[x], rates)
         for c, (kx, ky, kz) in enumerate(((0, 3, 4), (3, 1, 5), (4, 5, 2))):
             faces = (
                 lambda: jnp.where(odd_x, xg[0][5 + c], xg[1][5 + c]),
@@ -434,13 +420,25 @@
             )
             spot = (count + c * tall + lax.div(x, 8), pl.ds(lax.rem(x, 8), 1), slice(None))
             rows = low_high(odd_y, [y[spot] for y in yg])
-            xu, xl = shift_x(stress, (kx,), x, at, block, steps, faces)
+            xu, xl = shift_x(stress, (kx,), x, at, block, faces)
             yu, yl = shift_y(stress[ky, x], rows)
             zu, zl = shift_z(stress[kz, x], zg[x][:, c : c + 1], gz == 0)
             force = 0.5 * (((xu - xl) + (yu - yl)) + (zu - zl))
-            speed = vel[c, at] + rate * (force + loaded * impact[c])
-            vel_out[c, at] = speed
-            disp_out[c, at] = disp[c, at] + TIME_STEP * speed
+            speed = vel[c, x] + rate * (force + loaded * impact[c])
+            vel_out[c, x] = speed
+            disp_out[c, x] = disp[c, x] + TIME_STEP * speed
+
+    def several(step, carry):
+        for at in range(block):
+            body(step * block + at, at)
+        for copy in stores(step):
+            copy.start()
+        return carry
+
+    lax.fori_loop(0, CHUNKS, several, 0)
+    for step in range(CHUNKS):
+        for copy in stores(step):
+            copy.wait()
 
 
 def cg_coefficients(k):
@@ -529,22 +527,18 @@
         return pl.BlockSpec(memory_space=pltpu.HBM)
     if kind == "a":
         return pl.BlockSpec(memory_space=pl.ANY)
-    lead = len(a.shape) - 3
-    block = (*a.shape[:lead], a.shape[lead] // CHUNKS, *a.shape[lead + 1 :])
-    return pl.BlockSpec(block, lambda i: (*(0,) * lead, i, 0, 0))
-
-
-def call(kernel, kinds, ins, out_kinds, outs, flops, scratch=()):
+    raise ValueError(kind)
+
+
+def call(kernel, kinds, ins, out_kinds, outs, flops, scratch=(), vmem=VMEM_BYTES):
     moved = sum(4 * a.size for a in (*ins, *outs))
-    grid = (CHUNKS,) if "b" in (*kinds, *out_kinds) else ()
     return pl.pallas_call(
         kernel,
         out_shape=outs,
-        grid=grid,
         in_specs=[spec_of(k, a) for k, a in zip(kinds, ins, strict=True)],
         out_specs=[spec_of(k, a) for k, a in zip(out_kinds, outs, strict=True)],
         scratch_shapes=scratch,
-        compiler_params=pltpu.CompilerParams(vmem_limit_bytes=VMEM_BYTES),
+        compiler_params=pltpu.CompilerParams(vmem_limit_bytes=vmem),
         cost_estimate=pl.CostEstimate(flops=flops, bytes_accessed=moved, transcendentals=0),
     )(*ins)
 
@@ -557,6 +551,10 @@
         [lax.axis_index("gx") % 2, lax.axis_index("gy") % 2, lax.axis_index("gz")]
     ).astype(jnp.int32)
 
+    scaled = jnp.stack(
+        [table[0] / 8.0, table[1] / 8.0, TIME_STEP / table[2], table[3] + 6.0 * KAPPA_COEF]
+    )
+
     def arr(*shape):
         return jax.ShapeDtypeStruct(shape, F32)
 
@@ -564,14 +562,19 @@
     columns = arr(nx, ny, 128)
     z_pairs = [(0, 1)]
 
-    disp_here, damage_here, *sent = call(
+    sent = call(
         functools.partial(pack_kernel, n_y),
         "shh",
         (pos, displacement, damage),
-        "vv" + "v" * (3 + n_y),
-        [fields3, field, *[arr(4, ny, nz)] * 2, *[arr(4, nx, nz)] * n_y, columns],
+        "v" * (3 + n_y),
+        [*[arr(4, ny, nz)] * 2, *[arr(4, nx, nz)] * n_y, columns],
         size,
-        [pltpu.SemaphoreType.DMA((CHUNKS, 2))],
+        [
+            pltpu.VMEM((3, nx, ny, nz), F32),
+            pltpu.VMEM((nx, ny, nz), F32),
+            pltpu.SemaphoreType.DMA((CHUNKS, 2)),
+        ],
+        vmem=MOST_VMEM_BYTES,
     )
     got = [
         *swap_along("gx", sent[:2]),
@@ -582,8 +585,8 @@
     hist, rd, v0, stress, mom, *sent = call(
         functools.partial(local_kernel, n_y),
         "ssvvvvv" + "v" * (3 + n_y),
-        (pos, table, disp_here, damage_here, history, notch, labels, *got),
-        "bvvvv" + "v" * n_sent,
+        (pos, scaled, displacement, damage, history, notch, labels, *got),
+        "hvvvv" + "v" * n_sent,
         [
             field,
             field,
@@ -596,7 +599,7 @@
             columns,
         ],
         150 * size,
-        [pltpu.VMEM((8, 128), F32)],
+        [pltpu.VMEM((nx, ny, nz), F32), pltpu.SemaphoreType.DMA((CHUNKS,))],
     )
     xy = [
         *swap_along("gx", sent[:2]),
@@ -606,8 +609,8 @@
     stress_z = swap(sent[-1], "gz", z_pairs)
     (joined,) = call(
         functools.partial(join_kernel, n_y),
-        "svv" + "v" * len(xy),
-        (pos, v0, rd, *xy),
+        "svva" + "v" * len(xy),
+        (pos, v0, rd, stress_z, *xy),
         "v",
         [arr(nx + 6, ny + 8, 128)],
         4 * size,
@@ -615,10 +618,10 @@
     z_got = swap(joined, "gz", z_pairs)
     new_disp, new_vel, token = call(
         functools.partial(force_kernel, n_y),
-        "sssbbbbv" + "v" * (3 + n_y),
+        "sssvvvvv" + "v" * (3 + n_y),
         (
             pos,
-            table,
+            scaled,
             impact,
             displacement,
             velocity,
@@ -628,9 +631,14 @@
             *xy[: 2 + n_y],
             stress_z,
         ),
-        "bbv",
+        "hhv",
         [fields3, fields3, small],
         60 * size,
+        [
+            pltpu.VMEM((3, nx, ny, nz), F32),
+            pltpu.VMEM((3, nx, ny, nz), F32),
+            pltpu.SemaphoreType.DMA((CHUNKS, 2)),
+        ],
     )
     peers = lax.axis_size("gx") * lax.axis_size("gy") * lax.axis_size("gz")
     v1, v2, spread = call(

time: 56.5 us -> 61.1 us (1.081)
  blocking collectives: 13.5 us -> 17 us
  waiting for transfers between devices: 5.9 us -> 4.57 us
  local copies, waits for them, and re-layouts: 2.49 us -> 3.16 us
    all_to_all x1, blocking collectives: 13.5 us -> 17 us  [per_device(): mom = lax.all_to_all(spread, ('gx', 'gy', 'gz'), 0, 0, tiled=True)]
    ppermute x11, waiting for transfers between devices: 5.9 us -> 4.57 us  [swap(): return lax.ppermute(array, axis, pairs + [(b, a) for a, b in pairs])]
    unnamed x22 -> x20, local copies, waits for them, and re-layouts: 2.49 us -> 3.16 us
  transfers between devices with their start and end apart: 11 -> 11, of which waited for: 3 -> 3; matrix products, arithmetic and copies ran while one was open for 0% -> 0% of each run, Pallas kernels for 7% -> 6%
where the time goes in v4:
time: 61.1 us; the launch traced here: 60.7 us
  Pallas kernels  18 us (29%)
  blocking collectives  17 us (28%)
  starting transfers between devices  16.3 us (27%)
  waiting for transfers between devices  4.57 us (7%)
  local copies, waits for them, and re-layouts  3.16 us (5%)
  between operations  0.91 us (1%)
  other arithmetic  0.69 us (1%)
    pallas_call x6, Pallas kernels, call(): pl.pallas_call(kernel, out_shape=outs, in_specs=[spec_of(k, a) for k, a i...  18 us
    all_to_all x1, blocking collectives, per_device(): mom = lax.all_to_all(spread, ('gx', 'gy', 'gz'), 0, 0, tiled=True)  17 us
    ppermute x11, starting transfers between devices, swap(): return lax.ppermute(array, axis, pairs + [(b, a) for a, b in pairs])  16.3 us
    ppermute x11, waiting for transfers between devices, swap(): return lax.ppermute(array, axis, pairs + [(b, a) for a, b in pairs])  4.57 us
    unnamed x20, local copies, waits for them, and re-layouts  3.16 us
  transfers between devices with their start and end apart: 11, of which 3 were waited for; matrix products, arithmetic and copies ran while one was open for 0% of the time, Pallas kernels for 6%

profile of v4, /device:TPU:0, one launch (start us, length us, event | category | flops | bytes accessed | tf_op | source)
XLA Modules:
  0.0 60.7 jit_solution(15686851645625922979)
XLA Ops:
  0.6 0.0 copy-start.1
  0.6 0.0 copy-start
  0.7 0.0 copy-start.9
  0.7 0.7 %pad_add_fusion.pos = s32[3]{0:T(128)} fusion(s32[1]{0:T(128)} %bitcast.2, s32[1]{0:T(128)} %bitcast.1, s32[1]{0:T(128)} %bitcast), kind=kLoop, calls=%fused_computation.1 | loop fusion | flops 6 | bytes 24 | tf_op jit(solution)/shard_map/stack | solution.py:550
  1.4 0.0 copy-start.7
  1.4 3.2 %shard_map.120 = (f32[4,32,256]{2,1,0:T(8,128)}, f32[4,32,256]{2,1,0:T(8,128)}, f32[4,16,256]{2,1,0:T(8,128)}, f32[16,32,128]{2,1,0:T(8,128)}) custom-call(s32[3]{0:T(128)} %pad_add_fusion.pos, f32[3,16,32,256]{3,2,1,0:T(8,128)} %disp.3, f32[16,32,256]{2,1,0:T(8,128)} %damage_hbm.3), custom_call_target="tpu_custom_call" | custom-call | flops 131072 | bytes 2686988 | tf_op jit(solution)/shard_map/pallas_call | solution.py:535
  4.6 3.0 %collective-permute-start.2 = (f32[4,16,256]{2,1,0:T(8,128)}, f32[4,16,256]{2,1,0:T(8,128)S(1)}, u32[]{:S(2)}, u32[]{:S(2)}) collective-permute-start(f32[4,16,256]{2,1,0:T(8,128)} %get-tuple-element.27), channel_id=1, source_target_pairs={{0,2},{2,0},{1,3},{3,1},{4,6},{6,4},{5,7},{7,5},{8,10},{10,8},{9,1... | collective-permute-start | bytes 196616 | tf_op jit(solution)/shard_map/ppermute | solution.py:500
  7.6 1.6 %collective-permute-start = (f32[4,32,256]{2,1,0:T(8,128)}, f32[4,32,256]{2,1,0:T(8,128)S(1)}, u32[]{:S(2)}, u32[]{:S(2)}) collective-permute-start(f32[4,32,256]{2,1,0:T(8,128)} %get-tuple-element.25), channel_id=1, source_target_pairs={{0,4},{8,12},{4,0},{12,8},{1,5},{9,13},{5,1},{13,9},{2,6},{10,14},... | collective-permute-start | bytes 393224 | tf_op jit(solution)/shard_map/ppermute | solution.py:500
  9.1 0.7 %collective-permute-start.1 = (f32[4,32,256]{2,1,0:T(8,128)}, f32[4,32,256]{2,1,0:T(8,128)S(1)}, u32[]{:S(2)}, u32[]{:S(2)}) collective-permute-start(f32[4,32,256]{2,1,0:T(8,128)} %get-tuple-element.26), channel_id=1, source_target_pairs={{4,8},{8,4},{5,9},{9,5},{6,10},{10,6},{7,11},{11,7},{20,24},{24,20... | collective-permute-start | bytes 393224 | tf_op jit(solution)/shard_map/ppermute | solution.py:500
  9.8 0.1 collective-permute-start.3
  9.9 0.0 copy-done.9
  9.9 0.1 collective-permute-done.2.refs_2_
  10.0 2.7 %collective-permute-done.refs_0_ = f32[4,32,256]{2,1,0:T(8,128)S(1)} collective-permute-done((f32[4,32,256]{2,1,0:T(8,128)}, f32[4,32,256]{2,1,0:T(8,128)S(1)}, u32[]{:S(2)}, u32[]{:S(2)}) %collective-permute-start) | collective-permute-done | bytes 131104 | tf_op jit(solution)/shard_map/ppermute | solution.py:500
  12.7 0.0 collective-permute-done.1.refs_1_
  12.7 0.0 collective-permute-done.3.refs_3_
  12.8 0.0 copy-done.1
  12.8 0.0 copy-done
  12.8 0.0 copy-done.7
  12.8 0.0 copy-start.2
  12.8 1.0 %copy-done.2 = s32[16,32,256]{2,1,0:T(8,128)S(1)} copy-done((s32[16,32,256]{2,1,0:T(8,128)S(1)}, s32[16,32,256]{2,1,0:T(8,128)}, u32[]{:S(2)}) %copy-start.2) | copy-done | bytes 524312
  13.8 0.0 copy-start.5
  13.8 1.0 %copy-done.5 = f32[16,32,256]{2,1,0:T(8,128)S(1)} copy-done((f32[16,32,256]{2,1,0:T(8,128)S(1)}, f32[16,32,256]{2,1,0:T(8,128)}, u32[]{:S(2)}) %copy-start.5) | copy-done | bytes 524312
  14.9 0.0 copy-start.6
  14.9 1.0 %copy-done.6 = s32[16,32,256]{2,1,0:T(8,128)S(1)} copy-done((s32[16,32,256]{2,1,0:T(8,128)S(1)}, s32[16,32,256]{2,1,0:T(8,128)}, u32[]{:S(2)}) %copy-start.6) | copy-done | bytes 524312
  15.9 4.6 %shard_map.121 = (f32[16,32,256]{2,1,0:T(8,128)}, f32[16,32,256]{2,1,0:T(8,128)S(1)}, f32[16,32,256]{2,1,0:T(8,128)S(1)}, f32[6,16,32,256]{3,2,1,0:T(8,128)S(1)}...) custom-call(s32[3]{0:T(128)S(1)} %copy-done.7, ...), custom_call_target="tpu_custom_call" | custom-call | flops 19660800 | bytes 9982028 | tf_op jit(solution)/shard_map/pallas_call | solution.py:535
  20.5 0.0 copy-start.3
  20.5 0.0 copy-start.4
  20.5 0.0 copy-start.8
  20.5 4.7 %collective-permute-start.4 = (f32[8,32,256]{2,1,0:T(8,128)S(1)}, f32[8,32,256]{2,1,0:T(8,128)S(1)}, u32[]{:S(2)}, u32[]{:S(2)}) collective-permute-start(f32[8,32,256]{2,1,0:T(8,128)S(1)} %get-tuple-element.30), channel_id=1, source_target_pairs={{0,4},{8,12},{4,0},{12,8},{1,5},{9,13},{5,1},{13,9},{2,6},{10,14},... | collective-permute-start | bytes 786440 | tf_op jit(solution)/shard_map/ppermute | solution.py:500
  25.2 0.7 %collective-permute-start.5 = (f32[8,32,256]{2,1,0:T(8,128)S(1)}, f32[8,32,256]{2,1,0:T(8,128)S(1)}, u32[]{:S(2)}, u32[]{:S(2)}) collective-permute-start(f32[8,32,256]{2,1,0:T(8,128)S(1)} %get-tuple-element.31), channel_id=1, source_target_pairs={{4,8},{8,4},{5,9},{9,5},{6,10},{10,6},{7,11},{11,7},{20,24},{24,20... | collective-permute-start | bytes 786440 | tf_op jit(solution)/shard_map/ppermute | solution.py:500
  25.8 0.1 collective-permute-start.7
  25.9 0.6 collective-permute-start.6
  26.5 4.3 %collective-permute-start.8 = (f32[2,8,256]{2,1,0:T(8,128)S(1)}, f32[2,8,256]{2,1,0:T(8,128)S(1)}, u32[]{:S(2)}, u32[]{:S(2)}) collective-permute-start(f32[2,8,256]{2,1,0:T(8,128)S(1)} %get-tuple-element.41), channel_id=1, source_target_pairs={{0,6},{2,4},{8,14},{10,12},{6,0},{4,2},{14,8},{12,10},{1,7},{3,5},... | collective-permute-start | bytes 49160 | tf_op jit(solution)/shard_map/ppermute | solution.py:500
  30.9 1.7 %collective-permute-done.8.refs_3_ = f32[2,8,256]{2,1,0:T(8,128)S(1)} collective-permute-done((f32[2,8,256]{2,1,0:T(8,128)S(1)}, f32[2,8,256]{2,1,0:T(8,128)S(1)}, u32[]{:S(2)}, u32[]{:S(2)}) %collective-permute-start.8) | collective-permute-done | bytes 16416 | tf_op jit(solution)/shard_map/ppermute | solution.py:500
  32.6 0.7 %collective-permute-start.9 = (f32[2,8,256]{2,1,0:T(8,128)S(1)}, f32[2,8,256]{2,1,0:T(8,128)S(1)}, u32[]{:S(2)}, u32[]{:S(2)}) collective-permute-start(f32[2,8,256]{2,1,0:T(8,128)S(1)} %get-tuple-element.42), channel_id=1, source_target_pairs={{4,10},{6,8},{10,4},{8,6},{5,11},{7,9},{11,5},{9,7},{20,26},{22,24... | collective-permute-start | bytes 49160 | tf_op jit(solution)/shard_map/ppermute | solution.py:500
  33.3 0.0 collective-permute-done.9.refs_4_
  33.3 0.0 collective-permute-done.6.refs_2_
  33.3 0.0 collective-permute-done.4.refs_0_
  33.3 0.0 collective-permute-done.5.refs_1_
  33.3 0.0 collective-permute-done.7.refs_3_.stress_z
  33.3 1.0 %shard_map.123 = f32[22,40,128]{2,1,0:T(8,128)S(1)} custom-call(s32[3]{0:T(128)S(1)} %copy-done.7, f32[16,32,256]{2,1,0:T(8,128)S(1)} %get-tuple-element.37.v.v0, f32[16,32,256]{2,1,0:T(8,128)S(1)} %get-tuple-element.38.rd, f32[16,32,128]{2,1,0:T(8,128)S(1)} %collective-permute-done.7.refs_3_.stress_z, f32[8,32,256]{2,1,0:T(8,128)S(1)} %collective-permute-done.4.refs_0_, ...), custom_call_target="tpu_custom_call" | custom-call | flops 524288 | bytes 2498572 | tf_op jit(solution)/shard_map/pallas_call | solution.py:535
  34.3 0.1 collective-permute-start.10
  34.4 0.0 copy-done.3
  34.4 0.0 copy-done.4
  34.4 0.0 copy-done.8
  34.4 3.6 %shard_map.122 = (f32[3,16,32,256]{3,2,1,0:T(8,128)}, f32[3,16,32,256]{3,2,1,0:T(8,128)}, f32[8,128]{1,0:T(8,128)S(1)}) custom-call(s32[3]{0:T(128)S(1)} %copy-done.7, f32[4,4]{1,0:T(4,128)S(1)} %pad_maximum_fusion.table, f32[3]{0:T(128)S(1)} %copy-done.8, f32[3,16,32,256]{3,2,1,0:T(8,128)S(1)} %copy-done, f32[3,16,32,256]{3,2,1,0:T(8,128)S(1)} %copy-done.3, ...), custom_call_target="tpu_custom_call" | custom-call | flops 7864320 | bytes 11456600 | tf_op jit(solution)/shard_map/pallas_call | solution.py:535
  38.1 0.0 collective-permute-done.10.z_got
  38.1 3.8 %shard_map.124 = (f32[16,32,256]{2,1,0:T(8,128)S(1)}, f32[16,32,256]{2,1,0:T(8,128)S(1)}, f32[16,8,128]{2,1,0:T(8,128)S(1)}) custom-call(s32[3]{0:T(128)S(1)} %copy-done.7, f32[16,32,256]{2,1,0:T(8,128)S(1)} %get-tuple-element.37.v.v0, f32[16,32,256]{2,1,0:T(8,128)S(1)} %get-tuple-element.38.rd, f32[8,128]{1,0:T(8,128)S(1)} %get-tuple-element.39.mom, ...), custom_call_target="tpu_custom_call" | custom-call | flops 7864320 | bytes 3358732 | tf_op jit(solution)/shard_map/pallas_call | solution.py:535
  41.9 17.0 %all_to_all.5.mom = f32[16,8,128]{2,1,0:T(8,128)S(1)} all-to-all(f32[16,8,128]{2,1,0:T(8,128)S(1)} %get-tuple-element.43), channel_id=1, replica_groups=mesh['case'=2,'gx'=4,'gy'=2,'gz'=2] {'gx','gy','gz'}, dimensions={0} | all-to-all | bytes 131072 | tf_op jit(solution)/shard_map/all_to_all | solution.py:658
  58.9 1.8 %shard_map.125 = f32[16,32,256]{2,1,0:T(8,128)} custom-call(f32[16,8,128]{2,1,0:T(8,128)S(1)} %all_to_all.5.mom, f32[16,32,256]{2,1,0:T(8,128)S(1)} %get-tuple-element.37.v.v0, f32[16,32,256]{2,1,0:T(8,128)S(1)} %get-tuple-element.44.v1, f32[16,32,256]{2,1,0:T(8,128)S(1)} %get-tuple-element.45.v2, f32[16,32,256]{2,1,0:T(8,128)S(1)} %copy-done.1), custom_call_target="tpu_custom_call" | custom-call | flops 1048576 | bytes 2686976 | tf_op jit(solution)/shard_map/pallas_call | solution.py:535
  (2 shorter events, 0.0 us)
Async XLA Ops:
  0.6 12.1 %copy-start.1 = (f32[16,32,256]{2,1,0:T(8,128)S(1)}, f32[16,32,256]{2,1,0:T(8,128)}, u32[]{:S(2)}) copy-start(f32[16,32,256]{2,1,0:T(8,128)} %damage_hbm.3) | copy-start | bytes 1572868
  0.6 12.1 %copy-start = (f32[3,16,32,256]{3,2,1,0:T(8,128)S(1)}, f32[3,16,32,256]{3,2,1,0:T(8,128)}, u32[]{:S(2)}) copy-start(f32[3,16,32,256]{3,2,1,0:T(8,128)} %disp.3) | copy-start | bytes 4718596
  0.7 9.2 %copy-start.9 = (f32[4,4]{1,0:T(4,128)S(1)}, f32[4,4]{1,0:T(4,128)}, u32[]{:S(2)}) copy-start(f32[4,4]{1,0:T(4,128)} %param.16) | copy-start | bytes 196
  1.4 11.4 %copy-start.7 = (s32[3]{0:T(128)S(1)}, s32[3]{0:T(128)}, u32[]{:S(2)}) copy-start(s32[3]{0:T(128)} %pad_add_fusion.pos) | copy-start | bytes 40
  4.6 5.5 %collective-permute-start.2 = (f32[4,16,256]{2,1,0:T(8,128)}, f32[4,16,256]{2,1,0:T(8,128)S(1)}, u32[]{:S(2)}, u32[]{:S(2)}) collective-permute-start(f32[4,16,256]{2,1,0:T(8,128)} %get-tuple-element.27), channel_id=1, source_target_pairs={{0,2},{2,0},{1,3},{3,1},{4,6},{6,4},{5,7},{7,5},{8,10},{10,8},{9,1... | collective-permute-start | bytes 196616 | tf_op jit(solution)/shard_map/ppermute | solution.py:500
  7.6 5.2 %collective-permute-start = (f32[4,32,256]{2,1,0:T(8,128)}, f32[4,32,256]{2,1,0:T(8,128)S(1)}, u32[]{:S(2)}, u32[]{:S(2)}) collective-permute-start(f32[4,32,256]{2,1,0:T(8,128)} %get-tuple-element.25), channel_id=1, source_target_pairs={{0,4},{8,12},{4,0},{12,8},{1,5},{9,13},{5,1},{13,9},{2,6},{10,14},... | collective-permute-start | bytes 393224 | tf_op jit(solution)/shard_map/ppermute | solution.py:500
  9.1 3.6 %collective-permute-start.1 = (f32[4,32,256]{2,1,0:T(8,128)}, f32[4,32,256]{2,1,0:T(8,128)S(1)}, u32[]{:S(2)}, u32[]{:S(2)}) collective-permute-start(f32[4,32,256]{2,1,0:T(8,128)} %get-tuple-element.26), channel_id=1, source_target_pairs={{4,8},{8,4},{5,9},{9,5},{6,10},{10,6},{7,11},{11,7},{20,24},{24,20... | collective-permute-start | bytes 393224 | tf_op jit(solution)/shard_map/ppermute | solution.py:500
  9.8 2.9 %collective-permute-start.3 = (f32[16,32,128]{2,1,0:T(8,128)}, f32[16,32,128]{2,1,0:T(8,128)S(1)}, u32[]{:S(2)}, u32[]{:S(2)}) collective-permute-start(f32[16,32,128]{2,1,0:T(8,128)} %get-tuple-element.28), channel_id=1, source_target_pairs={{0,1},{1,0},{2,3},{3,2},{4,5},{5,4},{6,7},{7,6},{8,9},{9,8},{10,11... | collective-permute-start | bytes 786440 | tf_op jit(solution)/shard_map/ppermute | solution.py:500
  12.8 1.0 %copy-start.2 = (s32[16,32,256]{2,1,0:T(8,128)S(1)}, s32[16,32,256]{2,1,0:T(8,128)}, u32[]{:S(2)}) copy-start(s32[16,32,256]{2,1,0:T(8,128)} %labels.3) | copy-start | bytes 1572868
  13.8 1.0 %copy-start.5 = (f32[16,32,256]{2,1,0:T(8,128)S(1)}, f32[16,32,256]{2,1,0:T(8,128)}, u32[]{:S(2)}) copy-start(f32[16,32,256]{2,1,0:T(8,128)} %history.1) | copy-start | bytes 1572868
  14.9 1.0 %copy-start.6 = (s32[16,32,256]{2,1,0:T(8,128)S(1)}, s32[16,32,256]{2,1,0:T(8,128)}, u32[]{:S(2)}) copy-start(s32[16,32,256]{2,1,0:T(8,128)} %notch.1) | copy-start | bytes 1572868
  20.5 13.9 %copy-start.3 = (f32[3,16,32,256]{3,2,1,0:T(8,128)S(1)}, f32[3,16,32,256]{3,2,1,0:T(8,128)}, u32[]{:S(2)}) copy-start(f32[3,16,32,256]{3,2,1,0:T(8,128)} %vel.1) | copy-start | bytes 4718596
  20.5 13.9 %copy-start.4 = (s32[16,32,256]{2,1,0:T(8,128)S(1)}, s32[16,32,256]{2,1,0:T(8,128)}, u32[]{:S(2)}) copy-start(s32[16,32,256]{2,1,0:T(8,128)} %contact.1) | copy-start | bytes 1572868
  20.5 13.9 %copy-start.8 = (f32[3]{0:T(128)S(1)}, f32[3]{0:T(128)}, u32[]{:S(2)}) copy-start(f32[3]{0:T(128)} %impact.1) | copy-start | bytes 40
  20.5 12.8 %collective-permute-start.4 = (f32[8,32,256]{2,1,0:T(8,128)S(1)}, f32[8,32,256]{2,1,0:T(8,128)S(1)}, u32[]{:S(2)}, u32[]{:S(2)}) collective-permute-start(f32[8,32,256]{2,1,0:T(8,128)S(1)} %get-tuple-element.30), channel_id=1, source_target_pairs={{0,4},{8,12},{4,0},{12,8},{1,5},{9,13},{5,1},{13,9},{2,6},{10,14},... | collective-permute-start | bytes 786440 | tf_op jit(solution)/shard_map/ppermute | solution.py:500
  25.2 8.1 %collective-permute-start.5 = (f32[8,32,256]{2,1,0:T(8,128)S(1)}, f32[8,32,256]{2,1,0:T(8,128)S(1)}, u32[]{:S(2)}, u32[]{:S(2)}) collective-permute-start(f32[8,32,256]{2,1,0:T(8,128)S(1)} %get-tuple-element.31), channel_id=1, source_target_pairs={{4,8},{8,4},{5,9},{9,5},{6,10},{10,6},{7,11},{11,7},{20,24},{24,20... | collective-permute-start | bytes 786440 | tf_op jit(solution)/shard_map/ppermute | solution.py:500
  25.8 7.4 %collective-permute-start.7 = (f32[16,32,128]{2,1,0:T(8,128)S(1)}, f32[16,32,128]{2,1,0:T(8,128)S(1)}, u32[]{:S(2)}, u32[]{:S(2)}) collective-permute-start(f32[16,32,128]{2,1,0:T(8,128)S(1)} %get-tuple-element.33), channel_id=1, source_target_pairs={{0,1},{1,0},{2,3},{3,2},{4,5},{5,4},{6,7},{7,6},{8,9},{9,8},{10,11... | collective-permute-start | bytes 786440 | tf_op jit(solution)/shard_map/ppermute | solution.py:500
  25.9 7.3 %collective-permute-start.6 = (f32[22,8,256]{2,1,0:T(8,128)S(1)}, f32[22,8,256]{2,1,0:T(8,128)S(1)}, u32[]{:S(2)}, u32[]{:S(2)}) collective-permute-start(f32[22,8,256]{2,1,0:T(8,128)S(1)} %get-tuple-element.32), channel_id=1, source_target_pairs={{0,2},{2,0},{1,3},{3,1},{4,6},{6,4},{5,7},{7,5},{8,10},{10,8},{9,1... | collective-permute-start | bytes 540680 | tf_op jit(solution)/shard_map/ppermute | solution.py:500
  26.5 6.1 %collective-permute-start.8 = (f32[2,8,256]{2,1,0:T(8,128)S(1)}, f32[2,8,256]{2,1,0:T(8,128)S(1)}, u32[]{:S(2)}, u32[]{:S(2)}) collective-permute-start(f32[2,8,256]{2,1,0:T(8,128)S(1)} %get-tuple-element.41), channel_id=1, source_target_pairs={{0,6},{2,4},{8,14},{10,12},{6,0},{4,2},{14,8},{12,10},{1,7},{3,5},... | collective-permute-start | bytes 49160 | tf_op jit(solution)/shard_map/ppermute | solution.py:500
  32.6 0.7 %collective-permute-start.9 = (f32[2,8,256]{2,1,0:T(8,128)S(1)}, f32[2,8,256]{2,1,0:T(8,128)S(1)}, u32[]{:S(2)}, u32[]{:S(2)}) collective-permute-start(f32[2,8,256]{2,1,0:T(8,128)S(1)} %get-tuple-element.42), channel_id=1, source_target_pairs={{4,10},{6,8},{10,4},{8,6},{5,11},{7,9},{11,5},{9,7},{20,26},{22,24... | collective-permute-start | bytes 49160 | tf_op jit(solution)/shard_map/ppermute | solution.py:500
  34.3 3.8 %collective-permute-start.10 = (f32[22,40,128]{2,1,0:T(8,128)S(1)}, f32[22,40,128]{2,1,0:T(8,128)S(1)}, u32[]{:S(2)}, u32[]{:S(2)}) collective-permute-start(f32[22,40,128]{2,1,0:T(8,128)S(1)} %shard_map.123), channel_id=1, source_target_pairs={{0,1},{1,0},{2,3},{3,2},{4,5},{5,4},{6,7},{7,6},{8,9},{9,8},{10,11... | collective-permute-start | bytes 1351688 | tf_op jit(solution)/shard_map/ppermute | solution.py:500

commit v5 on v4

--- a/solution.py
+++ b/solution.py
@@ -12,7 +12,7 @@
 STIFF_FLOOR = 0.001
 ALPHA_LOW, ALPHA_HIGH = 0.5, 6.5
 VMEM_BYTES = 28 * 1024 * 1024
-MOST_VMEM_BYTES = 60 * 1024 * 1024
+STRESS_LANE = 32
 CHUNKS = 4
 F32 = jnp.float32
 
@@ -105,41 +105,20 @@
     return lax.fori_loop(0, count // many, several, carry)
 
 
-def pack_kernel(n_y, pos, disp_hbm, damage_hbm, *refs):
-    xs, ys, zs = refs[:2], refs[2 : 2 + n_y], refs[2 + n_y]
-    disp, damage, sems = refs[3 + n_y :]
-    odd_x, odd_y, gz = pos[0] == 1, pos[1] == 1, pos[2]
-    count = damage.shape[0]
-    block = count // CHUNKS
-    copies = []
-    for chunk in range(CHUNKS):
-        part = pl.ds(chunk * block, block)
-        for which, (src, dst) in enumerate(
-            (
-                (disp_hbm.at[:, part], disp.at[:, part]),
-                (damage_hbm.at[part], damage.at[part]),
-            )
-        ):
-            copy = pltpu.make_async_copy(src, dst, sems.at[chunk, which])
-            copy.start()
-            copies.append(copy)
-    for chunk in range(CHUNKS):
-        copies[2 * chunk].wait()
-        copies[2 * chunk + 1].wait()
-        for x in range(chunk * block, (chunk + 1) * block):
-            planes = [disp[0, x], disp[1, x], disp[2, x], damage[x]]
-            for field, plane in enumerate(planes):
-                last = plane.shape[0] - 1
-                send(
-                    odd_y,
-                    ys,
-                    (field, pl.ds(x, 1), slice(None)),
-                    plane[0:1],
-                    plane[last : last + 1],
-                )
-            send_columns(zs, x, planes, gz)
-    for field, src in enumerate((disp.at[0], disp.at[1], disp.at[2], damage)):
-        send(odd_x, xs, field, src[0], src[count - 1])
+def pack_kernel(n_y, pos, disp, damage, *refs):
+    ys, zs = refs[:n_y], refs[n_y]
+    odd_y, gz = pos[1] == 1, pos[2]
+
+    def body(x, carry):
+        planes = [disp[0, x], disp[1, x], disp[2, x], damage[x]]
+        for field, plane in enumerate(planes):
+            last = plane.shape[0] - 1
+            spot = (field, pl.ds(x, 1), slice(None))
+            send(odd_y, ys, spot, plane[0:1], plane[last : last + 1])
+        send_columns(zs, x, planes, gz)
+        return carry
+
+    unrolled(damage.shape[0], 8, body, 0)
 
 
 def row_tile(v, rd, is_high):
@@ -295,7 +274,7 @@
             yield count - 1 + depth, self.halo(False, depth)
 
 
-def join_kernel(n_y, pos, v, rd, stress_z, *refs):
+def join_kernel(n_y, pos, v, rd, columns, *refs):
     big = Enlarged(n_y, pos, v, rd, refs[:-1])
     out = refs[-1]
     first_z = pos[2] == 0
@@ -318,71 +297,96 @@
 
     def body(x, carry):
         put(x, big.own(x))
+        lanes = iota2((ny, 128), 1)
+        mark = (lanes >= STRESS_LANE) & (lanes < STRESS_LANE + 3)
+        moved = pltpu.roll(columns[x], STRESS_LANE, 1)
+        out[x + 3, 0:ny] = jnp.where(mark, moved, out[x + 3, 0:ny])
         return carry
 
     unrolled(count, 4, body, 0)
 
 
-def krylov_kernel(n_y, pos, v, rd, mom, token, z_got, *refs):
-    n_got = 2 + 3 * n_y
-    big = Enlarged(n_y, pos, v, rd, refs[:n_got])
-    v1_out, v2_out, spread, big_v, big_rd, big_v1, big_v2 = refs[n_got:]
-    count, ny, nz = v.shape
+def fill_kernel(n_y, pos, v, rd, *refs):
+    big = Enlarged(n_y, pos, v, rd, refs[:-2])
+    big_v, big_rd = refs[-2:]
+    count, ny, _ = v.shape
 
     def put(p, parts):
         v_own, v_rows, rd_own, rd_rows = parts
-        tile = z_got[p + 3]
-        keep = lax.shift_right_logical(iota2(tile.shape, 1), 6) == pos[2]
-        big_v[p + 3, 0:ny, 0:nz] = v_own
-        big_v[p + 3, ny : ny + 8, 0:nz] = v_rows
-        big_v[p + 3, :, nz : nz + 128] = jnp.where(keep, tile, 0.0)
-        big_rd[p + 3, 0:ny, 0:nz] = rd_own
-        big_rd[p + 3, ny : ny + 8, 0:nz] = rd_rows
-        big_rd[p + 3, :, nz : nz + 128] = jnp.where(keep, pltpu.roll(tile, 64, 1), 0.0)
+        big_v[p + 3, 0:ny] = v_own
+        big_v[p + 3, ny : ny + 8] = v_rows
+        big_rd[p + 3, 0:ny] = rd_own
+        big_rd[p + 3, ny : ny + 8] = rd_rows
 
     for p, parts in big.outer(count):
         put(p, parts)
 
-    def fill(x, carry):
+    def body(x, carry):
         put(x, big.own(x))
         return carry
 
-    unrolled(count, 4, fill, 0)
-
-    def image_of(ref, at):
-        plane = ref[at]
+    unrolled(count, 4, body, 0)
+
+
+def krylov_kernel(pos, main_v, main_rd, mom, token, z_got, *refs):
+    v1_out, v2_out, spread, z_v, z_rd, big_v1, big_v2 = refs
+    count, ny, nz = v1_out.shape
+
+    def split(p, carry):
+        tile = z_got[p]
+        keep = lax.shift_right_logical(iota2(tile.shape, 1), 6) == pos[2]
+        z_v[p] = jnp.where(keep, tile, 0.0)
+        z_rd[p] = jnp.where(keep, pltpu.roll(tile, 64, 1), 0.0)
+        return carry
+
+    unrolled(count + 6, 2, split, 0)
+
+    def v_at(at):
+        return jnp.concatenate([main_v[at], z_v[at]], axis=1)
+
+    def rd_at(at):
+        return jnp.concatenate([main_rd[at], z_rd[at]], axis=1)
+
+    def image_of(get, at):
+        plane = get(at)
         rows, lanes = plane.shape
-        near = (ref[at - 1] + ref[at + 1]) + (pltpu.roll(plane, 1, 0) + pltpu.roll(plane, rows - 1, 0))
+        near = (get(at - 1) + get(at + 1)) + (pltpu.roll(plane, 1, 0) + pltpu.roll(plane, rows - 1, 0))
         near = near + (pltpu.roll(plane, 1, 1) + pltpu.roll(plane, lanes - 1, 1))
         return plane, KAPPA_COEF * near
 
+    def v1_at(at):
+        return big_v1[at]
+
+    def v2_at(at):
+        return big_v2[at]
+
     def inside(values):
         return folded(values[0:ny, 0:nz])
 
     def first(x, totals):
-        plane, image = image_of(big_v, x + 3)
-        made = image * big_rd[x + 3]
+        plane, image = image_of(v_at, x + 3)
+        made = image * rd_at(x + 3)
         big_v1[x + 2] = made
         v1_out[x] = made[0:ny, 0:nz]
         return totals[0] + inside(plane * image), totals[1] + inside(made * image)
 
     def second(x, totals):
-        plane, image = image_of(big_v1, x + 2)
-        made = image * big_rd[x + 3]
+        plane, image = image_of(v1_at, x + 2)
+        made = image * rd_at(x + 3)
         big_v2[x + 1] = made
         v2_out[x] = made[0:ny, 0:nz]
         return totals[0] + inside(plane * image), totals[1] + inside(made * image)
 
     def third(x, total):
-        plane, image = image_of(big_v2, x + 1)
+        plane, image = image_of(v2_at, x + 1)
         return total + folded(plane[0:ny, 0:nz] * image[0:ny, 0:nz])
 
     zero = jnp.zeros((8, 128), F32)
     for p in (-2, -1, count, count + 1):
-        big_v1[p + 2] = image_of(big_v, p + 3)[1] * big_rd[p + 3]
+        big_v1[p + 2] = image_of(v_at, p + 3)[1] * rd_at(p + 3)
     k1, k2 = unrolled(count, 4, first, (zero, zero))
     for p in (-1, count):
-        big_v2[p + 1] = image_of(big_v1, p + 2)[1] * big_rd[p + 3]
+        big_v2[p + 1] = image_of(v1_at, p + 2)[1] * rd_at(p + 3)
     k3, k4 = unrolled(count, 4, second, (zero, zero))
     k5 = unrolled(count, 4, third, zero)
     rows = iota2((8, 128), 0)
@@ -409,6 +413,10 @@
             pltpu.make_async_copy(disp_out.at[:, part], disp_hbm.at[:, part], sems.at[step, 0]),
             pltpu.make_async_copy(vel_out.at[:, part], vel_hbm.at[:, part], sems.at[step, 1]),
         )
+
+    def column(x, c):
+        lane = STRESS_LANE + c
+        return zg[x + 3, 0 : contact.shape[1]][:, lane : lane + 1]
 
     def body(x, at):
         loaded = contact[x].astype(F32)
@@ -422,7 +430,7 @@
             rows = low_high(odd_y, [y[spot] for y in yg])
             xu, xl = shift_x(stress, (kx,), x, at, block, faces)
             yu, yl = shift_y(stress[ky, x], rows)
-            zu, zl = shift_z(stress[kz, x], zg[x][:, c : c + 1], gz == 0)
+            zu, zl = shift_z(stress[kz, x], column(x, c), gz == 0)
             force = 0.5 * (((xu - xl) + (yu - yl)) + (zu - zl))
             speed = vel[c, x] + rate * (force + loaded * impact[c])
             vel_out[c, x] = speed
@@ -530,7 +538,7 @@
     raise ValueError(kind)
 
 
-def call(kernel, kinds, ins, out_kinds, outs, flops, scratch=(), vmem=VMEM_BYTES):
+def call(kernel, kinds, ins, out_kinds, outs, flops, scratch=()):
     moved = sum(4 * a.size for a in (*ins, *outs))
     return pl.pallas_call(
         kernel,
@@ -538,7 +546,7 @@
         in_specs=[spec_of(k, a) for k, a in zip(kinds, ins, strict=True)],
         out_specs=[spec_of(k, a) for k, a in zip(out_kinds, outs, strict=True)],
         scratch_shapes=scratch,
-        compiler_params=pltpu.CompilerParams(vmem_limit_bytes=vmem),
+        compiler_params=pltpu.CompilerParams(vmem_limit_bytes=VMEM_BYTES),
         cost_estimate=pl.CostEstimate(flops=flops, bytes_accessed=moved, transcendentals=0),
     )(*ins)
 
@@ -562,25 +570,20 @@
     columns = arr(nx, ny, 128)
     z_pairs = [(0, 1)]
 
+    faces = [
+        jnp.concatenate([displacement[:, at], damage[None, at]]) for at in (0, nx - 1)
+    ]
+    odd = lax.axis_index("gx") % 2 == 1
+    got_x = swap_along("gx", [jnp.where(odd, *faces), jnp.where(odd, *faces[::-1])])
     sent = call(
         functools.partial(pack_kernel, n_y),
-        "shh",
+        "svv",
         (pos, displacement, damage),
-        "v" * (3 + n_y),
-        [*[arr(4, ny, nz)] * 2, *[arr(4, nx, nz)] * n_y, columns],
+        "v" * (1 + n_y),
+        [*[arr(4, nx, nz)] * n_y, columns],
         size,
-        [
-            pltpu.VMEM((3, nx, ny, nz), F32),
-            pltpu.VMEM((nx, ny, nz), F32),
-            pltpu.SemaphoreType.DMA((CHUNKS, 2)),
-        ],
-        vmem=MOST_VMEM_BYTES,
-    )
-    got = [
-        *swap_along("gx", sent[:2]),
-        *swap_along("gy", sent[2 : 2 + n_y]),
-        swap(sent[-1], "gz", z_pairs),
-    ]
+    )
+    got = [*got_x, *swap_along("gy", sent[:n_y]), swap(sent[-1], "gz", z_pairs)]
     n_sent = 3 + 3 * n_y
     hist, rd, v0, stress, mom, *sent = call(
         functools.partial(local_kernel, n_y),
@@ -606,16 +609,23 @@
         *swap_along("gy", sent[2 : 2 + n_y]),
         *swap_diagonal(sent[2 + n_y : 2 + 3 * n_y]),
     ]
-    stress_z = swap(sent[-1], "gz", z_pairs)
     (joined,) = call(
         functools.partial(join_kernel, n_y),
-        "svva" + "v" * len(xy),
-        (pos, v0, rd, stress_z, *xy),
+        "svvv" + "v" * len(xy),
+        (pos, v0, rd, sent[-1], *xy),
         "v",
         [arr(nx + 6, ny + 8, 128)],
         4 * size,
     )
     z_got = swap(joined, "gz", z_pairs)
+    main_v, main_rd = call(
+        functools.partial(fill_kernel, n_y),
+        "svv" + "v" * len(xy),
+        (pos, v0, rd, *xy),
+        "vv",
+        [arr(nx + 6, ny + 8, nz)] * 2,
+        4 * size,
+    )
     new_disp, new_vel, token = call(
         functools.partial(force_kernel, n_y),
         "sssvvvvv" + "v" * (3 + n_y),
@@ -629,7 +639,7 @@
             labels,
             stress,
             *xy[: 2 + n_y],
-            stress_z,
+            z_got,
         ),
         "hhv",
         [fields3, fields3, small],
@@ -642,15 +652,15 @@
     )
     peers = lax.axis_size("gx") * lax.axis_size("gy") * lax.axis_size("gz")
     v1, v2, spread = call(
-        functools.partial(krylov_kernel, n_y),
-        "svvvav" + "v" * len(xy),
-        (pos, v0, rd, mom, token, z_got, *xy),
+        krylov_kernel,
+        "svvvav",
+        (pos, main_v, main_rd, mom, token, z_got),
         "vvv",
         [field, field, arr(peers, 8, 128)],
         60 * size,
         [
-            pltpu.VMEM((nx + 6, ny + 8, nz + 128), F32),
-            pltpu.VMEM((nx + 6, ny + 8, nz + 128), F32),
+            pltpu.VMEM((nx + 6, ny + 8, 128), F32),
+            pltpu.VMEM((nx + 6, ny + 8, 128), F32),
             pltpu.VMEM((nx + 4, ny + 8, nz + 128), F32),
             pltpu.VMEM((nx + 2, ny + 8, nz + 128), F32),
         ],

time: 61.1 us -> 56.2 us (0.920)
  blocking collectives: 17 us -> 13.9 us
  starting transfers between devices: 16.3 us -> 14.8 us
  local copies, waits for them, and re-layouts: 3.16 us -> 4.35 us
  Pallas kernels: 18 us -> 16.9 us
    all_to_all x1, blocking collectives: 17 us -> 13.9 us  [per_device(): mom = lax.all_to_all(spread, ('gx', 'gy', 'gz'), 0, 0, tiled=True)]
    ppermute x11 -> x10, starting transfers between devices: 16.3 us -> 14.8 us  [swap(): return lax.ppermute(array, axis, pairs + [(b, a) for a, b in pairs])]
    pallas_call x6 -> x7, Pallas kernels: 18 us -> 16.9 us  [call(): pl.pallas_call(kernel, out_shape=outs, in_specs=[spec_of(k, a) for k, a i...]
    squeeze x0 -> x1, local copies, waits for them, and re-layouts: none -> 1.01 us  [per_device(): displacement[:, at]]
    slice x0 -> x1, local copies, waits for them, and re-layouts: none -> 0.84 us  [per_device(): damage[None, at]]
    unnamed x20 -> x22, local copies, waits for them, and re-layouts: 3.16 us -> 2.5 us
    ppermute x11 -> x10, waiting for transfers between devices: 4.57 us -> 4.96 us  [swap(): return lax.ppermute(array, axis, pairs + [(b, a) for a, b in pairs])]
  transfers between devices with their start and end apart: 11 -> 10, of which waited for: 3 -> 3; matrix products, arithmetic and copies ran while one was open for 0% -> 0% of each run, Pallas kernels for 6% -> 3%
where the time goes in v5:
time: 56.2 us; the launch traced here: 55.9 us
  Pallas kernels  16.9 us (30%)
  starting transfers between devices  14.8 us (26%)
  blocking collectives  13.9 us (25%)
  waiting for transfers between devices  4.96 us (9%)
  local copies, waits for them, and re-layouts  4.35 us (8%)
  between operations  0.87 us (2%)
    pallas_call x7, Pallas kernels, call(): pl.pallas_call(kernel, out_shape=outs, in_specs=[spec_of(k, a) for k, a i...  16.9 us
    ppermute x10, starting transfers between devices, swap(): return lax.ppermute(array, axis, pairs + [(b, a) for a, b in pairs])  14.8 us
    all_to_all x1, blocking collectives, per_device(): mom = lax.all_to_all(spread, ('gx', 'gy', 'gz'), 0, 0, tiled=True)  13.9 us
    ppermute x10, waiting for transfers between devices, swap(): return lax.ppermute(array, axis, pairs + [(b, a) for a, b in pairs])  4.96 us
    unnamed x22, local copies, waits for them, and re-layouts  2.5 us
  transfers between devices with their start and end apart: 10, of which 3 were waited for; matrix products, arithmetic and copies ran while one was open for 0% of the time, Pallas kernels for 3%

profile of v5, /device:TPU:0, one launch (start us, length us, event | category | flops | bytes accessed | tf_op | source)
XLA Modules:
  0.0 55.9 jit_solution(8476168313099547684)
XLA Ops:
  0.6 0.0 copy-start.10
  0.7 0.0 copy-start.7
  0.7 0.8 %fusion.2 = (f32[1,32,256]{2,1,0:T(8,128)S(1)}, f32[1,32,256]{2,1,0:T(8,128)S(1)}) fusion(f32[16,32,256]{2,1,0:T(8,128)} %damage_hbm.1), kind=kLoop, calls=%fused_computation.12 | loop fusion | bytes 131072 | tf_op jit(solution)/shard_map/slice | solution.py:574
  1.5 0.0 copy-start.4
  1.5 1.0 %slice_bitcast_fusion.1 = (f32[3,32,256]{2,1,0:T(8,128)S(1)}, f32[3,32,256]{2,1,0:T(8,128)S(1)}) fusion(f32[3,16,32,256]{3,2,1,0:T(8,128)} %disp.5), kind=kLoop, calls=%fused_computation.5 | loop fusion | bytes 393216 | tf_op jit(solution)/shard_map/squeeze | solution.py:574
  2.6 0.7 %collective-permute-start.1 = (f32[4,32,256]{2,1,0:T(8,128)S(1)}, f32[4,32,256]{2,1,0:T(8,128)S(1)}, u32[]{:S(2)}, u32[]{:S(2)}) collective-permute-start(f32[4,32,256]{2,1,0:T(8,128)S(1)} %get-tuple-element.50), channel_id=1, source_target_pairs={{4,8},{8,4},{5,9},{9,5},{6,10},{10,6},{7,11},{11,7},{20,24},{24,20... | collective-permute-start | bytes 393224 | tf_op jit(solution)/shard_map/ppermute | solution.py:508
  3.2 0.1 pad_add_fusion.pos
  3.3 5.8 %collective-permute-start = (f32[4,32,256]{2,1,0:T(8,128)S(1)}, f32[4,32,256]{2,1,0:T(8,128)S(1)}, u32[]{:S(2)}, u32[]{:S(2)}) collective-permute-start(f32[4,32,256]{2,1,0:T(8,128)S(1)} %get-tuple-element.51), channel_id=1, source_target_pairs={{0,4},{8,12},{4,0},{12,8},{1,5},{9,13},{5,1},{13,9},{2,6},{10,14},... | collective-permute-start | bytes 393224 | tf_op jit(solution)/shard_map/ppermute | solution.py:508
  9.2 0.0 copy-start
  9.2 1.4 %copy-done = f32[3,16,32,256]{3,2,1,0:T(8,128)S(1)} copy-done((f32[3,16,32,256]{3,2,1,0:T(8,128)S(1)}, f32[3,16,32,256]{3,2,1,0:T(8,128)}, u32[]{:S(2)}) %copy-start) | copy-done | bytes 1572888
  10.6 0.0 copy-start.2
  10.6 1.0 %copy-done.2 = f32[16,32,256]{2,1,0:T(8,128)S(1)} copy-done((f32[16,32,256]{2,1,0:T(8,128)S(1)}, f32[16,32,256]{2,1,0:T(8,128)}, u32[]{:S(2)}) %copy-start.2) | copy-done | bytes 524312
  11.6 0.0 copy-start.8
  11.6 1.0 %shard_map.120 = (f32[4,16,256]{2,1,0:T(8,128)S(1)}, f32[16,32,128]{2,1,0:T(8,128)S(1)}) custom-call(s32[3]{0:T(128)S(1)} %pad_add_fusion.pos, f32[3,16,32,256]{3,2,1,0:T(8,128)S(1)} %copy-done, f32[16,32,256]{2,1,0:T(8,128)S(1)} %copy-done.2), custom_call_target="tpu_custom_call" | custom-call | flops 131072 | bytes 2424844 | tf_op jit(solution)/shard_map/pallas_call | solution.py:543
  12.6 1.6 %collective-permute-start.2 = (f32[4,16,256]{2,1,0:T(8,128)S(1)}, f32[4,16,256]{2,1,0:T(8,128)S(1)}, u32[]{:S(2)}, u32[]{:S(2)}) collective-permute-start(f32[4,16,256]{2,1,0:T(8,128)S(1)} %get-tuple-element.25), channel_id=1, source_target_pairs={{0,2},{2,0},{1,3},{3,1},{4,6},{6,4},{5,7},{7,5},{8,10},{10,8},{9,1... | collective-permute-start | bytes 196616 | tf_op jit(solution)/shard_map/ppermute | solution.py:508
  14.1 0.0 collective-permute-start.3
  14.1 0.0 copy-done.10
  14.2 2.7 %collective-permute-done.2.refs_2_ = f32[4,16,256]{2,1,0:T(8,128)S(1)} collective-permute-done((f32[4,16,256]{2,1,0:T(8,128)S(1)}, f32[4,16,256]{2,1,0:T(8,128)S(1)}, u32[]{:S(2)}, u32[]{:S(2)}) %collective-permute-start.2) | collective-permute-done | bytes 65568 | tf_op jit(solution)/shard_map/ppermute | solution.py:508
  16.9 0.0 collective-permute-done.1.refs_1_
  16.9 0.0 collective-permute-done.refs_0_
  16.9 0.0 collective-permute-done.3.refs_3_
  16.9 0.0 copy-done.7
  16.9 0.0 copy-done.4
  16.9 0.0 copy-done.8
  17.0 4.7 %shard_map.121 = (f32[16,32,256]{2,1,0:T(8,128)}, f32[16,32,256]{2,1,0:T(8,128)S(1)}, f32[16,32,256]{2,1,0:T(8,128)S(1)}, f32[6,16,32,256]{3,2,1,0:T(8,128)S(1)}...) custom-call(s32[3]{0:T(128)S(1)} %pad_add_fusion.pos, ...), custom_call_target="tpu_custom_call" | custom-call | flops 19660800 | bytes 9982028 | tf_op jit(solution)/shard_map/pallas_call | solution.py:543
  21.6 0.1 collective-permute-start.4
  21.7 0.7 %collective-permute-start.5 = (f32[8,32,256]{2,1,0:T(8,128)S(1)}, f32[8,32,256]{2,1,0:T(8,128)S(1)}, u32[]{:S(2)}, u32[]{:S(2)}) collective-permute-start(f32[8,32,256]{2,1,0:T(8,128)S(1)} %get-tuple-element.29), channel_id=1, source_target_pairs={{4,8},{8,4},{5,9},{9,5},{6,10},{10,6},{7,11},{11,7},{20,24},{24,20... | collective-permute-start | bytes 786440 | tf_op jit(solution)/shard_map/ppermute | solution.py:508
  22.4 1.6 %collective-permute-start.6 = (f32[22,8,256]{2,1,0:T(8,128)S(1)}, f32[22,8,256]{2,1,0:T(8,128)S(1)}, u32[]{:S(2)}, u32[]{:S(2)}) collective-permute-start(f32[22,8,256]{2,1,0:T(8,128)S(1)} %get-tuple-element.30), channel_id=1, source_target_pairs={{0,2},{2,0},{1,3},{3,1},{4,6},{6,4},{5,7},{7,5},{8,10},{10,8},{9,1... | collective-permute-start | bytes 540680 | tf_op jit(solution)/shard_map/ppermute | solution.py:508
  24.0 3.7 %collective-permute-start.7 = (f32[2,8,256]{2,1,0:T(8,128)S(1)}, f32[2,8,256]{2,1,0:T(8,128)S(1)}, u32[]{:S(2)}, u32[]{:S(2)}) collective-permute-start(f32[2,8,256]{2,1,0:T(8,128)S(1)} %get-tuple-element.34), channel_id=1, source_target_pairs={{0,6},{2,4},{8,14},{10,12},{6,0},{4,2},{14,8},{12,10},{1,7},{3,5},... | collective-permute-start | bytes 49160 | tf_op jit(solution)/shard_map/ppermute | solution.py:508
  27.6 0.7 %collective-permute-start.8 = (f32[2,8,256]{2,1,0:T(8,128)S(1)}, f32[2,8,256]{2,1,0:T(8,128)S(1)}, u32[]{:S(2)}, u32[]{:S(2)}) collective-permute-start(f32[2,8,256]{2,1,0:T(8,128)S(1)} %get-tuple-element.35), channel_id=1, source_target_pairs={{4,10},{6,8},{10,4},{8,6},{5,11},{7,9},{11,5},{9,7},{20,26},{22,24... | collective-permute-start | bytes 49160 | tf_op jit(solution)/shard_map/ppermute | solution.py:508
  28.3 1.1 %collective-permute-done.7.refs_3_ = f32[2,8,256]{2,1,0:T(8,128)S(1)} collective-permute-done((f32[2,8,256]{2,1,0:T(8,128)S(1)}, f32[2,8,256]{2,1,0:T(8,128)S(1)}, u32[]{:S(2)}, u32[]{:S(2)}) %collective-permute-start.7) | collective-permute-done | bytes 16416 | tf_op jit(solution)/shard_map/ppermute | solution.py:508
  29.4 0.0 collective-permute-done.8.refs_4_
  29.4 0.0 collective-permute-done.6.refs_2_
  29.4 0.0 collective-permute-done.4.refs_0_
  29.4 0.0 collective-permute-done.5.refs_1_
  29.4 0.0 copy-start.1
  29.4 0.0 copy-start.5
  29.4 0.0 copy-start.6
  29.4 0.0 copy-start.9
  29.4 1.1 %shard_map.122 = f32[22,40,128]{2,1,0:T(8,128)S(1)} custom-call(s32[3]{0:T(128)S(1)} %pad_add_fusion.pos, f32[16,32,256]{2,1,0:T(8,128)S(1)} %get-tuple-element.31.v.v0, f32[16,32,256]{2,1,0:T(8,128)S(1)} %get-tuple-element.32.rd, f32[16,32,128]{2,1,0:T(8,128)S(1)} %get-tuple-element.33.columns, f32[8,32,256]{2,1,0:T(8,128)S(1)} %collective-permute-done.4.refs_0_, ...), custom_call_target="tpu_custom_call" | custom-call | flops 524288 | bytes 2498572 | tf_op jit(solution)/shard_map/pallas_call | solution.py:543
  30.5 0.1 collective-permute-start.9
  30.6 0.7 %shard_map.124 = (f32[22,40,256]{2,1,0:T(8,128)S(1)}, f32[22,40,256]{2,1,0:T(8,128)S(1)}) custom-call(s32[3]{0:T(128)S(1)} %pad_add_fusion.pos, f32[16,32,256]{2,1,0:T(8,128)S(1)} %get-tuple-element.31.v.v0, f32[16,32,256]{2,1,0:T(8,128)S(1)} %get-tuple-element.32.rd, f32[8,32,256]{2,1,0:T(8,128)S(1)} %collective-permute-done.4.refs_0_, ...), custom_call_target="tpu_custom_call" | custom-call | flops 524288 | bytes 3588108 | tf_op jit(solution)/shard_map/pallas_call | solution.py:543
  31.3 1.1 %collective-permute-done.9.refs_3_.z_got = f32[22,40,128]{2,1,0:T(8,128)S(1)} collective-permute-done((f32[22,40,128]{2,1,0:T(8,128)S(1)}, f32[22,40,128]{2,1,0:T(8,128)S(1)}, u32[]{:S(2)}, u32[]{:S(2)}) %collective-permute-start.9) | collective-permute-done | bytes 450592 | tf_op jit(solution)/shard_map/ppermute | solution.py:508
  32.4 0.0 copy-done.1
  32.4 0.0 copy-done.5
  32.4 0.0 copy-done.6
  32.4 0.0 copy-done.9
  32.4 3.6 %shard_map.123 = (f32[3,16,32,256]{3,2,1,0:T(8,128)}, f32[3,16,32,256]{3,2,1,0:T(8,128)}, f32[8,128]{1,0:T(8,128)S(1)}) custom-call(s32[3]{0:T(128)S(1)} %pad_add_fusion.pos, f32[4,4]{1,0:T(4,128)S(1)} %pad_maximum_fusion.2.table, f32[3]{0:T(128)S(1)} %copy-done.9, f32[3,16,32,256]{3,2,1,0:T(8,128)S(1)} %copy-done.1, f32[3,16,32,256]{3,2,1,0:T(8,128)S(1)} %copy-done.5, ...), custom_call_target="tpu_custom_call" | custom-call | flops 7864320 | bytes 11645016 | tf_op jit(solution)/shard_map/pallas_call | solution.py:543
  36.1 0.0 copy-start.3
  36.1 4.2 %shard_map.125 = (f32[16,32,256]{2,1,0:T(8,128)S(1)}, f32[16,32,256]{2,1,0:T(8,128)S(1)}, f32[16,8,128]{2,1,0:T(8,128)S(1)}) custom-call(s32[3]{0:T(128)S(1)} %pad_add_fusion.pos, f32[22,40,256]{2,1,0:T(8,128)S(1)} %get-tuple-element.39.main_v, f32[22,40,256]{2,1,0:T(8,128)S(1)} %get-tuple-element.40.main_rd, f32[8,128]{1,0:T(8,128)S(1)} %get-tuple-element.41.mom, ...), custom_call_target="tpu_custom_call" | custom-call | flops 7864320 | bytes 3375116 | tf_op jit(solution)/shard_map/pallas_call | solution.py:543
  40.2 13.9 %all_to_all.5.mom = f32[16,8,128]{2,1,0:T(8,128)S(1)} all-to-all(f32[16,8,128]{2,1,0:T(8,128)S(1)} %get-tuple-element.43), channel_id=1, replica_groups=mesh['case'=2,'gx'=4,'gy'=2,'gz'=2] {'gx','gy','gz'}, dimensions={0} | all-to-all | bytes 131072 | tf_op jit(solution)/shard_map/all_to_all | solution.py:668
  54.1 0.0 copy-done.3
  54.1 1.7 %shard_map.126 = f32[16,32,256]{2,1,0:T(8,128)} custom-call(f32[16,8,128]{2,1,0:T(8,128)S(1)} %all_to_all.5.mom, f32[16,32,256]{2,1,0:T(8,128)S(1)} %get-tuple-element.31.v.v0, f32[16,32,256]{2,1,0:T(8,128)S(1)} %get-tuple-element.44.v1, f32[16,32,256]{2,1,0:T(8,128)S(1)} %get-tuple-element.45.v2, f32[16,32,256]{2,1,0:T(8,128)S(1)} %copy-done.3), custom_call_target="tpu_custom_call" | custom-call | flops 1048576 | bytes 2686976 | tf_op jit(solution)/shard_map/pallas_call | solution.py:543
  (3 shorter events, 0.0 us)
Async XLA Ops:
  0.6 13.5 %copy-start.10 = (f32[4,4]{1,0:T(4,128)S(1)}, f32[4,4]{1,0:T(4,128)}, u32[]{:S(2)}) copy-start(f32[4,4]{1,0:T(4,128)} %param.16) | copy-start | bytes 196
  0.7 16.3 %copy-start.7 = (f32[16,32,256]{2,1,0:T(8,128)S(1)}, f32[16,32,256]{2,1,0:T(8,128)}, u32[]{:S(2)}) copy-start(f32[16,32,256]{2,1,0:T(8,128)} %history.1) | copy-start | bytes 1572868
  1.5 15.4 %copy-start.4 = (s32[16,32,256]{2,1,0:T(8,128)S(1)}, s32[16,32,256]{2,1,0:T(8,128)}, u32[]{:S(2)}) copy-start(s32[16,32,256]{2,1,0:T(8,128)} %labels.3) | copy-start | bytes 1572868
  2.6 14.4 %collective-permute-start.1 = (f32[4,32,256]{2,1,0:T(8,128)S(1)}, f32[4,32,256]{2,1,0:T(8,128)S(1)}, u32[]{:S(2)}, u32[]{:S(2)}) collective-permute-start(f32[4,32,256]{2,1,0:T(8,128)S(1)} %get-tuple-element.50), channel_id=1, source_target_pairs={{4,8},{8,4},{5,9},{9,5},{6,10},{10,6},{7,11},{11,7},{20,24},{24,20... | collective-permute-start | bytes 393224 | tf_op jit(solution)/shard_map/ppermute | solution.py:508
  3.3 13.6 %collective-permute-start = (f32[4,32,256]{2,1,0:T(8,128)S(1)}, f32[4,32,256]{2,1,0:T(8,128)S(1)}, u32[]{:S(2)}, u32[]{:S(2)}) collective-permute-start(f32[4,32,256]{2,1,0:T(8,128)S(1)} %get-tuple-element.51), channel_id=1, source_target_pairs={{0,4},{8,12},{4,0},{12,8},{1,5},{9,13},{5,1},{13,9},{2,6},{10,14},... | collective-permute-start | bytes 393224 | tf_op jit(solution)/shard_map/ppermute | solution.py:508
  9.2 1.4 %copy-start = (f32[3,16,32,256]{3,2,1,0:T(8,128)S(1)}, f32[3,16,32,256]{3,2,1,0:T(8,128)}, u32[]{:S(2)}) copy-start(f32[3,16,32,256]{3,2,1,0:T(8,128)} %disp.5) | copy-start | bytes 4718596
  10.6 1.0 %copy-start.2 = (f32[16,32,256]{2,1,0:T(8,128)S(1)}, f32[16,32,256]{2,1,0:T(8,128)}, u32[]{:S(2)}) copy-start(f32[16,32,256]{2,1,0:T(8,128)} %damage_hbm.1) | copy-start | bytes 1572868
  11.6 5.3 %copy-start.8 = (s32[16,32,256]{2,1,0:T(8,128)S(1)}, s32[16,32,256]{2,1,0:T(8,128)}, u32[]{:S(2)}) copy-start(s32[16,32,256]{2,1,0:T(8,128)} %notch.1) | copy-start | bytes 1572868
  12.6 4.3 %collective-permute-start.2 = (f32[4,16,256]{2,1,0:T(8,128)S(1)}, f32[4,16,256]{2,1,0:T(8,128)S(1)}, u32[]{:S(2)}, u32[]{:S(2)}) collective-permute-start(f32[4,16,256]{2,1,0:T(8,128)S(1)} %get-tuple-element.25), channel_id=1, source_target_pairs={{0,2},{2,0},{1,3},{3,1},{4,6},{6,4},{5,7},{7,5},{8,10},{10,8},{9,1... | collective-permute-start | bytes 196616 | tf_op jit(solution)/shard_map/ppermute | solution.py:508
  14.1 2.8 %collective-permute-start.3 = (f32[16,32,128]{2,1,0:T(8,128)S(1)}, f32[16,32,128]{2,1,0:T(8,128)S(1)}, u32[]{:S(2)}, u32[]{:S(2)}) collective-permute-start(f32[16,32,128]{2,1,0:T(8,128)S(1)} %get-tuple-element.26), channel_id=1, source_target_pairs={{0,1},{1,0},{2,3},{3,2},{4,5},{5,4},{6,7},{7,6},{8,9},{9,8},{10,11... | collective-permute-start | bytes 786440 | tf_op jit(solution)/shard_map/ppermute | solution.py:508
  21.6 7.7 %collective-permute-start.4 = (f32[8,32,256]{2,1,0:T(8,128)S(1)}, f32[8,32,256]{2,1,0:T(8,128)S(1)}, u32[]{:S(2)}, u32[]{:S(2)}) collective-permute-start(f32[8,32,256]{2,1,0:T(8,128)S(1)} %get-tuple-element.28), channel_id=1, source_target_pairs={{0,4},{8,12},{4,0},{12,8},{1,5},{9,13},{5,1},{13,9},{2,6},{10,14},... | collective-permute-start | bytes 786440 | tf_op jit(solution)/shard_map/ppermute | solution.py:508
  21.7 7.6 %collective-permute-start.5 = (f32[8,32,256]{2,1,0:T(8,128)S(1)}, f32[8,32,256]{2,1,0:T(8,128)S(1)}, u32[]{:S(2)}, u32[]{:S(2)}) collective-permute-start(f32[8,32,256]{2,1,0:T(8,128)S(1)} %get-tuple-element.29), channel_id=1, source_target_pairs={{4,8},{8,4},{5,9},{9,5},{6,10},{10,6},{7,11},{11,7},{20,24},{24,20... | collective-permute-start | bytes 786440 | tf_op jit(solution)/shard_map/ppermute | solution.py:508
  22.4 7.0 %collective-permute-start.6 = (f32[22,8,256]{2,1,0:T(8,128)S(1)}, f32[22,8,256]{2,1,0:T(8,128)S(1)}, u32[]{:S(2)}, u32[]{:S(2)}) collective-permute-start(f32[22,8,256]{2,1,0:T(8,128)S(1)} %get-tuple-element.30), channel_id=1, source_target_pairs={{0,2},{2,0},{1,3},{3,1},{4,6},{6,4},{5,7},{7,5},{8,10},{10,8},{9,1... | collective-permute-start | bytes 540680 | tf_op jit(solution)/shard_map/ppermute | solution.py:508
  24.0 5.4 %collective-permute-start.7 = (f32[2,8,256]{2,1,0:T(8,128)S(1)}, f32[2,8,256]{2,1,0:T(8,128)S(1)}, u32[]{:S(2)}, u32[]{:S(2)}) collective-permute-start(f32[2,8,256]{2,1,0:T(8,128)S(1)} %get-tuple-element.34), channel_id=1, source_target_pairs={{0,6},{2,4},{8,14},{10,12},{6,0},{4,2},{14,8},{12,10},{1,7},{3,5},... | collective-permute-start | bytes 49160 | tf_op jit(solution)/shard_map/ppermute | solution.py:508
  27.6 1.7 %collective-permute-start.8 = (f32[2,8,256]{2,1,0:T(8,128)S(1)}, f32[2,8,256]{2,1,0:T(8,128)S(1)}, u32[]{:S(2)}, u32[]{:S(2)}) collective-permute-start(f32[2,8,256]{2,1,0:T(8,128)S(1)} %get-tuple-element.35), channel_id=1, source_target_pairs={{4,10},{6,8},{10,4},{8,6},{5,11},{7,9},{11,5},{9,7},{20,26},{22,24... | collective-permute-start | bytes 49160 | tf_op jit(solution)/shard_map/ppermute | solution.py:508
  29.4 3.0 %copy-start.1 = (f32[3,16,32,256]{3,2,1,0:T(8,128)S(1)}, f32[3,16,32,256]{3,2,1,0:T(8,128)}, u32[]{:S(2)}) copy-start(f32[3,16,32,256]{3,2,1,0:T(8,128)} %disp.5) | copy-start | bytes 4718596
  29.4 3.0 %copy-start.5 = (f32[3,16,32,256]{3,2,1,0:T(8,128)S(1)}, f32[3,16,32,256]{3,2,1,0:T(8,128)}, u32[]{:S(2)}) copy-start(f32[3,16,32,256]{3,2,1,0:T(8,128)} %vel.1) | copy-start | bytes 4718596
  29.4 3.0 %copy-start.6 = (s32[16,32,256]{2,1,0:T(8,128)S(1)}, s32[16,32,256]{2,1,0:T(8,128)}, u32[]{:S(2)}) copy-start(s32[16,32,256]{2,1,0:T(8,128)} %contact.1) | copy-start | bytes 1572868
  29.4 3.0 %copy-start.9 = (f32[3]{0:T(128)S(1)}, f32[3]{0:T(128)}, u32[]{:S(2)}) copy-start(f32[3]{0:T(128)} %impact.1) | copy-start | bytes 40
  30.5 1.9 %collective-permute-start.9 = (f32[22,40,128]{2,1,0:T(8,128)S(1)}, f32[22,40,128]{2,1,0:T(8,128)S(1)}, u32[]{:S(2)}, u32[]{:S(2)}) collective-permute-start(f32[22,40,128]{2,1,0:T(8,128)S(1)} %shard_map.122), channel_id=1, source_target_pairs={{0,1},{1,0},{2,3},{3,2},{4,5},{5,4},{6,7},{7,6},{8,9},{9,8},{10,11... | collective-permute-start | bytes 1351688 | tf_op jit(solution)/shard_map/ppermute | solution.py:508
  36.1 18.1 %copy-start.3 = (f32[16,32,256]{2,1,0:T(8,128)S(1)}, f32[16,32,256]{2,1,0:T(8,128)}, u32[]{:S(2)}) copy-start(f32[16,32,256]{2,1,0:T(8,128)} %damage_hbm.1) | copy-start | bytes 1572868

commit v6 on v5

--- a/solution.py
+++ b/solution.py
@@ -12,7 +12,6 @@
 STIFF_FLOOR = 0.001
 ALPHA_LOW, ALPHA_HIGH = 0.5, 6.5
 VMEM_BYTES = 28 * 1024 * 1024
-STRESS_LANE = 32
 CHUNKS = 4
 F32 = jnp.float32
 
@@ -31,20 +30,6 @@
     refs[0][index] = jnp.where(odd, low, high)
     if len(refs) == 2:
         refs[1][index] = jnp.where(odd, high, low)
-
-
-def shift_x(ref, lead, x, at, block, faces):
-    count = ref.shape[-3]
-    lo, hi = faces
-    if at > 0:
-        lower = ref[(*lead, x - 1)]
-    else:
-        lower = jnp.where(x == 0, lo(), ref[(*lead, jnp.maximum(x - 1, 0))])
-    if at < block - 1:
-        upper = ref[(*lead, x + 1)]
-    else:
-        upper = jnp.where(x == count - 1, hi(), ref[(*lead, jnp.minimum(x + 1, count - 1))])
-    return upper, lower
 
 
 def shift_y(plane, rows):
@@ -121,6 +106,12 @@
     unrolled(damage.shape[0], 8, body, 0)
 
 
+def pack_x_kernel(pos, disp, damage, after, *xs):
+    odd_x, count = pos[0] == 1, damage.shape[0]
+    for field, src in enumerate((disp.at[0], disp.at[1], disp.at[2], damage)):
+        send(odd_x, xs, field, src[0], src[count - 1])
+
+
 def row_tile(v, rd, is_high):
     rows = v.shape[0]
     part = slice(rows - 8, rows) if is_high else slice(0, 8)
@@ -129,49 +120,35 @@
     return jnp.where(keep, v[part], pltpu.roll(rd[part], 4, 0))
 
 
-def local_kernel(n_y, pos, table, disp, damage, history, notch, labels, *refs):
-    xg, yg, zg = refs[:2], refs[2 : 2 + n_y], refs[2 + n_y]
-    refs = refs[3 + n_y :]
-    hist_hbm, rd_out, v_out, stress_out, mom_out = refs[:5]
-    refs = refs[5:]
-    xs, ys, ds = refs[:2], refs[2 : 2 + n_y], refs[2 + n_y : 2 + 3 * n_y]
-    zs, hist_out, sems = refs[2 + 3 * n_y :]
-    odd_x, odd_y, gz = pos[0] == 1, pos[1] == 1, pos[2]
-    count = damage.shape[0]
-    block = count // CHUNKS
-    tall = count // 8
-    regions = table.shape[1]
-    lames = [table[0, r] for r in range(regions)]
-    shears = [table[1, r] for r in range(regions)]
-    bases = [table[3, r] for r in range(regions)]
-
-    def store(step):
-        part = pl.ds(step * block, block)
-        return pltpu.make_async_copy(hist_out.at[part], hist_hbm.at[part], sems.at[step])
-
-    def around(ref, lead, field, plane, x, at):
-        faces = (
-            lambda: jnp.where(odd_x, xg[0][field], xg[1][field]),
-            lambda: jnp.where(odd_x, xg[1][field], xg[0][field]),
+class Local:
+    def __init__(self, pos, table, disp, damage, history, notch, labels, yg, zg):
+        self.odd_x, self.odd_y, self.gz = pos[0] == 1, pos[1] == 1, pos[2]
+        self.disp, self.damage, self.history = disp, damage, history
+        self.notch, self.labels, self.yg, self.zg = notch, labels, yg, zg
+        regions = range(table.shape[1])
+        self.lames = [table[0, r] for r in regions]
+        self.shears = [table[1, r] for r in regions]
+        self.bases = [table[3, r] for r in regions]
+
+    def around(self, field, plane, x, lower, upper):
+        rows = low_high(self.odd_y, [y[field, pl.ds(x, 1), :] for y in self.yg])
+        column = self.zg[x][:, field : field + 1]
+        return (
+            (upper, lower),
+            shift_y(plane, rows),
+            shift_z(plane, column, self.gz == 0),
         )
-        rows = low_high(odd_y, [y[field, pl.ds(x, 1), :] for y in yg])
-        column = zg[x][:, field : field + 1]
-        return (
-            shift_x(ref, lead, x, at, block, faces),
-            shift_y(plane, rows),
-            shift_z(plane, column, gz == 0),
-        )
-
-    def body(x, at):
+
+    def plane(self, x, lower, upper):
         g = []
         for c in range(3):
-            pairs = around(disp, (c,), c, disp[c, x], x, at)
-            g.append([upper - lower for upper, lower in pairs])
-        lab = labels[x]
-        lame = by_label(lab, lames)
-        shear = by_label(lab, shears)
-        base = by_label(lab, bases)
-        dmg = damage[x]
+            pairs = self.around(c, self.disp[c, x], x, lower(c), upper(c))
+            g.append([high - low for high, low in pairs])
+        lab = self.labels[x]
+        lame = by_label(lab, self.lames)
+        shear = by_label(lab, self.shears)
+        base = by_label(lab, self.bases)
+        dmg = self.damage[x]
         degrade = 4.0 * ((1.0 - dmg) * (1.0 - dmg) + STIFF_FLOOR)
         trace = g[0][0] + g[1][1] + g[2][2]
         shears3 = [g[0][1] + g[1][0], g[0][2] + g[2][0], g[1][2] + g[2][1]]
@@ -185,49 +162,146 @@
         whole = half + half
         level = (degrade * lame) * trace
         stress = [level + whole * g[k][k] for k in range(3)] + [half * e for e in shears3]
-        for k in range(6):
-            stress_out[k, x] = stress[k]
         hist = jnp.maximum(
-            jnp.maximum(history[x], energy), NOTCH_LOAD * notch[x].astype(F32)
+            jnp.maximum(self.history[x], energy), NOTCH_LOAD * self.notch[x].astype(F32)
         )
-        hist_out[x] = hist
         diagonal = base + 2.0 * hist
         rd = 1.0 / diagonal
-        rd_out[x] = rd
-        (xu, xl), (yu, yl), (zu, zl) = around(damage, (), 3, dmg, x, at)
+        (xu, xl), (yu, yl), (zu, zl) = self.around(3, dmg, x, lower(3), upper(3))
         near = ((xu + xl) + (yu + yl)) + (zu + zl)
         residual = 2.0 * hist - (diagonal * dmg - KAPPA_COEF * near)
         v = residual * rd
-        v_out[x] = v
-        send(odd_y, ys, x, row_tile(v, rd, False), row_tile(v, rd, True))
+        return stress, hist, rd, v, folded(residual * v)
+
+    def send_y(self, ys, x, v, rd, stress):
+        count = self.damage.shape[0]
+        tall, last = count // 8, v.shape[0] - 1
+        send(self.odd_y, ys, x, row_tile(v, rd, False), row_tile(v, rd, True))
         for c, k in enumerate((3, 1, 5)):
-            last = v.shape[0] - 1
             spot = (count + c * tall + lax.div(x, 8), pl.ds(lax.rem(x, 8), 1), slice(None))
-            send(odd_y, ys, spot, stress[k][0:1], stress[k][last : last + 1])
-        send_columns(zs, x, [stress[4], stress[5], stress[2]], gz)
-        return folded(residual * v)
+            send(self.odd_y, ys, spot, stress[k][0:1], stress[k][last : last + 1])
+
+    def send_z(self, zs, x, stress):
+        send_columns(zs, x, [stress[4], stress[5], stress[2]], self.gz)
+
+
+def inner_steps(count):
+    inner = count - 2
+    many = max(m for m in range(1, 8) if inner % m == 0)
+    return inner // many, many
+
+
+def inner_kernel(n_y, pos, table, disp, damage, history, notch, labels, *refs):
+    local = Local(
+        pos, table, disp, damage, history, notch, labels, refs[:n_y], refs[n_y]
+    )
+    hist_hbm, rd_out, v_out, stress_out, mom_out = refs[n_y + 1 : n_y + 6]
+    ys, (zs, hist, sems) = refs[n_y + 6 : 2 * n_y + 6], refs[2 * n_y + 6 :]
+    steps, many = inner_steps(damage.shape[0])
+
+    def store(step):
+        part = pl.ds(1 + step * many, many)
+        return pltpu.make_async_copy(hist.at[part], hist_hbm.at[part], sems.at[step])
 
     def several(step, total):
-        for at in range(block):
-            total = total + body(step * block + at, at)
+        for at in range(many):
+            x = 1 + step * many + at
+
+            def lower(c):
+                return damage[x - 1] if c == 3 else disp[c, x - 1]
+
+            def upper(c):
+                return damage[x + 1] if c == 3 else disp[c, x + 1]
+
+            stress, hist_x, rd, v, part = local.plane(x, lower, upper)
+            for k in range(6):
+                stress_out[k, x] = stress[k]
+            hist[x] = hist_x
+            rd_out[x] = rd
+            v_out[x] = v
+            local.send_y(ys, x, v, rd, stress)
+            local.send_z(zs, x, stress)
+            total = total + part
         store(step).start()
         return total
 
-    total = lax.fori_loop(0, CHUNKS, several, jnp.zeros((8, 128), F32))
+    mom_out[...] = lax.fori_loop(0, steps, several, jnp.zeros((8, 128), F32))
+    for step in range(steps):
+        store(step).wait()
+
+
+def ends_kernel(n_y, pos, table, disp, damage, history, notch, labels, *refs):
+    local = Local(
+        pos, table, disp, damage, history, notch, labels, refs[:n_y], refs[n_y]
+    )
+    refs = refs[n_y + 1 :]
+    xg, (_, rd_in, v_in, mom), ys_in, zs_in = (
+        refs[:2],
+        refs[2:6],
+        refs[6 : 6 + n_y],
+        refs[6 + n_y],
+    )
+    refs = refs[7 + n_y :]
+    hist_hbm, rd_out, v_out, stress_out, mom_out = refs[:5]
+    xs, ys, (zs, hist, sems) = refs[5:7], refs[7 : 7 + n_y], refs[7 + n_y :]
+    odd_x, count = local.odd_x, damage.shape[0]
+    total = mom[...]
+    copies, found = [], []
+    for end, x in enumerate((0, count - 1)):
+
+        def outside(c):
+            first, second = xg[0][c], xg[1][c]
+            if end == 0:
+                return jnp.where(odd_x, first, second)
+            return jnp.where(odd_x, second, first)
+
+        def beside(c):
+            at = 1 if end == 0 else count - 2
+            return damage[at] if c == 3 else disp[c, at]
+
+        sides = (outside, beside) if end == 0 else (beside, outside)
+        stress, hist_x, rd, v, part = local.plane(x, *sides)
+        hist[end] = hist_x
+        copies.append(pltpu.make_async_copy(hist.at[end], hist_hbm.at[x], sems.at[end]))
+        copies[-1].start()
+        for k in range(6):
+            stress_out[k, end] = stress[k]
+        rd_out[x] = rd
+        v_out[x] = v
+        total = total + part
+        found.append((stress, rd, v))
+    tall = count // 8
+    for mine, before in zip(ys, ys_in, strict=True):
+        for x in [*range(1, count - 1), *range(count, count + 3 * tall)]:
+            mine[x] = before[x]
+    for x in range(1, count - 1):
+        rd_out[x] = rd_in[x]
+        v_out[x] = v_in[x]
+        zs[x] = zs_in[x]
+    for end, x in enumerate((0, count - 1)):
+        stress, rd, v = found[end]
+        local.send_y(ys, x, v, rd, stress)
+        local.send_z(zs, x, stress)
     for depth in (1, 2, 3):
         low, high = depth - 1, count - depth
         send(odd_x, xs, depth - 1, v_out[low], v_out[high])
         if depth <= 2:
             send(odd_x, xs, 2 + depth, rd_out[low], rd_out[high])
-            for which in range(n_y):
-                pair = (ds[which], ds[n_y + which])
-                send(odd_x, pair, depth - 1, ys[which][low], ys[which][high])
     for slot, k in ((5, 0), (6, 3), (7, 4)):
-        send(odd_x, xs, slot, stress_out[k, 0], stress_out[k, count - 1])
+        send(odd_x, xs, slot, stress_out[k, 0], stress_out[k, 1])
     mom_out[...] = jnp.zeros((8, 128), F32)
     mom_out[0:1, :] = jnp.sum(total, axis=0, keepdims=True)
-    for step in range(CHUNKS):
-        store(step).wait()
+    for copy in copies:
+        copy.wait()
+
+
+def corner_kernel(n_y, pos, after, *refs):
+    ys, ds = refs[:n_y], refs[n_y:]
+    odd_x, count = pos[0] == 1, after.shape[0]
+    for which in range(n_y):
+        for depth in (1, 2):
+            pair = (ds[which], ds[n_y + which])
+            send(odd_x, pair, depth - 1, ys[which][depth - 1], ys[which][count - depth])
 
 
 class Enlarged:
@@ -274,7 +348,7 @@
             yield count - 1 + depth, self.halo(False, depth)
 
 
-def join_kernel(n_y, pos, v, rd, columns, *refs):
+def join_kernel(n_y, pos, v, rd, *refs):
     big = Enlarged(n_y, pos, v, rd, refs[:-1])
     out = refs[-1]
     first_z = pos[2] == 0
@@ -297,13 +371,9 @@
 
     def body(x, carry):
         put(x, big.own(x))
-        lanes = iota2((ny, 128), 1)
-        mark = (lanes >= STRESS_LANE) & (lanes < STRESS_LANE + 3)
-        moved = pltpu.roll(columns[x], STRESS_LANE, 1)
-        out[x + 3, 0:ny] = jnp.where(mark, moved, out[x + 3, 0:ny])
         return carry
 
-    unrolled(count, 4, body, 0)
+    unrolled(count, 8, body, 0)
 
 
 def fill_kernel(n_y, pos, v, rd, *refs):
@@ -339,7 +409,7 @@
         z_rd[p] = jnp.where(keep, pltpu.roll(tile, 64, 1), 0.0)
         return carry
 
-    unrolled(count + 6, 2, split, 0)
+    unrolled(count + 6, 11 if count % 11 == 5 else 1, split, 0)
 
     def v_at(at):
         return jnp.concatenate([main_v[at], z_v[at]], axis=1)
@@ -384,11 +454,11 @@
     zero = jnp.zeros((8, 128), F32)
     for p in (-2, -1, count, count + 1):
         big_v1[p + 2] = image_of(v_at, p + 3)[1] * rd_at(p + 3)
-    k1, k2 = unrolled(count, 4, first, (zero, zero))
+    k1, k2 = unrolled(count, 8, first, (zero, zero))
     for p in (-1, count):
         big_v2[p + 1] = image_of(v1_at, p + 2)[1] * rd_at(p + 3)
-    k3, k4 = unrolled(count, 4, second, (zero, zero))
-    k5 = unrolled(count, 4, third, zero)
+    k3, k4 = unrolled(count, 8, second, (zero, zero))
+    k5 = unrolled(count, 8, third, zero)
     rows = iota2((8, 128), 0)
     result = mom[...]
     for at, total in enumerate((k1, k2, k3, k4, k5)):
@@ -397,56 +467,99 @@
         spread[peer] = result
 
 
-def force_kernel(n_y, pos, table, impact, disp, vel, contact, labels, stress, *refs):
-    xg, yg, zg = refs[:2], refs[2 : 2 + n_y], refs[2 + n_y]
-    disp_hbm, vel_hbm, token, disp_out, vel_out, sems = refs[3 + n_y :]
-    token[...] = jnp.zeros((8, 128), F32)
-    odd_x, odd_y, gz = pos[0] == 1, pos[1] == 1, pos[2]
-    count = stress.shape[1]
-    block = count // CHUNKS
-    tall = count // 8
-    rates = [table[2, r] for r in range(table.shape[1])]
+PARTS = ((0, 3, 4), (3, 1, 5), (4, 5, 2))
+
+
+class Force:
+    def __init__(self, n_y, pos, table, impact, disp, vel, contact, labels, yg, zg):
+        self.odd_x, self.odd_y, self.gz = pos[0] == 1, pos[1] == 1, pos[2]
+        self.impact, self.disp, self.vel = impact, disp, vel
+        self.contact, self.labels, self.yg, self.zg = contact, labels, yg, zg
+        self.rates = [table[2, r] for r in range(table.shape[1])]
+
+    def plane(self, x, lower, mine, upper, vel_out, disp_out, at):
+        count = self.contact.shape[0]
+        tall = count // 8
+        loaded = self.contact[x].astype(F32)
+        rate = by_label(self.labels[x], self.rates)
+        for c, (kx, ky, kz) in enumerate(PARTS):
+            spot = (count + c * tall + lax.div(x, 8), pl.ds(lax.rem(x, 8), 1), slice(None))
+            rows = low_high(self.odd_y, [y[spot] for y in self.yg])
+            column = self.zg[x][:, c : c + 1]
+            yu, yl = shift_y(mine(ky), rows)
+            zu, zl = shift_z(mine(kz), column, self.gz == 0)
+            force = 0.5 * (((upper(c, kx) - lower(c, kx)) + (yu - yl)) + (zu - zl))
+            speed = self.vel[c, x] + rate * (force + loaded * self.impact[c])
+            vel_out[c, at] = speed
+            disp_out[c, at] = self.disp[c, x] + TIME_STEP * speed
+
+
+def force_inner_kernel(n_y, pos, table, impact, disp, vel, contact, labels, *refs):
+    yg, zg, stress, ends = refs[:n_y], refs[n_y], refs[n_y + 1], refs[n_y + 2]
+    disp_hbm, vel_hbm, disp_out, vel_out, sems = refs[n_y + 3 :]
+    force = Force(n_y, pos, table, impact, disp, vel, contact, labels, yg, zg)
+    count = contact.shape[0]
+    steps, many = inner_steps(count)
 
     def stores(step):
-        part = pl.ds(step * block, block)
+        part = pl.ds(1 + step * many, many)
         return (
             pltpu.make_async_copy(disp_out.at[:, part], disp_hbm.at[:, part], sems.at[step, 0]),
             pltpu.make_async_copy(vel_out.at[:, part], vel_hbm.at[:, part], sems.at[step, 1]),
         )
 
-    def column(x, c):
-        lane = STRESS_LANE + c
-        return zg[x + 3, 0 : contact.shape[1]][:, lane : lane + 1]
-
-    def body(x, at):
-        loaded = contact[x].astype(F32)
-        rate = by_label(labels[x], rates)
-        for c, (kx, ky, kz) in enumerate(((0, 3, 4), (3, 1, 5), (4, 5, 2))):
-            faces = (
-                lambda: jnp.where(odd_x, xg[0][5 + c], xg[1][5 + c]),
-                lambda: jnp.where(odd_x, xg[1][5 + c], xg[0][5 + c]),
-            )
-            spot = (count + c * tall + lax.div(x, 8), pl.ds(lax.rem(x, 8), 1), slice(None))
-            rows = low_high(odd_y, [y[spot] for y in yg])
-            xu, xl = shift_x(stress, (kx,), x, at, block, faces)
-            yu, yl = shift_y(stress[ky, x], rows)
-            zu, zl = shift_z(stress[kz, x], column(x, c), gz == 0)
-            force = 0.5 * (((xu - xl) + (yu - yl)) + (zu - zl))
-            speed = vel[c, x] + rate * (force + loaded * impact[c])
-            vel_out[c, x] = speed
-            disp_out[c, x] = disp[c, x] + TIME_STEP * speed
-
     def several(step, carry):
-        for at in range(block):
-            body(step * block + at, at)
+        for at in range(many):
+            x = 1 + step * many + at
+
+            def lower(c, k):
+                if at == 0:
+                    return jnp.where(step == 0, ends[k, 0], stress[k, x - 1])
+                return stress[k, x - 1]
+
+            def upper(c, k):
+                if at == many - 1:
+                    return jnp.where(step == steps - 1, ends[k, 1], stress[k, x + 1])
+                return stress[k, x + 1]
+
+            force.plane(x, lower, lambda k: stress[k, x], upper, vel_out, disp_out, x)
         for copy in stores(step):
             copy.start()
         return carry
 
-    lax.fori_loop(0, CHUNKS, several, 0)
-    for step in range(CHUNKS):
+    lax.fori_loop(0, steps, several, 0)
+    for step in range(steps):
         for copy in stores(step):
             copy.wait()
+
+
+def force_ends_kernel(n_y, pos, table, impact, disp, vel, contact, labels, *refs):
+    yg, zg, stress, ends = refs[:n_y], refs[n_y], refs[n_y + 1], refs[n_y + 2]
+    xg = refs[n_y + 3 : n_y + 5]
+    disp_hbm, vel_hbm, token, disp_out, vel_out, sems = refs[n_y + 7 :]
+    token[...] = jnp.zeros((8, 128), F32)
+    force = Force(n_y, pos, table, impact, disp, vel, contact, labels, yg, zg)
+    count = contact.shape[0]
+    copies = []
+    for end, x in enumerate((0, count - 1)):
+
+        def outside(c, k):
+            first, second = xg[0][5 + c], xg[1][5 + c]
+            if end == 0:
+                return jnp.where(force.odd_x, first, second)
+            return jnp.where(force.odd_x, second, first)
+
+        def beside(c, k):
+            return stress[k, 1 if end == 0 else count - 2]
+
+        lower, upper = (outside, beside) if end == 0 else (beside, outside)
+        force.plane(x, lower, lambda k: ends[k, end], upper, vel_out, disp_out, end)
+        for which, (src, dst) in enumerate(((disp_out, disp_hbm), (vel_out, vel_hbm))):
+            copy = pltpu.make_async_copy(src.at[:, end], dst.at[:, x], sems.at[end, which])
+            copy.start()
+            copies.append(copy)
+    for copy in copies:
+        copy.wait()
 
 
 def cg_coefficients(k):
@@ -538,7 +651,7 @@
     raise ValueError(kind)
 
 
-def call(kernel, kinds, ins, out_kinds, outs, flops, scratch=()):
+def call(kernel, kinds, ins, out_kinds, outs, flops, scratch=(), aliases=()):
     moved = sum(4 * a.size for a in (*ins, *outs))
     return pl.pallas_call(
         kernel,
@@ -546,6 +659,7 @@
         in_specs=[spec_of(k, a) for k, a in zip(kinds, ins, strict=True)],
         out_specs=[spec_of(k, a) for k, a in zip(out_kinds, outs, strict=True)],
         scratch_shapes=scratch,
+        input_output_aliases=dict(aliases),
         compiler_params=pltpu.CompilerParams(vmem_limit_bytes=VMEM_BYTES),
         cost_estimate=pl.CostEstimate(flops=flops, bytes_accessed=moved, transcendentals=0),
     )(*ins)
@@ -570,11 +684,6 @@
     columns = arr(nx, ny, 128)
     z_pairs = [(0, 1)]
 
-    faces = [
-        jnp.concatenate([displacement[:, at], damage[None, at]]) for at in (0, nx - 1)
-    ]
-    odd = lax.axis_index("gx") % 2 == 1
-    got_x = swap_along("gx", [jnp.where(odd, *faces), jnp.where(odd, *faces[::-1])])
     sent = call(
         functools.partial(pack_kernel, n_y),
         "svv",
@@ -583,36 +692,89 @@
         [*[arr(4, nx, nz)] * n_y, columns],
         size,
     )
-    got = [*got_x, *swap_along("gy", sent[:n_y]), swap(sent[-1], "gz", z_pairs)]
-    n_sent = 3 + 3 * n_y
+    got_yz = [*swap_along("gy", sent[:n_y]), swap(sent[-1], "gz", z_pairs)]
+    sent_x = call(
+        pack_x_kernel,
+        "svva",
+        (pos, displacement, damage, sent[-1]),
+        "vv",
+        [arr(4, ny, nz)] * 2,
+        size,
+    )
+    got_x = swap_along("gx", sent_x)
+    rows = [arr(nx + 3 * (nx // 8), 8, nz)] * n_y
+    voxels = (pos, scaled, displacement, damage, history, notch, labels, *got_yz)
     hist, rd, v0, stress, mom, *sent = call(
-        functools.partial(local_kernel, n_y),
-        "ssvvvvv" + "v" * (3 + n_y),
-        (pos, scaled, displacement, damage, history, notch, labels, *got),
-        "hvvvv" + "v" * n_sent,
+        functools.partial(inner_kernel, n_y),
+        "ssvvvvv" + "v" * (1 + n_y),
+        voxels,
+        "hvvvv" + "v" * (1 + n_y),
+        [field, field, field, arr(6, nx, ny, nz), small, *rows, columns],
+        140 * size,
+        [pltpu.VMEM((nx, ny, nz), F32), pltpu.SemaphoreType.DMA((inner_steps(nx)[0],))],
+    )
+    more = (*got_x, hist, rd, v0, mom, *sent)
+    hist, rd, v0, ends, mom, *sent = call(
+        functools.partial(ends_kernel, n_y),
+        "ssvvvvv" + "v" * (1 + n_y) + "vvhvvv" + "v" * (1 + n_y),
+        (*voxels, *more),
+        "hvvvv" + "v" * (3 + n_y),
         [
             field,
             field,
             field,
-            arr(6, nx, ny, nz),
+            arr(6, 2, ny, nz),
             small,
             *[arr(8, ny, nz)] * 2,
-            *[arr(nx + 3 * (nx // 8), 8, nz)] * n_y,
-            *[arr(2, 8, nz)] * (2 * n_y),
+            *rows,
             columns,
         ],
-        150 * size,
-        [pltpu.VMEM((nx, ny, nz), F32), pltpu.SemaphoreType.DMA((CHUNKS,))],
-    )
-    xy = [
-        *swap_along("gx", sent[:2]),
-        *swap_along("gy", sent[2 : 2 + n_y]),
-        *swap_diagonal(sent[2 + n_y : 2 + 3 * n_y]),
-    ]
+        20 * size,
+        [pltpu.VMEM((2, ny, nz), F32), pltpu.SemaphoreType.DMA((2,))],
+        [(len(voxels) + 2, 0)],
+    )
+    stress_z = swap(sent[-1], "gz", z_pairs)
+    xs = swap_along("gx", sent[:2])
+    ys = swap_along("gy", sent[2 : 2 + n_y])
+    corners = call(
+        functools.partial(corner_kernel, n_y),
+        "sa" + "v" * n_y,
+        (pos, stress_z, *sent[2 : 2 + n_y]),
+        "v" * (2 * n_y),
+        [arr(2, 8, nz)] * (2 * n_y),
+        1024,
+    )
+    xy = [*xs, *ys, *swap_diagonal(corners)]
+    moving = (
+        pos,
+        scaled,
+        impact,
+        displacement,
+        velocity,
+        contact,
+        labels,
+        *ys,
+        stress_z,
+        stress,
+        ends,
+    )
+    new_disp, new_vel = call(
+        functools.partial(force_inner_kernel, n_y),
+        "sssvvvv" + "v" * (3 + n_y),
+        moving,
+        "hh",
+        [fields3, fields3],
+        55 * size,
+        [
+            pltpu.VMEM((3, nx, ny, nz), F32),
+            pltpu.VMEM((3, nx, ny, nz), F32),
+            pltpu.SemaphoreType.DMA((inner_steps(nx)[0], 2)),
+        ],
+    )
     (joined,) = call(
         functools.partial(join_kernel, n_y),
-        "svvv" + "v" * len(xy),
-        (pos, v0, rd, sent[-1], *xy),
+        "svv" + "v" * len(xy),
+        (pos, v0, rd, *xy),
         "v",
         [arr(nx + 6, ny + 8, 128)],
         4 * size,
@@ -627,28 +789,18 @@
         4 * size,
     )
     new_disp, new_vel, token = call(
-        functools.partial(force_kernel, n_y),
-        "sssvvvvv" + "v" * (3 + n_y),
-        (
-            pos,
-            scaled,
-            impact,
-            displacement,
-            velocity,
-            contact,
-            labels,
-            stress,
-            *xy[: 2 + n_y],
-            z_got,
-        ),
+        functools.partial(force_ends_kernel, n_y),
+        "sssvvvv" + "v" * (3 + n_y) + "vvhh",
+        (*moving, *xs, new_disp, new_vel),
         "hhv",
         [fields3, fields3, small],
-        60 * size,
+        8 * size,
         [
-            pltpu.VMEM((3, nx, ny, nz), F32),
-            pltpu.VMEM((3, nx, ny, nz), F32),
-            pltpu.SemaphoreType.DMA((CHUNKS, 2)),
+            pltpu.VMEM((3, 2, ny, nz), F32),
+            pltpu.VMEM((3, 2, ny, nz), F32),
+            pltpu.SemaphoreType.DMA((2, 2)),
         ],
+        [(len(moving) + 2, 0), (len(moving) + 3, 1)],
     )
     peers = lax.axis_size("gx") * lax.axis_size("gy") * lax.axis_size("gz")
     v1, v2, spread = call(

time: 56.2 us -> 53 us (0.943)
  waiting for transfers between devices: 4.96 us -> 1.5 us
  Pallas kernels: 16.9 us -> 19.1 us
  local copies, waits for them, and re-layouts: 4.35 us -> 2.51 us
  blocking collectives: 13.9 us -> 13 us
  starting transfers between devices: 14.8 us -> 15.6 us
    ppermute x10 -> x11, waiting for transfers between devices: 4.96 us -> 1.5 us  [swap(): return lax.ppermute(array, axis, pairs + [(b, a) for a, b in pairs])]
    pallas_call x7 -> x11, Pallas kernels: 16.9 us -> 19.1 us  [call(): pl.pallas_call(kernel, out_shape=outs, in_specs=[spec_of(k, a) for k, a i...]
    squeeze x1 -> x0, local copies, waits for them, and re-layouts: 1.01 us -> none  [per_device(): displacement[:, at]]
    all_to_all x1, blocking collectives: 13.9 us -> 13 us  [per_device(): mom = lax.all_to_all(spread, ('gx', 'gy', 'gz'), 0, 0, tiled=True)]
    slice x1 -> x0, local copies, waits for them, and re-layouts: 0.84 us -> none  [per_device(): damage[None, at]]
    ppermute x10 -> x11, starting transfers between devices: 14.8 us -> 15.6 us  [swap(): return lax.ppermute(array, axis, pairs + [(b, a) for a, b in pairs])]
  transfers between devices with their start and end apart: 10 -> 11, of which waited for: 3 -> 1; matrix products, arithmetic and copies ran while one was open for 0% -> 0% of each run, Pallas kernels for 3% -> 20%
where the time goes in v6:
time: 53 us; the launch traced here: 52.7 us
  Pallas kernels  19.1 us (36%)
  starting transfers between devices  15.6 us (29%)
  blocking collectives  13 us (25%)
  local copies, waits for them, and re-layouts  2.51 us (5%)
  waiting for transfers between devices  1.5 us (3%)
  between operations  0.96 us (2%)
    pallas_call x11, Pallas kernels, call(): pl.pallas_call(kernel, out_shape=outs, in_specs=[spec_of(k, a) for k, a i...  19.1 us
    ppermute x11, starting transfers between devices, swap(): return lax.ppermute(array, axis, pairs + [(b, a) for a, b in pairs])  15.6 us
    all_to_all x1, blocking collectives, per_device(): mom = lax.all_to_all(spread, ('gx', 'gy', 'gz'), 0, 0, tiled=True)  13 us
    unnamed x22, local copies, waits for them, and re-layouts  2.51 us
    ppermute x11, waiting for transfers between devices, swap(): return lax.ppermute(array, axis, pairs + [(b, a) for a, b in pairs])  1.5 us
  transfers between devices with their start and end apart: 11, of which 1 were waited for; matrix products, arithmetic and copies ran while one was open for 0% of the time, Pallas kernels for 20%

profile of v6, /device:TPU:0, one launch (start us, length us, event | category | flops | bytes accessed | tf_op | source)
XLA Modules:
  0.0 52.7 jit_solution(3236279483371923014)
XLA Ops:
  0.6 0.1 pad_add_fusion.pos
  0.7 0.0 copy-start
  0.7 1.4 %copy-done = f32[3,16,32,256]{3,2,1,0:T(8,128)S(1)} copy-done((f32[3,16,32,256]{3,2,1,0:T(8,128)S(1)}, f32[3,16,32,256]{3,2,1,0:T(8,128)}, u32[]{:S(2)}) %copy-start) | copy-done | bytes 1572888
  2.1 0.0 copy-start.2
  2.1 1.0 %copy-done.2 = f32[16,32,256]{2,1,0:T(8,128)S(1)} copy-done((f32[16,32,256]{2,1,0:T(8,128)S(1)}, f32[16,32,256]{2,1,0:T(8,128)}, u32[]{:S(2)}) %copy-start.2) | copy-done | bytes 524312
  3.2 1.0 %shard_map.120 = (f32[4,16,256]{2,1,0:T(8,128)S(1)}, f32[16,32,128]{2,1,0:T(8,128)S(1)}) custom-call(s32[3]{0:T(128)S(1)} %pad_add_fusion.pos, f32[3,16,32,256]{3,2,1,0:T(8,128)S(1)} %copy-done, f32[16,32,256]{2,1,0:T(8,128)S(1)} %copy-done.2), custom_call_target="tpu_custom_call" | custom-call | flops 131072 | bytes 2424844 | tf_op jit(solution)/shard_map/pallas_call | solution.py:656
  4.1 0.0 copy-start.10
  4.1 0.0 copy-start.4
  4.2 0.0 copy-start.7
  4.2 0.0 copy-start.8
  4.2 3.0 %collective-permute-start = (f32[4,16,256]{2,1,0:T(8,128)S(1)}, f32[4,16,256]{2,1,0:T(8,128)S(1)}, u32[]{:S(2)}, u32[]{:S(2)}) collective-permute-start(f32[4,16,256]{2,1,0:T(8,128)S(1)} %get-tuple-element.36), channel_id=1, source_target_pairs={{0,2},{2,0},{1,3},{3,1},{4,6},{6,4},{5,7},{7,5},{8,10},{10,8},{9,1... | collective-permute-start | bytes 196616 | tf_op jit(solution)/shard_map/ppermute | solution.py:621
  7.2 0.0 collective-permute-start.1
  7.2 0.6 %shard_map.121 = (f32[4,32,256]{2,1,0:T(8,128)S(1)}, f32[4,32,256]{2,1,0:T(8,128)S(1)}) custom-call(s32[3]{0:T(128)S(1)} %pad_add_fusion.pos, f32[3,16,32,256]{3,2,1,0:T(8,128)S(1)} %copy-done, f32[16,32,256]{2,1,0:T(8,128)S(1)} %copy-done.2, f32[16,32,128]{2,1,0:T(8,128)S(1)} %get-tuple-element.37.after), custom_call_target="tpu_custom_call" | custom-call | flops 131072 | bytes 2621452 | tf_op jit(solution)/shard_map/pallas_call | solution.py:656
  7.8 1.6 %collective-permute-start.2 = (f32[4,32,256]{2,1,0:T(8,128)S(1)}, f32[4,32,256]{2,1,0:T(8,128)S(1)}, u32[]{:S(2)}, u32[]{:S(2)}) collective-permute-start(f32[4,32,256]{2,1,0:T(8,128)S(1)} %get-tuple-element.38), channel_id=1, source_target_pairs={{0,4},{8,12},{4,0},{12,8},{1,5},{9,13},{5,1},{13,9},{2,6},{10,14},... | collective-permute-start | bytes 393224 | tf_op jit(solution)/shard_map/ppermute | solution.py:621
  9.4 0.7 %collective-permute-start.3 = (f32[4,32,256]{2,1,0:T(8,128)S(1)}, f32[4,32,256]{2,1,0:T(8,128)S(1)}, u32[]{:S(2)}, u32[]{:S(2)}) collective-permute-start(f32[4,32,256]{2,1,0:T(8,128)S(1)} %get-tuple-element.39), channel_id=1, source_target_pairs={{4,8},{8,4},{5,9},{9,5},{6,10},{10,6},{7,11},{11,7},{20,24},{24,20... | collective-permute-start | bytes 393224 | tf_op jit(solution)/shard_map/ppermute | solution.py:621
  10.1 0.0 copy-done.10
  10.1 0.0 collective-permute-done.refs_0_
  10.1 0.0 collective-permute-done.1.refs_1_
  10.1 0.0 copy-done.4
  10.1 0.0 copy-done.7
  10.2 0.0 copy-done.8
  10.2 4.1 %shard_map.122 = (f32[16,32,256]{2,1,0:T(8,128)}, f32[16,32,256]{2,1,0:T(8,128)S(1)}, f32[16,32,256]{2,1,0:T(8,128)S(1)}, f32[6,16,32,256]{3,2,1,0:T(8,128)S(1)}...) custom-call(s32[3]{0:T(128)S(1)} %pad_add_fusion.pos, ...), custom_call_target="tpu_custom_call" | custom-call | flops 18350080 | bytes 9162828 | tf_op jit(solution)/shard_map/pallas_call | solution.py:656
  14.3 0.0 collective-permute-done.2.refs_2_
  14.3 0.0 collective-permute-done.3.refs_3_
  14.3 0.0 copy-start.5
  14.3 1.6 %shard_map.123 = (f32[16,32,256]{2,1,0:T(8,128)}, f32[16,32,256]{2,1,0:T(8,128)S(1)}, f32[16,32,256]{2,1,0:T(8,128)S(1)}, f32[6,2,32,256]{3,2,1,0:T(8,128)S(1)},...) custom-call(s32[3]{0:T(128)S(1)} %pad_add_fusion.pos, ...), custom_call_target="tpu_custom_call", output_to_operand_aliasing={{0}: (11, {})} | custom-call | flops 2621440 | bytes 9216076 | tf_op jit(solution)/shard_map/pallas_call | solution.py:656
  15.9 0.0 copy-start.1
  16.0 0.0 copy-start.6
  16.0 0.0 copy-start.9
  16.0 0.3 collective-permute-start.5
  16.3 4.2 %collective-permute-start.6 = (f32[8,32,256]{2,1,0:T(8,128)S(1)}, f32[8,32,256]{2,1,0:T(8,128)S(1)}, u32[]{:S(2)}, u32[]{:S(2)}) collective-permute-start(f32[8,32,256]{2,1,0:T(8,128)S(1)} %get-tuple-element.50), channel_id=1, source_target_pairs={{0,4},{8,12},{4,0},{12,8},{1,5},{9,13},{5,1},{13,9},{2,6},{10,14},... | collective-permute-start | bytes 786440 | tf_op jit(solution)/shard_map/ppermute | solution.py:621
  20.5 0.7 %collective-permute-start.7 = (f32[8,32,256]{2,1,0:T(8,128)S(1)}, f32[8,32,256]{2,1,0:T(8,128)S(1)}, u32[]{:S(2)}, u32[]{:S(2)}) collective-permute-start(f32[8,32,256]{2,1,0:T(8,128)S(1)} %get-tuple-element.51), channel_id=1, source_target_pairs={{4,8},{8,4},{5,9},{9,5},{6,10},{10,6},{7,11},{11,7},{20,24},{24,20... | collective-permute-start | bytes 786440 | tf_op jit(solution)/shard_map/ppermute | solution.py:621
  21.2 0.6 %collective-permute-start.4 = (f32[22,8,256]{2,1,0:T(8,128)S(1)}, f32[22,8,256]{2,1,0:T(8,128)S(1)}, u32[]{:S(2)}, u32[]{:S(2)}) collective-permute-start(f32[22,8,256]{2,1,0:T(8,128)S(1)} %get-tuple-element.46.refs_0_), channel_id=1, source_target_pairs={{0,2},{2,0},{1,3},{3,1},{4,6},{6,4},{5,7},{7,5},{8,10},{10,8},{9,1... | collective-permute-start | bytes 540680 | tf_op jit(solution)/shard_map/ppermute | solution.py:621
  21.8 0.0 collective-permute-done.5.refs_1_.after
  21.8 0.5 %shard_map.126 = (f32[2,8,256]{2,1,0:T(8,128)S(1)}, f32[2,8,256]{2,1,0:T(8,128)S(1)}) custom-call(s32[3]{0:T(128)S(1)} %pad_add_fusion.pos, f32[16,32,128]{2,1,0:T(8,128)S(1)} %collective-permute-done.5.refs_1_.after, f32[22,8,256]{2,1,0:T(8,128)S(1)} %get-tuple-element.46.refs_0_), custom_call_target="tpu_custom_call" | custom-call | flops 1024 | bytes 475148 | tf_op jit(solution)/shard_map/pallas_call | solution.py:656
  22.4 3.7 %collective-permute-start.8 = (f32[2,8,256]{2,1,0:T(8,128)S(1)}, f32[2,8,256]{2,1,0:T(8,128)S(1)}, u32[]{:S(2)}, u32[]{:S(2)}) collective-permute-start(f32[2,8,256]{2,1,0:T(8,128)S(1)} %get-tuple-element.59), channel_id=1, source_target_pairs={{0,6},{2,4},{8,14},{10,12},{6,0},{4,2},{14,8},{12,10},{1,7},{3,5},... | collective-permute-start | bytes 49160 | tf_op jit(solution)/shard_map/ppermute | solution.py:621
  26.1 0.7 %collective-permute-start.9 = (f32[2,8,256]{2,1,0:T(8,128)S(1)}, f32[2,8,256]{2,1,0:T(8,128)S(1)}, u32[]{:S(2)}, u32[]{:S(2)}) collective-permute-start(f32[2,8,256]{2,1,0:T(8,128)S(1)} %get-tuple-element.60), channel_id=1, source_target_pairs={{4,10},{6,8},{10,4},{8,6},{5,11},{7,9},{11,5},{9,7},{20,26},{22,24... | collective-permute-start | bytes 49160 | tf_op jit(solution)/shard_map/ppermute | solution.py:621
  26.8 1.5 %collective-permute-done.4.refs_0_.refs_2_ = f32[22,8,256]{2,1,0:T(8,128)S(1)} collective-permute-done((f32[22,8,256]{2,1,0:T(8,128)S(1)}, f32[22,8,256]{2,1,0:T(8,128)S(1)}, u32[]{:S(2)}, u32[]{:S(2)}) %collective-permute-start.4) | collective-permute-done | bytes 180256 | tf_op jit(solution)/shard_map/ppermute | solution.py:621
  28.2 0.0 collective-permute-done.6.refs_4_.refs_0_
  28.2 0.0 collective-permute-done.7.refs_5_.refs_1_
  28.2 0.0 collective-permute-done.8.refs_3_
  28.2 0.0 collective-permute-done.9.refs_4_
  28.3 0.9 %shard_map.128 = f32[22,40,128]{2,1,0:T(8,128)S(1)} custom-call(s32[3]{0:T(128)S(1)} %pad_add_fusion.pos, f32[16,32,256]{2,1,0:T(8,128)S(1)} %get-tuple-element.57.v.v0, f32[16,32,256]{2,1,0:T(8,128)S(1)} %get-tuple-element.58.rd, f32[8,32,256]{2,1,0:T(8,128)S(1)} %collective-permute-done.6.refs_4_.refs_0_, ...), custom_call_target="tpu_custom_call" | custom-call | flops 524288 | bytes 2236428 | tf_op jit(solution)/shard_map/pallas_call | solution.py:656
  29.1 0.1 collective-permute-start.10
  29.2 0.0 copy-done.5
  29.2 0.0 copy-done.1
  29.2 0.0 copy-done.6
  29.2 0.0 copy-done.9
  29.3 3.2 %shard_map.124 = (f32[3,16,32,256]{3,2,1,0:T(8,128)}, f32[3,16,32,256]{3,2,1,0:T(8,128)}) custom-call(s32[3]{0:T(128)S(1)} %pad_add_fusion.pos, f32[4,4]{1,0:T(4,128)S(1)} %pad_maximum_fusion.table, f32[3]{0:T(128)S(1)} %copy-done.9, f32[3,16,32,256]{3,2,1,0:T(8,128)S(1)} %copy-done.1, f32[3,16,32,256]{3,2,1,0:T(8,128)S(1)} %copy-done.5, ...), custom_call_target="tpu_custom_call" | custom-call | flops 7208960 | bytes 11321432 | tf_op jit(solution)/shard_map/pallas_call | solution.py:656
  32.5 1.6 %shard_map.125 = (f32[3,16,32,256]{3,2,1,0:T(8,128)}, f32[3,16,32,256]{3,2,1,0:T(8,128)}, f32[8,128]{1,0:T(8,128)S(1)}) custom-call(s32[3]{0:T(128)S(1)} %pad_add_fusion.pos, f32[4,4]{1,0:T(4,128)S(1)} %pad_maximum_fusion.table, f32[3]{0:T(128)S(1)} %copy-done.9, f32[3,16,32,256]{3,2,1,0:T(8,128)S(1)} %copy-done.1, ...), custom_call_target="tpu_custom_call", output_to_operand_aliasing={{0}: (13, {}), {1}: (14, {})} | custom-call | flops 1048576 | bytes 14995544 | tf_op jit(solution)/shard_map/pallas_call | solution.py:656
  34.1 0.7 %shard_map.127 = (f32[22,40,256]{2,1,0:T(8,128)S(1)}, f32[22,40,256]{2,1,0:T(8,128)S(1)}) custom-call(s32[3]{0:T(128)S(1)} %pad_add_fusion.pos, f32[16,32,256]{2,1,0:T(8,128)S(1)} %get-tuple-element.57.v.v0, f32[16,32,256]{2,1,0:T(8,128)S(1)} %get-tuple-element.58.rd, f32[8,32,256]{2,1,0:T(8,128)S(1)} %collective-permute-done.6.refs_4_.refs_0_, ...), custom_call_target="tpu_custom_call" | custom-call | flops 524288 | bytes 3588108 | tf_op jit(solution)/shard_map/pallas_call | solution.py:656
  34.8 0.0 copy-start.3
  34.8 0.0 collective-permute-done.10.z_got
  34.8 3.2 %shard_map.129 = (f32[16,32,256]{2,1,0:T(8,128)S(1)}, f32[16,32,256]{2,1,0:T(8,128)S(1)}, f32[16,8,128]{2,1,0:T(8,128)S(1)}) custom-call(s32[3]{0:T(128)S(1)} %pad_add_fusion.pos, f32[22,40,256]{2,1,0:T(8,128)S(1)} %get-tuple-element.61.main_v, f32[22,40,256]{2,1,0:T(8,128)S(1)} %get-tuple-element.62.main_rd, f32[8,128]{1,0:T(8,128)S(1)} %get-tuple-element.63.mom, ...), custom_call_target="tpu_custom_call" | custom-call | flops 7864320 | bytes 3375116 | tf_op jit(solution)/shard_map/pallas_call | solution.py:656
  38.0 13.0 %all_to_all.5.mom = f32[16,8,128]{2,1,0:T(8,128)S(1)} all-to-all(f32[16,8,128]{2,1,0:T(8,128)S(1)} %get-tuple-element.65), channel_id=1, replica_groups=mesh['case'=2,'gx'=4,'gy'=2,'gz'=2] {'gx','gy','gz'}, dimensions={0} | all-to-all | bytes 131072 | tf_op jit(solution)/shard_map/all_to_all | solution.py:820
  51.0 0.0 copy-done.3
  51.0 1.7 %shard_map.130 = f32[16,32,256]{2,1,0:T(8,128)} custom-call(f32[16,8,128]{2,1,0:T(8,128)S(1)} %all_to_all.5.mom, f32[16,32,256]{2,1,0:T(8,128)S(1)} %get-tuple-element.57.v.v0, f32[16,32,256]{2,1,0:T(8,128)S(1)} %get-tuple-element.66.v1, f32[16,32,256]{2,1,0:T(8,128)S(1)} %get-tuple-element.67.v2, f32[16,32,256]{2,1,0:T(8,128)S(1)} %copy-done.3), custom_call_target="tpu_custom_call" | custom-call | flops 1048576 | bytes 2686976 | tf_op jit(solution)/shard_map/pallas_call | solution.py:656
  (2 shorter events, 0.0 us)
Async XLA Ops:
  0.7 1.4 %copy-start = (f32[3,16,32,256]{3,2,1,0:T(8,128)S(1)}, f32[3,16,32,256]{3,2,1,0:T(8,128)}, u32[]{:S(2)}) copy-start(f32[3,16,32,256]{3,2,1,0:T(8,128)} %disp.11) | copy-start | bytes 4718596
  2.1 1.0 %copy-start.2 = (f32[16,32,256]{2,1,0:T(8,128)S(1)}, f32[16,32,256]{2,1,0:T(8,128)}, u32[]{:S(2)}) copy-start(f32[16,32,256]{2,1,0:T(8,128)} %damage_hbm.1) | copy-start | bytes 1572868
  4.1 5.9 %copy-start.10 = (f32[4,4]{1,0:T(4,128)S(1)}, f32[4,4]{1,0:T(4,128)}, u32[]{:S(2)}) copy-start(f32[4,4]{1,0:T(4,128)} %param.16) | copy-start | bytes 196
  4.1 6.0 %copy-start.4 = (s32[16,32,256]{2,1,0:T(8,128)S(1)}, s32[16,32,256]{2,1,0:T(8,128)}, u32[]{:S(2)}) copy-start(s32[16,32,256]{2,1,0:T(8,128)} %labels.7) | copy-start | bytes 1572868
  4.2 6.0 %copy-start.7 = (f32[16,32,256]{2,1,0:T(8,128)S(1)}, f32[16,32,256]{2,1,0:T(8,128)}, u32[]{:S(2)}) copy-start(f32[16,32,256]{2,1,0:T(8,128)} %history.3) | copy-start | bytes 1572868
  4.2 6.0 %copy-start.8 = (s32[16,32,256]{2,1,0:T(8,128)S(1)}, s32[16,32,256]{2,1,0:T(8,128)}, u32[]{:S(2)}) copy-start(s32[16,32,256]{2,1,0:T(8,128)} %notch.3) | copy-start | bytes 1572868
  4.2 5.9 %collective-permute-start = (f32[4,16,256]{2,1,0:T(8,128)S(1)}, f32[4,16,256]{2,1,0:T(8,128)S(1)}, u32[]{:S(2)}, u32[]{:S(2)}) collective-permute-start(f32[4,16,256]{2,1,0:T(8,128)S(1)} %get-tuple-element.36), channel_id=1, source_target_pairs={{0,2},{2,0},{1,3},{3,1},{4,6},{6,4},{5,7},{7,5},{8,10},{10,8},{9,1... | collective-permute-start | bytes 196616 | tf_op jit(solution)/shard_map/ppermute | solution.py:621
  7.2 2.9 %collective-permute-start.1 = (f32[16,32,128]{2,1,0:T(8,128)S(1)}, f32[16,32,128]{2,1,0:T(8,128)S(1)}, u32[]{:S(2)}, u32[]{:S(2)}) collective-permute-start(f32[16,32,128]{2,1,0:T(8,128)S(1)} %get-tuple-element.37.after), channel_id=1, source_target_pairs={{0,1},{1,0},{2,3},{3,2},{4,5},{5,4},{6,7},{7,6},{8,9},{9,8},{10,11... | collective-permute-start | bytes 786440 | tf_op jit(solution)/shard_map/ppermute | solution.py:621
  7.8 6.5 %collective-permute-start.2 = (f32[4,32,256]{2,1,0:T(8,128)S(1)}, f32[4,32,256]{2,1,0:T(8,128)S(1)}, u32[]{:S(2)}, u32[]{:S(2)}) collective-permute-start(f32[4,32,256]{2,1,0:T(8,128)S(1)} %get-tuple-element.38), channel_id=1, source_target_pairs={{0,4},{8,12},{4,0},{12,8},{1,5},{9,13},{5,1},{13,9},{2,6},{10,14},... | collective-permute-start | bytes 393224 | tf_op jit(solution)/shard_map/ppermute | solution.py:621
  9.4 4.9 %collective-permute-start.3 = (f32[4,32,256]{2,1,0:T(8,128)S(1)}, f32[4,32,256]{2,1,0:T(8,128)S(1)}, u32[]{:S(2)}, u32[]{:S(2)}) collective-permute-start(f32[4,32,256]{2,1,0:T(8,128)S(1)} %get-tuple-element.39), channel_id=1, source_target_pairs={{4,8},{8,4},{5,9},{9,5},{6,10},{10,6},{7,11},{11,7},{20,24},{24,20... | collective-permute-start | bytes 393224 | tf_op jit(solution)/shard_map/ppermute | solution.py:621
  14.3 14.9 %copy-start.5 = (f32[3,16,32,256]{3,2,1,0:T(8,128)S(1)}, f32[3,16,32,256]{3,2,1,0:T(8,128)}, u32[]{:S(2)}) copy-start(f32[3,16,32,256]{3,2,1,0:T(8,128)} %vel.3) | copy-start | bytes 4718596
  15.9 13.3 %copy-start.1 = (f32[3,16,32,256]{3,2,1,0:T(8,128)S(1)}, f32[3,16,32,256]{3,2,1,0:T(8,128)}, u32[]{:S(2)}) copy-start(f32[3,16,32,256]{3,2,1,0:T(8,128)} %disp.11) | copy-start | bytes 4718596
  16.0 13.3 %copy-start.6 = (s32[16,32,256]{2,1,0:T(8,128)S(1)}, s32[16,32,256]{2,1,0:T(8,128)}, u32[]{:S(2)}) copy-start(s32[16,32,256]{2,1,0:T(8,128)} %contact.3) | copy-start | bytes 1572868
  16.0 13.3 %copy-start.9 = (f32[3]{0:T(128)S(1)}, f32[3]{0:T(128)}, u32[]{:S(2)}) copy-start(f32[3]{0:T(128)} %impact.3) | copy-start | bytes 40
  16.0 5.8 %collective-permute-start.5 = (f32[16,32,128]{2,1,0:T(8,128)S(1)}, f32[16,32,128]{2,1,0:T(8,128)S(1)}, u32[]{:S(2)}, u32[]{:S(2)}) collective-permute-start(f32[16,32,128]{2,1,0:T(8,128)S(1)} %get-tuple-element.47), channel_id=1, source_target_pairs={{0,1},{1,0},{2,3},{3,2},{4,5},{5,4},{6,7},{7,6},{8,9},{9,8},{10,11... | collective-permute-start | bytes 786440 | tf_op jit(solution)/shard_map/ppermute | solution.py:621
  16.3 12.0 %collective-permute-start.6 = (f32[8,32,256]{2,1,0:T(8,128)S(1)}, f32[8,32,256]{2,1,0:T(8,128)S(1)}, u32[]{:S(2)}, u32[]{:S(2)}) collective-permute-start(f32[8,32,256]{2,1,0:T(8,128)S(1)} %get-tuple-element.50), channel_id=1, source_target_pairs={{0,4},{8,12},{4,0},{12,8},{1,5},{9,13},{5,1},{13,9},{2,6},{10,14},... | collective-permute-start | bytes 786440 | tf_op jit(solution)/shard_map/ppermute | solution.py:621
  20.5 7.7 %collective-permute-start.7 = (f32[8,32,256]{2,1,0:T(8,128)S(1)}, f32[8,32,256]{2,1,0:T(8,128)S(1)}, u32[]{:S(2)}, u32[]{:S(2)}) collective-permute-start(f32[8,32,256]{2,1,0:T(8,128)S(1)} %get-tuple-element.51), channel_id=1, source_target_pairs={{4,8},{8,4},{5,9},{9,5},{6,10},{10,6},{7,11},{11,7},{20,24},{24,20... | collective-permute-start | bytes 786440 | tf_op jit(solution)/shard_map/ppermute | solution.py:621
  21.2 7.0 %collective-permute-start.4 = (f32[22,8,256]{2,1,0:T(8,128)S(1)}, f32[22,8,256]{2,1,0:T(8,128)S(1)}, u32[]{:S(2)}, u32[]{:S(2)}) collective-permute-start(f32[22,8,256]{2,1,0:T(8,128)S(1)} %get-tuple-element.46.refs_0_), channel_id=1, source_target_pairs={{0,2},{2,0},{1,3},{3,1},{4,6},{6,4},{5,7},{7,5},{8,10},{10,8},{9,1... | collective-permute-start | bytes 540680 | tf_op jit(solution)/shard_map/ppermute | solution.py:621
  22.4 5.9 %collective-permute-start.8 = (f32[2,8,256]{2,1,0:T(8,128)S(1)}, f32[2,8,256]{2,1,0:T(8,128)S(1)}, u32[]{:S(2)}, u32[]{:S(2)}) collective-permute-start(f32[2,8,256]{2,1,0:T(8,128)S(1)} %get-tuple-element.59), channel_id=1, source_target_pairs={{0,6},{2,4},{8,14},{10,12},{6,0},{4,2},{14,8},{12,10},{1,7},{3,5},... | collective-permute-start | bytes 49160 | tf_op jit(solution)/shard_map/ppermute | solution.py:621
  26.1 2.2 %collective-permute-start.9 = (f32[2,8,256]{2,1,0:T(8,128)S(1)}, f32[2,8,256]{2,1,0:T(8,128)S(1)}, u32[]{:S(2)}, u32[]{:S(2)}) collective-permute-start(f32[2,8,256]{2,1,0:T(8,128)S(1)} %get-tuple-element.60), channel_id=1, source_target_pairs={{4,10},{6,8},{10,4},{8,6},{5,11},{7,9},{11,5},{9,7},{20,26},{22,24... | collective-permute-start | bytes 49160 | tf_op jit(solution)/shard_map/ppermute | solution.py:621
  29.1 5.7 %collective-permute-start.10 = (f32[22,40,128]{2,1,0:T(8,128)S(1)}, f32[22,40,128]{2,1,0:T(8,128)S(1)}, u32[]{:S(2)}, u32[]{:S(2)}) collective-permute-start(f32[22,40,128]{2,1,0:T(8,128)S(1)} %shard_map.128), channel_id=1, source_target_pairs={{0,1},{1,0},{2,3},{3,2},{4,5},{5,4},{6,7},{7,6},{8,9},{9,8},{10,11... | collective-permute-start | bytes 1351688 | tf_op jit(solution)/shard_map/ppermute | solution.py:621
  34.8 16.2 %copy-start.3 = (f32[16,32,256]{2,1,0:T(8,128)S(1)}, f32[16,32,256]{2,1,0:T(8,128)}, u32[]{:S(2)}) copy-start(f32[16,32,256]{2,1,0:T(8,128)} %damage_hbm.1) | copy-start | bytes 1572868

commit v7 on v6

--- a/solution.py
+++ b/solution.py
@@ -130,48 +130,55 @@
         self.shears = [table[1, r] for r in regions]
         self.bases = [table[3, r] for r in regions]
 
-    def around(self, field, plane, x, lower, upper):
-        rows = low_high(self.odd_y, [y[field, pl.ds(x, 1), :] for y in self.yg])
-        column = self.zg[x][:, field : field + 1]
-        return (
-            (upper, lower),
-            shift_y(plane, rows),
-            shift_z(plane, column, self.gz == 0),
-        )
-
-    def plane(self, x, lower, upper):
-        g = []
-        for c in range(3):
-            pairs = self.around(c, self.disp[c, x], x, lower(c), upper(c))
-            g.append([high - low for high, low in pairs])
+    def plane(self, x, lower, upper, put):
         lab = self.labels[x]
-        lame = by_label(lab, self.lames)
         shear = by_label(lab, self.shears)
-        base = by_label(lab, self.bases)
         dmg = self.damage[x]
         degrade = 4.0 * ((1.0 - dmg) * (1.0 - dmg) + STIFF_FLOOR)
-        trace = g[0][0] + g[1][1] + g[2][2]
-        shears3 = [g[0][1] + g[1][0], g[0][2] + g[2][0], g[1][2] + g[2][1]]
+        half = degrade * shear
+        fields = [self.disp[c, x] for c in range(3)]
+
+        def d(c, j):
+            if j == 0:
+                return upper(c) - lower(c)
+            if j == 1:
+                rows = low_high(self.odd_y, [y[c, pl.ds(x, 1), :] for y in self.yg])
+                high, low = shift_y(fields[c], rows)
+            else:
+                column = self.zg[x][:, c : c + 1]
+                high, low = shift_z(fields[c], column, self.gz == 0)
+            return high - low
+
+        squares = None
+        for k, (i, j) in ((3, (0, 1)), (4, (0, 2)), (5, (1, 2))):
+            e = d(i, j) + d(j, i)
+            put(k, half * e)
+            squares = e * e if squares is None else squares + e * e
+        straight = [d(c, c) for c in range(3)]
+        trace = straight[0] + straight[1] + straight[2]
+        lame = by_label(lab, self.lames)
+        level = (degrade * lame) * trace
+        whole = half + half
+        for k in range(3):
+            put(k, level + whole * straight[k])
+        twice = (
+            straight[0] * straight[0] + straight[1] * straight[1] + straight[2] * straight[2]
+        )
+        squares = squares + (twice + twice)
         positive = jnp.maximum(trace, 0.0)
-        squares = g[0][0] * g[0][0] + g[1][1] * g[1][1] + g[2][2] * g[2][2]
-        squares = (squares + squares) + (
-            shears3[0] * shears3[0] + shears3[1] * shears3[1] + shears3[2] * shears3[2]
-        )
         energy = lame * positive * positive + shear * squares
-        half = degrade * shear
-        whole = half + half
-        level = (degrade * lame) * trace
-        stress = [level + whole * g[k][k] for k in range(3)] + [half * e for e in shears3]
         hist = jnp.maximum(
             jnp.maximum(self.history[x], energy), NOTCH_LOAD * self.notch[x].astype(F32)
         )
-        diagonal = base + 2.0 * hist
+        diagonal = by_label(lab, self.bases) + 2.0 * hist
         rd = 1.0 / diagonal
-        (xu, xl), (yu, yl), (zu, zl) = self.around(3, dmg, x, lower(3), upper(3))
-        near = ((xu + xl) + (yu + yl)) + (zu + zl)
+        rows = low_high(self.odd_y, [y[3, pl.ds(x, 1), :] for y in self.yg])
+        yu, yl = shift_y(dmg, rows)
+        zu, zl = shift_z(dmg, self.zg[x][:, 3:4], self.gz == 0)
+        near = ((upper(3) + lower(3)) + (yu + yl)) + (zu + zl)
         residual = 2.0 * hist - (diagonal * dmg - KAPPA_COEF * near)
         v = residual * rd
-        return stress, hist, rd, v, folded(residual * v)
+        return hist, rd, v, folded(residual * v)
 
     def send_y(self, ys, x, v, rd, stress):
         count = self.damage.shape[0]
@@ -213,9 +220,12 @@
             def upper(c):
                 return damage[x + 1] if c == 3 else disp[c, x + 1]
 
-            stress, hist_x, rd, v, part = local.plane(x, lower, upper)
-            for k in range(6):
-                stress_out[k, x] = stress[k]
+            stress = {}
+
+            def put(k, plane):
+                stress[k] = stress_out[k, x] = plane
+
+            hist_x, rd, v, part = local.plane(x, lower, upper, put)
             hist[x] = hist_x
             rd_out[x] = rd
             v_out[x] = v
@@ -260,12 +270,15 @@
             return damage[at] if c == 3 else disp[c, at]
 
         sides = (outside, beside) if end == 0 else (beside, outside)
-        stress, hist_x, rd, v, part = local.plane(x, *sides)
+        stress = {}
+
+        def put(k, plane):
+            stress[k] = stress_out[k, end] = plane
+
+        hist_x, rd, v, part = local.plane(x, *sides, put)
         hist[end] = hist_x
         copies.append(pltpu.make_async_copy(hist.at[end], hist_hbm.at[x], sems.at[end]))
         copies[-1].start()
-        for k in range(6):
-            stress_out[k, end] = stress[k]
         rd_out[x] = rd
         v_out[x] = v
         total = total + part
@@ -348,7 +361,7 @@
             yield count - 1 + depth, self.halo(False, depth)
 
 
-def join_kernel(n_y, pos, v, rd, *refs):
+def join_kernel(n_y, pos, v, rd, token, *refs):
     big = Enlarged(n_y, pos, v, rd, refs[:-1])
     out = refs[-1]
     first_z = pos[2] == 0
@@ -376,29 +389,7 @@
     unrolled(count, 8, body, 0)
 
 
-def fill_kernel(n_y, pos, v, rd, *refs):
-    big = Enlarged(n_y, pos, v, rd, refs[:-2])
-    big_v, big_rd = refs[-2:]
-    count, ny, _ = v.shape
-
-    def put(p, parts):
-        v_own, v_rows, rd_own, rd_rows = parts
-        big_v[p + 3, 0:ny] = v_own
-        big_v[p + 3, ny : ny + 8] = v_rows
-        big_rd[p + 3, 0:ny] = rd_own
-        big_rd[p + 3, ny : ny + 8] = rd_rows
-
-    for p, parts in big.outer(count):
-        put(p, parts)
-
-    def body(x, carry):
-        put(x, big.own(x))
-        return carry
-
-    unrolled(count, 4, body, 0)
-
-
-def krylov_kernel(pos, main_v, main_rd, mom, token, z_got, *refs):
+def krylov_kernel(pos, main_v, main_rd, mom, z_got, *refs):
     v1_out, v2_out, spread, z_v, z_rd, big_v1, big_v2 = refs
     count, ny, nz = v1_out.shape
 
@@ -496,7 +487,8 @@
 
 def force_inner_kernel(n_y, pos, table, impact, disp, vel, contact, labels, *refs):
     yg, zg, stress, ends = refs[:n_y], refs[n_y], refs[n_y + 1], refs[n_y + 2]
-    disp_hbm, vel_hbm, disp_out, vel_out, sems = refs[n_y + 3 :]
+    disp_hbm, vel_hbm, token, disp_out, vel_out, sems = refs[n_y + 3 :]
+    token[...] = jnp.zeros((8, 128), F32)
     force = Force(n_y, pos, table, impact, disp, vel, contact, labels, yg, zg)
     count = contact.shape[0]
     steps, many = inner_steps(count)
@@ -533,13 +525,14 @@
             copy.wait()
 
 
-def force_ends_kernel(n_y, pos, table, impact, disp, vel, contact, labels, *refs):
+def rest_kernel(n_y, pos, table, impact, disp, vel, contact, labels, *refs):
     yg, zg, stress, ends = refs[:n_y], refs[n_y], refs[n_y + 1], refs[n_y + 2]
-    xg = refs[n_y + 3 : n_y + 5]
-    disp_hbm, vel_hbm, token, disp_out, vel_out, sems = refs[n_y + 7 :]
-    token[...] = jnp.zeros((8, 128), F32)
+    refs = refs[n_y + 3 :]
+    v, rd, xy = refs[0], refs[1], refs[2 : 4 + 3 * n_y]
+    xg = xy[:2]
+    disp_hbm, vel_hbm, big_v, big_rd, disp_out, vel_out, sems = refs[6 + 3 * n_y :]
     force = Force(n_y, pos, table, impact, disp, vel, contact, labels, yg, zg)
-    count = contact.shape[0]
+    count, ny = contact.shape[0], contact.shape[1]
     copies = []
     for end, x in enumerate((0, count - 1)):
 
@@ -558,6 +551,23 @@
             copy = pltpu.make_async_copy(src.at[:, end], dst.at[:, x], sems.at[end, which])
             copy.start()
             copies.append(copy)
+    big = Enlarged(n_y, pos, v, rd, xy)
+
+    def put(p, parts):
+        v_own, v_rows, rd_own, rd_rows = parts
+        big_v[p + 3, 0:ny] = v_own
+        big_v[p + 3, ny : ny + 8] = v_rows
+        big_rd[p + 3, 0:ny] = rd_own
+        big_rd[p + 3, ny : ny + 8] = rd_rows
+
+    for p, parts in big.outer(count):
+        put(p, parts)
+
+    def body(x, carry):
+        put(x, big.own(x))
+        return carry
+
+    unrolled(count, 4, body, 0)
     for copy in copies:
         copy.wait()
 
@@ -758,12 +768,12 @@
         stress,
         ends,
     )
-    new_disp, new_vel = call(
+    new_disp, new_vel, token = call(
         functools.partial(force_inner_kernel, n_y),
         "sssvvvv" + "v" * (3 + n_y),
         moving,
-        "hh",
-        [fields3, fields3],
+        "hhv",
+        [fields3, fields3, small],
         55 * size,
         [
             pltpu.VMEM((3, nx, ny, nz), F32),
@@ -773,40 +783,32 @@
     )
     (joined,) = call(
         functools.partial(join_kernel, n_y),
-        "svv" + "v" * len(xy),
-        (pos, v0, rd, *xy),
+        "svva" + "v" * len(xy),
+        (pos, v0, rd, token, *xy),
         "v",
         [arr(nx + 6, ny + 8, 128)],
         4 * size,
     )
     z_got = swap(joined, "gz", z_pairs)
-    main_v, main_rd = call(
-        functools.partial(fill_kernel, n_y),
-        "svv" + "v" * len(xy),
-        (pos, v0, rd, *xy),
-        "vv",
-        [arr(nx + 6, ny + 8, nz)] * 2,
-        4 * size,
-    )
-    new_disp, new_vel, token = call(
-        functools.partial(force_ends_kernel, n_y),
-        "sssvvvv" + "v" * (3 + n_y) + "vvhh",
-        (*moving, *xs, new_disp, new_vel),
-        "hhv",
-        [fields3, fields3, small],
-        8 * size,
+    new_disp, new_vel, main_v, main_rd = call(
+        functools.partial(rest_kernel, n_y),
+        "sssvvvv" + "v" * (3 + n_y) + "vv" + "v" * len(xy) + "hh",
+        (*moving, v0, rd, *xy, new_disp, new_vel),
+        "hhvv",
+        [fields3, fields3, *[arr(nx + 6, ny + 8, nz)] * 2],
+        12 * size,
         [
             pltpu.VMEM((3, 2, ny, nz), F32),
             pltpu.VMEM((3, 2, ny, nz), F32),
             pltpu.SemaphoreType.DMA((2, 2)),
         ],
-        [(len(moving) + 2, 0), (len(moving) + 3, 1)],
+        [(len(moving) + 2 + len(xy), 0), (len(moving) + 3 + len(xy), 1)],
     )
     peers = lax.axis_size("gx") * lax.axis_size("gy") * lax.axis_size("gz")
     v1, v2, spread = call(
         krylov_kernel,
-        "svvvav",
-        (pos, main_v, main_rd, mom, token, z_got),
+        "svvvv",
+        (pos, main_v, main_rd, mom, z_got),
         "vvv",
         [field, field, arr(peers, 8, 128)],
         60 * size,

time: 53 us -> 50.4 us (0.951)
  blocking collectives: 13 us -> 10.9 us
  Pallas kernels: 19.1 us -> 18.5 us
    all_to_all x1, blocking collectives: 13 us -> 10.9 us  [per_device(): mom = lax.all_to_all(spread, ('gx', 'gy', 'gz'), 0, 0, tiled=True)]
    pallas_call x11 -> x10, Pallas kernels: 19.1 us -> 18.5 us  [call(): pl.pallas_call(kernel, out_shape=outs, in_specs=[spec_of(k, a) for k, a i...]
  transfers between devices with their start and end apart: 11 -> 11, of which waited for: 1 -> 2; matrix products, arithmetic and copies ran while one was open for 0% -> 0% of each run, Pallas kernels for 20% -> 20%
where the time goes in v7:
time: 50.4 us; the launch traced here: 50.1 us
  Pallas kernels  18.5 us (37%)
  starting transfers between devices  15.4 us (31%)
  blocking collectives  10.9 us (22%)
  local copies, waits for them, and re-layouts  2.51 us (5%)
  waiting for transfers between devices  1.76 us (3%)
  between operations  0.95 us (2%)
    pallas_call x10, Pallas kernels, call(): pl.pallas_call(kernel, out_shape=outs, in_specs=[spec_of(k, a) for k, a i...  18.5 us
    ppermute x11, starting transfers between devices, swap(): return lax.ppermute(array, axis, pairs + [(b, a) for a, b in pairs])  15.4 us
    all_to_all x1, blocking collectives, per_device(): mom = lax.all_to_all(spread, ('gx', 'gy', 'gz'), 0, 0, tiled=True)  10.9 us
    unnamed x22, local copies, waits for them, and re-layouts  2.51 us
    ppermute x11, waiting for transfers between devices, swap(): return lax.ppermute(array, axis, pairs + [(b, a) for a, b in pairs])  1.76 us
  transfers between devices with their start and end apart: 11, of which 2 were waited for; matrix products, arithmetic and copies ran while one was open for 0% of the time, Pallas kernels for 20%

profile of v7, /device:TPU:0, one launch (start us, length us, event | category | flops | bytes accessed | tf_op | source)
XLA Modules:
  0.0 50.1 jit_solution(13261974539158022054)
XLA Ops:
  0.6 0.1 pad_add_fusion.pos
  0.7 0.0 copy-start
  0.7 1.4 %copy-done = f32[3,16,32,256]{3,2,1,0:T(8,128)S(1)} copy-done((f32[3,16,32,256]{3,2,1,0:T(8,128)S(1)}, f32[3,16,32,256]{3,2,1,0:T(8,128)}, u32[]{:S(2)}) %copy-start) | copy-done | bytes 1572888
  2.1 0.0 copy-start.2
  2.1 1.0 %copy-done.2 = f32[16,32,256]{2,1,0:T(8,128)S(1)} copy-done((f32[16,32,256]{2,1,0:T(8,128)S(1)}, f32[16,32,256]{2,1,0:T(8,128)}, u32[]{:S(2)}) %copy-start.2) | copy-done | bytes 524312
  3.2 1.0 %shard_map.120 = (f32[4,16,256]{2,1,0:T(8,128)S(1)}, f32[16,32,128]{2,1,0:T(8,128)S(1)}) custom-call(s32[3]{0:T(128)S(1)} %pad_add_fusion.pos, f32[3,16,32,256]{3,2,1,0:T(8,128)S(1)} %copy-done, f32[16,32,256]{2,1,0:T(8,128)S(1)} %copy-done.2), custom_call_target="tpu_custom_call" | custom-call | flops 131072 | bytes 2424844 | tf_op jit(solution)/shard_map/pallas_call | solution.py:666
  4.1 0.0 copy-start.10
  4.1 0.0 copy-start.4
  4.2 0.0 copy-start.7
  4.2 0.0 copy-start.8
  4.2 3.0 %collective-permute-start = (f32[4,16,256]{2,1,0:T(8,128)S(1)}, f32[4,16,256]{2,1,0:T(8,128)S(1)}, u32[]{:S(2)}, u32[]{:S(2)}) collective-permute-start(f32[4,16,256]{2,1,0:T(8,128)S(1)} %get-tuple-element.36), channel_id=1, source_target_pairs={{0,2},{2,0},{1,3},{3,1},{4,6},{6,4},{5,7},{7,5},{8,10},{10,8},{9,1... | collective-permute-start | bytes 196616 | tf_op jit(solution)/shard_map/ppermute | solution.py:631
  7.2 0.0 collective-permute-start.1
  7.2 0.6 %shard_map.121 = (f32[4,32,256]{2,1,0:T(8,128)S(1)}, f32[4,32,256]{2,1,0:T(8,128)S(1)}) custom-call(s32[3]{0:T(128)S(1)} %pad_add_fusion.pos, f32[3,16,32,256]{3,2,1,0:T(8,128)S(1)} %copy-done, f32[16,32,256]{2,1,0:T(8,128)S(1)} %copy-done.2, f32[16,32,128]{2,1,0:T(8,128)S(1)} %get-tuple-element.37.after), custom_call_target="tpu_custom_call" | custom-call | flops 131072 | bytes 2621452 | tf_op jit(solution)/shard_map/pallas_call | solution.py:666
  7.8 1.6 %collective-permute-start.2 = (f32[4,32,256]{2,1,0:T(8,128)S(1)}, f32[4,32,256]{2,1,0:T(8,128)S(1)}, u32[]{:S(2)}, u32[]{:S(2)}) collective-permute-start(f32[4,32,256]{2,1,0:T(8,128)S(1)} %get-tuple-element.38), channel_id=1, source_target_pairs={{0,4},{8,12},{4,0},{12,8},{1,5},{9,13},{5,1},{13,9},{2,6},{10,14},... | collective-permute-start | bytes 393224 | tf_op jit(solution)/shard_map/ppermute | solution.py:631
  9.4 0.7 %collective-permute-start.3 = (f32[4,32,256]{2,1,0:T(8,128)S(1)}, f32[4,32,256]{2,1,0:T(8,128)S(1)}, u32[]{:S(2)}, u32[]{:S(2)}) collective-permute-start(f32[4,32,256]{2,1,0:T(8,128)S(1)} %get-tuple-element.39), channel_id=1, source_target_pairs={{4,8},{8,4},{5,9},{9,5},{6,10},{10,6},{7,11},{11,7},{20,24},{24,20... | collective-permute-start | bytes 393224 | tf_op jit(solution)/shard_map/ppermute | solution.py:631
  10.1 0.0 copy-done.10
  10.1 0.0 collective-permute-done.refs_0_
  10.1 0.0 collective-permute-done.1.refs_1_
  10.1 0.0 copy-done.4
  10.1 0.0 copy-done.7
  10.2 0.0 copy-done.8
  10.2 4.1 %shard_map.122 = (f32[16,32,256]{2,1,0:T(8,128)}, f32[16,32,256]{2,1,0:T(8,128)S(1)}, f32[16,32,256]{2,1,0:T(8,128)S(1)}, f32[6,16,32,256]{3,2,1,0:T(8,128)S(1)}...) custom-call(s32[3]{0:T(128)S(1)} %pad_add_fusion.pos, ...), custom_call_target="tpu_custom_call" | custom-call | flops 18350080 | bytes 9162828 | tf_op jit(solution)/shard_map/pallas_call | solution.py:666
  14.2 0.0 collective-permute-done.2.refs_2_
  14.3 0.0 collective-permute-done.3.refs_3_
  14.3 0.0 copy-start.1
  14.3 0.0 copy-start.5
  14.3 0.0 copy-start.6
  14.3 0.0 copy-start.9
  14.3 1.6 %shard_map.123 = (f32[16,32,256]{2,1,0:T(8,128)}, f32[16,32,256]{2,1,0:T(8,128)S(1)}, f32[16,32,256]{2,1,0:T(8,128)S(1)}, f32[6,2,32,256]{3,2,1,0:T(8,128)S(1)},...) custom-call(s32[3]{0:T(128)S(1)} %pad_add_fusion.pos, ...), custom_call_target="tpu_custom_call", output_to_operand_aliasing={{0}: (11, {})} | custom-call | flops 2621440 | bytes 9216076 | tf_op jit(solution)/shard_map/pallas_call | solution.py:666
  16.0 0.3 collective-permute-start.5
  16.3 4.2 %collective-permute-start.6 = (f32[8,32,256]{2,1,0:T(8,128)S(1)}, f32[8,32,256]{2,1,0:T(8,128)S(1)}, u32[]{:S(2)}, u32[]{:S(2)}) collective-permute-start(f32[8,32,256]{2,1,0:T(8,128)S(1)} %get-tuple-element.52), channel_id=1, source_target_pairs={{0,4},{8,12},{4,0},{12,8},{1,5},{9,13},{5,1},{13,9},{2,6},{10,14},... | collective-permute-start | bytes 786440 | tf_op jit(solution)/shard_map/ppermute | solution.py:631
  20.5 0.7 %collective-permute-start.7 = (f32[8,32,256]{2,1,0:T(8,128)S(1)}, f32[8,32,256]{2,1,0:T(8,128)S(1)}, u32[]{:S(2)}, u32[]{:S(2)}) collective-permute-start(f32[8,32,256]{2,1,0:T(8,128)S(1)} %get-tuple-element.53), channel_id=1, source_target_pairs={{4,8},{8,4},{5,9},{9,5},{6,10},{10,6},{7,11},{11,7},{20,24},{24,20... | collective-permute-start | bytes 786440 | tf_op jit(solution)/shard_map/ppermute | solution.py:631
  21.2 0.6 %collective-permute-start.4 = (f32[22,8,256]{2,1,0:T(8,128)S(1)}, f32[22,8,256]{2,1,0:T(8,128)S(1)}, u32[]{:S(2)}, u32[]{:S(2)}) collective-permute-start(f32[22,8,256]{2,1,0:T(8,128)S(1)} %get-tuple-element.46.refs_0_), channel_id=1, source_target_pairs={{0,2},{2,0},{1,3},{3,1},{4,6},{6,4},{5,7},{7,5},{8,10},{10,8},{9,1... | collective-permute-start | bytes 540680 | tf_op jit(solution)/shard_map/ppermute | solution.py:631
  21.8 0.0 collective-permute-done.5.after.refs_1_
  21.8 0.5 %shard_map.124 = (f32[2,8,256]{2,1,0:T(8,128)S(1)}, f32[2,8,256]{2,1,0:T(8,128)S(1)}) custom-call(s32[3]{0:T(128)S(1)} %pad_add_fusion.pos, f32[16,32,128]{2,1,0:T(8,128)S(1)} %collective-permute-done.5.after.refs_1_, f32[22,8,256]{2,1,0:T(8,128)S(1)} %get-tuple-element.46.refs_0_), custom_call_target="tpu_custom_call" | custom-call | flops 1024 | bytes 475148 | tf_op jit(solution)/shard_map/pallas_call | solution.py:666
  22.3 3.6 %collective-permute-start.8 = (f32[2,8,256]{2,1,0:T(8,128)S(1)}, f32[2,8,256]{2,1,0:T(8,128)S(1)}, u32[]{:S(2)}, u32[]{:S(2)}) collective-permute-start(f32[2,8,256]{2,1,0:T(8,128)S(1)} %get-tuple-element.54), channel_id=1, source_target_pairs={{0,6},{2,4},{8,14},{10,12},{6,0},{4,2},{14,8},{12,10},{1,7},{3,5},... | collective-permute-start | bytes 49160 | tf_op jit(solution)/shard_map/ppermute | solution.py:631
  26.0 0.7 %collective-permute-start.9 = (f32[2,8,256]{2,1,0:T(8,128)S(1)}, f32[2,8,256]{2,1,0:T(8,128)S(1)}, u32[]{:S(2)}, u32[]{:S(2)}) collective-permute-start(f32[2,8,256]{2,1,0:T(8,128)S(1)} %get-tuple-element.55), channel_id=1, source_target_pairs={{4,10},{6,8},{10,4},{8,6},{5,11},{7,9},{11,5},{9,7},{20,26},{22,24... | collective-permute-start | bytes 49160 | tf_op jit(solution)/shard_map/ppermute | solution.py:631
  26.6 1.6 %collective-permute-done.4.refs_0_.refs_8_.refs_2_ = f32[22,8,256]{2,1,0:T(8,128)S(1)} collective-permute-done((f32[22,8,256]{2,1,0:T(8,128)S(1)}, f32[22,8,256]{2,1,0:T(8,128)S(1)}, u32[]{:S(2)}, u32[]{:S(2)}) %collective-permute-start.4) | collective-permute-done | bytes 180256 | tf_op jit(solution)/shard_map/ppermute | solution.py:631
  28.2 0.0 copy-done.1
  28.2 0.0 copy-done.5
  28.2 0.0 copy-done.6
  28.2 0.0 copy-done.9
  28.2 3.3 %shard_map.125 = (f32[3,16,32,256]{3,2,1,0:T(8,128)}, f32[3,16,32,256]{3,2,1,0:T(8,128)}, f32[8,128]{1,0:T(8,128)S(1)}) custom-call(s32[3]{0:T(128)S(1)} %pad_add_fusion.pos, f32[4,4]{1,0:T(4,128)S(1)} %pad_maximum_fusion.table, f32[3]{0:T(128)S(1)} %copy-done.9, f32[3,16,32,256]{3,2,1,0:T(8,128)S(1)} %copy-done.1, f32[3,16,32,256]{3,2,1,0:T(8,128)S(1)} %copy-done.5, ...), custom_call_target="tpu_custom_call" | custom-call | flops 7208960 | bytes 11325528 | tf_op jit(solution)/shard_map/pallas_call | solution.py:666
  31.6 0.0 collective-permute-done.6.refs_6_.refs_0_
  31.6 0.0 collective-permute-done.7.refs_7_.refs_1_
  31.6 0.0 collective-permute-done.8.refs_9_.refs_3_
  31.6 0.0 collective-permute-done.9.refs_10_.refs_4_
  31.6 0.9 %shard_map.127 = f32[22,40,128]{2,1,0:T(8,128)S(1)} custom-call(s32[3]{0:T(128)S(1)} %pad_add_fusion.pos, f32[16,32,256]{2,1,0:T(8,128)S(1)} %get-tuple-element.50.refs_4_.v.v0, f32[16,32,256]{2,1,0:T(8,128)S(1)} %get-tuple-element.51.refs_5_.rd, f32[8,128]{1,0:T(8,128)S(1)} %get-tuple-element.64.token, ...), custom_call_target="tpu_custom_call" | custom-call | flops 524288 | bytes 2240524 | tf_op jit(solution)/shard_map/pallas_call | solution.py:666
  32.5 0.1 collective-permute-start.10
  32.6 1.6 %shard_map.126 = (f32[3,16,32,256]{3,2,1,0:T(8,128)}, f32[3,16,32,256]{3,2,1,0:T(8,128)}, f32[22,40,256]{2,1,0:T(8,128)S(1)}, f32[22,40,256]{2,1,0:T(8,128)S(1)}) custom-call(s32[3]{0:T(128)S(1)} %pad_add_fusion.pos, f32[4,4]{1,0:T(4,128)S(1)} %pad_maximum_fusion.table, f32[3]{0:T(128)S(1)} %copy-done.9, ...), custom_call_target="tpu_custom_call", output_to_operand_aliasing={{0}: (18, {}), {1}: (19, {})} | custom-call | flops 1572864 | bytes 18055256 | tf_op jit(solution)/shard_map/pallas_call | solution.py:666
  34.2 0.0 copy-start.3
  34.2 0.1 collective-permute-done.10.z_got
  34.4 3.1 %shard_map.128 = (f32[16,32,256]{2,1,0:T(8,128)S(1)}, f32[16,32,256]{2,1,0:T(8,128)S(1)}, f32[16,8,128]{2,1,0:T(8,128)S(1)}) custom-call(s32[3]{0:T(128)S(1)} %pad_add_fusion.pos, f32[22,40,256]{2,1,0:T(8,128)S(1)} %get-tuple-element.61.main_v, f32[22,40,256]{2,1,0:T(8,128)S(1)} %get-tuple-element.62.main_rd, f32[8,128]{1,0:T(8,128)S(1)} %get-tuple-element.63.mom, ...), custom_call_target="tpu_custom_call" | custom-call | flops 7864320 | bytes 3371020 | tf_op jit(solution)/shard_map/pallas_call | solution.py:666
  37.5 10.9 %all_to_all.5.mom = f32[16,8,128]{2,1,0:T(8,128)S(1)} all-to-all(f32[16,8,128]{2,1,0:T(8,128)S(1)} %get-tuple-element.65), channel_id=1, replica_groups=mesh['case'=2,'gx'=4,'gy'=2,'gz'=2] {'gx','gy','gz'}, dimensions={0} | all-to-all | bytes 131072 | tf_op jit(solution)/shard_map/all_to_all | solution.py:822
  48.4 0.0 copy-done.3
  48.4 1.7 %shard_map.129 = f32[16,32,256]{2,1,0:T(8,128)} custom-call(f32[16,8,128]{2,1,0:T(8,128)S(1)} %all_to_all.5.mom, f32[16,32,256]{2,1,0:T(8,128)S(1)} %get-tuple-element.50.refs_4_.v.v0, f32[16,32,256]{2,1,0:T(8,128)S(1)} %get-tuple-element.66.v1, f32[16,32,256]{2,1,0:T(8,128)S(1)} %get-tuple-element.67.v2, f32[16,32,256]{2,1,0:T(8,128)S(1)} %copy-done.3), custom_call_target="tpu_custom_call" | custom-call | flops 1048576 | bytes 2686976 | tf_op jit(solution)/shard_map/pallas_call | solution.py:666
  (2 shorter events, 0.0 us)
Async XLA Ops:
  0.7 1.4 %copy-start = (f32[3,16,32,256]{3,2,1,0:T(8,128)S(1)}, f32[3,16,32,256]{3,2,1,0:T(8,128)}, u32[]{:S(2)}) copy-start(f32[3,16,32,256]{3,2,1,0:T(8,128)} %disp.11) | copy-start | bytes 4718596
  2.1 1.0 %copy-start.2 = (f32[16,32,256]{2,1,0:T(8,128)S(1)}, f32[16,32,256]{2,1,0:T(8,128)}, u32[]{:S(2)}) copy-start(f32[16,32,256]{2,1,0:T(8,128)} %damage_hbm.1) | copy-start | bytes 1572868
  4.1 5.9 %copy-start.10 = (f32[4,4]{1,0:T(4,128)S(1)}, f32[4,4]{1,0:T(4,128)}, u32[]{:S(2)}) copy-start(f32[4,4]{1,0:T(4,128)} %param.16) | copy-start | bytes 196
  4.1 6.0 %copy-start.4 = (s32[16,32,256]{2,1,0:T(8,128)S(1)}, s32[16,32,256]{2,1,0:T(8,128)}, u32[]{:S(2)}) copy-start(s32[16,32,256]{2,1,0:T(8,128)} %labels.7) | copy-start | bytes 1572868
  4.2 6.0 %copy-start.7 = (f32[16,32,256]{2,1,0:T(8,128)S(1)}, f32[16,32,256]{2,1,0:T(8,128)}, u32[]{:S(2)}) copy-start(f32[16,32,256]{2,1,0:T(8,128)} %history.3) | copy-start | bytes 1572868
  4.2 6.0 %copy-start.8 = (s32[16,32,256]{2,1,0:T(8,128)S(1)}, s32[16,32,256]{2,1,0:T(8,128)}, u32[]{:S(2)}) copy-start(s32[16,32,256]{2,1,0:T(8,128)} %notch.3) | copy-start | bytes 1572868
  4.2 5.9 %collective-permute-start = (f32[4,16,256]{2,1,0:T(8,128)S(1)}, f32[4,16,256]{2,1,0:T(8,128)S(1)}, u32[]{:S(2)}, u32[]{:S(2)}) collective-permute-start(f32[4,16,256]{2,1,0:T(8,128)S(1)} %get-tuple-element.36), channel_id=1, source_target_pairs={{0,2},{2,0},{1,3},{3,1},{4,6},{6,4},{5,7},{7,5},{8,10},{10,8},{9,1... | collective-permute-start | bytes 196616 | tf_op jit(solution)/shard_map/ppermute | solution.py:631
  7.2 2.9 %collective-permute-start.1 = (f32[16,32,128]{2,1,0:T(8,128)S(1)}, f32[16,32,128]{2,1,0:T(8,128)S(1)}, u32[]{:S(2)}, u32[]{:S(2)}) collective-permute-start(f32[16,32,128]{2,1,0:T(8,128)S(1)} %get-tuple-element.37.after), channel_id=1, source_target_pairs={{0,1},{1,0},{2,3},{3,2},{4,5},{5,4},{6,7},{7,6},{8,9},{9,8},{10,11... | collective-permute-start | bytes 786440 | tf_op jit(solution)/shard_map/ppermute | solution.py:631
  7.8 6.5 %collective-permute-start.2 = (f32[4,32,256]{2,1,0:T(8,128)S(1)}, f32[4,32,256]{2,1,0:T(8,128)S(1)}, u32[]{:S(2)}, u32[]{:S(2)}) collective-permute-start(f32[4,32,256]{2,1,0:T(8,128)S(1)} %get-tuple-element.38), channel_id=1, source_target_pairs={{0,4},{8,12},{4,0},{12,8},{1,5},{9,13},{5,1},{13,9},{2,6},{10,14},... | collective-permute-start | bytes 393224 | tf_op jit(solution)/shard_map/ppermute | solution.py:631
  9.4 4.9 %collective-permute-start.3 = (f32[4,32,256]{2,1,0:T(8,128)S(1)}, f32[4,32,256]{2,1,0:T(8,128)S(1)}, u32[]{:S(2)}, u32[]{:S(2)}) collective-permute-start(f32[4,32,256]{2,1,0:T(8,128)S(1)} %get-tuple-element.39), channel_id=1, source_target_pairs={{4,8},{8,4},{5,9},{9,5},{6,10},{10,6},{7,11},{11,7},{20,24},{24,20... | collective-permute-start | bytes 393224 | tf_op jit(solution)/shard_map/ppermute | solution.py:631
  14.3 13.9 %copy-start.1 = (f32[3,16,32,256]{3,2,1,0:T(8,128)S(1)}, f32[3,16,32,256]{3,2,1,0:T(8,128)}, u32[]{:S(2)}) copy-start(f32[3,16,32,256]{3,2,1,0:T(8,128)} %disp.11) | copy-start | bytes 4718596
  14.3 13.9 %copy-start.5 = (f32[3,16,32,256]{3,2,1,0:T(8,128)S(1)}, f32[3,16,32,256]{3,2,1,0:T(8,128)}, u32[]{:S(2)}) copy-start(f32[3,16,32,256]{3,2,1,0:T(8,128)} %vel.3) | copy-start | bytes 4718596
  14.3 13.9 %copy-start.6 = (s32[16,32,256]{2,1,0:T(8,128)S(1)}, s32[16,32,256]{2,1,0:T(8,128)}, u32[]{:S(2)}) copy-start(s32[16,32,256]{2,1,0:T(8,128)} %contact.3) | copy-start | bytes 1572868
  14.3 13.9 %copy-start.9 = (f32[3]{0:T(128)S(1)}, f32[3]{0:T(128)}, u32[]{:S(2)}) copy-start(f32[3]{0:T(128)} %impact.3) | copy-start | bytes 40
  16.0 5.8 %collective-permute-start.5 = (f32[16,32,128]{2,1,0:T(8,128)S(1)}, f32[16,32,128]{2,1,0:T(8,128)S(1)}, u32[]{:S(2)}, u32[]{:S(2)}) collective-permute-start(f32[16,32,128]{2,1,0:T(8,128)S(1)} %get-tuple-element.47), channel_id=1, source_target_pairs={{0,1},{1,0},{2,3},{3,2},{4,5},{5,4},{6,7},{7,6},{8,9},{9,8},{10,11... | collective-permute-start | bytes 786440 | tf_op jit(solution)/shard_map/ppermute | solution.py:631
  16.3 15.3 %collective-permute-start.6 = (f32[8,32,256]{2,1,0:T(8,128)S(1)}, f32[8,32,256]{2,1,0:T(8,128)S(1)}, u32[]{:S(2)}, u32[]{:S(2)}) collective-permute-start(f32[8,32,256]{2,1,0:T(8,128)S(1)} %get-tuple-element.52), channel_id=1, source_target_pairs={{0,4},{8,12},{4,0},{12,8},{1,5},{9,13},{5,1},{13,9},{2,6},{10,14},... | collective-permute-start | bytes 786440 | tf_op jit(solution)/shard_map/ppermute | solution.py:631
  20.5 11.1 %collective-permute-start.7 = (f32[8,32,256]{2,1,0:T(8,128)S(1)}, f32[8,32,256]{2,1,0:T(8,128)S(1)}, u32[]{:S(2)}, u32[]{:S(2)}) collective-permute-start(f32[8,32,256]{2,1,0:T(8,128)S(1)} %get-tuple-element.53), channel_id=1, source_target_pairs={{4,8},{8,4},{5,9},{9,5},{6,10},{10,6},{7,11},{11,7},{20,24},{24,20... | collective-permute-start | bytes 786440 | tf_op jit(solution)/shard_map/ppermute | solution.py:631
  21.2 7.0 %collective-permute-start.4 = (f32[22,8,256]{2,1,0:T(8,128)S(1)}, f32[22,8,256]{2,1,0:T(8,128)S(1)}, u32[]{:S(2)}, u32[]{:S(2)}) collective-permute-start(f32[22,8,256]{2,1,0:T(8,128)S(1)} %get-tuple-element.46.refs_0_), channel_id=1, source_target_pairs={{0,2},{2,0},{1,3},{3,1},{4,6},{6,4},{5,7},{7,5},{8,10},{10,8},{9,1... | collective-permute-start | bytes 540680 | tf_op jit(solution)/shard_map/ppermute | solution.py:631
  22.3 9.3 %collective-permute-start.8 = (f32[2,8,256]{2,1,0:T(8,128)S(1)}, f32[2,8,256]{2,1,0:T(8,128)S(1)}, u32[]{:S(2)}, u32[]{:S(2)}) collective-permute-start(f32[2,8,256]{2,1,0:T(8,128)S(1)} %get-tuple-element.54), channel_id=1, source_target_pairs={{0,6},{2,4},{8,14},{10,12},{6,0},{4,2},{14,8},{12,10},{1,7},{3,5},... | collective-permute-start | bytes 49160 | tf_op jit(solution)/shard_map/ppermute | solution.py:631
  26.0 5.7 %collective-permute-start.9 = (f32[2,8,256]{2,1,0:T(8,128)S(1)}, f32[2,8,256]{2,1,0:T(8,128)S(1)}, u32[]{:S(2)}, u32[]{:S(2)}) collective-permute-start(f32[2,8,256]{2,1,0:T(8,128)S(1)} %get-tuple-element.55), channel_id=1, source_target_pairs={{4,10},{6,8},{10,4},{8,6},{5,11},{7,9},{11,5},{9,7},{20,26},{22,24... | collective-permute-start | bytes 49160 | tf_op jit(solution)/shard_map/ppermute | solution.py:631
  32.5 1.9 %collective-permute-start.10 = (f32[22,40,128]{2,1,0:T(8,128)S(1)}, f32[22,40,128]{2,1,0:T(8,128)S(1)}, u32[]{:S(2)}, u32[]{:S(2)}) collective-permute-start(f32[22,40,128]{2,1,0:T(8,128)S(1)} %shard_map.127), channel_id=1, source_target_pairs={{0,1},{1,0},{2,3},{3,2},{4,5},{5,4},{6,7},{7,6},{8,9},{9,8},{10,11... | collective-permute-start | bytes 1351688 | tf_op jit(solution)/shard_map/ppermute | solution.py:631
  34.2 14.2 %copy-start.3 = (f32[16,32,256]{2,1,0:T(8,128)S(1)}, f32[16,32,256]{2,1,0:T(8,128)}, u32[]{:S(2)}) copy-start(f32[16,32,256]{2,1,0:T(8,128)} %damage_hbm.1) | copy-start | bytes 1572868

commit v8 on v7

--- a/solution.py
+++ b/solution.py
@@ -51,10 +51,9 @@
     return upper, lower
 
 
-def send_columns(ref, x, planes, gz):
+def send_columns(ref, x, planes, gz, tile=None):
     depth = planes[0].shape[1]
     lanes = iota2((planes[0].shape[0], 128), 1)
-    tile = None
     for field, plane in enumerate(planes):
         part = jnp.where(gz == 0, plane[:, depth - 128 :], plane[:, :128])
         part = pltpu.roll(part, field + 1 - gz, 1)
@@ -90,34 +89,47 @@
     return lax.fori_loop(0, count // many, several, carry)
 
 
-def pack_kernel(n_y, pos, disp, damage, *refs):
+def pack_damage_kernel(n_y, pos, damage, *refs):
     ys, zs = refs[:n_y], refs[n_y]
     odd_y, gz = pos[1] == 1, pos[2]
 
     def body(x, carry):
-        planes = [disp[0, x], disp[1, x], disp[2, x], damage[x]]
+        plane = damage[x]
+        last = plane.shape[0] - 1
+        send(odd_y, ys, (pl.ds(x, 1), slice(None)), plane[0:1], plane[last : last + 1])
+        send_columns(zs, x, [plane], gz)
+        return carry
+
+    unrolled(damage.shape[0], 8, body, 0)
+
+
+def pack_kernel(n_y, pos, disp, *refs):
+    ys_damage, zs_damage, ys, zs = (
+        refs[:n_y],
+        refs[n_y],
+        refs[n_y + 1 : 2 * n_y + 1],
+        refs[2 * n_y + 1],
+    )
+    odd_y, gz = pos[1] == 1, pos[2]
+    for mine, before in zip(ys, ys_damage, strict=True):
+        mine[3] = before[...]
+
+    def body(x, carry):
+        planes = [disp[0, x], disp[1, x], disp[2, x]]
         for field, plane in enumerate(planes):
             last = plane.shape[0] - 1
             spot = (field, pl.ds(x, 1), slice(None))
             send(odd_y, ys, spot, plane[0:1], plane[last : last + 1])
-        send_columns(zs, x, planes, gz)
+        send_columns(zs, x, planes, gz, pltpu.roll(zs_damage[x], 3, 1))
         return carry
 
-    unrolled(damage.shape[0], 8, body, 0)
+    unrolled(disp.shape[1], 8, body, 0)
 
 
 def pack_x_kernel(pos, disp, damage, after, *xs):
     odd_x, count = pos[0] == 1, damage.shape[0]
     for field, src in enumerate((disp.at[0], disp.at[1], disp.at[2], damage)):
         send(odd_x, xs, field, src[0], src[count - 1])
-
-
-def row_tile(v, rd, is_high):
-    rows = v.shape[0]
-    part = slice(rows - 8, rows) if is_high else slice(0, 8)
-    at = iota2((8, v.shape[1]), 0)
-    keep = at >= 4 if is_high else at < 4
-    return jnp.where(keep, v[part], pltpu.roll(rd[part], 4, 0))
 
 
 class Local:
@@ -181,12 +193,12 @@
         return hist, rd, v, folded(residual * v)
 
     def send_y(self, ys, x, v, rd, stress):
-        count = self.damage.shape[0]
-        tall, last = count // 8, v.shape[0] - 1
-        send(self.odd_y, ys, x, row_tile(v, rd, False), row_tile(v, rd, True))
-        for c, k in enumerate((3, 1, 5)):
-            spot = (count + c * tall + lax.div(x, 8), pl.ds(lax.rem(x, 8), 1), slice(None))
-            send(self.odd_y, ys, spot, stress[k][0:1], stress[k][last : last + 1])
+        rows = v.shape[0]
+        sources = [(v, depth) for depth in (1, 2, 3)] + [(rd, depth) for depth in (1, 2)]
+        sources += [(stress[k], 1) for k in (3, 1, 5)]
+        for slot, (plane, depth) in enumerate(sources):
+            low, high = plane[depth - 1 : depth], plane[rows - depth : rows - depth + 1]
+            send(self.odd_y, ys, (slot, pl.ds(x, 1), slice(None)), low, high)
 
     def send_z(self, zs, x, stress):
         send_columns(zs, x, [stress[4], stress[5], stress[2]], self.gz)
@@ -206,9 +218,8 @@
     ys, (zs, hist, sems) = refs[n_y + 6 : 2 * n_y + 6], refs[2 * n_y + 6 :]
     steps, many = inner_steps(damage.shape[0])
 
-    def store(step):
-        part = pl.ds(1 + step * many, many)
-        return pltpu.make_async_copy(hist.at[part], hist_hbm.at[part], sems.at[step])
+    def store(x):
+        return pltpu.make_async_copy(hist.at[x], hist_hbm.at[x], sems.at[x])
 
     def several(step, total):
         for at in range(many):
@@ -231,13 +242,13 @@
             v_out[x] = v
             local.send_y(ys, x, v, rd, stress)
             local.send_z(zs, x, stress)
+            store(x).start()
             total = total + part
-        store(step).start()
         return total
 
     mom_out[...] = lax.fori_loop(0, steps, several, jnp.zeros((8, 128), F32))
-    for step in range(steps):
-        store(step).wait()
+    for x in range(1, damage.shape[0] - 1):
+        store(x).wait()
 
 
 def ends_kernel(n_y, pos, table, disp, damage, history, notch, labels, *refs):
@@ -283,10 +294,9 @@
         v_out[x] = v
         total = total + part
         found.append((stress, rd, v))
-    tall = count // 8
     for mine, before in zip(ys, ys_in, strict=True):
-        for x in [*range(1, count - 1), *range(count, count + 3 * tall)]:
-            mine[x] = before[x]
+        for slot in range(8):
+            mine[slot] = before[slot]
     for x in range(1, count - 1):
         rd_out[x] = rd_in[x]
         v_out[x] = v_in[x]
@@ -308,13 +318,21 @@
         copy.wait()
 
 
-def corner_kernel(n_y, pos, after, *refs):
-    ys, ds = refs[:n_y], refs[n_y:]
-    odd_x, count = pos[0] == 1, after.shape[0]
-    for which in range(n_y):
-        for depth in (1, 2):
-            pair = (ds[which], ds[n_y + which])
-            send(odd_x, pair, depth - 1, ys[which][depth - 1], ys[which][count - depth])
+def corner_kernel(n_y, pos, after, v, rd, *ds):
+    odd_x, odd_y = pos[0] == 1, pos[1] == 1
+    count, rows = v.shape[0], v.shape[1]
+    for depth in (1, 2):
+        for slot, (src, deep) in enumerate(((v, 1), (v, 2), (v, 3), (rd, 1), (rd, 2))):
+            near, far = pl.ds(deep - 1, 1), pl.ds(rows - deep, 1)
+            planes = (depth - 1, count - depth)
+            by_y = [(src[x, near, :], src[x, far, :]) for x in planes]
+            for which in range(n_y):
+                pair = (ds[which], ds[n_y + which])
+                picked = [
+                    jnp.where(odd_y, *(rows_of if which == 0 else rows_of[::-1]))
+                    for rows_of in by_y
+                ]
+                send(odd_x, pair, (depth - 1, pl.ds(slot, 1), slice(None)), *picked)
 
 
 class Enlarged:
@@ -323,19 +341,27 @@
         self.v, self.rd, self.n_y = v, rd, n_y
         self.xg, self.yg, self.dg = refs[:2], refs[2 : 2 + n_y], refs[2 + n_y : 2 + 3 * n_y]
 
-    def rows(self, tiles):
-        at = iota2(tiles[0].shape, 0)
-        if self.n_y == 1:
-            keep = lax.shift_right_logical(at, 2) == self.odd_y.astype(jnp.int32)
-            tile = tiles[0]
-            return jnp.where(keep, tile, 0.0), jnp.where(keep, pltpu.roll(tile, 4, 0), 0.0)
-        lo, hi = low_high(self.odd_y, tiles)
-        tile = jnp.where(at >= 4, lo, hi)
-        moved = jnp.where(at >= 4, pltpu.roll(lo, 4, 0), pltpu.roll(hi, 4, 0))
-        return tile, moved
+    def rows(self, found):
+        nz = self.v.shape[2]
+        at = iota2((8, nz), 0)
+
+        def tile(first, depths):
+            out = jnp.zeros((8, nz), F32)
+            for depth in range(1, depths + 1):
+                got = [found(w, first + depth - 1) for w in range(self.n_y)]
+                if self.n_y == 1:
+                    spot = jnp.where(self.odd_y, 8 - depth, depth - 1)
+                    out = jnp.where(at == spot, got[0], out)
+                else:
+                    lo, hi = low_high(self.odd_y, got)
+                    out = jnp.where(at == depth - 1, hi, out)
+                    out = jnp.where(at == 8 - depth, lo, out)
+            return out
+
+        return tile(0, 3), tile(3, 2)
 
     def own(self, x):
-        v_rows, rd_rows = self.rows([y[x] for y in self.yg])
+        v_rows, rd_rows = self.rows(lambda w, slot: self.yg[w][slot, pl.ds(x, 1), :])
         return self.v[x], v_rows, self.rd[x], rd_rows
 
     def halo(self, is_low, depth):
@@ -349,10 +375,12 @@
         if depth > 2:
             return v, nothing, jnp.zeros_like(v), nothing
         rd = of(self.xg[0][2 + depth], self.xg[1][2 + depth])
-        tiles = [
-            of(self.dg[w][depth - 1], self.dg[self.n_y + w][depth - 1]) for w in range(self.n_y)
-        ]
-        v_rows, rd_rows = self.rows(tiles)
+
+        def found(w, slot):
+            spot = (depth - 1, pl.ds(slot, 1), slice(None))
+            return of(self.dg[w][spot], self.dg[self.n_y + w][spot])
+
+        v_rows, rd_rows = self.rows(found)
         return v, v_rows, rd, rd_rows
 
     def outer(self, count):
@@ -469,13 +497,10 @@
         self.rates = [table[2, r] for r in range(table.shape[1])]
 
     def plane(self, x, lower, mine, upper, vel_out, disp_out, at):
-        count = self.contact.shape[0]
-        tall = count // 8
         loaded = self.contact[x].astype(F32)
         rate = by_label(self.labels[x], self.rates)
         for c, (kx, ky, kz) in enumerate(PARTS):
-            spot = (count + c * tall + lax.div(x, 8), pl.ds(lax.rem(x, 8), 1), slice(None))
-            rows = low_high(self.odd_y, [y[spot] for y in self.yg])
+            rows = low_high(self.odd_y, [y[5 + c, pl.ds(x, 1), :] for y in self.yg])
             column = self.zg[x][:, c : c + 1]
             yu, yl = shift_y(mine(ky), rows)
             zu, zl = shift_z(mine(kz), column, self.gz == 0)
@@ -493,11 +518,10 @@
     count = contact.shape[0]
     steps, many = inner_steps(count)
 
-    def stores(step):
-        part = pl.ds(1 + step * many, many)
+    def stores(x):
         return (
-            pltpu.make_async_copy(disp_out.at[:, part], disp_hbm.at[:, part], sems.at[step, 0]),
-            pltpu.make_async_copy(vel_out.at[:, part], vel_hbm.at[:, part], sems.at[step, 1]),
+            pltpu.make_async_copy(disp_out.at[:, x], disp_hbm.at[:, x], sems.at[x, 0]),
+            pltpu.make_async_copy(vel_out.at[:, x], vel_hbm.at[:, x], sems.at[x, 1]),
         )
 
     def several(step, carry):
@@ -515,13 +539,13 @@
                 return stress[k, x + 1]
 
             force.plane(x, lower, lambda k: stress[k, x], upper, vel_out, disp_out, x)
-        for copy in stores(step):
-            copy.start()
+            for copy in stores(x):
+                copy.start()
         return carry
 
     lax.fori_loop(0, steps, several, 0)
-    for step in range(steps):
-        for copy in stores(step):
+    for x in range(1, count - 1):
+        for copy in stores(x):
             copy.wait()
 
 
@@ -695,9 +719,17 @@
     z_pairs = [(0, 1)]
 
     sent = call(
+        functools.partial(pack_damage_kernel, n_y),
+        "sv",
+        (pos, damage),
+        "v" * (1 + n_y),
+        [*[arr(nx, nz)] * n_y, columns],
+        100 * size,
+    )
+    sent = call(
         functools.partial(pack_kernel, n_y),
-        "svv",
-        (pos, displacement, damage),
+        "sv" + "v" * (1 + n_y),
+        (pos, displacement, *sent),
         "v" * (1 + n_y),
         [*[arr(4, nx, nz)] * n_y, columns],
         size,
@@ -712,7 +744,7 @@
         size,
     )
     got_x = swap_along("gx", sent_x)
-    rows = [arr(nx + 3 * (nx // 8), 8, nz)] * n_y
+    rows = [arr(8, nx, nz)] * n_y
     voxels = (pos, scaled, displacement, damage, history, notch, labels, *got_yz)
     hist, rd, v0, stress, mom, *sent = call(
         functools.partial(inner_kernel, n_y),
@@ -721,7 +753,7 @@
         "hvvvv" + "v" * (1 + n_y),
         [field, field, field, arr(6, nx, ny, nz), small, *rows, columns],
         140 * size,
-        [pltpu.VMEM((nx, ny, nz), F32), pltpu.SemaphoreType.DMA((inner_steps(nx)[0],))],
+        [pltpu.VMEM((nx, ny, nz), F32), pltpu.SemaphoreType.DMA((nx,))],
     )
     more = (*got_x, hist, rd, v0, mom, *sent)
     hist, rd, v0, ends, mom, *sent = call(
@@ -748,8 +780,8 @@
     ys = swap_along("gy", sent[2 : 2 + n_y])
     corners = call(
         functools.partial(corner_kernel, n_y),
-        "sa" + "v" * n_y,
-        (pos, stress_z, *sent[2 : 2 + n_y]),
+        "savv",
+        (pos, stress_z, v0, rd),
         "v" * (2 * n_y),
         [arr(2, 8, nz)] * (2 * n_y),
         1024,
@@ -778,7 +810,7 @@
         [
             pltpu.VMEM((3, nx, ny, nz), F32),
             pltpu.VMEM((3, nx, ny, nz), F32),
-            pltpu.SemaphoreType.DMA((inner_steps(nx)[0], 2)),
+            pltpu.SemaphoreType.DMA((nx, 2)),
         ],
     )
     (joined,) = call(

time: 50.4 us -> 50.1 us (level)
  waiting for transfers between devices: 1.76 us -> 0.47 us
  Pallas kernels: 18.5 us -> 19.6 us
    ppermute x11, waiting for transfers between devices: 1.76 us -> 0.47 us  [swap(): return lax.ppermute(array, axis, pairs + [(b, a) for a, b in pairs])]
    pallas_call x10 -> x11, Pallas kernels: 18.5 us -> 19.6 us  [call(): pl.pallas_call(kernel, out_shape=outs, in_specs=[spec_of(k, a) for k, a i...]
  transfers between devices with their start and end apart: 11 -> 11, of which waited for: 2 -> 2; matrix products, arithmetic and copies ran while one was open for 0% -> 0% of each run, Pallas kernels for 20% -> 21%
where the time goes in v8:
time: 50.1 us; the launch traced here: 49.9 us
  Pallas kernels  19.6 us (39%)
  starting transfers between devices  15.3 us (31%)
  blocking collectives  10.9 us (22%)
  local copies, waits for them, and re-layouts  2.5 us (5%)
  between operations  0.94 us (2%)
    pallas_call x11, Pallas kernels, call(): pl.pallas_call(kernel, out_shape=outs, in_specs=[spec_of(k, a) for k, a i...  19.6 us
    ppermute x11, starting transfers between devices, swap(): return lax.ppermute(array, axis, pairs + [(b, a) for a, b in pairs])  15.3 us
    all_to_all x1, blocking collectives, per_device(): mom = lax.all_to_all(spread, ('gx', 'gy', 'gz'), 0, 0, tiled=True)  10.9 us
    unnamed x22, local copies, waits for them, and re-layouts  2.5 us
  transfers between devices with their start and end apart: 11, of which 2 were waited for; matrix products, arithmetic and copies ran while one was open for 0% of the time, Pallas kernels for 21%

profile of v8, /device:TPU:0, one launch (start us, length us, event | category | flops | bytes accessed | tf_op | source)
XLA Modules:
  0.0 49.9 jit_solution(6578822447311683247)
XLA Ops:
  0.6 0.1 pad_add_fusion.pos
  0.7 0.0 copy-start.2
  0.7 1.0 %copy-done.2 = f32[16,32,256]{2,1,0:T(8,128)S(1)} copy-done((f32[16,32,256]{2,1,0:T(8,128)S(1)}, f32[16,32,256]{2,1,0:T(8,128)}, u32[]{:S(2)}) %copy-start.2) | copy-done | bytes 524312
  1.8 0.0 copy-start.3
  1.8 0.7 %shard_map.120 = (f32[16,256]{1,0:T(8,128)S(1)}, f32[16,32,128]{2,1,0:T(8,128)S(1)}) custom-call(s32[3]{0:T(128)S(1)} %pad_add_fusion.pos, f32[16,32,256]{2,1,0:T(8,128)S(1)} %copy-done.2), custom_call_target="tpu_custom_call" | custom-call | flops 13107200 | bytes 802828 | tf_op jit(solution)/shard_map/pallas_call | solution.py:690
  2.5 0.0 copy-start
  2.5 1.4 %copy-done = f32[3,16,32,256]{3,2,1,0:T(8,128)S(1)} copy-done((f32[3,16,32,256]{3,2,1,0:T(8,128)S(1)}, f32[3,16,32,256]{3,2,1,0:T(8,128)}, u32[]{:S(2)}) %copy-start) | copy-done | bytes 1572888
  3.9 0.0 copy-start.1
  3.9 0.9 %shard_map.121 = (f32[4,16,256]{2,1,0:T(8,128)S(1)}, f32[16,32,128]{2,1,0:T(8,128)S(1)}) custom-call(s32[3]{0:T(128)S(1)} %pad_add_fusion.pos, f32[3,16,32,256]{3,2,1,0:T(8,128)S(1)} %copy-done, f32[16,256]{1,0:T(8,128)S(1)} %get-tuple-element.38.refs_0_, f32[16,32,128]{2,1,0:T(8,128)S(1)} %get-tuple-element.39.refs_1_), custom_call_target="tpu_custom_call" | custom-call | flops 131072 | bytes 2179084 | tf_op jit(solution)/shard_map/pallas_call | solution.py:690
  4.9 0.0 copy-start.10
  4.9 0.0 copy-start.4
  4.9 0.0 copy-start.7
  4.9 0.0 copy-start.8
  4.9 3.0 %collective-permute-start = (f32[4,16,256]{2,1,0:T(8,128)S(1)}, f32[4,16,256]{2,1,0:T(8,128)S(1)}, u32[]{:S(2)}, u32[]{:S(2)}) collective-permute-start(f32[4,16,256]{2,1,0:T(8,128)S(1)} %get-tuple-element.40), channel_id=1, source_target_pairs={{0,2},{2,0},{1,3},{3,1},{4,6},{6,4},{5,7},{7,5},{8,10},{10,8},{9,1... | collective-permute-start | bytes 196616 | tf_op jit(solution)/shard_map/ppermute | solution.py:655
  7.9 0.0 collective-permute-start.1
  7.9 0.0 copy-done.3
  7.9 0.0 copy-done.1
  7.9 0.6 %shard_map.122 = (f32[4,32,256]{2,1,0:T(8,128)S(1)}, f32[4,32,256]{2,1,0:T(8,128)S(1)}) custom-call(s32[3]{0:T(128)S(1)} %pad_add_fusion.pos, f32[3,16,32,256]{3,2,1,0:T(8,128)S(1)} %copy-done.1, f32[16,32,256]{2,1,0:T(8,128)S(1)} %copy-done.3, f32[16,32,128]{2,1,0:T(8,128)S(1)} %get-tuple-element.41.after), custom_call_target="tpu_custom_call" | custom-call | flops 131072 | bytes 2621452 | tf_op jit(solution)/shard_map/pallas_call | solution.py:690
  8.5 1.6 %collective-permute-start.2 = (f32[4,32,256]{2,1,0:T(8,128)S(1)}, f32[4,32,256]{2,1,0:T(8,128)S(1)}, u32[]{:S(2)}, u32[]{:S(2)}) collective-permute-start(f32[4,32,256]{2,1,0:T(8,128)S(1)} %get-tuple-element.42), channel_id=1, source_target_pairs={{0,4},{8,12},{4,0},{12,8},{1,5},{9,13},{5,1},{13,9},{2,6},{10,14},... | collective-permute-start | bytes 393224 | tf_op jit(solution)/shard_map/ppermute | solution.py:655
  10.2 0.7 %collective-permute-start.3 = (f32[4,32,256]{2,1,0:T(8,128)S(1)}, f32[4,32,256]{2,1,0:T(8,128)S(1)}, u32[]{:S(2)}, u32[]{:S(2)}) collective-permute-start(f32[4,32,256]{2,1,0:T(8,128)S(1)} %get-tuple-element.43), channel_id=1, source_target_pairs={{4,8},{8,4},{5,9},{9,5},{6,10},{10,6},{7,11},{11,7},{20,24},{24,20... | collective-permute-start | bytes 393224 | tf_op jit(solution)/shard_map/ppermute | solution.py:655
  10.8 0.0 copy-done.10
  10.9 0.0 collective-permute-done.refs_0_
  10.9 0.0 collective-permute-done.1.refs_1_
  10.9 0.0 copy-done.4
  10.9 0.0 copy-done.7
  10.9 0.0 copy-done.8
  10.9 4.2 %shard_map.123 = (f32[16,32,256]{2,1,0:T(8,128)}, f32[16,32,256]{2,1,0:T(8,128)S(1)}, f32[16,32,256]{2,1,0:T(8,128)S(1)}, f32[6,16,32,256]{3,2,1,0:T(8,128)S(1)}...) custom-call(s32[3]{0:T(128)S(1)} %pad_add_fusion.pos, ...), custom_call_target="tpu_custom_call" | custom-call | flops 18350080 | bytes 9113676 | tf_op jit(solution)/shard_map/pallas_call | solution.py:690
  15.1 0.0 collective-permute-done.2.refs_2_
  15.1 0.0 collective-permute-done.3.refs_3_
  15.1 0.0 copy-start.5
  15.1 0.0 copy-start.9
  15.1 1.7 %shard_map.124 = (f32[16,32,256]{2,1,0:T(8,128)}, f32[16,32,256]{2,1,0:T(8,128)S(1)}, f32[16,32,256]{2,1,0:T(8,128)S(1)}, f32[6,2,32,256]{3,2,1,0:T(8,128)S(1)},...) custom-call(s32[3]{0:T(128)S(1)} %pad_add_fusion.pos, ...), custom_call_target="tpu_custom_call", output_to_operand_aliasing={{0}: (11, {})} | custom-call | flops 2621440 | bytes 9117772 | tf_op jit(solution)/shard_map/pallas_call | solution.py:690
  16.8 0.0 copy-start.6
  16.8 0.3 collective-permute-start.5
  17.1 4.2 %collective-permute-start.6 = (f32[8,32,256]{2,1,0:T(8,128)S(1)}, f32[8,32,256]{2,1,0:T(8,128)S(1)}, u32[]{:S(2)}, u32[]{:S(2)}) collective-permute-start(f32[8,32,256]{2,1,0:T(8,128)S(1)} %get-tuple-element.56), channel_id=1, source_target_pairs={{0,4},{8,12},{4,0},{12,8},{1,5},{9,13},{5,1},{13,9},{2,6},{10,14},... | collective-permute-start | bytes 786440 | tf_op jit(solution)/shard_map/ppermute | solution.py:655
  21.4 0.7 %collective-permute-start.7 = (f32[8,32,256]{2,1,0:T(8,128)S(1)}, f32[8,32,256]{2,1,0:T(8,128)S(1)}, u32[]{:S(2)}, u32[]{:S(2)}) collective-permute-start(f32[8,32,256]{2,1,0:T(8,128)S(1)} %get-tuple-element.57), channel_id=1, source_target_pairs={{4,8},{8,4},{5,9},{9,5},{6,10},{10,6},{7,11},{11,7},{20,24},{24,20... | collective-permute-start | bytes 786440 | tf_op jit(solution)/shard_map/ppermute | solution.py:655
  22.0 0.6 %collective-permute-start.4 = (f32[8,16,256]{2,1,0:T(8,128)S(1)}, f32[8,16,256]{2,1,0:T(8,128)S(1)}, u32[]{:S(2)}, u32[]{:S(2)}) collective-permute-start(f32[8,16,256]{2,1,0:T(8,128)S(1)} %get-tuple-element.50), channel_id=1, source_target_pairs={{0,2},{2,0},{1,3},{3,1},{4,6},{6,4},{5,7},{7,5},{8,10},{10,8},{9,1... | collective-permute-start | bytes 393224 | tf_op jit(solution)/shard_map/ppermute | solution.py:655
  22.6 0.0 collective-permute-done.5.after.refs_1_
  22.6 0.6 %shard_map.125 = (f32[2,8,256]{2,1,0:T(8,128)S(1)}, f32[2,8,256]{2,1,0:T(8,128)S(1)}) custom-call(s32[3]{0:T(128)S(1)} %pad_add_fusion.pos, f32[16,32,128]{2,1,0:T(8,128)S(1)} %collective-permute-done.5.after.refs_1_, f32[16,32,256]{2,1,0:T(8,128)S(1)} %get-tuple-element.54.v.refs_4_.v0, f32[16,32,256]{2,1,0:T(8,128)S(1)} %get-tuple-element.55.rd.refs_5_), custom_call_target="tpu_custom_call" | custom-call | flops 1024 | bytes 1343500 | tf_op jit(solution)/shard_map/pallas_call | solution.py:690
  23.2 3.5 %collective-permute-start.8 = (f32[2,8,256]{2,1,0:T(8,128)S(1)}, f32[2,8,256]{2,1,0:T(8,128)S(1)}, u32[]{:S(2)}, u32[]{:S(2)}) collective-permute-start(f32[2,8,256]{2,1,0:T(8,128)S(1)} %get-tuple-element.58), channel_id=1, source_target_pairs={{0,6},{2,4},{8,14},{10,12},{6,0},{4,2},{14,8},{12,10},{1,7},{3,5},... | collective-permute-start | bytes 49160 | tf_op jit(solution)/shard_map/ppermute | solution.py:655
  26.7 0.7 %collective-permute-start.9 = (f32[2,8,256]{2,1,0:T(8,128)S(1)}, f32[2,8,256]{2,1,0:T(8,128)S(1)}, u32[]{:S(2)}, u32[]{:S(2)}) collective-permute-start(f32[2,8,256]{2,1,0:T(8,128)S(1)} %get-tuple-element.59), channel_id=1, source_target_pairs={{4,10},{6,8},{10,4},{8,6},{5,11},{7,9},{11,5},{9,7},{20,26},{22,24... | collective-permute-start | bytes 49160 | tf_op jit(solution)/shard_map/ppermute | solution.py:655
  27.4 0.3 collective-permute-done.4.refs_0_.refs_8_.refs_2_
  27.7 0.0 copy-done.5
  27.7 0.0 copy-done.9
  27.7 0.0 copy-done.6
  27.7 3.6 %shard_map.126 = (f32[3,16,32,256]{3,2,1,0:T(8,128)}, f32[3,16,32,256]{3,2,1,0:T(8,128)}, f32[8,128]{1,0:T(8,128)S(1)}) custom-call(s32[3]{0:T(128)S(1)} %pad_add_fusion.pos, f32[4,4]{1,0:T(4,128)S(1)} %pad_maximum_fusion.table, f32[3]{0:T(128)S(1)} %copy-done.9, f32[3,16,32,256]{3,2,1,0:T(8,128)S(1)} %copy-done.1, f32[3,16,32,256]{3,2,1,0:T(8,128)S(1)} %copy-done.5, ...), custom_call_target="tpu_custom_call" | custom-call | flops 7208960 | bytes 11276376 | tf_op jit(solution)/shard_map/pallas_call | solution.py:690
  31.3 0.0 collective-permute-done.6.refs_6_.refs_0_
  31.3 0.0 collective-permute-done.7.refs_7_.refs_1_
  31.3 0.0 collective-permute-done.8.refs_9_.refs_3_
  31.3 0.0 collective-permute-done.9.refs_10_.refs_4_
  31.3 0.9 %shard_map.128 = f32[22,40,128]{2,1,0:T(8,128)S(1)} custom-call(s32[3]{0:T(128)S(1)} %pad_add_fusion.pos, f32[16,32,256]{2,1,0:T(8,128)S(1)} %get-tuple-element.54.v.refs_4_.v0, f32[16,32,256]{2,1,0:T(8,128)S(1)} %get-tuple-element.55.rd.refs_5_, f32[8,128]{1,0:T(8,128)S(1)} %get-tuple-element.68.token, ...), custom_call_target="tpu_custom_call" | custom-call | flops 524288 | bytes 2191372 | tf_op jit(solution)/shard_map/pallas_call | solution.py:690
  32.2 0.1 collective-permute-start.10
  32.3 1.6 %shard_map.127 = (f32[3,16,32,256]{3,2,1,0:T(8,128)}, f32[3,16,32,256]{3,2,1,0:T(8,128)}, f32[22,40,256]{2,1,0:T(8,128)S(1)}, f32[22,40,256]{2,1,0:T(8,128)S(1)}) custom-call(s32[3]{0:T(128)S(1)} %pad_add_fusion.pos, f32[4,4]{1,0:T(4,128)S(1)} %pad_maximum_fusion.table, f32[3]{0:T(128)S(1)} %copy-done.9, ...), custom_call_target="tpu_custom_call", output_to_operand_aliasing={{0}: (18, {}), {1}: (19, {})} | custom-call | flops 1572864 | bytes 17956952 | tf_op jit(solution)/shard_map/pallas_call | solution.py:690
  33.9 0.2 collective-permute-done.10.z_got
  34.1 3.1 %shard_map.129 = (f32[16,32,256]{2,1,0:T(8,128)S(1)}, f32[16,32,256]{2,1,0:T(8,128)S(1)}, f32[16,8,128]{2,1,0:T(8,128)S(1)}) custom-call(s32[3]{0:T(128)S(1)} %pad_add_fusion.pos, f32[22,40,256]{2,1,0:T(8,128)S(1)} %get-tuple-element.65.main_v, f32[22,40,256]{2,1,0:T(8,128)S(1)} %get-tuple-element.66.main_rd, f32[8,128]{1,0:T(8,128)S(1)} %get-tuple-element.67.mom, ...), custom_call_target="tpu_custom_call" | custom-call | flops 7864320 | bytes 3371020 | tf_op jit(solution)/shard_map/pallas_call | solution.py:690
  37.2 10.9 %all_to_all.5.mom = f32[16,8,128]{2,1,0:T(8,128)S(1)} all-to-all(f32[16,8,128]{2,1,0:T(8,128)S(1)} %get-tuple-element.69), channel_id=1, replica_groups=mesh['case'=2,'gx'=4,'gy'=2,'gz'=2] {'gx','gy','gz'}, dimensions={0} | all-to-all | bytes 131072 | tf_op jit(solution)/shard_map/all_to_all | solution.py:854
  48.1 1.7 %shard_map.130 = f32[16,32,256]{2,1,0:T(8,128)} custom-call(f32[16,8,128]{2,1,0:T(8,128)S(1)} %all_to_all.5.mom, f32[16,32,256]{2,1,0:T(8,128)S(1)} %get-tuple-element.54.v.refs_4_.v0, f32[16,32,256]{2,1,0:T(8,128)S(1)} %get-tuple-element.70.v1, f32[16,32,256]{2,1,0:T(8,128)S(1)} %get-tuple-element.71.v2, f32[16,32,256]{2,1,0:T(8,128)S(1)} %copy-done.3), custom_call_target="tpu_custom_call" | custom-call | flops 1048576 | bytes 2686976 | tf_op jit(solution)/shard_map/pallas_call | solution.py:690
  (2 shorter events, 0.0 us)
Async XLA Ops:
  0.7 1.0 %copy-start.2 = (f32[16,32,256]{2,1,0:T(8,128)S(1)}, f32[16,32,256]{2,1,0:T(8,128)}, u32[]{:S(2)}) copy-start(f32[16,32,256]{2,1,0:T(8,128)} %damage_hbm.1) | copy-start | bytes 1572868
  1.8 6.2 %copy-start.3 = (f32[16,32,256]{2,1,0:T(8,128)S(1)}, f32[16,32,256]{2,1,0:T(8,128)}, u32[]{:S(2)}) copy-start(f32[16,32,256]{2,1,0:T(8,128)} %damage_hbm.1) | copy-start | bytes 1572868
  2.5 1.4 %copy-start = (f32[3,16,32,256]{3,2,1,0:T(8,128)S(1)}, f32[3,16,32,256]{3,2,1,0:T(8,128)}, u32[]{:S(2)}) copy-start(f32[3,16,32,256]{3,2,1,0:T(8,128)} %disp.11) | copy-start | bytes 4718596
  3.9 4.0 %copy-start.1 = (f32[3,16,32,256]{3,2,1,0:T(8,128)S(1)}, f32[3,16,32,256]{3,2,1,0:T(8,128)}, u32[]{:S(2)}) copy-start(f32[3,16,32,256]{3,2,1,0:T(8,128)} %disp.11) | copy-start | bytes 4718596
  4.9 5.9 %copy-start.10 = (f32[4,4]{1,0:T(4,128)S(1)}, f32[4,4]{1,0:T(4,128)}, u32[]{:S(2)}) copy-start(f32[4,4]{1,0:T(4,128)} %param.16) | copy-start | bytes 196
  4.9 6.0 %copy-start.4 = (s32[16,32,256]{2,1,0:T(8,128)S(1)}, s32[16,32,256]{2,1,0:T(8,128)}, u32[]{:S(2)}) copy-start(s32[16,32,256]{2,1,0:T(8,128)} %labels.7) | copy-start | bytes 1572868
  4.9 6.0 %copy-start.7 = (f32[16,32,256]{2,1,0:T(8,128)S(1)}, f32[16,32,256]{2,1,0:T(8,128)}, u32[]{:S(2)}) copy-start(f32[16,32,256]{2,1,0:T(8,128)} %history.3) | copy-start | bytes 1572868
  4.9 6.0 %copy-start.8 = (s32[16,32,256]{2,1,0:T(8,128)S(1)}, s32[16,32,256]{2,1,0:T(8,128)}, u32[]{:S(2)}) copy-start(s32[16,32,256]{2,1,0:T(8,128)} %notch.3) | copy-start | bytes 1572868
  4.9 5.9 %collective-permute-start = (f32[4,16,256]{2,1,0:T(8,128)S(1)}, f32[4,16,256]{2,1,0:T(8,128)S(1)}, u32[]{:S(2)}, u32[]{:S(2)}) collective-permute-start(f32[4,16,256]{2,1,0:T(8,128)S(1)} %get-tuple-element.40), channel_id=1, source_target_pairs={{0,2},{2,0},{1,3},{3,1},{4,6},{6,4},{5,7},{7,5},{8,10},{10,8},{9,1... | collective-permute-start | bytes 196616 | tf_op jit(solution)/shard_map/ppermute | solution.py:655
  7.9 2.9 %collective-permute-start.1 = (f32[16,32,128]{2,1,0:T(8,128)S(1)}, f32[16,32,128]{2,1,0:T(8,128)S(1)}, u32[]{:S(2)}, u32[]{:S(2)}) collective-permute-start(f32[16,32,128]{2,1,0:T(8,128)S(1)} %get-tuple-element.41.after), channel_id=1, source_target_pairs={{0,1},{1,0},{2,3},{3,2},{4,5},{5,4},{6,7},{7,6},{8,9},{9,8},{10,11... | collective-permute-start | bytes 786440 | tf_op jit(solution)/shard_map/ppermute | solution.py:655
  8.5 6.6 %collective-permute-start.2 = (f32[4,32,256]{2,1,0:T(8,128)S(1)}, f32[4,32,256]{2,1,0:T(8,128)S(1)}, u32[]{:S(2)}, u32[]{:S(2)}) collective-permute-start(f32[4,32,256]{2,1,0:T(8,128)S(1)} %get-tuple-element.42), channel_id=1, source_target_pairs={{0,4},{8,12},{4,0},{12,8},{1,5},{9,13},{5,1},{13,9},{2,6},{10,14},... | collective-permute-start | bytes 393224 | tf_op jit(solution)/shard_map/ppermute | solution.py:655
  10.2 5.0 %collective-permute-start.3 = (f32[4,32,256]{2,1,0:T(8,128)S(1)}, f32[4,32,256]{2,1,0:T(8,128)S(1)}, u32[]{:S(2)}, u32[]{:S(2)}) collective-permute-start(f32[4,32,256]{2,1,0:T(8,128)S(1)} %get-tuple-element.43), channel_id=1, source_target_pairs={{4,8},{8,4},{5,9},{9,5},{6,10},{10,6},{7,11},{11,7},{20,24},{24,20... | collective-permute-start | bytes 393224 | tf_op jit(solution)/shard_map/ppermute | solution.py:655
  15.1 12.5 %copy-start.5 = (f32[3,16,32,256]{3,2,1,0:T(8,128)S(1)}, f32[3,16,32,256]{3,2,1,0:T(8,128)}, u32[]{:S(2)}) copy-start(f32[3,16,32,256]{3,2,1,0:T(8,128)} %vel.3) | copy-start | bytes 4718596
  15.1 12.5 %copy-start.9 = (f32[3]{0:T(128)S(1)}, f32[3]{0:T(128)}, u32[]{:S(2)}) copy-start(f32[3]{0:T(128)} %impact.3) | copy-start | bytes 40
  16.8 10.9 %copy-start.6 = (s32[16,32,256]{2,1,0:T(8,128)S(1)}, s32[16,32,256]{2,1,0:T(8,128)}, u32[]{:S(2)}) copy-start(s32[16,32,256]{2,1,0:T(8,128)} %contact.3) | copy-start | bytes 1572868
  16.8 5.8 %collective-permute-start.5 = (f32[16,32,128]{2,1,0:T(8,128)S(1)}, f32[16,32,128]{2,1,0:T(8,128)S(1)}, u32[]{:S(2)}, u32[]{:S(2)}) collective-permute-start(f32[16,32,128]{2,1,0:T(8,128)S(1)} %get-tuple-element.51), channel_id=1, source_target_pairs={{0,1},{1,0},{2,3},{3,2},{4,5},{5,4},{6,7},{7,6},{8,9},{9,8},{10,11... | collective-permute-start | bytes 786440 | tf_op jit(solution)/shard_map/ppermute | solution.py:655
  17.1 14.2 %collective-permute-start.6 = (f32[8,32,256]{2,1,0:T(8,128)S(1)}, f32[8,32,256]{2,1,0:T(8,128)S(1)}, u32[]{:S(2)}, u32[]{:S(2)}) collective-permute-start(f32[8,32,256]{2,1,0:T(8,128)S(1)} %get-tuple-element.56), channel_id=1, source_target_pairs={{0,4},{8,12},{4,0},{12,8},{1,5},{9,13},{5,1},{13,9},{2,6},{10,14},... | collective-permute-start | bytes 786440 | tf_op jit(solution)/shard_map/ppermute | solution.py:655
  21.4 9.9 %collective-permute-start.7 = (f32[8,32,256]{2,1,0:T(8,128)S(1)}, f32[8,32,256]{2,1,0:T(8,128)S(1)}, u32[]{:S(2)}, u32[]{:S(2)}) collective-permute-start(f32[8,32,256]{2,1,0:T(8,128)S(1)} %get-tuple-element.57), channel_id=1, source_target_pairs={{4,8},{8,4},{5,9},{9,5},{6,10},{10,6},{7,11},{11,7},{20,24},{24,20... | collective-permute-start | bytes 786440 | tf_op jit(solution)/shard_map/ppermute | solution.py:655
  22.0 5.6 %collective-permute-start.4 = (f32[8,16,256]{2,1,0:T(8,128)S(1)}, f32[8,16,256]{2,1,0:T(8,128)S(1)}, u32[]{:S(2)}, u32[]{:S(2)}) collective-permute-start(f32[8,16,256]{2,1,0:T(8,128)S(1)} %get-tuple-element.50), channel_id=1, source_target_pairs={{0,2},{2,0},{1,3},{3,1},{4,6},{6,4},{5,7},{7,5},{8,10},{10,8},{9,1... | collective-permute-start | bytes 393224 | tf_op jit(solution)/shard_map/ppermute | solution.py:655
  23.2 8.1 %collective-permute-start.8 = (f32[2,8,256]{2,1,0:T(8,128)S(1)}, f32[2,8,256]{2,1,0:T(8,128)S(1)}, u32[]{:S(2)}, u32[]{:S(2)}) collective-permute-start(f32[2,8,256]{2,1,0:T(8,128)S(1)} %get-tuple-element.58), channel_id=1, source_target_pairs={{0,6},{2,4},{8,14},{10,12},{6,0},{4,2},{14,8},{12,10},{1,7},{3,5},... | collective-permute-start | bytes 49160 | tf_op jit(solution)/shard_map/ppermute | solution.py:655
  26.7 4.6 %collective-permute-start.9 = (f32[2,8,256]{2,1,0:T(8,128)S(1)}, f32[2,8,256]{2,1,0:T(8,128)S(1)}, u32[]{:S(2)}, u32[]{:S(2)}) collective-permute-start(f32[2,8,256]{2,1,0:T(8,128)S(1)} %get-tuple-element.59), channel_id=1, source_target_pairs={{4,10},{6,8},{10,4},{8,6},{5,11},{7,9},{11,5},{9,7},{20,26},{22,24... | collective-permute-start | bytes 49160 | tf_op jit(solution)/shard_map/ppermute | solution.py:655
  32.2 1.9 %collective-permute-start.10 = (f32[22,40,128]{2,1,0:T(8,128)S(1)}, f32[22,40,128]{2,1,0:T(8,128)S(1)}, u32[]{:S(2)}, u32[]{:S(2)}) collective-permute-start(f32[22,40,128]{2,1,0:T(8,128)S(1)} %shard_map.128), channel_id=1, source_target_pairs={{0,1},{1,0},{2,3},{3,2},{4,5},{5,4},{6,7},{7,6},{8,9},{9,8},{10,11... | collective-permute-start | bytes 1351688 | tf_op jit(solution)/shard_map/ppermute | solution.py:655

commit v9 on v8

--- a/solution.py
+++ b/solution.py
@@ -34,26 +34,31 @@
 
 def shift_y(plane, rows):
     lo, hi = rows
-    at = iota2(plane.shape, 0)
-    last = plane.shape[0] - 1
-    upper = jnp.where(at == last, hi, pltpu.roll(plane, last, 0))
-    lower = jnp.where(at == 0, lo, pltpu.roll(plane, 1, 0))
-    return upper, lower
+    tiles = [plane[start : start + 8] for start in range(0, plane.shape[0], 8)]
+    at = iota2(tiles[0].shape, 0)
+    ahead = [pltpu.roll(tile, 7, 0) for tile in tiles]
+    behind = [pltpu.roll(tile, 1, 0) for tile in tiles]
+    upper = [jnp.where(at == 7, b, a) for a, b in zip(ahead, [*ahead[1:], hi])]
+    lower = [jnp.where(at == 0, b, a) for a, b in zip(behind, [lo, *behind[:-1]])]
+    return jnp.concatenate(upper, axis=0), jnp.concatenate(lower, axis=0)
 
 
 def shift_z(plane, column, first_z):
-    at = iota2(plane.shape, 1)
-    last = plane.shape[1] - 1
-    lo = jnp.where(first_z, 0.0, column)
-    hi = jnp.where(first_z, column, 0.0)
-    upper = jnp.where(at == last, hi, pltpu.roll(plane, last, 1))
-    lower = jnp.where(at == 0, lo, pltpu.roll(plane, 1, 1))
-    return upper, lower
-
-
-def send_columns(ref, x, planes, gz, tile=None):
+    tiles = [plane[:, start : start + 128] for start in range(0, plane.shape[1], 128)]
+    at = iota2(tiles[0].shape, 1)
+    wide = jnp.broadcast_to(column, tiles[0].shape)
+    lo, hi = jnp.where(first_z, 0.0, wide), jnp.where(first_z, wide, 0.0)
+    ahead = [pltpu.roll(tile, 127, 1) for tile in tiles]
+    behind = [pltpu.roll(tile, 1, 1) for tile in tiles]
+    upper = [jnp.where(at == 127, b, a) for a, b in zip(ahead, [*ahead[1:], hi])]
+    lower = [jnp.where(at == 0, b, a) for a, b in zip(behind, [lo, *behind[:-1]])]
+    return jnp.concatenate(upper, axis=1), jnp.concatenate(lower, axis=1)
+
+
+def send_columns(ref, x, planes, gz):
     depth = planes[0].shape[1]
     lanes = iota2((planes[0].shape[0], 128), 1)
+    tile = None
     for field, plane in enumerate(planes):
         part = jnp.where(gz == 0, plane[:, depth - 128 :], plane[:, :128])
         part = pltpu.roll(part, field + 1 - gz, 1)
@@ -89,41 +94,20 @@
     return lax.fori_loop(0, count // many, several, carry)
 
 
-def pack_damage_kernel(n_y, pos, damage, *refs):
+def pack_kernel(n_y, pos, disp, damage, *refs):
     ys, zs = refs[:n_y], refs[n_y]
     odd_y, gz = pos[1] == 1, pos[2]
 
     def body(x, carry):
-        plane = damage[x]
-        last = plane.shape[0] - 1
-        send(odd_y, ys, (pl.ds(x, 1), slice(None)), plane[0:1], plane[last : last + 1])
-        send_columns(zs, x, [plane], gz)
-        return carry
-
-    unrolled(damage.shape[0], 8, body, 0)
-
-
-def pack_kernel(n_y, pos, disp, *refs):
-    ys_damage, zs_damage, ys, zs = (
-        refs[:n_y],
-        refs[n_y],
-        refs[n_y + 1 : 2 * n_y + 1],
-        refs[2 * n_y + 1],
-    )
-    odd_y, gz = pos[1] == 1, pos[2]
-    for mine, before in zip(ys, ys_damage, strict=True):
-        mine[3] = before[...]
-
-    def body(x, carry):
-        planes = [disp[0, x], disp[1, x], disp[2, x]]
+        planes = [disp[0, x], disp[1, x], disp[2, x], damage[x]]
         for field, plane in enumerate(planes):
             last = plane.shape[0] - 1
             spot = (field, pl.ds(x, 1), slice(None))
             send(odd_y, ys, spot, plane[0:1], plane[last : last + 1])
-        send_columns(zs, x, planes, gz, pltpu.roll(zs_damage[x], 3, 1))
+        send_columns(zs, x, planes, gz)
         return carry
 
-    unrolled(disp.shape[1], 8, body, 0)
+    unrolled(damage.shape[0], 8, body, 0)
 
 
 def pack_x_kernel(pos, disp, damage, after, *xs):
@@ -218,8 +202,9 @@
     ys, (zs, hist, sems) = refs[n_y + 6 : 2 * n_y + 6], refs[2 * n_y + 6 :]
     steps, many = inner_steps(damage.shape[0])
 
-    def store(x):
-        return pltpu.make_async_copy(hist.at[x], hist_hbm.at[x], sems.at[x])
+    def store(step):
+        part = pl.ds(1 + step * many, many)
+        return pltpu.make_async_copy(hist.at[part], hist_hbm.at[part], sems.at[step])
 
     def several(step, total):
         for at in range(many):
@@ -242,13 +227,13 @@
             v_out[x] = v
             local.send_y(ys, x, v, rd, stress)
             local.send_z(zs, x, stress)
-            store(x).start()
             total = total + part
+        store(step).start()
         return total
 
     mom_out[...] = lax.fori_loop(0, steps, several, jnp.zeros((8, 128), F32))
-    for x in range(1, damage.shape[0] - 1):
-        store(x).wait()
+    for step in range(steps):
+        store(step).wait()
 
 
 def ends_kernel(n_y, pos, table, disp, damage, history, notch, labels, *refs):
@@ -518,10 +503,11 @@
     count = contact.shape[0]
     steps, many = inner_steps(count)
 
-    def stores(x):
+    def stores(step):
+        part = pl.ds(1 + step * many, many)
         return (
-            pltpu.make_async_copy(disp_out.at[:, x], disp_hbm.at[:, x], sems.at[x, 0]),
-            pltpu.make_async_copy(vel_out.at[:, x], vel_hbm.at[:, x], sems.at[x, 1]),
+            pltpu.make_async_copy(disp_out.at[:, part], disp_hbm.at[:, part], sems.at[step, 0]),
+            pltpu.make_async_copy(vel_out.at[:, part], vel_hbm.at[:, part], sems.at[step, 1]),
         )
 
     def several(step, carry):
@@ -539,13 +525,13 @@
                 return stress[k, x + 1]
 
             force.plane(x, lower, lambda k: stress[k, x], upper, vel_out, disp_out, x)
-            for copy in stores(x):
-                copy.start()
+        for copy in stores(step):
+            copy.start()
         return carry
 
     lax.fori_loop(0, steps, several, 0)
-    for x in range(1, count - 1):
-        for copy in stores(x):
+    for step in range(steps):
+        for copy in stores(step):
             copy.wait()
 
 
@@ -719,17 +705,9 @@
     z_pairs = [(0, 1)]
 
     sent = call(
-        functools.partial(pack_damage_kernel, n_y),
-        "sv",
-        (pos, damage),
-        "v" * (1 + n_y),
-        [*[arr(nx, nz)] * n_y, columns],
-        100 * size,
-    )
-    sent = call(
         functools.partial(pack_kernel, n_y),
-        "sv" + "v" * (1 + n_y),
-        (pos, displacement, *sent),
+        "svv",
+        (pos, displacement, damage),
         "v" * (1 + n_y),
         [*[arr(4, nx, nz)] * n_y, columns],
         size,

time: 50.1 us -> 49 us (0.978)
  Pallas kernels: 19.6 us -> 18.4 us
    pallas_call x11 -> x10, Pallas kernels: 19.6 us -> 18.4 us  [call(): pl.pallas_call(kernel, out_shape=outs, in_specs=[spec_of(k, a) for k, a i...]
where the time goes in v9:
time: 49 us; the launch traced here: 48.8 us
  Pallas kernels  18.4 us (38%)
  starting transfers between devices  15.4 us (31%)
  blocking collectives  10.9 us (22%)
  local copies, waits for them, and re-layouts  2.51 us (5%)
  between operations  0.95 us (2%)
    pallas_call x10, Pallas kernels, call(): pl.pallas_call(kernel, out_shape=outs, in_specs=[spec_of(k, a) for k, a i...  18.4 us
    ppermute x11, starting transfers between devices, swap(): return lax.ppermute(array, axis, pairs + [(b, a) for a, b in pairs])  15.4 us
    all_to_all x1, blocking collectives, per_device(): mom = lax.all_to_all(spread, ('gx', 'gy', 'gz'), 0, 0, tiled=True)  10.9 us
    unnamed x22, local copies, waits for them, and re-layouts  2.51 us
  transfers between devices with their start and end apart: 11, of which 2 were waited for; matrix products, arithmetic and copies ran while one was open for 0% of the time, Pallas kernels for 21%

profile of v9, /device:TPU:0, one launch (start us, length us, event | category | flops | bytes accessed | tf_op | source)
XLA Modules:
  0.0 48.8 jit_solution(512485441790948349)
XLA Ops:
  0.6 0.1 pad_add_fusion.pos
  0.7 0.0 copy-start
  0.7 1.4 %copy-done = f32[3,16,32,256]{3,2,1,0:T(8,128)S(1)} copy-done((f32[3,16,32,256]{3,2,1,0:T(8,128)S(1)}, f32[3,16,32,256]{3,2,1,0:T(8,128)}, u32[]{:S(2)}) %copy-start) | copy-done | bytes 1572888
  2.1 0.0 copy-start.2
  2.1 1.0 %copy-done.2 = f32[16,32,256]{2,1,0:T(8,128)S(1)} copy-done((f32[16,32,256]{2,1,0:T(8,128)S(1)}, f32[16,32,256]{2,1,0:T(8,128)}, u32[]{:S(2)}) %copy-start.2) | copy-done | bytes 524312
  3.2 1.0 %shard_map.120 = (f32[4,16,256]{2,1,0:T(8,128)S(1)}, f32[16,32,128]{2,1,0:T(8,128)S(1)}) custom-call(s32[3]{0:T(128)S(1)} %pad_add_fusion.pos, f32[3,16,32,256]{3,2,1,0:T(8,128)S(1)} %copy-done, f32[16,32,256]{2,1,0:T(8,128)S(1)} %copy-done.2), custom_call_target="tpu_custom_call" | custom-call | flops 131072 | bytes 2424844 | tf_op jit(solution)/shard_map/pallas_call | solution.py:676
  4.1 0.0 copy-start.10
  4.1 0.0 copy-start.4
  4.2 0.0 copy-start.7
  4.2 0.0 copy-start.8
  4.2 3.0 %collective-permute-start = (f32[4,16,256]{2,1,0:T(8,128)S(1)}, f32[4,16,256]{2,1,0:T(8,128)S(1)}, u32[]{:S(2)}, u32[]{:S(2)}) collective-permute-start(f32[4,16,256]{2,1,0:T(8,128)S(1)} %get-tuple-element.36), channel_id=1, source_target_pairs={{0,2},{2,0},{1,3},{3,1},{4,6},{6,4},{5,7},{7,5},{8,10},{10,8},{9,1... | collective-permute-start | bytes 196616 | tf_op jit(solution)/shard_map/ppermute | solution.py:641
  7.2 0.0 collective-permute-start.1
  7.2 0.6 %shard_map.121 = (f32[4,32,256]{2,1,0:T(8,128)S(1)}, f32[4,32,256]{2,1,0:T(8,128)S(1)}) custom-call(s32[3]{0:T(128)S(1)} %pad_add_fusion.pos, f32[3,16,32,256]{3,2,1,0:T(8,128)S(1)} %copy-done, f32[16,32,256]{2,1,0:T(8,128)S(1)} %copy-done.2, f32[16,32,128]{2,1,0:T(8,128)S(1)} %get-tuple-element.37.after), custom_call_target="tpu_custom_call" | custom-call | flops 131072 | bytes 2621452 | tf_op jit(solution)/shard_map/pallas_call | solution.py:676
  7.8 1.6 %collective-permute-start.2 = (f32[4,32,256]{2,1,0:T(8,128)S(1)}, f32[4,32,256]{2,1,0:T(8,128)S(1)}, u32[]{:S(2)}, u32[]{:S(2)}) collective-permute-start(f32[4,32,256]{2,1,0:T(8,128)S(1)} %get-tuple-element.38), channel_id=1, source_target_pairs={{0,4},{8,12},{4,0},{12,8},{1,5},{9,13},{5,1},{13,9},{2,6},{10,14},... | collective-permute-start | bytes 393224 | tf_op jit(solution)/shard_map/ppermute | solution.py:641
  9.4 0.7 %collective-permute-start.3 = (f32[4,32,256]{2,1,0:T(8,128)S(1)}, f32[4,32,256]{2,1,0:T(8,128)S(1)}, u32[]{:S(2)}, u32[]{:S(2)}) collective-permute-start(f32[4,32,256]{2,1,0:T(8,128)S(1)} %get-tuple-element.39), channel_id=1, source_target_pairs={{4,8},{8,4},{5,9},{9,5},{6,10},{10,6},{7,11},{11,7},{20,24},{24,20... | collective-permute-start | bytes 393224 | tf_op jit(solution)/shard_map/ppermute | solution.py:641
  10.1 0.0 copy-done.10
  10.1 0.0 collective-permute-done.refs_0_
  10.1 0.0 collective-permute-done.1.refs_1_
  10.1 0.0 copy-done.4
  10.1 0.0 copy-done.7
  10.2 0.0 copy-done.8
  10.2 4.1 %shard_map.122 = (f32[16,32,256]{2,1,0:T(8,128)}, f32[16,32,256]{2,1,0:T(8,128)S(1)}, f32[16,32,256]{2,1,0:T(8,128)S(1)}, f32[6,16,32,256]{3,2,1,0:T(8,128)S(1)}...) custom-call(s32[3]{0:T(128)S(1)} %pad_add_fusion.pos, ...), custom_call_target="tpu_custom_call" | custom-call | flops 18350080 | bytes 9113676 | tf_op jit(solution)/shard_map/pallas_call | solution.py:676
  14.3 0.0 collective-permute-done.2.refs_2_
  14.3 0.0 collective-permute-done.3.refs_3_
  14.3 0.0 copy-start.1
  14.3 0.0 copy-start.5
  14.3 0.0 copy-start.9
  14.3 1.6 %shard_map.123 = (f32[16,32,256]{2,1,0:T(8,128)}, f32[16,32,256]{2,1,0:T(8,128)S(1)}, f32[16,32,256]{2,1,0:T(8,128)S(1)}, f32[6,2,32,256]{3,2,1,0:T(8,128)S(1)},...) custom-call(s32[3]{0:T(128)S(1)} %pad_add_fusion.pos, ...), custom_call_target="tpu_custom_call", output_to_operand_aliasing={{0}: (11, {})} | custom-call | flops 2621440 | bytes 9117772 | tf_op jit(solution)/shard_map/pallas_call | solution.py:676
  15.9 0.0 copy-start.6
  15.9 0.3 collective-permute-start.5
  16.2 4.2 %collective-permute-start.6 = (f32[8,32,256]{2,1,0:T(8,128)S(1)}, f32[8,32,256]{2,1,0:T(8,128)S(1)}, u32[]{:S(2)}, u32[]{:S(2)}) collective-permute-start(f32[8,32,256]{2,1,0:T(8,128)S(1)} %get-tuple-element.52), channel_id=1, source_target_pairs={{0,4},{8,12},{4,0},{12,8},{1,5},{9,13},{5,1},{13,9},{2,6},{10,14},... | collective-permute-start | bytes 786440 | tf_op jit(solution)/shard_map/ppermute | solution.py:641
  20.5 0.7 %collective-permute-start.7 = (f32[8,32,256]{2,1,0:T(8,128)S(1)}, f32[8,32,256]{2,1,0:T(8,128)S(1)}, u32[]{:S(2)}, u32[]{:S(2)}) collective-permute-start(f32[8,32,256]{2,1,0:T(8,128)S(1)} %get-tuple-element.53), channel_id=1, source_target_pairs={{4,8},{8,4},{5,9},{9,5},{6,10},{10,6},{7,11},{11,7},{20,24},{24,20... | collective-permute-start | bytes 786440 | tf_op jit(solution)/shard_map/ppermute | solution.py:641
  21.1 0.6 %collective-permute-start.4 = (f32[8,16,256]{2,1,0:T(8,128)S(1)}, f32[8,16,256]{2,1,0:T(8,128)S(1)}, u32[]{:S(2)}, u32[]{:S(2)}) collective-permute-start(f32[8,16,256]{2,1,0:T(8,128)S(1)} %get-tuple-element.46), channel_id=1, source_target_pairs={{0,2},{2,0},{1,3},{3,1},{4,6},{6,4},{5,7},{7,5},{8,10},{10,8},{9,1... | collective-permute-start | bytes 393224 | tf_op jit(solution)/shard_map/ppermute | solution.py:641
  21.7 0.0 collective-permute-done.5.after.refs_1_
  21.7 0.6 %shard_map.124 = (f32[2,8,256]{2,1,0:T(8,128)S(1)}, f32[2,8,256]{2,1,0:T(8,128)S(1)}) custom-call(s32[3]{0:T(128)S(1)} %pad_add_fusion.pos, f32[16,32,128]{2,1,0:T(8,128)S(1)} %collective-permute-done.5.after.refs_1_, f32[16,32,256]{2,1,0:T(8,128)S(1)} %get-tuple-element.50.v.refs_4_.v0, f32[16,32,256]{2,1,0:T(8,128)S(1)} %get-tuple-element.51.rd.refs_5_), custom_call_target="tpu_custom_call" | custom-call | flops 1024 | bytes 1343500 | tf_op jit(solution)/shard_map/pallas_call | solution.py:676
  22.3 3.6 %collective-permute-start.8 = (f32[2,8,256]{2,1,0:T(8,128)S(1)}, f32[2,8,256]{2,1,0:T(8,128)S(1)}, u32[]{:S(2)}, u32[]{:S(2)}) collective-permute-start(f32[2,8,256]{2,1,0:T(8,128)S(1)} %get-tuple-element.54), channel_id=1, source_target_pairs={{0,6},{2,4},{8,14},{10,12},{6,0},{4,2},{14,8},{12,10},{1,7},{3,5},... | collective-permute-start | bytes 49160 | tf_op jit(solution)/shard_map/ppermute | solution.py:641
  25.9 0.7 %collective-permute-start.9 = (f32[2,8,256]{2,1,0:T(8,128)S(1)}, f32[2,8,256]{2,1,0:T(8,128)S(1)}, u32[]{:S(2)}, u32[]{:S(2)}) collective-permute-start(f32[2,8,256]{2,1,0:T(8,128)S(1)} %get-tuple-element.55), channel_id=1, source_target_pairs={{4,10},{6,8},{10,4},{8,6},{5,11},{7,9},{11,5},{9,7},{20,26},{22,24... | collective-permute-start | bytes 49160 | tf_op jit(solution)/shard_map/ppermute | solution.py:641
  26.6 0.2 collective-permute-done.4.refs_0_.refs_8_.refs_2_
  26.8 0.0 copy-done.1
  26.8 0.0 copy-done.5
  26.8 0.0 copy-done.9
  26.8 0.0 copy-done.6
  26.8 3.4 %shard_map.125 = (f32[3,16,32,256]{3,2,1,0:T(8,128)}, f32[3,16,32,256]{3,2,1,0:T(8,128)}, f32[8,128]{1,0:T(8,128)S(1)}) custom-call(s32[3]{0:T(128)S(1)} %pad_add_fusion.pos, f32[4,4]{1,0:T(4,128)S(1)} %pad_maximum_fusion.table, f32[3]{0:T(128)S(1)} %copy-done.9, f32[3,16,32,256]{3,2,1,0:T(8,128)S(1)} %copy-done.1, f32[3,16,32,256]{3,2,1,0:T(8,128)S(1)} %copy-done.5, ...), custom_call_target="tpu_custom_call" | custom-call | flops 7208960 | bytes 11276376 | tf_op jit(solution)/shard_map/pallas_call | solution.py:676
  30.2 0.0 collective-permute-done.6.refs_6_.refs_0_
  30.2 0.0 collective-permute-done.7.refs_7_.refs_1_
  30.2 0.0 collective-permute-done.8.refs_9_.refs_3_
  30.2 0.0 collective-permute-done.9.refs_10_.refs_4_
  30.2 0.9 %shard_map.127 = f32[22,40,128]{2,1,0:T(8,128)S(1)} custom-call(s32[3]{0:T(128)S(1)} %pad_add_fusion.pos, f32[16,32,256]{2,1,0:T(8,128)S(1)} %get-tuple-element.50.v.refs_4_.v0, f32[16,32,256]{2,1,0:T(8,128)S(1)} %get-tuple-element.51.rd.refs_5_, f32[8,128]{1,0:T(8,128)S(1)} %get-tuple-element.64.token, ...), custom_call_target="tpu_custom_call" | custom-call | flops 524288 | bytes 2191372 | tf_op jit(solution)/shard_map/pallas_call | solution.py:676
  31.1 0.1 collective-permute-start.10
  31.2 1.6 %shard_map.126 = (f32[3,16,32,256]{3,2,1,0:T(8,128)}, f32[3,16,32,256]{3,2,1,0:T(8,128)}, f32[22,40,256]{2,1,0:T(8,128)S(1)}, f32[22,40,256]{2,1,0:T(8,128)S(1)}) custom-call(s32[3]{0:T(128)S(1)} %pad_add_fusion.pos, f32[4,4]{1,0:T(4,128)S(1)} %pad_maximum_fusion.table, f32[3]{0:T(128)S(1)} %copy-done.9, ...), custom_call_target="tpu_custom_call", output_to_operand_aliasing={{0}: (18, {}), {1}: (19, {})} | custom-call | flops 1572864 | bytes 17956952 | tf_op jit(solution)/shard_map/pallas_call | solution.py:676
  32.8 0.0 copy-start.3
  32.8 0.2 collective-permute-done.10.z_got
  33.0 3.1 %shard_map.128 = (f32[16,32,256]{2,1,0:T(8,128)S(1)}, f32[16,32,256]{2,1,0:T(8,128)S(1)}, f32[16,8,128]{2,1,0:T(8,128)S(1)}) custom-call(s32[3]{0:T(128)S(1)} %pad_add_fusion.pos, f32[22,40,256]{2,1,0:T(8,128)S(1)} %get-tuple-element.61.main_v, f32[22,40,256]{2,1,0:T(8,128)S(1)} %get-tuple-element.62.main_rd, f32[8,128]{1,0:T(8,128)S(1)} %get-tuple-element.63.mom, ...), custom_call_target="tpu_custom_call" | custom-call | flops 7864320 | bytes 3371020 | tf_op jit(solution)/shard_map/pallas_call | solution.py:676
  36.1 10.9 %all_to_all.5.mom = f32[16,8,128]{2,1,0:T(8,128)S(1)} all-to-all(f32[16,8,128]{2,1,0:T(8,128)S(1)} %get-tuple-element.65), channel_id=1, replica_groups=mesh['case'=2,'gx'=4,'gy'=2,'gz'=2] {'gx','gy','gz'}, dimensions={0} | all-to-all | bytes 131072 | tf_op jit(solution)/shard_map/all_to_all | solution.py:832
  47.0 0.0 copy-done.3
  47.0 1.7 %shard_map.129 = f32[16,32,256]{2,1,0:T(8,128)} custom-call(f32[16,8,128]{2,1,0:T(8,128)S(1)} %all_to_all.5.mom, f32[16,32,256]{2,1,0:T(8,128)S(1)} %get-tuple-element.50.v.refs_4_.v0, f32[16,32,256]{2,1,0:T(8,128)S(1)} %get-tuple-element.66.v1, f32[16,32,256]{2,1,0:T(8,128)S(1)} %get-tuple-element.67.v2, f32[16,32,256]{2,1,0:T(8,128)S(1)} %copy-done.3), custom_call_target="tpu_custom_call" | custom-call | flops 1048576 | bytes 2686976 | tf_op jit(solution)/shard_map/pallas_call | solution.py:676
  (2 shorter events, 0.0 us)
Async XLA Ops:
  0.7 1.4 %copy-start = (f32[3,16,32,256]{3,2,1,0:T(8,128)S(1)}, f32[3,16,32,256]{3,2,1,0:T(8,128)}, u32[]{:S(2)}) copy-start(f32[3,16,32,256]{3,2,1,0:T(8,128)} %disp.11) | copy-start | bytes 4718596
  2.1 1.0 %copy-start.2 = (f32[16,32,256]{2,1,0:T(8,128)S(1)}, f32[16,32,256]{2,1,0:T(8,128)}, u32[]{:S(2)}) copy-start(f32[16,32,256]{2,1,0:T(8,128)} %damage_hbm.1) | copy-start | bytes 1572868
  4.1 5.9 %copy-start.10 = (f32[4,4]{1,0:T(4,128)S(1)}, f32[4,4]{1,0:T(4,128)}, u32[]{:S(2)}) copy-start(f32[4,4]{1,0:T(4,128)} %param.16) | copy-start | bytes 196
  4.1 6.0 %copy-start.4 = (s32[16,32,256]{2,1,0:T(8,128)S(1)}, s32[16,32,256]{2,1,0:T(8,128)}, u32[]{:S(2)}) copy-start(s32[16,32,256]{2,1,0:T(8,128)} %labels.7) | copy-start | bytes 1572868
  4.2 6.0 %copy-start.7 = (f32[16,32,256]{2,1,0:T(8,128)S(1)}, f32[16,32,256]{2,1,0:T(8,128)}, u32[]{:S(2)}) copy-start(f32[16,32,256]{2,1,0:T(8,128)} %history.3) | copy-start | bytes 1572868
  4.2 6.0 %copy-start.8 = (s32[16,32,256]{2,1,0:T(8,128)S(1)}, s32[16,32,256]{2,1,0:T(8,128)}, u32[]{:S(2)}) copy-start(s32[16,32,256]{2,1,0:T(8,128)} %notch.3) | copy-start | bytes 1572868
  4.2 5.9 %collective-permute-start = (f32[4,16,256]{2,1,0:T(8,128)S(1)}, f32[4,16,256]{2,1,0:T(8,128)S(1)}, u32[]{:S(2)}, u32[]{:S(2)}) collective-permute-start(f32[4,16,256]{2,1,0:T(8,128)S(1)} %get-tuple-element.36), channel_id=1, source_target_pairs={{0,2},{2,0},{1,3},{3,1},{4,6},{6,4},{5,7},{7,5},{8,10},{10,8},{9,1... | collective-permute-start | bytes 196616 | tf_op jit(solution)/shard_map/ppermute | solution.py:641
  7.2 2.9 %collective-permute-start.1 = (f32[16,32,128]{2,1,0:T(8,128)S(1)}, f32[16,32,128]{2,1,0:T(8,128)S(1)}, u32[]{:S(2)}, u32[]{:S(2)}) collective-permute-start(f32[16,32,128]{2,1,0:T(8,128)S(1)} %get-tuple-element.37.after), channel_id=1, source_target_pairs={{0,1},{1,0},{2,3},{3,2},{4,5},{5,4},{6,7},{7,6},{8,9},{9,8},{10,11... | collective-permute-start | bytes 786440 | tf_op jit(solution)/shard_map/ppermute | solution.py:641
  7.8 6.5 %collective-permute-start.2 = (f32[4,32,256]{2,1,0:T(8,128)S(1)}, f32[4,32,256]{2,1,0:T(8,128)S(1)}, u32[]{:S(2)}, u32[]{:S(2)}) collective-permute-start(f32[4,32,256]{2,1,0:T(8,128)S(1)} %get-tuple-element.38), channel_id=1, source_target_pairs={{0,4},{8,12},{4,0},{12,8},{1,5},{9,13},{5,1},{13,9},{2,6},{10,14},... | collective-permute-start | bytes 393224 | tf_op jit(solution)/shard_map/ppermute | solution.py:641
  9.4 4.9 %collective-permute-start.3 = (f32[4,32,256]{2,1,0:T(8,128)S(1)}, f32[4,32,256]{2,1,0:T(8,128)S(1)}, u32[]{:S(2)}, u32[]{:S(2)}) collective-permute-start(f32[4,32,256]{2,1,0:T(8,128)S(1)} %get-tuple-element.39), channel_id=1, source_target_pairs={{4,8},{8,4},{5,9},{9,5},{6,10},{10,6},{7,11},{11,7},{20,24},{24,20... | collective-permute-start | bytes 393224 | tf_op jit(solution)/shard_map/ppermute | solution.py:641
  14.3 12.5 %copy-start.1 = (f32[3,16,32,256]{3,2,1,0:T(8,128)S(1)}, f32[3,16,32,256]{3,2,1,0:T(8,128)}, u32[]{:S(2)}) copy-start(f32[3,16,32,256]{3,2,1,0:T(8,128)} %disp.11) | copy-start | bytes 4718596
  14.3 12.5 %copy-start.5 = (f32[3,16,32,256]{3,2,1,0:T(8,128)S(1)}, f32[3,16,32,256]{3,2,1,0:T(8,128)}, u32[]{:S(2)}) copy-start(f32[3,16,32,256]{3,2,1,0:T(8,128)} %vel.3) | copy-start | bytes 4718596
  14.3 12.5 %copy-start.9 = (f32[3]{0:T(128)S(1)}, f32[3]{0:T(128)}, u32[]{:S(2)}) copy-start(f32[3]{0:T(128)} %impact.3) | copy-start | bytes 40
  15.9 10.9 %copy-start.6 = (s32[16,32,256]{2,1,0:T(8,128)S(1)}, s32[16,32,256]{2,1,0:T(8,128)}, u32[]{:S(2)}) copy-start(s32[16,32,256]{2,1,0:T(8,128)} %contact.3) | copy-start | bytes 1572868
  15.9 5.8 %collective-permute-start.5 = (f32[16,32,128]{2,1,0:T(8,128)S(1)}, f32[16,32,128]{2,1,0:T(8,128)S(1)}, u32[]{:S(2)}, u32[]{:S(2)}) collective-permute-start(f32[16,32,128]{2,1,0:T(8,128)S(1)} %get-tuple-element.47), channel_id=1, source_target_pairs={{0,1},{1,0},{2,3},{3,2},{4,5},{5,4},{6,7},{7,6},{8,9},{9,8},{10,11... | collective-permute-start | bytes 786440 | tf_op jit(solution)/shard_map/ppermute | solution.py:641
  16.2 14.0 %collective-permute-start.6 = (f32[8,32,256]{2,1,0:T(8,128)S(1)}, f32[8,32,256]{2,1,0:T(8,128)S(1)}, u32[]{:S(2)}, u32[]{:S(2)}) collective-permute-start(f32[8,32,256]{2,1,0:T(8,128)S(1)} %get-tuple-element.52), channel_id=1, source_target_pairs={{0,4},{8,12},{4,0},{12,8},{1,5},{9,13},{5,1},{13,9},{2,6},{10,14},... | collective-permute-start | bytes 786440 | tf_op jit(solution)/shard_map/ppermute | solution.py:641
  20.5 9.7 %collective-permute-start.7 = (f32[8,32,256]{2,1,0:T(8,128)S(1)}, f32[8,32,256]{2,1,0:T(8,128)S(1)}, u32[]{:S(2)}, u32[]{:S(2)}) collective-permute-start(f32[8,32,256]{2,1,0:T(8,128)S(1)} %get-tuple-element.53), channel_id=1, source_target_pairs={{4,8},{8,4},{5,9},{9,5},{6,10},{10,6},{7,11},{11,7},{20,24},{24,20... | collective-permute-start | bytes 786440 | tf_op jit(solution)/shard_map/ppermute | solution.py:641
  21.1 5.6 %collective-permute-start.4 = (f32[8,16,256]{2,1,0:T(8,128)S(1)}, f32[8,16,256]{2,1,0:T(8,128)S(1)}, u32[]{:S(2)}, u32[]{:S(2)}) collective-permute-start(f32[8,16,256]{2,1,0:T(8,128)S(1)} %get-tuple-element.46), channel_id=1, source_target_pairs={{0,2},{2,0},{1,3},{3,1},{4,6},{6,4},{5,7},{7,5},{8,10},{10,8},{9,1... | collective-permute-start | bytes 393224 | tf_op jit(solution)/shard_map/ppermute | solution.py:641
  22.3 7.9 %collective-permute-start.8 = (f32[2,8,256]{2,1,0:T(8,128)S(1)}, f32[2,8,256]{2,1,0:T(8,128)S(1)}, u32[]{:S(2)}, u32[]{:S(2)}) collective-permute-start(f32[2,8,256]{2,1,0:T(8,128)S(1)} %get-tuple-element.54), channel_id=1, source_target_pairs={{0,6},{2,4},{8,14},{10,12},{6,0},{4,2},{14,8},{12,10},{1,7},{3,5},... | collective-permute-start | bytes 49160 | tf_op jit(solution)/shard_map/ppermute | solution.py:641
  25.9 4.3 %collective-permute-start.9 = (f32[2,8,256]{2,1,0:T(8,128)S(1)}, f32[2,8,256]{2,1,0:T(8,128)S(1)}, u32[]{:S(2)}, u32[]{:S(2)}) collective-permute-start(f32[2,8,256]{2,1,0:T(8,128)S(1)} %get-tuple-element.55), channel_id=1, source_target_pairs={{4,10},{6,8},{10,4},{8,6},{5,11},{7,9},{11,5},{9,7},{20,26},{22,24... | collective-permute-start | bytes 49160 | tf_op jit(solution)/shard_map/ppermute | solution.py:641
  31.1 1.9 %collective-permute-start.10 = (f32[22,40,128]{2,1,0:T(8,128)S(1)}, f32[22,40,128]{2,1,0:T(8,128)S(1)}, u32[]{:S(2)}, u32[]{:S(2)}) collective-permute-start(f32[22,40,128]{2,1,0:T(8,128)S(1)} %shard_map.127), channel_id=1, source_target_pairs={{0,1},{1,0},{2,3},{3,2},{4,5},{5,4},{6,7},{7,6},{8,9},{9,8},{10,11... | collective-permute-start | bytes 1351688 | tf_op jit(solution)/shard_map/ppermute | solution.py:641
  32.8 14.3 %copy-start.3 = (f32[16,32,256]{2,1,0:T(8,128)S(1)}, f32[16,32,256]{2,1,0:T(8,128)}, u32[]{:S(2)}) copy-start(f32[16,32,256]{2,1,0:T(8,128)} %damage_hbm.1) | copy-start | bytes 1572868

commit v10 on v9

--- a/solution.py
+++ b/solution.py
@@ -198,13 +198,9 @@
     local = Local(
         pos, table, disp, damage, history, notch, labels, refs[:n_y], refs[n_y]
     )
-    hist_hbm, rd_out, v_out, stress_out, mom_out = refs[n_y + 1 : n_y + 6]
-    ys, (zs, hist, sems) = refs[n_y + 6 : 2 * n_y + 6], refs[2 * n_y + 6 :]
+    hist, rd_out, v_out, stress_out, mom_out = refs[n_y + 1 : n_y + 6]
+    ys, zs = refs[n_y + 6 : 2 * n_y + 6], refs[2 * n_y + 6]
     steps, many = inner_steps(damage.shape[0])
-
-    def store(step):
-        part = pl.ds(1 + step * many, many)
-        return pltpu.make_async_copy(hist.at[part], hist_hbm.at[part], sems.at[step])
 
     def several(step, total):
         for at in range(many):
@@ -228,12 +224,9 @@
             local.send_y(ys, x, v, rd, stress)
             local.send_z(zs, x, stress)
             total = total + part
-        store(step).start()
         return total
 
     mom_out[...] = lax.fori_loop(0, steps, several, jnp.zeros((8, 128), F32))
-    for step in range(steps):
-        store(step).wait()
 
 
 def ends_kernel(n_y, pos, table, disp, damage, history, notch, labels, *refs):
@@ -241,18 +234,18 @@
         pos, table, disp, damage, history, notch, labels, refs[:n_y], refs[n_y]
     )
     refs = refs[n_y + 1 :]
-    xg, (_, rd_in, v_in, mom), ys_in, zs_in = (
+    xg, (rd_in, v_in, mom), ys_in, zs_in = (
         refs[:2],
-        refs[2:6],
-        refs[6 : 6 + n_y],
-        refs[6 + n_y],
-    )
-    refs = refs[7 + n_y :]
-    hist_hbm, rd_out, v_out, stress_out, mom_out = refs[:5]
-    xs, ys, (zs, hist, sems) = refs[5:7], refs[7 : 7 + n_y], refs[7 + n_y :]
+        refs[2:5],
+        refs[5 : 5 + n_y],
+        refs[5 + n_y],
+    )
+    refs = refs[6 + n_y :]
+    hist, rd_out, v_out, stress_out, mom_out = refs[:5]
+    xs, ys, zs = refs[5:7], refs[7 : 7 + n_y], refs[7 + n_y]
     odd_x, count = local.odd_x, damage.shape[0]
     total = mom[...]
-    copies, found = [], []
+    found = []
     for end, x in enumerate((0, count - 1)):
 
         def outside(c):
@@ -273,8 +266,6 @@
 
         hist_x, rd, v, part = local.plane(x, *sides, put)
         hist[end] = hist_x
-        copies.append(pltpu.make_async_copy(hist.at[end], hist_hbm.at[x], sems.at[end]))
-        copies[-1].start()
         rd_out[x] = rd
         v_out[x] = v
         total = total + part
@@ -299,8 +290,6 @@
         send(odd_x, xs, slot, stress_out[k, 0], stress_out[k, 1])
     mom_out[...] = jnp.zeros((8, 128), F32)
     mom_out[0:1, :] = jnp.sum(total, axis=0, keepdims=True)
-    for copy in copies:
-        copy.wait()
 
 
 def corner_kernel(n_y, pos, after, v, rd, *ds):
@@ -403,8 +392,19 @@
 
 
 def krylov_kernel(pos, main_v, main_rd, mom, z_got, *refs):
-    v1_out, v2_out, spread, z_v, z_rd, big_v1, big_v2 = refs
+    moved, moved_ends, moved_hbm = refs[:2], refs[2:4], refs[4:6]
+    v1_out, v2_out, spread, z_v, z_rd, big_v1, big_v2, sems = refs[6:]
     count, ny, nz = v1_out.shape
+    inner = pl.ds(1, count - 2)
+    copies = []
+    for which, (src, ends, dst) in enumerate(zip(moved, moved_ends, moved_hbm)):
+        for c in range(3):
+            copies.append((src.at[c, inner], dst.at[c, inner], sems.at[which, c]))
+        copies.append((ends.at[:, 0], dst.at[:, 0], sems.at[which, 3]))
+        copies.append((ends.at[:, 1], dst.at[:, count - 1], sems.at[which, 4]))
+    copies = [pltpu.make_async_copy(*copy) for copy in copies]
+    for copy in copies:
+        copy.start()
 
     def split(p, carry):
         tile = z_got[p]
@@ -469,6 +469,8 @@
         result = jnp.where(rows == at + 1, jnp.sum(total, axis=0, keepdims=True), result)
     for peer in range(spread.shape[0]):
         spread[peer] = result
+    for copy in copies:
+        copy.wait()
 
 
 PARTS = ((0, 3, 4), (3, 1, 5), (4, 5, 2))
@@ -497,18 +499,20 @@
 
 def force_inner_kernel(n_y, pos, table, impact, disp, vel, contact, labels, *refs):
     yg, zg, stress, ends = refs[:n_y], refs[n_y], refs[n_y + 1], refs[n_y + 2]
-    disp_hbm, vel_hbm, token, disp_out, vel_out, sems = refs[n_y + 3 :]
+    hist, hist_ends, hist_hbm, disp_out, vel_out, token, sems = refs[n_y + 3 :]
     token[...] = jnp.zeros((8, 128), F32)
     force = Force(n_y, pos, table, impact, disp, vel, contact, labels, yg, zg)
     count = contact.shape[0]
     steps, many = inner_steps(count)
 
-    def stores(step):
-        part = pl.ds(1 + step * many, many)
-        return (
-            pltpu.make_async_copy(disp_out.at[:, part], disp_hbm.at[:, part], sems.at[step, 0]),
-            pltpu.make_async_copy(vel_out.at[:, part], vel_hbm.at[:, part], sems.at[step, 1]),
-        )
+    inside = pl.ds(1, count - 2)
+    copies = [
+        pltpu.make_async_copy(hist.at[inside], hist_hbm.at[inside], sems.at[0]),
+        pltpu.make_async_copy(hist_ends.at[0], hist_hbm.at[0], sems.at[1]),
+        pltpu.make_async_copy(hist_ends.at[1], hist_hbm.at[count - 1], sems.at[2]),
+    ]
+    for copy in copies:
+        copy.start()
 
     def several(step, carry):
         for at in range(many):
@@ -525,14 +529,11 @@
                 return stress[k, x + 1]
 
             force.plane(x, lower, lambda k: stress[k, x], upper, vel_out, disp_out, x)
-        for copy in stores(step):
-            copy.start()
         return carry
 
     lax.fori_loop(0, steps, several, 0)
-    for step in range(steps):
-        for copy in stores(step):
-            copy.wait()
+    for copy in copies:
+        copy.wait()
 
 
 def rest_kernel(n_y, pos, table, impact, disp, vel, contact, labels, *refs):
@@ -540,10 +541,9 @@
     refs = refs[n_y + 3 :]
     v, rd, xy = refs[0], refs[1], refs[2 : 4 + 3 * n_y]
     xg = xy[:2]
-    disp_hbm, vel_hbm, big_v, big_rd, disp_out, vel_out, sems = refs[6 + 3 * n_y :]
+    disp_out, vel_out, big_v, big_rd = refs[4 + 3 * n_y :]
     force = Force(n_y, pos, table, impact, disp, vel, contact, labels, yg, zg)
     count, ny = contact.shape[0], contact.shape[1]
-    copies = []
     for end, x in enumerate((0, count - 1)):
 
         def outside(c, k):
@@ -557,10 +557,6 @@
 
         lower, upper = (outside, beside) if end == 0 else (beside, outside)
         force.plane(x, lower, lambda k: ends[k, end], upper, vel_out, disp_out, end)
-        for which, (src, dst) in enumerate(((disp_out, disp_hbm), (vel_out, vel_hbm))):
-            copy = pltpu.make_async_copy(src.at[:, end], dst.at[:, x], sems.at[end, which])
-            copy.start()
-            copies.append(copy)
     big = Enlarged(n_y, pos, v, rd, xy)
 
     def put(p, parts):
@@ -578,8 +574,6 @@
         return carry
 
     unrolled(count, 4, body, 0)
-    for copy in copies:
-        copy.wait()
 
 
 def cg_coefficients(k):
@@ -610,25 +604,21 @@
     return out
 
 
-def final_kernel(mom, v0, v1, v2, damage_hbm, out_hbm, damage, out, in_sems, out_sems):
+def final_kernel(mom, v0, v1, v2, damage, out_hbm, out, sems):
     count = v0.shape[0]
     block = count // CHUNKS
-    loads, stores = [], []
-    for chunk in range(CHUNKS):
-        part = pl.ds(chunk * block, block)
-        loads.append(pltpu.make_async_copy(damage_hbm.at[part], damage.at[part], in_sems.at[chunk]))
-        stores.append(pltpu.make_async_copy(out.at[part], out_hbm.at[part], out_sems.at[chunk]))
-        loads[-1].start()
     sums = jnp.sum(jnp.sum(mom[...], axis=0), axis=1, keepdims=True)
     c0, c1, c2 = cg_coefficients([sums[j : j + 1, :] for j in range(6)])
+    copies = []
     for chunk in range(CHUNKS):
-        loads[chunk].wait()
         for x in range(chunk * block, (chunk + 1) * block):
             dmg = damage[x]
             out[x] = jnp.maximum(dmg + (c0 * v0[x] + c1 * v1[x] + c2 * v2[x]), dmg)
-        stores[chunk].start()
-    for store in stores:
-        store.wait()
+        part = pl.ds(chunk * block, block)
+        copies.append(pltpu.make_async_copy(out.at[part], out_hbm.at[part], sems.at[chunk]))
+        copies[-1].start()
+    for copy in copies:
+        copy.wait()
 
 
 def pairs_of(axis):
@@ -728,19 +718,18 @@
         functools.partial(inner_kernel, n_y),
         "ssvvvvv" + "v" * (1 + n_y),
         voxels,
-        "hvvvv" + "v" * (1 + n_y),
+        "vvvvv" + "v" * (1 + n_y),
         [field, field, field, arr(6, nx, ny, nz), small, *rows, columns],
         140 * size,
-        [pltpu.VMEM((nx, ny, nz), F32), pltpu.SemaphoreType.DMA((nx,))],
-    )
-    more = (*got_x, hist, rd, v0, mom, *sent)
-    hist, rd, v0, ends, mom, *sent = call(
+    )
+    more = (*got_x, rd, v0, mom, *sent)
+    hist_ends, rd, v0, ends, mom, *sent = call(
         functools.partial(ends_kernel, n_y),
-        "ssvvvvv" + "v" * (1 + n_y) + "vvhvvv" + "v" * (1 + n_y),
+        "ssvvvvv" + "v" * (1 + n_y) + "vvvvv" + "v" * (1 + n_y),
         (*voxels, *more),
-        "hvvvv" + "v" * (3 + n_y),
+        "vvvvv" + "v" * (3 + n_y),
         [
-            field,
+            arr(2, ny, nz),
             field,
             field,
             arr(6, 2, ny, nz),
@@ -750,8 +739,6 @@
             columns,
         ],
         20 * size,
-        [pltpu.VMEM((2, ny, nz), F32), pltpu.SemaphoreType.DMA((2,))],
-        [(len(voxels) + 2, 0)],
     )
     stress_z = swap(sent[-1], "gz", z_pairs)
     xs = swap_along("gx", sent[:2])
@@ -778,18 +765,14 @@
         stress,
         ends,
     )
-    new_disp, new_vel, token = call(
+    hist_new, *moved, token = call(
         functools.partial(force_inner_kernel, n_y),
-        "sssvvvv" + "v" * (3 + n_y),
-        moving,
-        "hhv",
-        [fields3, fields3, small],
+        "sssvvvv" + "v" * (3 + n_y) + "vv",
+        (*moving, hist, hist_ends),
+        "hvvv",
+        [field, fields3, fields3, small],
         55 * size,
-        [
-            pltpu.VMEM((3, nx, ny, nz), F32),
-            pltpu.VMEM((3, nx, ny, nz), F32),
-            pltpu.SemaphoreType.DMA((nx, 2)),
-        ],
+        [pltpu.SemaphoreType.DMA((3,))],
     )
     (joined,) = call(
         functools.partial(join_kernel, n_y),
@@ -800,51 +783,41 @@
         4 * size,
     )
     z_got = swap(joined, "gz", z_pairs)
-    new_disp, new_vel, main_v, main_rd = call(
+    *moved_ends, main_v, main_rd = call(
         functools.partial(rest_kernel, n_y),
-        "sssvvvv" + "v" * (3 + n_y) + "vv" + "v" * len(xy) + "hh",
-        (*moving, v0, rd, *xy, new_disp, new_vel),
-        "hhvv",
-        [fields3, fields3, *[arr(nx + 6, ny + 8, nz)] * 2],
+        "sssvvvv" + "v" * (3 + n_y) + "vv" + "v" * len(xy),
+        (*moving, v0, rd, *xy),
+        "vvvv",
+        [arr(3, 2, ny, nz)] * 2 + [arr(nx + 6, ny + 8, nz)] * 2,
         12 * size,
-        [
-            pltpu.VMEM((3, 2, ny, nz), F32),
-            pltpu.VMEM((3, 2, ny, nz), F32),
-            pltpu.SemaphoreType.DMA((2, 2)),
-        ],
-        [(len(moving) + 2 + len(xy), 0), (len(moving) + 3 + len(xy), 1)],
     )
     peers = lax.axis_size("gx") * lax.axis_size("gy") * lax.axis_size("gz")
-    v1, v2, spread = call(
+    new_disp, new_vel, v1, v2, spread = call(
         krylov_kernel,
-        "svvvv",
-        (pos, main_v, main_rd, mom, z_got),
-        "vvv",
-        [field, field, arr(peers, 8, 128)],
+        "svvvvvvvv",
+        (pos, main_v, main_rd, mom, z_got, *moved, *moved_ends),
+        "hhvvv",
+        [fields3, fields3, field, field, arr(peers, 8, 128)],
         60 * size,
         [
             pltpu.VMEM((nx + 6, ny + 8, 128), F32),
             pltpu.VMEM((nx + 6, ny + 8, 128), F32),
             pltpu.VMEM((nx + 4, ny + 8, nz + 128), F32),
             pltpu.VMEM((nx + 2, ny + 8, nz + 128), F32),
+            pltpu.SemaphoreType.DMA((2, 5)),
         ],
     )
     mom = lax.all_to_all(spread, ("gx", "gy", "gz"), 0, 0, tiled=True)
     (damage_new,) = call(
         final_kernel,
-        "vvvvh",
+        "vvvvv",
         (mom, v0, v1, v2, damage),
         "h",
         [field],
         8 * size,
-        [
-            pltpu.VMEM((nx, ny, nz), F32),
-            pltpu.VMEM((nx, ny, nz), F32),
-            pltpu.SemaphoreType.DMA((CHUNKS,)),
-            pltpu.SemaphoreType.DMA((CHUNKS,)),
-        ],
-    )
-    return new_disp, new_vel, hist, damage_new
+        [pltpu.VMEM((nx, ny, nz), F32), pltpu.SemaphoreType.DMA((CHUNKS,))],
+    )
+    return new_disp, new_vel, hist_new, damage_new
 
 
 def solution(mesh):

time: 49 us -> 47.6 us (0.971)
  Pallas kernels: 18.4 us -> 14.6 us
  blocking collectives: 10.9 us -> 12.4 us
  starting transfers between devices: 15.4 us -> 16 us
    pallas_call x10, Pallas kernels: 18.4 us -> 14.6 us  [call(): pl.pallas_call(kernel, out_shape=outs, in_specs=[spec_of(k, a) for k, a i...]
    all_to_all x1, blocking collectives: 10.9 us -> 12.4 us  [per_device(): mom = lax.all_to_all(spread, ('gx', 'gy', 'gz'), 0, 0, tiled=True)]
    ppermute x11, starting transfers between devices: 15.4 us -> 16 us  [swap(): return lax.ppermute(array, axis, pairs + [(b, a) for a, b in pairs])]
  transfers between devices with their start and end apart: 11 -> 11, of which waited for: 2 -> 1; matrix products, arithmetic and copies ran while one was open for 0% -> 0% of each run, Pallas kernels for 21% -> 16%
where the time goes in v10:
time: 47.6 us; the launch traced here: 47.4 us
  starting transfers between devices  16 us (34%)
  Pallas kernels  14.6 us (31%)
  blocking collectives  12.4 us (26%)
  local copies, waits for them, and re-layouts  2.5 us (5%)
  between operations  0.96 us (2%)
  waiting for transfers between devices  0.83 us (2%)
    ppermute x11, starting transfers between devices, swap(): return lax.ppermute(array, axis, pairs + [(b, a) for a, b in pairs])  16 us
    pallas_call x10, Pallas kernels, call(): pl.pallas_call(kernel, out_shape=outs, in_specs=[spec_of(k, a) for k, a i...  14.6 us
    all_to_all x1, blocking collectives, per_device(): mom = lax.all_to_all(spread, ('gx', 'gy', 'gz'), 0, 0, tiled=True)  12.4 us
    unnamed x22, local copies, waits for them, and re-layouts  2.5 us
  transfers between devices with their start and end apart: 11, of which 1 were waited for; matrix products, arithmetic and copies ran while one was open for 0% of the time, Pallas kernels for 16%

profile of v10, /device:TPU:0, one launch (start us, length us, event | category | flops | bytes accessed | tf_op | source)
XLA Modules:
  0.0 47.4 jit_solution(14264663363679923819)
XLA Ops:
  0.6 0.1 pad_add_fusion.pos
  0.7 0.0 copy-start
  0.7 1.4 %copy-done = f32[3,16,32,256]{3,2,1,0:T(8,128)S(1)} copy-done((f32[3,16,32,256]{3,2,1,0:T(8,128)S(1)}, f32[3,16,32,256]{3,2,1,0:T(8,128)}, u32[]{:S(2)}) %copy-start) | copy-done | bytes 1572888
  2.1 0.0 copy-start.2
  2.1 1.0 %copy-done.2 = f32[16,32,256]{2,1,0:T(8,128)S(1)} copy-done((f32[16,32,256]{2,1,0:T(8,128)S(1)}, f32[16,32,256]{2,1,0:T(8,128)}, u32[]{:S(2)}) %copy-start.2) | copy-done | bytes 524312
  3.2 1.0 %shard_map.120 = (f32[4,16,256]{2,1,0:T(8,128)S(1)}, f32[16,32,128]{2,1,0:T(8,128)S(1)}) custom-call(s32[3]{0:T(128)S(1)} %pad_add_fusion.pos, f32[3,16,32,256]{3,2,1,0:T(8,128)S(1)} %copy-done, f32[16,32,256]{2,1,0:T(8,128)S(1)} %copy-done.2), custom_call_target="tpu_custom_call" | custom-call | flops 131072 | bytes 2424844 | tf_op jit(solution)/shard_map/pallas_call | solution.py:666
  4.1 0.0 copy-start.10
  4.1 0.0 copy-start.4
  4.2 0.0 copy-start.7
  4.2 0.0 copy-start.8
  4.2 0.5 %collective-permute-start.1 = (f32[16,32,128]{2,1,0:T(8,128)S(1)}, f32[16,32,128]{2,1,0:T(8,128)S(1)}, u32[]{:S(2)}, u32[]{:S(2)}) collective-permute-start(f32[16,32,128]{2,1,0:T(8,128)S(1)} %get-tuple-element.40.after), channel_id=1, source_target_pairs={{0,1},{1,0},{2,3},{3,2},{4,5},{5,4},{6,7},{7,6},{8,9},{9,8},{10,11... | collective-permute-start | bytes 786440 | tf_op jit(solution)/shard_map/ppermute | solution.py:631
  4.7 2.6 %collective-permute-start = (f32[4,16,256]{2,1,0:T(8,128)S(1)}, f32[4,16,256]{2,1,0:T(8,128)S(1)}, u32[]{:S(2)}, u32[]{:S(2)}) collective-permute-start(f32[4,16,256]{2,1,0:T(8,128)S(1)} %get-tuple-element.39), channel_id=1, source_target_pairs={{0,2},{2,0},{1,3},{3,1},{4,6},{6,4},{5,7},{7,5},{8,10},{10,8},{9,1... | collective-permute-start | bytes 196616 | tf_op jit(solution)/shard_map/ppermute | solution.py:631
  7.3 0.6 %shard_map.121 = (f32[4,32,256]{2,1,0:T(8,128)S(1)}, f32[4,32,256]{2,1,0:T(8,128)S(1)}) custom-call(s32[3]{0:T(128)S(1)} %pad_add_fusion.pos, f32[3,16,32,256]{3,2,1,0:T(8,128)S(1)} %copy-done, f32[16,32,256]{2,1,0:T(8,128)S(1)} %copy-done.2, f32[16,32,128]{2,1,0:T(8,128)S(1)} %get-tuple-element.40.after), custom_call_target="tpu_custom_call" | custom-call | flops 131072 | bytes 2621452 | tf_op jit(solution)/shard_map/pallas_call | solution.py:666
  7.8 1.6 %collective-permute-start.2 = (f32[4,32,256]{2,1,0:T(8,128)S(1)}, f32[4,32,256]{2,1,0:T(8,128)S(1)}, u32[]{:S(2)}, u32[]{:S(2)}) collective-permute-start(f32[4,32,256]{2,1,0:T(8,128)S(1)} %get-tuple-element.41), channel_id=1, source_target_pairs={{0,4},{8,12},{4,0},{12,8},{1,5},{9,13},{5,1},{13,9},{2,6},{10,14},... | collective-permute-start | bytes 393224 | tf_op jit(solution)/shard_map/ppermute | solution.py:631
  9.5 0.7 %collective-permute-start.3 = (f32[4,32,256]{2,1,0:T(8,128)S(1)}, f32[4,32,256]{2,1,0:T(8,128)S(1)}, u32[]{:S(2)}, u32[]{:S(2)}) collective-permute-start(f32[4,32,256]{2,1,0:T(8,128)S(1)} %get-tuple-element.42), channel_id=1, source_target_pairs={{4,8},{8,4},{5,9},{9,5},{6,10},{10,6},{7,11},{11,7},{20,24},{24,20... | collective-permute-start | bytes 393224 | tf_op jit(solution)/shard_map/ppermute | solution.py:631
  10.1 0.0 copy-done.10
  10.2 0.0 collective-permute-done.refs_0_
  10.2 0.0 collective-permute-done.1.refs_1_
  10.2 0.0 copy-done.4
  10.2 0.0 copy-done.7
  10.2 0.0 copy-done.8
  10.2 3.3 %shard_map.122 = (f32[16,32,256]{2,1,0:T(8,128)S(1)}, f32[16,32,256]{2,1,0:T(8,128)S(1)}, f32[16,32,256]{2,1,0:T(8,128)S(1)}, f32[6,16,32,256]{3,2,1,0:T(8,128)S...) custom-call(s32[3]{0:T(128)S(1)} %pad_add_fusion.pos, ...), custom_call_target="tpu_custom_call" | custom-call | flops 18350080 | bytes 9113676 | tf_op jit(solution)/shard_map/pallas_call | solution.py:666
  13.5 0.0 collective-permute-done.2.refs_2_
  13.5 0.0 collective-permute-done.3.refs_3_
  13.5 0.0 copy-start.1
  13.6 0.0 copy-start.5
  13.6 0.0 copy-start.9
  13.6 1.0 %shard_map.123 = (f32[2,32,256]{2,1,0:T(8,128)S(1)}, f32[16,32,256]{2,1,0:T(8,128)S(1)}, f32[16,32,256]{2,1,0:T(8,128)S(1)}, f32[6,2,32,256]{3,2,1,0:T(8,128)S(1...) custom-call(s32[3]{0:T(128)S(1)} %pad_add_fusion.pos, ...), custom_call_target="tpu_custom_call" | custom-call | flops 2621440 | bytes 8134732 | tf_op jit(solution)/shard_map/pallas_call | solution.py:666
  14.6 0.0 copy-start.6
  14.6 0.1 collective-permute-start.5
  14.7 4.5 %collective-permute-start.6 = (f32[8,32,256]{2,1,0:T(8,128)S(1)}, f32[8,32,256]{2,1,0:T(8,128)S(1)}, u32[]{:S(2)}, u32[]{:S(2)}) collective-permute-start(f32[8,32,256]{2,1,0:T(8,128)S(1)} %get-tuple-element.54), channel_id=1, source_target_pairs={{0,4},{8,12},{4,0},{12,8},{1,5},{9,13},{5,1},{13,9},{2,6},{10,14},... | collective-permute-start | bytes 786440 | tf_op jit(solution)/shard_map/ppermute | solution.py:631
  19.2 0.7 %collective-permute-start.7 = (f32[8,32,256]{2,1,0:T(8,128)S(1)}, f32[8,32,256]{2,1,0:T(8,128)S(1)}, u32[]{:S(2)}, u32[]{:S(2)}) collective-permute-start(f32[8,32,256]{2,1,0:T(8,128)S(1)} %get-tuple-element.55), channel_id=1, source_target_pairs={{4,8},{8,4},{5,9},{9,5},{6,10},{10,6},{7,11},{11,7},{20,24},{24,20... | collective-permute-start | bytes 786440 | tf_op jit(solution)/shard_map/ppermute | solution.py:631
  19.9 0.6 %collective-permute-start.4 = (f32[8,16,256]{2,1,0:T(8,128)S(1)}, f32[8,16,256]{2,1,0:T(8,128)S(1)}, u32[]{:S(2)}, u32[]{:S(2)}) collective-permute-start(f32[8,16,256]{2,1,0:T(8,128)S(1)} %get-tuple-element.48), channel_id=1, source_target_pairs={{0,2},{2,0},{1,3},{3,1},{4,6},{6,4},{5,7},{7,5},{8,10},{10,8},{9,1... | collective-permute-start | bytes 393224 | tf_op jit(solution)/shard_map/ppermute | solution.py:631
  20.5 0.0 collective-permute-done.5.after.refs_1_
  20.5 0.6 %shard_map.124 = (f32[2,8,256]{2,1,0:T(8,128)S(1)}, f32[2,8,256]{2,1,0:T(8,128)S(1)}) custom-call(s32[3]{0:T(128)S(1)} %pad_add_fusion.pos, f32[16,32,128]{2,1,0:T(8,128)S(1)} %collective-permute-done.5.after.refs_1_, f32[16,32,256]{2,1,0:T(8,128)S(1)} %get-tuple-element.52.v.refs_4_.v0, f32[16,32,256]{2,1,0:T(8,128)S(1)} %get-tuple-element.53.rd.refs_5_), custom_call_target="tpu_custom_call" | custom-call | flops 1024 | bytes 1343500 | tf_op jit(solution)/shard_map/pallas_call | solution.py:666
  21.1 4.0 %collective-permute-start.8 = (f32[2,8,256]{2,1,0:T(8,128)S(1)}, f32[2,8,256]{2,1,0:T(8,128)S(1)}, u32[]{:S(2)}, u32[]{:S(2)}) collective-permute-start(f32[2,8,256]{2,1,0:T(8,128)S(1)} %get-tuple-element.56), channel_id=1, source_target_pairs={{0,6},{2,4},{8,14},{10,12},{6,0},{4,2},{14,8},{12,10},{1,7},{3,5},... | collective-permute-start | bytes 49160 | tf_op jit(solution)/shard_map/ppermute | solution.py:631
  25.1 0.7 %collective-permute-start.9 = (f32[2,8,256]{2,1,0:T(8,128)S(1)}, f32[2,8,256]{2,1,0:T(8,128)S(1)}, u32[]{:S(2)}, u32[]{:S(2)}) collective-permute-start(f32[2,8,256]{2,1,0:T(8,128)S(1)} %get-tuple-element.57), channel_id=1, source_target_pairs={{4,10},{6,8},{10,4},{8,6},{5,11},{7,9},{11,5},{9,7},{20,26},{22,24... | collective-permute-start | bytes 49160 | tf_op jit(solution)/shard_map/ppermute | solution.py:631
  25.7 0.0 collective-permute-done.4.refs_0_.refs_8_.refs_2_
  25.7 0.0 copy-done.1
  25.8 0.0 copy-done.5
  25.8 0.0 copy-done.9
  25.8 0.0 copy-done.6
  25.8 2.1 %shard_map.126 = (f32[16,32,256]{2,1,0:T(8,128)}, f32[3,16,32,256]{3,2,1,0:T(8,128)S(1)}, f32[3,16,32,256]{3,2,1,0:T(8,128)S(1)}, f32[8,128]{1,0:T(8,128)S(1)}) custom-call(s32[3]{0:T(128)S(1)} %pad_add_fusion.pos, f32[4,4]{1,0:T(4,128)S(1)} %pad_maximum_fusion.table, f32[3]{0:T(128)S(1)} %copy-done.9, f32[3,16,32,256]{3,2,1,0:T(8,128)S(1)} %copy-done.1, ...), custom_call_target="tpu_custom_call" | custom-call | flops 7208960 | bytes 12390488 | tf_op jit(solution)/shard_map/pallas_call | solution.py:666
  27.9 0.0 collective-permute-done.6.refs_6_.refs_0_
  27.9 0.0 collective-permute-done.7.refs_7_.refs_1_
  27.9 0.0 collective-permute-done.8.refs_9_.refs_3_
  27.9 0.0 collective-permute-done.9.refs_10_.refs_4_
  27.9 0.9 %shard_map.127 = f32[22,40,128]{2,1,0:T(8,128)S(1)} custom-call(s32[3]{0:T(128)S(1)} %pad_add_fusion.pos, f32[16,32,256]{2,1,0:T(8,128)S(1)} %get-tuple-element.52.v.refs_4_.v0, f32[16,32,256]{2,1,0:T(8,128)S(1)} %get-tuple-element.53.rd.refs_5_, f32[8,128]{1,0:T(8,128)S(1)} %get-tuple-element.63.token, ...), custom_call_target="tpu_custom_call" | custom-call | flops 524288 | bytes 2191372 | tf_op jit(solution)/shard_map/pallas_call | solution.py:666
  28.8 0.1 collective-permute-start.10
  28.9 1.0 %shard_map.125 = (f32[3,2,32,256]{3,2,1,0:T(8,128)S(1)}, f32[3,2,32,256]{3,2,1,0:T(8,128)S(1)}, f32[22,40,256]{2,1,0:T(8,128)S(1)}, f32[22,40,256]{2,1,0:T(8,128)S(1)}) custom-call(s32[3]{0:T(128)S(1)} %pad_add_fusion.pos, f32[4,4]{1,0:T(4,128)S(1)} %pad_maximum_fusion.table, f32[3]{0:T(128)S(1)} %copy-done.9, f32[3,16,32,256]{3,2,1,0:T(8,128)S(1)} %copy-done.1, ...), custom_call_target="tpu_custom_call" | custom-call | flops 1572864 | bytes 12058712 | tf_op jit(solution)/shard_map/pallas_call | solution.py:666
  29.8 0.8 %collective-permute-done.10.z_got = f32[22,40,128]{2,1,0:T(8,128)S(1)} collective-permute-done((f32[22,40,128]{2,1,0:T(8,128)S(1)}, f32[22,40,128]{2,1,0:T(8,128)S(1)}, u32[]{:S(2)}, u32[]{:S(2)}) %collective-permute-start.10) | collective-permute-done | bytes 450592 | tf_op jit(solution)/shard_map/ppermute | solution.py:631
  30.7 0.0 copy-start.3
  30.7 3.3 %shard_map.128 = (f32[3,16,32,256]{3,2,1,0:T(8,128)}, f32[3,16,32,256]{3,2,1,0:T(8,128)}, f32[16,32,256]{2,1,0:T(8,128)S(1)}, f32[16,32,256]{2,1,0:T(8,128)S(1)}, f32[16,8,128]{2,1,0:T(8,128)S(1)}) custom-call(s32[3]{0:T(128)S(1)} %pad_add_fusion.pos, f32[22,40,256]{2,1,0:T(8,128)S(1)} %get-tuple-element.58.main_v, ...), custom_call_target="tpu_custom_call" | custom-call | flops 7864320 | bytes 10055692 | tf_op jit(solution)/shard_map/pallas_call | solution.py:666
  33.9 12.4 %all_to_all.5.mom = f32[16,8,128]{2,1,0:T(8,128)S(1)} all-to-all(f32[16,8,128]{2,1,0:T(8,128)S(1)} %get-tuple-element.71), channel_id=1, replica_groups=mesh['case'=2,'gx'=4,'gy'=2,'gz'=2] {'gx','gy','gz'}, dimensions={0} | all-to-all | bytes 131072 | tf_op jit(solution)/shard_map/all_to_all | solution.py:810
  46.3 0.0 copy-done.3
  46.3 1.1 %shard_map.129 = f32[16,32,256]{2,1,0:T(8,128)} custom-call(f32[16,8,128]{2,1,0:T(8,128)S(1)} %all_to_all.5.mom, f32[16,32,256]{2,1,0:T(8,128)S(1)} %get-tuple-element.52.v.refs_4_.v0, f32[16,32,256]{2,1,0:T(8,128)S(1)} %get-tuple-element.72.v1, f32[16,32,256]{2,1,0:T(8,128)S(1)} %get-tuple-element.73.v2, f32[16,32,256]{2,1,0:T(8,128)S(1)} %copy-done.3), custom_call_target="tpu_custom_call" | custom-call | flops 1048576 | bytes 2686976 | tf_op jit(solution)/shard_map/pallas_call | solution.py:666
  (2 shorter events, 0.0 us)
Async XLA Ops:
  0.7 1.4 %copy-start = (f32[3,16,32,256]{3,2,1,0:T(8,128)S(1)}, f32[3,16,32,256]{3,2,1,0:T(8,128)}, u32[]{:S(2)}) copy-start(f32[3,16,32,256]{3,2,1,0:T(8,128)} %disp.11) | copy-start | bytes 4718596
  2.1 1.0 %copy-start.2 = (f32[16,32,256]{2,1,0:T(8,128)S(1)}, f32[16,32,256]{2,1,0:T(8,128)}, u32[]{:S(2)}) copy-start(f32[16,32,256]{2,1,0:T(8,128)} %damage.9) | copy-start | bytes 1572868
  4.1 6.0 %copy-start.10 = (f32[4,4]{1,0:T(4,128)S(1)}, f32[4,4]{1,0:T(4,128)}, u32[]{:S(2)}) copy-start(f32[4,4]{1,0:T(4,128)} %param.16) | copy-start | bytes 196
  4.1 6.1 %copy-start.4 = (s32[16,32,256]{2,1,0:T(8,128)S(1)}, s32[16,32,256]{2,1,0:T(8,128)}, u32[]{:S(2)}) copy-start(s32[16,32,256]{2,1,0:T(8,128)} %labels.7) | copy-start | bytes 1572868
  4.2 6.1 %copy-start.7 = (f32[16,32,256]{2,1,0:T(8,128)S(1)}, f32[16,32,256]{2,1,0:T(8,128)}, u32[]{:S(2)}) copy-start(f32[16,32,256]{2,1,0:T(8,128)} %history.3) | copy-start | bytes 1572868
  4.2 6.1 %copy-start.8 = (s32[16,32,256]{2,1,0:T(8,128)S(1)}, s32[16,32,256]{2,1,0:T(8,128)}, u32[]{:S(2)}) copy-start(s32[16,32,256]{2,1,0:T(8,128)} %notch.3) | copy-start | bytes 1572868
  4.2 6.0 %collective-permute-start.1 = (f32[16,32,128]{2,1,0:T(8,128)S(1)}, f32[16,32,128]{2,1,0:T(8,128)S(1)}, u32[]{:S(2)}, u32[]{:S(2)}) collective-permute-start(f32[16,32,128]{2,1,0:T(8,128)S(1)} %get-tuple-element.40.after), channel_id=1, source_target_pairs={{0,1},{1,0},{2,3},{3,2},{4,5},{5,4},{6,7},{7,6},{8,9},{9,8},{10,11... | collective-permute-start | bytes 786440 | tf_op jit(solution)/shard_map/ppermute | solution.py:631
  4.7 5.5 %collective-permute-start = (f32[4,16,256]{2,1,0:T(8,128)S(1)}, f32[4,16,256]{2,1,0:T(8,128)S(1)}, u32[]{:S(2)}, u32[]{:S(2)}) collective-permute-start(f32[4,16,256]{2,1,0:T(8,128)S(1)} %get-tuple-element.39), channel_id=1, source_target_pairs={{0,2},{2,0},{1,3},{3,1},{4,6},{6,4},{5,7},{7,5},{8,10},{10,8},{9,1... | collective-permute-start | bytes 196616 | tf_op jit(solution)/shard_map/ppermute | solution.py:631
  7.8 5.7 %collective-permute-start.2 = (f32[4,32,256]{2,1,0:T(8,128)S(1)}, f32[4,32,256]{2,1,0:T(8,128)S(1)}, u32[]{:S(2)}, u32[]{:S(2)}) collective-permute-start(f32[4,32,256]{2,1,0:T(8,128)S(1)} %get-tuple-element.41), channel_id=1, source_target_pairs={{0,4},{8,12},{4,0},{12,8},{1,5},{9,13},{5,1},{13,9},{2,6},{10,14},... | collective-permute-start | bytes 393224 | tf_op jit(solution)/shard_map/ppermute | solution.py:631
  9.5 4.1 %collective-permute-start.3 = (f32[4,32,256]{2,1,0:T(8,128)S(1)}, f32[4,32,256]{2,1,0:T(8,128)S(1)}, u32[]{:S(2)}, u32[]{:S(2)}) collective-permute-start(f32[4,32,256]{2,1,0:T(8,128)S(1)} %get-tuple-element.42), channel_id=1, source_target_pairs={{4,8},{8,4},{5,9},{9,5},{6,10},{10,6},{7,11},{11,7},{20,24},{24,20... | collective-permute-start | bytes 393224 | tf_op jit(solution)/shard_map/ppermute | solution.py:631
  13.5 12.2 %copy-start.1 = (f32[3,16,32,256]{3,2,1,0:T(8,128)S(1)}, f32[3,16,32,256]{3,2,1,0:T(8,128)}, u32[]{:S(2)}) copy-start(f32[3,16,32,256]{3,2,1,0:T(8,128)} %disp.11) | copy-start | bytes 4718596
  13.6 12.2 %copy-start.5 = (f32[3,16,32,256]{3,2,1,0:T(8,128)S(1)}, f32[3,16,32,256]{3,2,1,0:T(8,128)}, u32[]{:S(2)}) copy-start(f32[3,16,32,256]{3,2,1,0:T(8,128)} %vel.3) | copy-start | bytes 4718596
  13.6 12.2 %copy-start.9 = (f32[3]{0:T(128)S(1)}, f32[3]{0:T(128)}, u32[]{:S(2)}) copy-start(f32[3]{0:T(128)} %impact.3) | copy-start | bytes 40
  14.6 11.2 %copy-start.6 = (s32[16,32,256]{2,1,0:T(8,128)S(1)}, s32[16,32,256]{2,1,0:T(8,128)}, u32[]{:S(2)}) copy-start(s32[16,32,256]{2,1,0:T(8,128)} %contact.3) | copy-start | bytes 1572868
  14.6 5.9 %collective-permute-start.5 = (f32[16,32,128]{2,1,0:T(8,128)S(1)}, f32[16,32,128]{2,1,0:T(8,128)S(1)}, u32[]{:S(2)}, u32[]{:S(2)}) collective-permute-start(f32[16,32,128]{2,1,0:T(8,128)S(1)} %get-tuple-element.49), channel_id=1, source_target_pairs={{0,1},{1,0},{2,3},{3,2},{4,5},{5,4},{6,7},{7,6},{8,9},{9,8},{10,11... | collective-permute-start | bytes 786440 | tf_op jit(solution)/shard_map/ppermute | solution.py:631
  14.7 13.2 %collective-permute-start.6 = (f32[8,32,256]{2,1,0:T(8,128)S(1)}, f32[8,32,256]{2,1,0:T(8,128)S(1)}, u32[]{:S(2)}, u32[]{:S(2)}) collective-permute-start(f32[8,32,256]{2,1,0:T(8,128)S(1)} %get-tuple-element.54), channel_id=1, source_target_pairs={{0,4},{8,12},{4,0},{12,8},{1,5},{9,13},{5,1},{13,9},{2,6},{10,14},... | collective-permute-start | bytes 786440 | tf_op jit(solution)/shard_map/ppermute | solution.py:631
  19.2 8.6 %collective-permute-start.7 = (f32[8,32,256]{2,1,0:T(8,128)S(1)}, f32[8,32,256]{2,1,0:T(8,128)S(1)}, u32[]{:S(2)}, u32[]{:S(2)}) collective-permute-start(f32[8,32,256]{2,1,0:T(8,128)S(1)} %get-tuple-element.55), channel_id=1, source_target_pairs={{4,8},{8,4},{5,9},{9,5},{6,10},{10,6},{7,11},{11,7},{20,24},{24,20... | collective-permute-start | bytes 786440 | tf_op jit(solution)/shard_map/ppermute | solution.py:631
  19.9 5.8 %collective-permute-start.4 = (f32[8,16,256]{2,1,0:T(8,128)S(1)}, f32[8,16,256]{2,1,0:T(8,128)S(1)}, u32[]{:S(2)}, u32[]{:S(2)}) collective-permute-start(f32[8,16,256]{2,1,0:T(8,128)S(1)} %get-tuple-element.48), channel_id=1, source_target_pairs={{0,2},{2,0},{1,3},{3,1},{4,6},{6,4},{5,7},{7,5},{8,10},{10,8},{9,1... | collective-permute-start | bytes 393224 | tf_op jit(solution)/shard_map/ppermute | solution.py:631
  21.1 6.8 %collective-permute-start.8 = (f32[2,8,256]{2,1,0:T(8,128)S(1)}, f32[2,8,256]{2,1,0:T(8,128)S(1)}, u32[]{:S(2)}, u32[]{:S(2)}) collective-permute-start(f32[2,8,256]{2,1,0:T(8,128)S(1)} %get-tuple-element.56), channel_id=1, source_target_pairs={{0,6},{2,4},{8,14},{10,12},{6,0},{4,2},{14,8},{12,10},{1,7},{3,5},... | collective-permute-start | bytes 49160 | tf_op jit(solution)/shard_map/ppermute | solution.py:631
  25.1 2.8 %collective-permute-start.9 = (f32[2,8,256]{2,1,0:T(8,128)S(1)}, f32[2,8,256]{2,1,0:T(8,128)S(1)}, u32[]{:S(2)}, u32[]{:S(2)}) collective-permute-start(f32[2,8,256]{2,1,0:T(8,128)S(1)} %get-tuple-element.57), channel_id=1, source_target_pairs={{4,10},{6,8},{10,4},{8,6},{5,11},{7,9},{11,5},{9,7},{20,26},{22,24... | collective-permute-start | bytes 49160 | tf_op jit(solution)/shard_map/ppermute | solution.py:631
  28.8 1.9 %collective-permute-start.10 = (f32[22,40,128]{2,1,0:T(8,128)S(1)}, f32[22,40,128]{2,1,0:T(8,128)S(1)}, u32[]{:S(2)}, u32[]{:S(2)}) collective-permute-start(f32[22,40,128]{2,1,0:T(8,128)S(1)} %shard_map.127), channel_id=1, source_target_pairs={{0,1},{1,0},{2,3},{3,2},{4,5},{5,4},{6,7},{7,6},{8,9},{9,8},{10,11... | collective-permute-start | bytes 1351688 | tf_op jit(solution)/shard_map/ppermute | solution.py:631
  30.7 15.7 %copy-start.3 = (f32[16,32,256]{2,1,0:T(8,128)S(1)}, f32[16,32,256]{2,1,0:T(8,128)}, u32[]{:S(2)}) copy-start(f32[16,32,256]{2,1,0:T(8,128)} %damage.9) | copy-start | bytes 1572868

commit v11 on v10

--- a/solution.py
+++ b/solution.py
@@ -94,7 +94,8 @@
     return lax.fori_loop(0, count // many, several, carry)
 
 
-def pack_kernel(n_y, pos, disp, damage, *refs):
+def pack_kernel(n_y, pos, disp, *refs):
+    damage = disp.at[3]
     ys, zs = refs[:n_y], refs[n_y]
     odd_y, gz = pos[1] == 1, pos[2]
 
@@ -110,7 +111,8 @@
     unrolled(damage.shape[0], 8, body, 0)
 
 
-def pack_x_kernel(pos, disp, damage, after, *xs):
+def pack_x_kernel(pos, disp, after, *xs):
+    damage = disp.at[3]
     odd_x, count = pos[0] == 1, damage.shape[0]
     for field, src in enumerate((disp.at[0], disp.at[1], disp.at[2], damage)):
         send(odd_x, xs, field, src[0], src[count - 1])
@@ -194,7 +196,8 @@
     return inner // many, many
 
 
-def inner_kernel(n_y, pos, table, disp, damage, history, notch, labels, *refs):
+def inner_kernel(n_y, pos, table, disp, history, notch, labels, *refs):
+    damage = disp.at[3]
     local = Local(
         pos, table, disp, damage, history, notch, labels, refs[:n_y], refs[n_y]
     )
@@ -229,7 +232,8 @@
     mom_out[...] = lax.fori_loop(0, steps, several, jnp.zeros((8, 128), F32))
 
 
-def ends_kernel(n_y, pos, table, disp, damage, history, notch, labels, *refs):
+def ends_kernel(n_y, pos, table, disp, history, notch, labels, *refs):
+    damage = disp.at[3]
     local = Local(
         pos, table, disp, damage, history, notch, labels, refs[:n_y], refs[n_y]
     )
@@ -467,8 +471,12 @@
     result = mom[...]
     for at, total in enumerate((k1, k2, k3, k4, k5)):
         result = jnp.where(rows == at + 1, jnp.sum(total, axis=0, keepdims=True), result)
+    mine = rows == iota2((8, 128), 1)
+    line = jnp.sum(
+        jnp.where(mine, jnp.sum(result, axis=1, keepdims=True), 0.0), axis=0, keepdims=True
+    )
     for peer in range(spread.shape[0]):
-        spread[peer] = result
+        spread[peer] = line
     for copy in copies:
         copy.wait()
 
@@ -607,8 +615,8 @@
 def final_kernel(mom, v0, v1, v2, damage, out_hbm, out, sems):
     count = v0.shape[0]
     block = count // CHUNKS
-    sums = jnp.sum(jnp.sum(mom[...], axis=0), axis=1, keepdims=True)
-    c0, c1, c2 = cg_coefficients([sums[j : j + 1, :] for j in range(6)])
+    sums = jnp.sum(mom[...], axis=0)
+    c0, c1, c2 = cg_coefficients([sums[:, j : j + 1] for j in range(6)])
     copies = []
     for chunk in range(CHUNKS):
         for x in range(chunk * block, (chunk + 1) * block):
@@ -694,10 +702,11 @@
     columns = arr(nx, ny, 128)
     z_pairs = [(0, 1)]
 
+    both = jnp.concatenate([displacement, damage[None]])
     sent = call(
         functools.partial(pack_kernel, n_y),
-        "svv",
-        (pos, displacement, damage),
+        "sv",
+        (pos, both),
         "v" * (1 + n_y),
         [*[arr(4, nx, nz)] * n_y, columns],
         size,
@@ -705,18 +714,18 @@
     got_yz = [*swap_along("gy", sent[:n_y]), swap(sent[-1], "gz", z_pairs)]
     sent_x = call(
         pack_x_kernel,
-        "svva",
-        (pos, displacement, damage, sent[-1]),
+        "sva",
+        (pos, both, sent[-1]),
         "vv",
         [arr(4, ny, nz)] * 2,
         size,
     )
     got_x = swap_along("gx", sent_x)
     rows = [arr(8, nx, nz)] * n_y
-    voxels = (pos, scaled, displacement, damage, history, notch, labels, *got_yz)
+    voxels = (pos, scaled, both, history, notch, labels, *got_yz)
     hist, rd, v0, stress, mom, *sent = call(
         functools.partial(inner_kernel, n_y),
-        "ssvvvvv" + "v" * (1 + n_y),
+        "ssvvvv" + "v" * (1 + n_y),
         voxels,
         "vvvvv" + "v" * (1 + n_y),
         [field, field, field, arr(6, nx, ny, nz), small, *rows, columns],
@@ -725,7 +734,7 @@
     more = (*got_x, rd, v0, mom, *sent)
     hist_ends, rd, v0, ends, mom, *sent = call(
         functools.partial(ends_kernel, n_y),
-        "ssvvvvv" + "v" * (1 + n_y) + "vvvvv" + "v" * (1 + n_y),
+        "ssvvvv" + "v" * (1 + n_y) + "vvvvv" + "v" * (1 + n_y),
         (*voxels, *more),
         "vvvvv" + "v" * (3 + n_y),
         [
@@ -756,7 +765,7 @@
         pos,
         scaled,
         impact,
-        displacement,
+        both,
         velocity,
         contact,
         labels,
@@ -797,7 +806,7 @@
         "svvvvvvvv",
         (pos, main_v, main_rd, mom, z_got, *moved, *moved_ends),
         "hhvvv",
-        [fields3, fields3, field, field, arr(peers, 8, 128)],
+        [fields3, fields3, field, field, arr(peers, 1, 128)],
         60 * size,
         [
             pltpu.VMEM((nx + 6, ny + 8, 128), F32),

time: 47.6 us -> 46.5 us (0.977)
  local copies, waits for them, and re-layouts: 2.5 us -> 0.05 us
  other arithmetic: 0.1 us -> 1.82 us
  blocking collectives: 12.4 us -> 11.9 us
    unnamed x22 -> x16, local copies, waits for them, and re-layouts: 2.5 us -> 0.05 us
    concatenate x0 -> x1, other arithmetic: none -> 1.72 us  [per_device(): both = jnp.concatenate([displacement, damage[None]])]
    all_to_all x1, blocking collectives: 12.4 us -> 11.9 us  [per_device(): mom = lax.all_to_all(spread, ('gx', 'gy', 'gz'), 0, 0, tiled=True)]
where the time goes in v11:
time: 46.5 us; the launch traced here: 46.3 us
  starting transfers between devices  16 us (34%)
  Pallas kernels  14.8 us (32%)
  blocking collectives  11.9 us (26%)
  other arithmetic  1.82 us (4%)
  between operations  0.95 us (2%)
  waiting for transfers between devices  0.82 us (2%)
    ppermute x11, starting transfers between devices, swap(): return lax.ppermute(array, axis, pairs + [(b, a) for a, b in pairs])  16 us
    pallas_call x10, Pallas kernels, call(): pl.pallas_call(kernel, out_shape=outs, in_specs=[spec_of(k, a) for k, a i...  14.8 us
    all_to_all x1, blocking collectives, per_device(): mom = lax.all_to_all(spread, ('gx', 'gy', 'gz'), 0, 0, tiled=True)  11.9 us
    concatenate x1, other arithmetic, per_device(): both = jnp.concatenate([displacement, damage[None]])  1.72 us
  transfers between devices with their start and end apart: 11, of which 1 were waited for; matrix products, arithmetic and copies ran while one was open for 0% of the time, Pallas kernels for 16%

profile of v11, /device:TPU:0, one launch (start us, length us, event | category | flops | bytes accessed | tf_op | source)
XLA Modules:
  0.0 46.3 jit_solution(6163345253378767836)
XLA Ops:
  0.6 1.7 %pad_maximum_fusion.disp = f32[4,16,32,256]{3,2,1,0:T(8,128)S(1)} fusion(f32[1,16,32,256]{3,2,1,0:T(8,128)} %bitcast.4, f32[3,16,32,256]{3,2,1,0:T(8,128)} %param.9), kind=kLoop, calls=%fused_computation | loop fusion | flops 524288 | bytes 4194304 | tf_op jit(solution)/shard_map/concatenate | solution.py:705
  2.4 0.1 pad_add_fusion.pos
  2.4 1.0 %shard_map.120 = (f32[4,16,256]{2,1,0:T(8,128)S(1)}, f32[16,32,128]{2,1,0:T(8,128)S(1)}) custom-call(s32[3]{0:T(128)S(1)} %pad_add_fusion.pos, f32[4,16,32,256]{3,2,1,0:T(8,128)S(1)} %pad_maximum_fusion.disp), custom_call_target="tpu_custom_call" | custom-call | flops 131072 | bytes 2424844 | tf_op jit(solution)/shard_map/pallas_call | solution.py:674
  3.4 0.0 copy-start.7
  3.4 0.0 copy-start
  3.4 0.0 copy-start.2
  3.4 0.0 copy-start.3
  3.5 0.5 %collective-permute-start.1 = (f32[16,32,128]{2,1,0:T(8,128)S(1)}, f32[16,32,128]{2,1,0:T(8,128)S(1)}, u32[]{:S(2)}, u32[]{:S(2)}) collective-permute-start(f32[16,32,128]{2,1,0:T(8,128)S(1)} %get-tuple-element.40.after), channel_id=1, source_target_pairs={{0,1},{1,0},{2,3},{3,2},{4,5},{5,4},{6,7},{7,6},{8,9},{9,8},{10,11... | collective-permute-start | bytes 786440 | tf_op jit(solution)/shard_map/ppermute | solution.py:639
  4.0 2.6 %collective-permute-start = (f32[4,16,256]{2,1,0:T(8,128)S(1)}, f32[4,16,256]{2,1,0:T(8,128)S(1)}, u32[]{:S(2)}, u32[]{:S(2)}) collective-permute-start(f32[4,16,256]{2,1,0:T(8,128)S(1)} %get-tuple-element.39), channel_id=1, source_target_pairs={{0,2},{2,0},{1,3},{3,1},{4,6},{6,4},{5,7},{7,5},{8,10},{10,8},{9,1... | collective-permute-start | bytes 196616 | tf_op jit(solution)/shard_map/ppermute | solution.py:639
  6.5 0.6 %shard_map.121 = (f32[4,32,256]{2,1,0:T(8,128)S(1)}, f32[4,32,256]{2,1,0:T(8,128)S(1)}) custom-call(s32[3]{0:T(128)S(1)} %pad_add_fusion.pos, f32[4,16,32,256]{3,2,1,0:T(8,128)S(1)} %pad_maximum_fusion.disp, f32[16,32,128]{2,1,0:T(8,128)S(1)} %get-tuple-element.40.after), custom_call_target="tpu_custom_call" | custom-call | flops 131072 | bytes 2621452 | tf_op jit(solution)/shard_map/pallas_call | solution.py:674
  7.1 1.6 %collective-permute-start.2 = (f32[4,32,256]{2,1,0:T(8,128)S(1)}, f32[4,32,256]{2,1,0:T(8,128)S(1)}, u32[]{:S(2)}, u32[]{:S(2)}) collective-permute-start(f32[4,32,256]{2,1,0:T(8,128)S(1)} %get-tuple-element.41), channel_id=1, source_target_pairs={{0,4},{8,12},{4,0},{12,8},{1,5},{9,13},{5,1},{13,9},{2,6},{10,14},... | collective-permute-start | bytes 393224 | tf_op jit(solution)/shard_map/ppermute | solution.py:639
  8.8 0.7 %collective-permute-start.3 = (f32[4,32,256]{2,1,0:T(8,128)S(1)}, f32[4,32,256]{2,1,0:T(8,128)S(1)}, u32[]{:S(2)}, u32[]{:S(2)}) collective-permute-start(f32[4,32,256]{2,1,0:T(8,128)S(1)} %get-tuple-element.42), channel_id=1, source_target_pairs={{4,8},{8,4},{5,9},{9,5},{6,10},{10,6},{7,11},{11,7},{20,24},{24,20... | collective-permute-start | bytes 393224 | tf_op jit(solution)/shard_map/ppermute | solution.py:639
  9.4 0.0 copy-done.7
  9.5 0.0 collective-permute-done.refs_0_
  9.5 0.0 collective-permute-done.1.refs_1_
  9.5 0.0 copy-done
  9.5 0.0 copy-done.2
  9.5 0.0 copy-done.3
  9.5 3.3 %shard_map.122 = (f32[16,32,256]{2,1,0:T(8,128)S(1)}, f32[16,32,256]{2,1,0:T(8,128)S(1)}, f32[16,32,256]{2,1,0:T(8,128)S(1)}, f32[6,16,32,256]{3,2,1,0:T(8,128)S...) custom-call(s32[3]{0:T(128)S(1)} %pad_add_fusion.pos, ...), custom_call_target="tpu_custom_call" | custom-call | flops 18350080 | bytes 9113676 | tf_op jit(solution)/shard_map/pallas_call | solution.py:674
  12.8 0.0 collective-permute-done.2.refs_2_
  12.8 0.0 collective-permute-done.3.refs_3_
  12.8 0.0 copy-start.1
  12.8 0.0 copy-start.6
  12.8 1.0 %shard_map.123 = (f32[2,32,256]{2,1,0:T(8,128)S(1)}, f32[16,32,256]{2,1,0:T(8,128)S(1)}, f32[16,32,256]{2,1,0:T(8,128)S(1)}, f32[6,2,32,256]{3,2,1,0:T(8,128)S(1...) custom-call(s32[3]{0:T(128)S(1)} %pad_add_fusion.pos, ...), custom_call_target="tpu_custom_call" | custom-call | flops 2621440 | bytes 8134732 | tf_op jit(solution)/shard_map/pallas_call | solution.py:674
  13.9 0.0 copy-start.5
  13.9 0.1 collective-permute-start.5
  14.0 4.6 %collective-permute-start.6 = (f32[8,32,256]{2,1,0:T(8,128)S(1)}, f32[8,32,256]{2,1,0:T(8,128)S(1)}, u32[]{:S(2)}, u32[]{:S(2)}) collective-permute-start(f32[8,32,256]{2,1,0:T(8,128)S(1)} %get-tuple-element.54), channel_id=1, source_target_pairs={{0,4},{8,12},{4,0},{12,8},{1,5},{9,13},{5,1},{13,9},{2,6},{10,14},... | collective-permute-start | bytes 786440 | tf_op jit(solution)/shard_map/ppermute | solution.py:639
  18.5 0.7 %collective-permute-start.7 = (f32[8,32,256]{2,1,0:T(8,128)S(1)}, f32[8,32,256]{2,1,0:T(8,128)S(1)}, u32[]{:S(2)}, u32[]{:S(2)}) collective-permute-start(f32[8,32,256]{2,1,0:T(8,128)S(1)} %get-tuple-element.55), channel_id=1, source_target_pairs={{4,8},{8,4},{5,9},{9,5},{6,10},{10,6},{7,11},{11,7},{20,24},{24,20... | collective-permute-start | bytes 786440 | tf_op jit(solution)/shard_map/ppermute | solution.py:639
  19.2 0.6 %collective-permute-start.4 = (f32[8,16,256]{2,1,0:T(8,128)S(1)}, f32[8,16,256]{2,1,0:T(8,128)S(1)}, u32[]{:S(2)}, u32[]{:S(2)}) collective-permute-start(f32[8,16,256]{2,1,0:T(8,128)S(1)} %get-tuple-element.48), channel_id=1, source_target_pairs={{0,2},{2,0},{1,3},{3,1},{4,6},{6,4},{5,7},{7,5},{8,10},{10,8},{9,1... | collective-permute-start | bytes 393224 | tf_op jit(solution)/shard_map/ppermute | solution.py:639
  19.8 0.0 collective-permute-done.5.after.refs_1_
  19.8 0.6 %shard_map.124 = (f32[2,8,256]{2,1,0:T(8,128)S(1)}, f32[2,8,256]{2,1,0:T(8,128)S(1)}) custom-call(s32[3]{0:T(128)S(1)} %pad_add_fusion.pos, f32[16,32,128]{2,1,0:T(8,128)S(1)} %collective-permute-done.5.after.refs_1_, f32[16,32,256]{2,1,0:T(8,128)S(1)} %get-tuple-element.52.v.refs_4_.v0, f32[16,32,256]{2,1,0:T(8,128)S(1)} %get-tuple-element.53.rd.refs_5_), custom_call_target="tpu_custom_call" | custom-call | flops 1024 | bytes 1343500 | tf_op jit(solution)/shard_map/pallas_call | solution.py:674
  20.4 4.0 %collective-permute-start.8 = (f32[2,8,256]{2,1,0:T(8,128)S(1)}, f32[2,8,256]{2,1,0:T(8,128)S(1)}, u32[]{:S(2)}, u32[]{:S(2)}) collective-permute-start(f32[2,8,256]{2,1,0:T(8,128)S(1)} %get-tuple-element.56), channel_id=1, source_target_pairs={{0,6},{2,4},{8,14},{10,12},{6,0},{4,2},{14,8},{12,10},{1,7},{3,5},... | collective-permute-start | bytes 49160 | tf_op jit(solution)/shard_map/ppermute | solution.py:639
  24.3 0.7 %collective-permute-start.9 = (f32[2,8,256]{2,1,0:T(8,128)S(1)}, f32[2,8,256]{2,1,0:T(8,128)S(1)}, u32[]{:S(2)}, u32[]{:S(2)}) collective-permute-start(f32[2,8,256]{2,1,0:T(8,128)S(1)} %get-tuple-element.57), channel_id=1, source_target_pairs={{4,10},{6,8},{10,4},{8,6},{5,11},{7,9},{11,5},{9,7},{20,26},{22,24... | collective-permute-start | bytes 49160 | tf_op jit(solution)/shard_map/ppermute | solution.py:639
  25.0 0.0 collective-permute-done.4.refs_0_.refs_8_.refs_2_
  25.0 0.0 copy-done.1
  25.0 0.0 copy-done.6
  25.0 0.0 copy-done.5
  25.0 2.1 %shard_map.126 = (f32[16,32,256]{2,1,0:T(8,128)}, f32[3,16,32,256]{3,2,1,0:T(8,128)S(1)}, f32[3,16,32,256]{3,2,1,0:T(8,128)S(1)}, f32[8,128]{1,0:T(8,128)S(1)}) custom-call(s32[3]{0:T(128)S(1)} %pad_add_fusion.pos, f32[4,4]{1,0:T(4,128)S(1)} %pad_maximum_fusion.1.table, f32[3]{0:T(128)S(1)} %copy-done.6, f32[4,16,32,256]{3,2,1,0:T(8,128)S(1)} %pad_maximum_fusion.disp, ...), custom_call_target="tpu_custom_call" | custom-call | flops 7208960 | bytes 12914776 | tf_op jit(solution)/shard_map/pallas_call | solution.py:674
  27.1 0.0 collective-permute-done.6.refs_6_.refs_0_
  27.1 0.0 collective-permute-done.7.refs_7_.refs_1_
  27.1 0.0 collective-permute-done.8.refs_9_.refs_3_
  27.2 0.0 collective-permute-done.9.refs_10_.refs_4_
  27.2 0.9 %shard_map.127 = f32[22,40,128]{2,1,0:T(8,128)S(1)} custom-call(s32[3]{0:T(128)S(1)} %pad_add_fusion.pos, f32[16,32,256]{2,1,0:T(8,128)S(1)} %get-tuple-element.52.v.refs_4_.v0, f32[16,32,256]{2,1,0:T(8,128)S(1)} %get-tuple-element.53.rd.refs_5_, f32[8,128]{1,0:T(8,128)S(1)} %get-tuple-element.63.token, ...), custom_call_target="tpu_custom_call" | custom-call | flops 524288 | bytes 2191372 | tf_op jit(solution)/shard_map/pallas_call | solution.py:674
  28.0 0.1 collective-permute-start.10
  28.1 1.0 %shard_map.125 = (f32[3,2,32,256]{3,2,1,0:T(8,128)S(1)}, f32[3,2,32,256]{3,2,1,0:T(8,128)S(1)}, f32[22,40,256]{2,1,0:T(8,128)S(1)}, f32[22,40,256]{2,1,0:T(8,128)S(1)}) custom-call(s32[3]{0:T(128)S(1)} %pad_add_fusion.pos, f32[4,4]{1,0:T(4,128)S(1)} %pad_maximum_fusion.1.table, f32[3]{0:T(128)S(1)} %copy-done.6, ...), custom_call_target="tpu_custom_call" | custom-call | flops 1572864 | bytes 12583000 | tf_op jit(solution)/shard_map/pallas_call | solution.py:674
  29.1 0.8 %collective-permute-done.10.z_got = f32[22,40,128]{2,1,0:T(8,128)S(1)} collective-permute-done((f32[22,40,128]{2,1,0:T(8,128)S(1)}, f32[22,40,128]{2,1,0:T(8,128)S(1)}, u32[]{:S(2)}, u32[]{:S(2)}) %collective-permute-start.10) | collective-permute-done | bytes 450592 | tf_op jit(solution)/shard_map/ppermute | solution.py:639
  29.9 0.0 copy-start.4
  29.9 3.3 %shard_map.128 = (f32[3,16,32,256]{3,2,1,0:T(8,128)}, f32[3,16,32,256]{3,2,1,0:T(8,128)}, f32[16,32,256]{2,1,0:T(8,128)S(1)}, f32[16,32,256]{2,1,0:T(8,128)S(1)}, f32[16,1,128]{2,1,0:T(1,128)S(1)}) custom-call(s32[3]{0:T(128)S(1)} %pad_add_fusion.pos, f32[22,40,256]{2,1,0:T(8,128)S(1)} %get-tuple-element.58.main_v, ...), custom_call_target="tpu_custom_call" | custom-call | flops 7864320 | bytes 9998348 | tf_op jit(solution)/shard_map/pallas_call | solution.py:674
  33.3 11.9 %all_to_all.5.mom = f32[16,1,128]{2,1,0:T(1,128)S(1)} all-to-all(f32[16,1,128]{2,1,0:T(1,128)S(1)} %get-tuple-element.71), channel_id=1, replica_groups=mesh['case'=2,'gx'=4,'gy'=2,'gz'=2] {'gx','gy','gz'}, dimensions={0} | all-to-all | bytes 16384 | tf_op jit(solution)/shard_map/all_to_all | solution.py:819
  45.2 0.0 copy-done.4
  45.2 1.1 %shard_map.129 = f32[16,32,256]{2,1,0:T(8,128)} custom-call(f32[16,1,128]{2,1,0:T(1,128)S(1)} %all_to_all.5.mom, f32[16,32,256]{2,1,0:T(8,128)S(1)} %get-tuple-element.52.v.refs_4_.v0, f32[16,32,256]{2,1,0:T(8,128)S(1)} %get-tuple-element.72.v1, f32[16,32,256]{2,1,0:T(8,128)S(1)} %get-tuple-element.73.v2, f32[16,32,256]{2,1,0:T(8,128)S(1)} %copy-done.4), custom_call_target="tpu_custom_call" | custom-call | flops 1048576 | bytes 2629632 | tf_op jit(solution)/shard_map/pallas_call | solution.py:674
  (2 shorter events, 0.0 us)
Async XLA Ops:
  3.4 6.0 %copy-start.7 = (f32[4,4]{1,0:T(4,128)S(1)}, f32[4,4]{1,0:T(4,128)}, u32[]{:S(2)}) copy-start(f32[4,4]{1,0:T(4,128)} %param.16) | copy-start | bytes 196
  3.4 6.1 %copy-start = (s32[16,32,256]{2,1,0:T(8,128)S(1)}, s32[16,32,256]{2,1,0:T(8,128)}, u32[]{:S(2)}) copy-start(s32[16,32,256]{2,1,0:T(8,128)} %labels.7) | copy-start | bytes 1572868
  3.4 6.1 %copy-start.2 = (f32[16,32,256]{2,1,0:T(8,128)S(1)}, f32[16,32,256]{2,1,0:T(8,128)}, u32[]{:S(2)}) copy-start(f32[16,32,256]{2,1,0:T(8,128)} %history.3) | copy-start | bytes 1572868
  3.4 6.1 %copy-start.3 = (s32[16,32,256]{2,1,0:T(8,128)S(1)}, s32[16,32,256]{2,1,0:T(8,128)}, u32[]{:S(2)}) copy-start(s32[16,32,256]{2,1,0:T(8,128)} %notch.3) | copy-start | bytes 1572868
  3.5 6.0 %collective-permute-start.1 = (f32[16,32,128]{2,1,0:T(8,128)S(1)}, f32[16,32,128]{2,1,0:T(8,128)S(1)}, u32[]{:S(2)}, u32[]{:S(2)}) collective-permute-start(f32[16,32,128]{2,1,0:T(8,128)S(1)} %get-tuple-element.40.after), channel_id=1, source_target_pairs={{0,1},{1,0},{2,3},{3,2},{4,5},{5,4},{6,7},{7,6},{8,9},{9,8},{10,11... | collective-permute-start | bytes 786440 | tf_op jit(solution)/shard_map/ppermute | solution.py:639
  4.0 5.5 %collective-permute-start = (f32[4,16,256]{2,1,0:T(8,128)S(1)}, f32[4,16,256]{2,1,0:T(8,128)S(1)}, u32[]{:S(2)}, u32[]{:S(2)}) collective-permute-start(f32[4,16,256]{2,1,0:T(8,128)S(1)} %get-tuple-element.39), channel_id=1, source_target_pairs={{0,2},{2,0},{1,3},{3,1},{4,6},{6,4},{5,7},{7,5},{8,10},{10,8},{9,1... | collective-permute-start | bytes 196616 | tf_op jit(solution)/shard_map/ppermute | solution.py:639
  7.1 5.7 %collective-permute-start.2 = (f32[4,32,256]{2,1,0:T(8,128)S(1)}, f32[4,32,256]{2,1,0:T(8,128)S(1)}, u32[]{:S(2)}, u32[]{:S(2)}) collective-permute-start(f32[4,32,256]{2,1,0:T(8,128)S(1)} %get-tuple-element.41), channel_id=1, source_target_pairs={{0,4},{8,12},{4,0},{12,8},{1,5},{9,13},{5,1},{13,9},{2,6},{10,14},... | collective-permute-start | bytes 393224 | tf_op jit(solution)/shard_map/ppermute | solution.py:639
  8.8 4.1 %collective-permute-start.3 = (f32[4,32,256]{2,1,0:T(8,128)S(1)}, f32[4,32,256]{2,1,0:T(8,128)S(1)}, u32[]{:S(2)}, u32[]{:S(2)}) collective-permute-start(f32[4,32,256]{2,1,0:T(8,128)S(1)} %get-tuple-element.42), channel_id=1, source_target_pairs={{4,8},{8,4},{5,9},{9,5},{6,10},{10,6},{7,11},{11,7},{20,24},{24,20... | collective-permute-start | bytes 393224 | tf_op jit(solution)/shard_map/ppermute | solution.py:639
  12.8 12.2 %copy-start.1 = (f32[3,16,32,256]{3,2,1,0:T(8,128)S(1)}, f32[3,16,32,256]{3,2,1,0:T(8,128)}, u32[]{:S(2)}) copy-start(f32[3,16,32,256]{3,2,1,0:T(8,128)} %vel.3) | copy-start | bytes 4718596
  12.8 12.2 %copy-start.6 = (f32[3]{0:T(128)S(1)}, f32[3]{0:T(128)}, u32[]{:S(2)}) copy-start(f32[3]{0:T(128)} %impact.3) | copy-start | bytes 40
  13.9 11.2 %copy-start.5 = (s32[16,32,256]{2,1,0:T(8,128)S(1)}, s32[16,32,256]{2,1,0:T(8,128)}, u32[]{:S(2)}) copy-start(s32[16,32,256]{2,1,0:T(8,128)} %contact.3) | copy-start | bytes 1572868
  13.9 5.9 %collective-permute-start.5 = (f32[16,32,128]{2,1,0:T(8,128)S(1)}, f32[16,32,128]{2,1,0:T(8,128)S(1)}, u32[]{:S(2)}, u32[]{:S(2)}) collective-permute-start(f32[16,32,128]{2,1,0:T(8,128)S(1)} %get-tuple-element.49), channel_id=1, source_target_pairs={{0,1},{1,0},{2,3},{3,2},{4,5},{5,4},{6,7},{7,6},{8,9},{9,8},{10,11... | collective-permute-start | bytes 786440 | tf_op jit(solution)/shard_map/ppermute | solution.py:639
  14.0 13.2 %collective-permute-start.6 = (f32[8,32,256]{2,1,0:T(8,128)S(1)}, f32[8,32,256]{2,1,0:T(8,128)S(1)}, u32[]{:S(2)}, u32[]{:S(2)}) collective-permute-start(f32[8,32,256]{2,1,0:T(8,128)S(1)} %get-tuple-element.54), channel_id=1, source_target_pairs={{0,4},{8,12},{4,0},{12,8},{1,5},{9,13},{5,1},{13,9},{2,6},{10,14},... | collective-permute-start | bytes 786440 | tf_op jit(solution)/shard_map/ppermute | solution.py:639
  18.5 8.6 %collective-permute-start.7 = (f32[8,32,256]{2,1,0:T(8,128)S(1)}, f32[8,32,256]{2,1,0:T(8,128)S(1)}, u32[]{:S(2)}, u32[]{:S(2)}) collective-permute-start(f32[8,32,256]{2,1,0:T(8,128)S(1)} %get-tuple-element.55), channel_id=1, source_target_pairs={{4,8},{8,4},{5,9},{9,5},{6,10},{10,6},{7,11},{11,7},{20,24},{24,20... | collective-permute-start | bytes 786440 | tf_op jit(solution)/shard_map/ppermute | solution.py:639
  19.2 5.8 %collective-permute-start.4 = (f32[8,16,256]{2,1,0:T(8,128)S(1)}, f32[8,16,256]{2,1,0:T(8,128)S(1)}, u32[]{:S(2)}, u32[]{:S(2)}) collective-permute-start(f32[8,16,256]{2,1,0:T(8,128)S(1)} %get-tuple-element.48), channel_id=1, source_target_pairs={{0,2},{2,0},{1,3},{3,1},{4,6},{6,4},{5,7},{7,5},{8,10},{10,8},{9,1... | collective-permute-start | bytes 393224 | tf_op jit(solution)/shard_map/ppermute | solution.py:639
  20.4 6.8 %collective-permute-start.8 = (f32[2,8,256]{2,1,0:T(8,128)S(1)}, f32[2,8,256]{2,1,0:T(8,128)S(1)}, u32[]{:S(2)}, u32[]{:S(2)}) collective-permute-start(f32[2,8,256]{2,1,0:T(8,128)S(1)} %get-tuple-element.56), channel_id=1, source_target_pairs={{0,6},{2,4},{8,14},{10,12},{6,0},{4,2},{14,8},{12,10},{1,7},{3,5},... | collective-permute-start | bytes 49160 | tf_op jit(solution)/shard_map/ppermute | solution.py:639
  24.3 2.8 %collective-permute-start.9 = (f32[2,8,256]{2,1,0:T(8,128)S(1)}, f32[2,8,256]{2,1,0:T(8,128)S(1)}, u32[]{:S(2)}, u32[]{:S(2)}) collective-permute-start(f32[2,8,256]{2,1,0:T(8,128)S(1)} %get-tuple-element.57), channel_id=1, source_target_pairs={{4,10},{6,8},{10,4},{8,6},{5,11},{7,9},{11,5},{9,7},{20,26},{22,24... | collective-permute-start | bytes 49160 | tf_op jit(solution)/shard_map/ppermute | solution.py:639
  28.0 1.9 %collective-permute-start.10 = (f32[22,40,128]{2,1,0:T(8,128)S(1)}, f32[22,40,128]{2,1,0:T(8,128)S(1)}, u32[]{:S(2)}, u32[]{:S(2)}) collective-permute-start(f32[22,40,128]{2,1,0:T(8,128)S(1)} %shard_map.127), channel_id=1, source_target_pairs={{0,1},{1,0},{2,3},{3,2},{4,5},{5,4},{6,7},{7,6},{8,9},{9,8},{10,11... | collective-permute-start | bytes 1351688 | tf_op jit(solution)/shard_map/ppermute | solution.py:639
  29.9 15.3 %copy-start.4 = (f32[16,32,256]{2,1,0:T(8,128)S(1)}, f32[16,32,256]{2,1,0:T(8,128)}, u32[]{:S(2)}) copy-start(f32[16,32,256]{2,1,0:T(8,128)} %damage.1) | copy-start | bytes 1572868

commit v12 on v11

--- a/solution.py
+++ b/solution.py
@@ -13,6 +13,7 @@
 ALPHA_LOW, ALPHA_HIGH = 0.5, 6.5
 VMEM_BYTES = 28 * 1024 * 1024
 CHUNKS = 4
+STRESS_LANE = 32
 F32 = jnp.float32
 
 
@@ -55,15 +56,22 @@
     return jnp.concatenate(upper, axis=1), jnp.concatenate(lower, axis=1)
 
 
-def send_columns(ref, x, planes, gz):
+def send_columns(ref, x, planes, gz, tile=None, first=0):
     depth = planes[0].shape[1]
     lanes = iota2((planes[0].shape[0], 128), 1)
-    tile = None
     for field, plane in enumerate(planes):
         part = jnp.where(gz == 0, plane[:, depth - 128 :], plane[:, :128])
-        part = pltpu.roll(part, field + 1 - gz, 1)
-        tile = part if tile is None else jnp.where(lanes == field, part, tile)
+        part = pltpu.roll(part, first + field + 1 - gz, 1)
+        tile = part if tile is None else jnp.where(lanes == first + field, part, tile)
     ref[x] = tile
+
+
+def z_tile(v, rd, gz):
+    depth = v.shape[1]
+    keep = lax.shift_right_logical(iota2((v.shape[0], 128), 1), 6) == 1 - gz
+    mine = jnp.where(gz == 0, v[:, depth - 128 :], v[:, :128])
+    moved = jnp.where(gz == 0, rd[:, depth - 128 :], rd[:, :128])
+    return jnp.where(keep, mine, pltpu.roll(moved, 64, 1))
 
 
 def folded(values):
@@ -91,6 +99,8 @@
             carry = body(block * many + at, carry)
         return carry
 
+    if many == count:
+        return several(0, carry)
     return lax.fori_loop(0, count // many, several, carry)
 
 
@@ -108,7 +118,7 @@
         send_columns(zs, x, planes, gz)
         return carry
 
-    unrolled(damage.shape[0], 8, body, 0)
+    unrolled(damage.shape[0], damage.shape[0], body, 0)
 
 
 def pack_x_kernel(pos, disp, after, *xs):
@@ -186,13 +196,15 @@
             low, high = plane[depth - 1 : depth], plane[rows - depth : rows - depth + 1]
             send(self.odd_y, ys, (slot, pl.ds(x, 1), slice(None)), low, high)
 
-    def send_z(self, zs, x, stress):
-        send_columns(zs, x, [stress[4], stress[5], stress[2]], self.gz)
+    def send_z(self, zs, x, v, rd, stress):
+        base = z_tile(v, rd, self.gz)
+        planes = [stress[4], stress[5], stress[2]]
+        send_columns(zs, x, planes, self.gz, base, STRESS_LANE)
 
 
 def inner_steps(count):
     inner = count - 2
-    many = max(m for m in range(1, 8) if inner % m == 0)
+    many = max(m for m in range(1, 16) if inner % m == 0)
     return inner // many, many
 
 
@@ -225,11 +237,11 @@
             rd_out[x] = rd
             v_out[x] = v
             local.send_y(ys, x, v, rd, stress)
-            local.send_z(zs, x, stress)
+            local.send_z(zs, x, v, rd, stress)
             total = total + part
         return total
 
-    mom_out[...] = lax.fori_loop(0, steps, several, jnp.zeros((8, 128), F32))
+    mom_out[...] = unrolled(steps, 1, several, jnp.zeros((8, 128), F32))
 
 
 def ends_kernel(n_y, pos, table, disp, history, notch, labels, *refs):
@@ -284,7 +296,7 @@
     for end, x in enumerate((0, count - 1)):
         stress, rd, v = found[end]
         local.send_y(ys, x, v, rd, stress)
-        local.send_z(zs, x, stress)
+        local.send_z(zs, x, v, rd, stress)
     for depth in (1, 2, 3):
         low, high = depth - 1, count - depth
         send(odd_x, xs, depth - 1, v_out[low], v_out[high])
@@ -367,35 +379,29 @@
             yield count - 1 + depth, self.halo(False, depth)
 
 
+def outer_index(p, count):
+    return -p - 1 if p < 0 else 3 + p - count
+
+
 def join_kernel(n_y, pos, v, rd, token, *refs):
     big = Enlarged(n_y, pos, v, rd, refs[:-1])
-    out = refs[-1]
-    first_z = pos[2] == 0
-    count, ny, depth = v.shape
-
-    def tile(v_part, rd_part):
-        lanes = iota2((v_part.shape[0], 128), 1)
-        keep = lax.shift_right_logical(lanes, 6) == 1 - pos[2]
-        mine = jnp.where(first_z, v_part[:, depth - 128 :], v_part[:, :128])
-        moved = jnp.where(first_z, rd_part[:, depth - 128 :], rd_part[:, :128])
-        return jnp.where(keep, mine, pltpu.roll(moved, 64, 1))
-
-    def put(p, parts):
-        v_own, v_rows, rd_own, rd_rows = parts
-        out[p + 3, 0:ny] = tile(v_own, rd_own)
-        out[p + 3, ny : ny + 8] = tile(v_rows, rd_rows)
-
-    for p, parts in big.outer(count):
-        put(p, parts)
+    out, gz = refs[-1], pos[2]
+    count, ny, _ = v.shape
+    tall = ny // 8
+    for p, (v_own, v_rows, rd_own, rd_rows) in big.outer(count):
+        out[p + 3] = z_tile(v_rows, rd_rows, gz)
+        start = count + 6 + tall * outer_index(p, count)
+        out[start : start + tall] = z_tile(v_own, rd_own, gz).reshape(tall, 8, 128)
 
     def body(x, carry):
-        put(x, big.own(x))
+        _, v_rows, _, rd_rows = big.own(x)
+        out[x + 3] = z_tile(v_rows, rd_rows, gz)
         return carry
 
-    unrolled(count, 8, body, 0)
-
-
-def krylov_kernel(pos, main_v, main_rd, mom, z_got, *refs):
+    unrolled(count, count, body, 0)
+
+
+def krylov_kernel(pos, main_v, main_rd, mom, z_own, z_got, *refs):
     moved, moved_ends, moved_hbm = refs[:2], refs[2:4], refs[4:6]
     v1_out, v2_out, spread, z_v, z_rd, big_v1, big_v2, sems = refs[6:]
     count, ny, nz = v1_out.shape
@@ -410,14 +416,20 @@
     for copy in copies:
         copy.start()
 
-    def split(p, carry):
-        tile = z_got[p]
+    tall = ny // 8
+
+    def split(at, rows, tile):
         keep = lax.shift_right_logical(iota2(tile.shape, 1), 6) == pos[2]
-        z_v[p] = jnp.where(keep, tile, 0.0)
-        z_rd[p] = jnp.where(keep, pltpu.roll(tile, 64, 1), 0.0)
-        return carry
-
-    unrolled(count + 6, 11 if count % 11 == 5 else 1, split, 0)
+        z_v[at, rows] = jnp.where(keep, tile, 0.0)
+        z_rd[at, rows] = jnp.where(keep, pltpu.roll(tile, 64, 1), 0.0)
+
+    for p in (-3, -2, -1, count, count + 1, count + 2):
+        start = count + 6 + tall * outer_index(p, count)
+        split(p + 3, slice(0, ny), z_got[start : start + tall].reshape(ny, 128))
+        split(p + 3, slice(ny, ny + 8), z_got[p + 3])
+    for x in range(count):
+        split(x + 3, slice(0, ny), z_own[x])
+        split(x + 3, slice(ny, ny + 8), z_got[x + 3])
 
     def v_at(at):
         return jnp.concatenate([main_v[at], z_v[at]], axis=1)
@@ -462,11 +474,11 @@
     zero = jnp.zeros((8, 128), F32)
     for p in (-2, -1, count, count + 1):
         big_v1[p + 2] = image_of(v_at, p + 3)[1] * rd_at(p + 3)
-    k1, k2 = unrolled(count, 8, first, (zero, zero))
+    k1, k2 = unrolled(count, count, first, (zero, zero))
     for p in (-1, count):
         big_v2[p + 1] = image_of(v1_at, p + 2)[1] * rd_at(p + 3)
-    k3, k4 = unrolled(count, 8, second, (zero, zero))
-    k5 = unrolled(count, 8, third, zero)
+    k3, k4 = unrolled(count, count, second, (zero, zero))
+    k5 = unrolled(count, count, third, zero)
     rows = iota2((8, 128), 0)
     result = mom[...]
     for at, total in enumerate((k1, k2, k3, k4, k5)):
@@ -496,7 +508,8 @@
         rate = by_label(self.labels[x], self.rates)
         for c, (kx, ky, kz) in enumerate(PARTS):
             rows = low_high(self.odd_y, [y[5 + c, pl.ds(x, 1), :] for y in self.yg])
-            column = self.zg[x][:, c : c + 1]
+            lane = STRESS_LANE + c
+            column = self.zg[x][:, lane : lane + 1]
             yu, yl = shift_y(mine(ky), rows)
             zu, zl = shift_z(mine(kz), column, self.gz == 0)
             force = 0.5 * (((upper(c, kx) - lower(c, kx)) + (yu - yl)) + (zu - zl))
@@ -539,7 +552,7 @@
             force.plane(x, lower, lambda k: stress[k, x], upper, vel_out, disp_out, x)
         return carry
 
-    lax.fori_loop(0, steps, several, 0)
+    unrolled(steps, 1, several, 0)
     for copy in copies:
         copy.wait()
 
@@ -788,7 +801,7 @@
         "svva" + "v" * len(xy),
         (pos, v0, rd, token, *xy),
         "v",
-        [arr(nx + 6, ny + 8, 128)],
+        [arr(nx + 6 + 6 * (ny // 8), 8, 128)],
         4 * size,
     )
     z_got = swap(joined, "gz", z_pairs)
@@ -803,8 +816,8 @@
     peers = lax.axis_size("gx") * lax.axis_size("gy") * lax.axis_size("gz")
     new_disp, new_vel, v1, v2, spread = call(
         krylov_kernel,
-        "svvvvvvvv",
-        (pos, main_v, main_rd, mom, z_got, *moved, *moved_ends),
+        "svvvvvvvvv",
+        (pos, main_v, main_rd, mom, stress_z, z_got, *moved, *moved_ends),
         "hhvvv",
         [fields3, fields3, field, field, arr(peers, 1, 128)],
         60 * size,

time: 46.5 us -> 46.7 us (level)
  Pallas kernels: 14.8 us -> 16.3 us
  blocking collectives: 11.9 us -> 11.3 us
    pallas_call x10, Pallas kernels: 14.8 us -> 16.3 us  [call(): pl.pallas_call(kernel, out_shape=outs, in_specs=[spec_of(k, a) for k, a i...]
    all_to_all x1, blocking collectives: 11.9 us -> 11.3 us  [per_device(): mom = lax.all_to_all(spread, ('gx', 'gy', 'gz'), 0, 0, tiled=True)]
  transfers between devices with their start and end apart: 11 -> 11, of which waited for: 1 -> 2; matrix products, arithmetic and copies ran while one was open for 0% -> 0% of each run, Pallas kernels for 16% -> 18%
where the time goes in v12:
time: 46.7 us; the launch traced here: 46.5 us
  Pallas kernels  16.3 us (35%)
  starting transfers between devices  15.6 us (33%)
  blocking collectives  11.3 us (24%)
  other arithmetic  1.82 us (4%)
  between operations  0.92 us (2%)
  waiting for transfers between devices  0.57 us (1%)
    pallas_call x10, Pallas kernels, call(): pl.pallas_call(kernel, out_shape=outs, in_specs=[spec_of(k, a) for k, a i...  16.3 us
    ppermute x11, starting transfers between devices, swap(): return lax.ppermute(array, axis, pairs + [(b, a) for a, b in pairs])  15.6 us
    all_to_all x1, blocking collectives, per_device(): mom = lax.all_to_all(spread, ('gx', 'gy', 'gz'), 0, 0, tiled=True)  11.3 us
    concatenate x1, other arithmetic, per_device(): both = jnp.concatenate([displacement, damage[None]])  1.72 us
  transfers between devices with their start and end apart: 11, of which 2 were waited for; matrix products, arithmetic and copies ran while one was open for 0% of the time, Pallas kernels for 18%

profile of v12, /device:TPU:0, one launch (start us, length us, event | category | flops | bytes accessed | tf_op | source)
XLA Modules:
  0.0 46.5 jit_solution(8403229162992499507)
XLA Ops:
  0.6 1.7 %pad_maximum_fusion.disp = f32[4,16,32,256]{3,2,1,0:T(8,128)S(1)} fusion(f32[1,16,32,256]{3,2,1,0:T(8,128)} %bitcast.4, f32[3,16,32,256]{3,2,1,0:T(8,128)} %param.9), kind=kLoop, calls=%fused_computation | loop fusion | flops 524288 | bytes 4194304 | tf_op jit(solution)/shard_map/concatenate | solution.py:718
  2.4 0.1 pad_add_fusion.pos
  2.4 0.9 %shard_map.120 = (f32[4,16,256]{2,1,0:T(8,128)S(1)}, f32[16,32,128]{2,1,0:T(8,128)S(1)}) custom-call(s32[3]{0:T(128)S(1)} %pad_add_fusion.pos, f32[4,16,32,256]{3,2,1,0:T(8,128)S(1)} %pad_maximum_fusion.disp), custom_call_target="tpu_custom_call" | custom-call | flops 131072 | bytes 2424844 | tf_op jit(solution)/shard_map/pallas_call | solution.py:687
  3.3 0.0 copy-start.7
  3.4 0.0 copy-start
  3.4 0.0 copy-start.2
  3.4 0.0 copy-start.3
  3.4 0.5 %collective-permute-start.1 = (f32[16,32,128]{2,1,0:T(8,128)S(1)}, f32[16,32,128]{2,1,0:T(8,128)S(1)}, u32[]{:S(2)}, u32[]{:S(2)}) collective-permute-start(f32[16,32,128]{2,1,0:T(8,128)S(1)} %get-tuple-element.40.after), channel_id=1, source_target_pairs={{0,1},{1,0},{2,3},{3,2},{4,5},{5,4},{6,7},{7,6},{8,9},{9,8},{10,11... | collective-permute-start | bytes 786440 | tf_op jit(solution)/shard_map/ppermute | solution.py:652
  3.9 2.6 %collective-permute-start = (f32[4,16,256]{2,1,0:T(8,128)S(1)}, f32[4,16,256]{2,1,0:T(8,128)S(1)}, u32[]{:S(2)}, u32[]{:S(2)}) collective-permute-start(f32[4,16,256]{2,1,0:T(8,128)S(1)} %get-tuple-element.39), channel_id=1, source_target_pairs={{0,2},{2,0},{1,3},{3,1},{4,6},{6,4},{5,7},{7,5},{8,10},{10,8},{9,1... | collective-permute-start | bytes 196616 | tf_op jit(solution)/shard_map/ppermute | solution.py:652
  6.5 0.6 %shard_map.121 = (f32[4,32,256]{2,1,0:T(8,128)S(1)}, f32[4,32,256]{2,1,0:T(8,128)S(1)}) custom-call(s32[3]{0:T(128)S(1)} %pad_add_fusion.pos, f32[4,16,32,256]{3,2,1,0:T(8,128)S(1)} %pad_maximum_fusion.disp, f32[16,32,128]{2,1,0:T(8,128)S(1)} %get-tuple-element.40.after), custom_call_target="tpu_custom_call" | custom-call | flops 131072 | bytes 2621452 | tf_op jit(solution)/shard_map/pallas_call | solution.py:687
  7.0 1.6 %collective-permute-start.2 = (f32[4,32,256]{2,1,0:T(8,128)S(1)}, f32[4,32,256]{2,1,0:T(8,128)S(1)}, u32[]{:S(2)}, u32[]{:S(2)}) collective-permute-start(f32[4,32,256]{2,1,0:T(8,128)S(1)} %get-tuple-element.41), channel_id=1, source_target_pairs={{0,4},{8,12},{4,0},{12,8},{1,5},{9,13},{5,1},{13,9},{2,6},{10,14},... | collective-permute-start | bytes 393224 | tf_op jit(solution)/shard_map/ppermute | solution.py:652
  8.7 0.7 %collective-permute-start.3 = (f32[4,32,256]{2,1,0:T(8,128)S(1)}, f32[4,32,256]{2,1,0:T(8,128)S(1)}, u32[]{:S(2)}, u32[]{:S(2)}) collective-permute-start(f32[4,32,256]{2,1,0:T(8,128)S(1)} %get-tuple-element.42), channel_id=1, source_target_pairs={{4,8},{8,4},{5,9},{9,5},{6,10},{10,6},{7,11},{11,7},{20,24},{24,20... | collective-permute-start | bytes 393224 | tf_op jit(solution)/shard_map/ppermute | solution.py:652
  9.4 0.0 copy-done.7
  9.4 0.0 collective-permute-done.refs_0_
  9.4 0.0 collective-permute-done.1.refs_1_
  9.4 0.0 copy-done
  9.4 0.0 copy-done.2
  9.4 0.0 copy-done.3
  9.4 3.7 %shard_map.122 = (f32[16,32,256]{2,1,0:T(8,128)S(1)}, f32[16,32,256]{2,1,0:T(8,128)S(1)}, f32[16,32,256]{2,1,0:T(8,128)S(1)}, f32[6,16,32,256]{3,2,1,0:T(8,128)S...) custom-call(s32[3]{0:T(128)S(1)} %pad_add_fusion.pos, ...), custom_call_target="tpu_custom_call" | custom-call | flops 18350080 | bytes 9113676 | tf_op jit(solution)/shard_map/pallas_call | solution.py:687
  13.1 0.0 collective-permute-done.2.refs_2_
  13.1 0.0 collective-permute-done.3.refs_3_
  13.1 0.0 copy-start.1
  13.2 0.0 copy-start.6
  13.2 1.1 %shard_map.123 = (f32[2,32,256]{2,1,0:T(8,128)S(1)}, f32[16,32,256]{2,1,0:T(8,128)S(1)}, f32[16,32,256]{2,1,0:T(8,128)S(1)}, f32[6,2,32,256]{3,2,1,0:T(8,128)S(1...) custom-call(s32[3]{0:T(128)S(1)} %pad_add_fusion.pos, ...), custom_call_target="tpu_custom_call" | custom-call | flops 2621440 | bytes 8134732 | tf_op jit(solution)/shard_map/pallas_call | solution.py:687
  14.2 0.0 copy-start.5
  14.2 0.1 collective-permute-start.5
  14.3 4.5 %collective-permute-start.6 = (f32[8,32,256]{2,1,0:T(8,128)S(1)}, f32[8,32,256]{2,1,0:T(8,128)S(1)}, u32[]{:S(2)}, u32[]{:S(2)}) collective-permute-start(f32[8,32,256]{2,1,0:T(8,128)S(1)} %get-tuple-element.54), channel_id=1, source_target_pairs={{0,4},{8,12},{4,0},{12,8},{1,5},{9,13},{5,1},{13,9},{2,6},{10,14},... | collective-permute-start | bytes 786440 | tf_op jit(solution)/shard_map/ppermute | solution.py:652
  18.8 0.7 %collective-permute-start.7 = (f32[8,32,256]{2,1,0:T(8,128)S(1)}, f32[8,32,256]{2,1,0:T(8,128)S(1)}, u32[]{:S(2)}, u32[]{:S(2)}) collective-permute-start(f32[8,32,256]{2,1,0:T(8,128)S(1)} %get-tuple-element.55), channel_id=1, source_target_pairs={{4,8},{8,4},{5,9},{9,5},{6,10},{10,6},{7,11},{11,7},{20,24},{24,20... | collective-permute-start | bytes 786440 | tf_op jit(solution)/shard_map/ppermute | solution.py:652
  19.4 0.6 %collective-permute-start.4 = (f32[8,16,256]{2,1,0:T(8,128)S(1)}, f32[8,16,256]{2,1,0:T(8,128)S(1)}, u32[]{:S(2)}, u32[]{:S(2)}) collective-permute-start(f32[8,16,256]{2,1,0:T(8,128)S(1)} %get-tuple-element.48), channel_id=1, source_target_pairs={{0,2},{2,0},{1,3},{3,1},{4,6},{6,4},{5,7},{7,5},{8,10},{10,8},{9,1... | collective-permute-start | bytes 393224 | tf_op jit(solution)/shard_map/ppermute | solution.py:652
  20.0 0.0 collective-permute-done.5.after.refs_1_.z_own
  20.1 0.6 %shard_map.124 = (f32[2,8,256]{2,1,0:T(8,128)S(1)}, f32[2,8,256]{2,1,0:T(8,128)S(1)}) custom-call(s32[3]{0:T(128)S(1)} %pad_add_fusion.pos, f32[16,32,128]{2,1,0:T(8,128)S(1)} %collective-permute-done.5.after.refs_1_.z_own, f32[16,32,256]{2,1,0:T(8,128)S(1)} %get-tuple-element.52.v.refs_4_.v0, f32[16,32,256]{2,1,0:T(8,128)S(1)} %get-tuple-element.53.rd.refs_5_), custom_call_target="tpu_custom_call" | custom-call | flops 1024 | bytes 1343500 | tf_op jit(solution)/shard_map/pallas_call | solution.py:687
  20.6 3.7 %collective-permute-start.8 = (f32[2,8,256]{2,1,0:T(8,128)S(1)}, f32[2,8,256]{2,1,0:T(8,128)S(1)}, u32[]{:S(2)}, u32[]{:S(2)}) collective-permute-start(f32[2,8,256]{2,1,0:T(8,128)S(1)} %get-tuple-element.56), channel_id=1, source_target_pairs={{0,6},{2,4},{8,14},{10,12},{6,0},{4,2},{14,8},{12,10},{1,7},{3,5},... | collective-permute-start | bytes 49160 | tf_op jit(solution)/shard_map/ppermute | solution.py:652
  24.3 0.7 %collective-permute-start.9 = (f32[2,8,256]{2,1,0:T(8,128)S(1)}, f32[2,8,256]{2,1,0:T(8,128)S(1)}, u32[]{:S(2)}, u32[]{:S(2)}) collective-permute-start(f32[2,8,256]{2,1,0:T(8,128)S(1)} %get-tuple-element.57), channel_id=1, source_target_pairs={{4,10},{6,8},{10,4},{8,6},{5,11},{7,9},{11,5},{9,7},{20,26},{22,24... | collective-permute-start | bytes 49160 | tf_op jit(solution)/shard_map/ppermute | solution.py:652
  25.0 0.1 collective-permute-done.4.refs_0_.refs_8_.refs_2_
  25.1 0.0 copy-done.1
  25.1 0.0 copy-done.6
  25.1 0.0 copy-done.5
  25.1 2.6 %shard_map.126 = (f32[16,32,256]{2,1,0:T(8,128)}, f32[3,16,32,256]{3,2,1,0:T(8,128)S(1)}, f32[3,16,32,256]{3,2,1,0:T(8,128)S(1)}, f32[8,128]{1,0:T(8,128)S(1)}) custom-call(s32[3]{0:T(128)S(1)} %pad_add_fusion.pos, f32[4,4]{1,0:T(4,128)S(1)} %pad_maximum_fusion.1.table, f32[3]{0:T(128)S(1)} %copy-done.6, f32[4,16,32,256]{3,2,1,0:T(8,128)S(1)} %pad_maximum_fusion.disp, ...), custom_call_target="tpu_custom_call" | custom-call | flops 7208960 | bytes 12914776 | tf_op jit(solution)/shard_map/pallas_call | solution.py:687
  27.7 0.0 collective-permute-done.6.refs_6_.refs_0_
  27.7 0.0 collective-permute-done.7.refs_7_.refs_1_
  27.8 0.0 collective-permute-done.8.refs_9_.refs_3_
  27.8 0.0 collective-permute-done.9.refs_10_.refs_4_
  27.8 0.7 %shard_map.127 = f32[46,8,128]{2,1,0:T(8,128)S(1)} custom-call(s32[3]{0:T(128)S(1)} %pad_add_fusion.pos, f32[16,32,256]{2,1,0:T(8,128)S(1)} %get-tuple-element.52.v.refs_4_.v0, f32[16,32,256]{2,1,0:T(8,128)S(1)} %get-tuple-element.53.rd.refs_5_, f32[8,128]{1,0:T(8,128)S(1)} %get-tuple-element.63.token, ...), custom_call_target="tpu_custom_call" | custom-call | flops 524288 | bytes 1929228 | tf_op jit(solution)/shard_map/pallas_call | solution.py:687
  28.4 0.1 collective-permute-start.10
  28.5 1.0 %shard_map.125 = (f32[3,2,32,256]{3,2,1,0:T(8,128)S(1)}, f32[3,2,32,256]{3,2,1,0:T(8,128)S(1)}, f32[22,40,256]{2,1,0:T(8,128)S(1)}, f32[22,40,256]{2,1,0:T(8,128)S(1)}) custom-call(s32[3]{0:T(128)S(1)} %pad_add_fusion.pos, f32[4,4]{1,0:T(4,128)S(1)} %pad_maximum_fusion.1.table, f32[3]{0:T(128)S(1)} %copy-done.6, ...), custom_call_target="tpu_custom_call" | custom-call | flops 1572864 | bytes 12583000 | tf_op jit(solution)/shard_map/pallas_call | solution.py:687
  29.5 0.4 collective-permute-done.10.z_got
  29.9 0.0 copy-start.4
  29.9 4.2 %shard_map.128 = (f32[3,16,32,256]{3,2,1,0:T(8,128)}, f32[3,16,32,256]{3,2,1,0:T(8,128)}, f32[16,32,256]{2,1,0:T(8,128)S(1)}, f32[16,32,256]{2,1,0:T(8,128)S(1)}, f32[16,1,128]{2,1,0:T(1,128)S(1)}) custom-call(s32[3]{0:T(128)S(1)} %pad_add_fusion.pos, f32[22,40,256]{2,1,0:T(8,128)S(1)} %get-tuple-element.58.main_v, ...), custom_call_target="tpu_custom_call" | custom-call | flops 7864320 | bytes 9998348 | tf_op jit(solution)/shard_map/pallas_call | solution.py:687
  34.1 11.3 %all_to_all.5.mom = f32[16,1,128]{2,1,0:T(1,128)S(1)} all-to-all(f32[16,1,128]{2,1,0:T(1,128)S(1)} %get-tuple-element.71), channel_id=1, replica_groups=mesh['case'=2,'gx'=4,'gy'=2,'gz'=2] {'gx','gy','gz'}, dimensions={0} | all-to-all | bytes 16384 | tf_op jit(solution)/shard_map/all_to_all | solution.py:832
  45.4 0.0 copy-done.4
  45.4 1.1 %shard_map.129 = f32[16,32,256]{2,1,0:T(8,128)} custom-call(f32[16,1,128]{2,1,0:T(1,128)S(1)} %all_to_all.5.mom, f32[16,32,256]{2,1,0:T(8,128)S(1)} %get-tuple-element.52.v.refs_4_.v0, f32[16,32,256]{2,1,0:T(8,128)S(1)} %get-tuple-element.72.v1, f32[16,32,256]{2,1,0:T(8,128)S(1)} %get-tuple-element.73.v2, f32[16,32,256]{2,1,0:T(8,128)S(1)} %copy-done.4), custom_call_target="tpu_custom_call" | custom-call | flops 1048576 | bytes 2629632 | tf_op jit(solution)/shard_map/pallas_call | solution.py:687
  (2 shorter events, 0.0 us)
Async XLA Ops:
  3.3 6.0 %copy-start.7 = (f32[4,4]{1,0:T(4,128)S(1)}, f32[4,4]{1,0:T(4,128)}, u32[]{:S(2)}) copy-start(f32[4,4]{1,0:T(4,128)} %param.16) | copy-start | bytes 196
  3.4 6.1 %copy-start = (s32[16,32,256]{2,1,0:T(8,128)S(1)}, s32[16,32,256]{2,1,0:T(8,128)}, u32[]{:S(2)}) copy-start(s32[16,32,256]{2,1,0:T(8,128)} %labels.7) | copy-start | bytes 1572868
  3.4 6.1 %copy-start.2 = (f32[16,32,256]{2,1,0:T(8,128)S(1)}, f32[16,32,256]{2,1,0:T(8,128)}, u32[]{:S(2)}) copy-start(f32[16,32,256]{2,1,0:T(8,128)} %history.3) | copy-start | bytes 1572868
  3.4 6.1 %copy-start.3 = (s32[16,32,256]{2,1,0:T(8,128)S(1)}, s32[16,32,256]{2,1,0:T(8,128)}, u32[]{:S(2)}) copy-start(s32[16,32,256]{2,1,0:T(8,128)} %notch.3) | copy-start | bytes 1572868
  3.4 6.0 %collective-permute-start.1 = (f32[16,32,128]{2,1,0:T(8,128)S(1)}, f32[16,32,128]{2,1,0:T(8,128)S(1)}, u32[]{:S(2)}, u32[]{:S(2)}) collective-permute-start(f32[16,32,128]{2,1,0:T(8,128)S(1)} %get-tuple-element.40.after), channel_id=1, source_target_pairs={{0,1},{1,0},{2,3},{3,2},{4,5},{5,4},{6,7},{7,6},{8,9},{9,8},{10,11... | collective-permute-start | bytes 786440 | tf_op jit(solution)/shard_map/ppermute | solution.py:652
  3.9 5.5 %collective-permute-start = (f32[4,16,256]{2,1,0:T(8,128)S(1)}, f32[4,16,256]{2,1,0:T(8,128)S(1)}, u32[]{:S(2)}, u32[]{:S(2)}) collective-permute-start(f32[4,16,256]{2,1,0:T(8,128)S(1)} %get-tuple-element.39), channel_id=1, source_target_pairs={{0,2},{2,0},{1,3},{3,1},{4,6},{6,4},{5,7},{7,5},{8,10},{10,8},{9,1... | collective-permute-start | bytes 196616 | tf_op jit(solution)/shard_map/ppermute | solution.py:652
  7.0 6.1 %collective-permute-start.2 = (f32[4,32,256]{2,1,0:T(8,128)S(1)}, f32[4,32,256]{2,1,0:T(8,128)S(1)}, u32[]{:S(2)}, u32[]{:S(2)}) collective-permute-start(f32[4,32,256]{2,1,0:T(8,128)S(1)} %get-tuple-element.41), channel_id=1, source_target_pairs={{0,4},{8,12},{4,0},{12,8},{1,5},{9,13},{5,1},{13,9},{2,6},{10,14},... | collective-permute-start | bytes 393224 | tf_op jit(solution)/shard_map/ppermute | solution.py:652
  8.7 4.4 %collective-permute-start.3 = (f32[4,32,256]{2,1,0:T(8,128)S(1)}, f32[4,32,256]{2,1,0:T(8,128)S(1)}, u32[]{:S(2)}, u32[]{:S(2)}) collective-permute-start(f32[4,32,256]{2,1,0:T(8,128)S(1)} %get-tuple-element.42), channel_id=1, source_target_pairs={{4,8},{8,4},{5,9},{9,5},{6,10},{10,6},{7,11},{11,7},{20,24},{24,20... | collective-permute-start | bytes 393224 | tf_op jit(solution)/shard_map/ppermute | solution.py:652
  13.1 11.9 %copy-start.1 = (f32[3,16,32,256]{3,2,1,0:T(8,128)S(1)}, f32[3,16,32,256]{3,2,1,0:T(8,128)}, u32[]{:S(2)}) copy-start(f32[3,16,32,256]{3,2,1,0:T(8,128)} %vel.3) | copy-start | bytes 4718596
  13.2 11.9 %copy-start.6 = (f32[3]{0:T(128)S(1)}, f32[3]{0:T(128)}, u32[]{:S(2)}) copy-start(f32[3]{0:T(128)} %impact.3) | copy-start | bytes 40
  14.2 10.9 %copy-start.5 = (s32[16,32,256]{2,1,0:T(8,128)S(1)}, s32[16,32,256]{2,1,0:T(8,128)}, u32[]{:S(2)}) copy-start(s32[16,32,256]{2,1,0:T(8,128)} %contact.3) | copy-start | bytes 1572868
  14.2 5.8 %collective-permute-start.5 = (f32[16,32,128]{2,1,0:T(8,128)S(1)}, f32[16,32,128]{2,1,0:T(8,128)S(1)}, u32[]{:S(2)}, u32[]{:S(2)}) collective-permute-start(f32[16,32,128]{2,1,0:T(8,128)S(1)} %get-tuple-element.49), channel_id=1, source_target_pairs={{0,1},{1,0},{2,3},{3,2},{4,5},{5,4},{6,7},{7,6},{8,9},{9,8},{10,11... | collective-permute-start | bytes 786440 | tf_op jit(solution)/shard_map/ppermute | solution.py:652
  14.3 13.4 %collective-permute-start.6 = (f32[8,32,256]{2,1,0:T(8,128)S(1)}, f32[8,32,256]{2,1,0:T(8,128)S(1)}, u32[]{:S(2)}, u32[]{:S(2)}) collective-permute-start(f32[8,32,256]{2,1,0:T(8,128)S(1)} %get-tuple-element.54), channel_id=1, source_target_pairs={{0,4},{8,12},{4,0},{12,8},{1,5},{9,13},{5,1},{13,9},{2,6},{10,14},... | collective-permute-start | bytes 786440 | tf_op jit(solution)/shard_map/ppermute | solution.py:652
  18.8 9.0 %collective-permute-start.7 = (f32[8,32,256]{2,1,0:T(8,128)S(1)}, f32[8,32,256]{2,1,0:T(8,128)S(1)}, u32[]{:S(2)}, u32[]{:S(2)}) collective-permute-start(f32[8,32,256]{2,1,0:T(8,128)S(1)} %get-tuple-element.55), channel_id=1, source_target_pairs={{4,8},{8,4},{5,9},{9,5},{6,10},{10,6},{7,11},{11,7},{20,24},{24,20... | collective-permute-start | bytes 786440 | tf_op jit(solution)/shard_map/ppermute | solution.py:652
  19.4 5.6 %collective-permute-start.4 = (f32[8,16,256]{2,1,0:T(8,128)S(1)}, f32[8,16,256]{2,1,0:T(8,128)S(1)}, u32[]{:S(2)}, u32[]{:S(2)}) collective-permute-start(f32[8,16,256]{2,1,0:T(8,128)S(1)} %get-tuple-element.48), channel_id=1, source_target_pairs={{0,2},{2,0},{1,3},{3,1},{4,6},{6,4},{5,7},{7,5},{8,10},{10,8},{9,1... | collective-permute-start | bytes 393224 | tf_op jit(solution)/shard_map/ppermute | solution.py:652
  20.6 7.1 %collective-permute-start.8 = (f32[2,8,256]{2,1,0:T(8,128)S(1)}, f32[2,8,256]{2,1,0:T(8,128)S(1)}, u32[]{:S(2)}, u32[]{:S(2)}) collective-permute-start(f32[2,8,256]{2,1,0:T(8,128)S(1)} %get-tuple-element.56), channel_id=1, source_target_pairs={{0,6},{2,4},{8,14},{10,12},{6,0},{4,2},{14,8},{12,10},{1,7},{3,5},... | collective-permute-start | bytes 49160 | tf_op jit(solution)/shard_map/ppermute | solution.py:652
  24.3 3.5 %collective-permute-start.9 = (f32[2,8,256]{2,1,0:T(8,128)S(1)}, f32[2,8,256]{2,1,0:T(8,128)S(1)}, u32[]{:S(2)}, u32[]{:S(2)}) collective-permute-start(f32[2,8,256]{2,1,0:T(8,128)S(1)} %get-tuple-element.57), channel_id=1, source_target_pairs={{4,10},{6,8},{10,4},{8,6},{5,11},{7,9},{11,5},{9,7},{20,26},{22,24... | collective-permute-start | bytes 49160 | tf_op jit(solution)/shard_map/ppermute | solution.py:652
  28.4 1.5 %collective-permute-start.10 = (f32[46,8,128]{2,1,0:T(8,128)S(1)}, f32[46,8,128]{2,1,0:T(8,128)S(1)}, u32[]{:S(2)}, u32[]{:S(2)}) collective-permute-start(f32[46,8,128]{2,1,0:T(8,128)S(1)} %shard_map.127), channel_id=1, source_target_pairs={{0,1},{1,0},{2,3},{3,2},{4,5},{5,4},{6,7},{7,6},{8,9},{9,8},{10,11... | collective-permute-start | bytes 565256 | tf_op jit(solution)/shard_map/ppermute | solution.py:652
  29.9 15.4 %copy-start.4 = (f32[16,32,256]{2,1,0:T(8,128)S(1)}, f32[16,32,256]{2,1,0:T(8,128)}, u32[]{:S(2)}) copy-start(f32[16,32,256]{2,1,0:T(8,128)} %damage.1) | copy-start | bytes 1572868

commit v13 on v12

--- a/solution.py
+++ b/solution.py
@@ -202,9 +202,9 @@
         send_columns(zs, x, planes, self.gz, base, STRESS_LANE)
 
 
-def inner_steps(count):
+def inner_steps(count, most):
     inner = count - 2
-    many = max(m for m in range(1, 16) if inner % m == 0)
+    many = max(m for m in range(1, most + 1) if inner % m == 0)
     return inner // many, many
 
 
@@ -215,7 +215,7 @@
     )
     hist, rd_out, v_out, stress_out, mom_out = refs[n_y + 1 : n_y + 6]
     ys, zs = refs[n_y + 6 : 2 * n_y + 6], refs[2 * n_y + 6]
-    steps, many = inner_steps(damage.shape[0])
+    steps, many = inner_steps(damage.shape[0], 2)
 
     def several(step, total):
         for at in range(many):
@@ -427,9 +427,13 @@
         start = count + 6 + tall * outer_index(p, count)
         split(p + 3, slice(0, ny), z_got[start : start + tall].reshape(ny, 128))
         split(p + 3, slice(ny, ny + 8), z_got[p + 3])
-    for x in range(count):
+
+    def split_own(x, carry):
         split(x + 3, slice(0, ny), z_own[x])
         split(x + 3, slice(ny, ny + 8), z_got[x + 3])
+        return carry
+
+    unrolled(count, 8, split_own, 0)
 
     def v_at(at):
         return jnp.concatenate([main_v[at], z_v[at]], axis=1)
@@ -474,11 +478,11 @@
     zero = jnp.zeros((8, 128), F32)
     for p in (-2, -1, count, count + 1):
         big_v1[p + 2] = image_of(v_at, p + 3)[1] * rd_at(p + 3)
-    k1, k2 = unrolled(count, count, first, (zero, zero))
+    k1, k2 = unrolled(count, 8, first, (zero, zero))
     for p in (-1, count):
         big_v2[p + 1] = image_of(v1_at, p + 2)[1] * rd_at(p + 3)
-    k3, k4 = unrolled(count, count, second, (zero, zero))
-    k5 = unrolled(count, count, third, zero)
+    k3, k4 = unrolled(count, 8, second, (zero, zero))
+    k5 = unrolled(count, 8, third, zero)
     rows = iota2((8, 128), 0)
     result = mom[...]
     for at, total in enumerate((k1, k2, k3, k4, k5)):
@@ -524,7 +528,7 @@
     token[...] = jnp.zeros((8, 128), F32)
     force = Force(n_y, pos, table, impact, disp, vel, contact, labels, yg, zg)
     count = contact.shape[0]
-    steps, many = inner_steps(count)
+    steps, many = inner_steps(count, 7)
 
     inside = pl.ds(1, count - 2)
     copies = [

time: 46.7 us -> 45.9 us (0.983)
  Pallas kernels: 16.3 us -> 15.1 us
    pallas_call x10, Pallas kernels: 16.3 us -> 15.1 us  [call(): pl.pallas_call(kernel, out_shape=outs, in_specs=[spec_of(k, a) for k, a i...]
where the time goes in v13:
time: 45.9 us; the launch traced here: 45.7 us
  starting transfers between devices  15.4 us (34%)
  Pallas kernels  15.1 us (33%)
  blocking collectives  11.6 us (25%)
  other arithmetic  1.82 us (4%)
  between operations  0.93 us (2%)
  waiting for transfers between devices  0.8 us (2%)
    ppermute x11, starting transfers between devices, swap(): return lax.ppermute(array, axis, pairs + [(b, a) for a, b in pairs])  15.4 us
    pallas_call x10, Pallas kernels, call(): pl.pallas_call(kernel, out_shape=outs, in_specs=[spec_of(k, a) for k, a i...  15.1 us
    all_to_all x1, blocking collectives, per_device(): mom = lax.all_to_all(spread, ('gx', 'gy', 'gz'), 0, 0, tiled=True)  11.6 us
    concatenate x1, other arithmetic, per_device(): both = jnp.concatenate([displacement, damage[None]])  1.72 us
  transfers between devices with their start and end apart: 11, of which 2 were waited for; matrix products, arithmetic and copies ran while one was open for 0% of the time, Pallas kernels for 18%

profile of v13, /device:TPU:0, one launch (start us, length us, event | category | flops | bytes accessed | tf_op | source)
XLA Modules:
  0.0 45.7 jit_solution(16618058694255663337)
XLA Ops:
  0.6 1.7 %pad_maximum_fusion.disp = f32[4,16,32,256]{3,2,1,0:T(8,128)S(1)} fusion(f32[1,16,32,256]{3,2,1,0:T(8,128)} %bitcast.4, f32[3,16,32,256]{3,2,1,0:T(8,128)} %param.9), kind=kLoop, calls=%fused_computation | loop fusion | flops 524288 | bytes 4194304 | tf_op jit(solution)/shard_map/concatenate | solution.py:722
  2.4 0.1 pad_add_fusion.pos
  2.4 0.9 %shard_map.120 = (f32[4,16,256]{2,1,0:T(8,128)S(1)}, f32[16,32,128]{2,1,0:T(8,128)S(1)}) custom-call(s32[3]{0:T(128)S(1)} %pad_add_fusion.pos, f32[4,16,32,256]{3,2,1,0:T(8,128)S(1)} %pad_maximum_fusion.disp), custom_call_target="tpu_custom_call" | custom-call | flops 131072 | bytes 2424844 | tf_op jit(solution)/shard_map/pallas_call | solution.py:691
  3.3 0.0 copy-start.7
  3.4 0.0 copy-start
  3.4 0.0 copy-start.2
  3.4 0.0 copy-start.3
  3.4 0.5 %collective-permute-start.1 = (f32[16,32,128]{2,1,0:T(8,128)S(1)}, f32[16,32,128]{2,1,0:T(8,128)S(1)}, u32[]{:S(2)}, u32[]{:S(2)}) collective-permute-start(f32[16,32,128]{2,1,0:T(8,128)S(1)} %get-tuple-element.40.after), channel_id=1, source_target_pairs={{0,1},{1,0},{2,3},{3,2},{4,5},{5,4},{6,7},{7,6},{8,9},{9,8},{10,11... | collective-permute-start | bytes 786440 | tf_op jit(solution)/shard_map/ppermute | solution.py:656
  3.9 2.6 %collective-permute-start = (f32[4,16,256]{2,1,0:T(8,128)S(1)}, f32[4,16,256]{2,1,0:T(8,128)S(1)}, u32[]{:S(2)}, u32[]{:S(2)}) collective-permute-start(f32[4,16,256]{2,1,0:T(8,128)S(1)} %get-tuple-element.39), channel_id=1, source_target_pairs={{0,2},{2,0},{1,3},{3,1},{4,6},{6,4},{5,7},{7,5},{8,10},{10,8},{9,1... | collective-permute-start | bytes 196616 | tf_op jit(solution)/shard_map/ppermute | solution.py:656
  6.5 0.6 %shard_map.121 = (f32[4,32,256]{2,1,0:T(8,128)S(1)}, f32[4,32,256]{2,1,0:T(8,128)S(1)}) custom-call(s32[3]{0:T(128)S(1)} %pad_add_fusion.pos, f32[4,16,32,256]{3,2,1,0:T(8,128)S(1)} %pad_maximum_fusion.disp, f32[16,32,128]{2,1,0:T(8,128)S(1)} %get-tuple-element.40.after), custom_call_target="tpu_custom_call" | custom-call | flops 131072 | bytes 2621452 | tf_op jit(solution)/shard_map/pallas_call | solution.py:691
  7.0 1.6 %collective-permute-start.2 = (f32[4,32,256]{2,1,0:T(8,128)S(1)}, f32[4,32,256]{2,1,0:T(8,128)S(1)}, u32[]{:S(2)}, u32[]{:S(2)}) collective-permute-start(f32[4,32,256]{2,1,0:T(8,128)S(1)} %get-tuple-element.41), channel_id=1, source_target_pairs={{0,4},{8,12},{4,0},{12,8},{1,5},{9,13},{5,1},{13,9},{2,6},{10,14},... | collective-permute-start | bytes 393224 | tf_op jit(solution)/shard_map/ppermute | solution.py:656
  8.7 0.7 %collective-permute-start.3 = (f32[4,32,256]{2,1,0:T(8,128)S(1)}, f32[4,32,256]{2,1,0:T(8,128)S(1)}, u32[]{:S(2)}, u32[]{:S(2)}) collective-permute-start(f32[4,32,256]{2,1,0:T(8,128)S(1)} %get-tuple-element.42), channel_id=1, source_target_pairs={{4,8},{8,4},{5,9},{9,5},{6,10},{10,6},{7,11},{11,7},{20,24},{24,20... | collective-permute-start | bytes 393224 | tf_op jit(solution)/shard_map/ppermute | solution.py:656
  9.4 0.0 copy-done.7
  9.4 0.0 collective-permute-done.refs_0_
  9.4 0.0 collective-permute-done.1.refs_1_
  9.4 0.0 copy-done
  9.4 0.0 copy-done.2
  9.4 0.0 copy-done.3
  9.4 3.9 %shard_map.122 = (f32[16,32,256]{2,1,0:T(8,128)S(1)}, f32[16,32,256]{2,1,0:T(8,128)S(1)}, f32[16,32,256]{2,1,0:T(8,128)S(1)}, f32[6,16,32,256]{3,2,1,0:T(8,128)S...) custom-call(s32[3]{0:T(128)S(1)} %pad_add_fusion.pos, ...), custom_call_target="tpu_custom_call" | custom-call | flops 18350080 | bytes 9113676 | tf_op jit(solution)/shard_map/pallas_call | solution.py:691
  13.3 0.0 collective-permute-done.2.refs_2_
  13.4 0.0 collective-permute-done.3.refs_3_
  13.4 0.0 copy-start.1
  13.4 0.0 copy-start.6
  13.4 1.1 %shard_map.123 = (f32[2,32,256]{2,1,0:T(8,128)S(1)}, f32[16,32,256]{2,1,0:T(8,128)S(1)}, f32[16,32,256]{2,1,0:T(8,128)S(1)}, f32[6,2,32,256]{3,2,1,0:T(8,128)S(1...) custom-call(s32[3]{0:T(128)S(1)} %pad_add_fusion.pos, ...), custom_call_target="tpu_custom_call" | custom-call | flops 2621440 | bytes 8134732 | tf_op jit(solution)/shard_map/pallas_call | solution.py:691
  14.5 0.0 copy-start.5
  14.5 0.1 collective-permute-start.5
  14.5 4.5 %collective-permute-start.6 = (f32[8,32,256]{2,1,0:T(8,128)S(1)}, f32[8,32,256]{2,1,0:T(8,128)S(1)}, u32[]{:S(2)}, u32[]{:S(2)}) collective-permute-start(f32[8,32,256]{2,1,0:T(8,128)S(1)} %get-tuple-element.54), channel_id=1, source_target_pairs={{0,4},{8,12},{4,0},{12,8},{1,5},{9,13},{5,1},{13,9},{2,6},{10,14},... | collective-permute-start | bytes 786440 | tf_op jit(solution)/shard_map/ppermute | solution.py:656
  19.0 0.7 %collective-permute-start.7 = (f32[8,32,256]{2,1,0:T(8,128)S(1)}, f32[8,32,256]{2,1,0:T(8,128)S(1)}, u32[]{:S(2)}, u32[]{:S(2)}) collective-permute-start(f32[8,32,256]{2,1,0:T(8,128)S(1)} %get-tuple-element.55), channel_id=1, source_target_pairs={{4,8},{8,4},{5,9},{9,5},{6,10},{10,6},{7,11},{11,7},{20,24},{24,20... | collective-permute-start | bytes 786440 | tf_op jit(solution)/shard_map/ppermute | solution.py:656
  19.7 0.6 %collective-permute-start.4 = (f32[8,16,256]{2,1,0:T(8,128)S(1)}, f32[8,16,256]{2,1,0:T(8,128)S(1)}, u32[]{:S(2)}, u32[]{:S(2)}) collective-permute-start(f32[8,16,256]{2,1,0:T(8,128)S(1)} %get-tuple-element.48), channel_id=1, source_target_pairs={{0,2},{2,0},{1,3},{3,1},{4,6},{6,4},{5,7},{7,5},{8,10},{10,8},{9,1... | collective-permute-start | bytes 393224 | tf_op jit(solution)/shard_map/ppermute | solution.py:656
  20.3 0.0 collective-permute-done.5.after.refs_1_.z_own
  20.3 0.6 %shard_map.124 = (f32[2,8,256]{2,1,0:T(8,128)S(1)}, f32[2,8,256]{2,1,0:T(8,128)S(1)}) custom-call(s32[3]{0:T(128)S(1)} %pad_add_fusion.pos, f32[16,32,128]{2,1,0:T(8,128)S(1)} %collective-permute-done.5.after.refs_1_.z_own, f32[16,32,256]{2,1,0:T(8,128)S(1)} %get-tuple-element.52.v.refs_4_.v0, f32[16,32,256]{2,1,0:T(8,128)S(1)} %get-tuple-element.53.rd.refs_5_), custom_call_target="tpu_custom_call" | custom-call | flops 1024 | bytes 1343500 | tf_op jit(solution)/shard_map/pallas_call | solution.py:691
  20.8 3.5 %collective-permute-start.8 = (f32[2,8,256]{2,1,0:T(8,128)S(1)}, f32[2,8,256]{2,1,0:T(8,128)S(1)}, u32[]{:S(2)}, u32[]{:S(2)}) collective-permute-start(f32[2,8,256]{2,1,0:T(8,128)S(1)} %get-tuple-element.56), channel_id=1, source_target_pairs={{0,6},{2,4},{8,14},{10,12},{6,0},{4,2},{14,8},{12,10},{1,7},{3,5},... | collective-permute-start | bytes 49160 | tf_op jit(solution)/shard_map/ppermute | solution.py:656
  24.3 0.7 %collective-permute-start.9 = (f32[2,8,256]{2,1,0:T(8,128)S(1)}, f32[2,8,256]{2,1,0:T(8,128)S(1)}, u32[]{:S(2)}, u32[]{:S(2)}) collective-permute-start(f32[2,8,256]{2,1,0:T(8,128)S(1)} %get-tuple-element.57), channel_id=1, source_target_pairs={{4,10},{6,8},{10,4},{8,6},{5,11},{7,9},{11,5},{9,7},{20,26},{22,24... | collective-permute-start | bytes 49160 | tf_op jit(solution)/shard_map/ppermute | solution.py:656
  25.0 0.3 collective-permute-done.4.refs_0_.refs_8_.refs_2_
  25.3 0.0 copy-done.1
  25.3 0.0 copy-done.6
  25.3 0.0 copy-done.5
  25.3 2.1 %shard_map.126 = (f32[16,32,256]{2,1,0:T(8,128)}, f32[3,16,32,256]{3,2,1,0:T(8,128)S(1)}, f32[3,16,32,256]{3,2,1,0:T(8,128)S(1)}, f32[8,128]{1,0:T(8,128)S(1)}) custom-call(s32[3]{0:T(128)S(1)} %pad_add_fusion.pos, f32[4,4]{1,0:T(4,128)S(1)} %pad_maximum_fusion.1.table, f32[3]{0:T(128)S(1)} %copy-done.6, f32[4,16,32,256]{3,2,1,0:T(8,128)S(1)} %pad_maximum_fusion.disp, ...), custom_call_target="tpu_custom_call" | custom-call | flops 7208960 | bytes 12914776 | tf_op jit(solution)/shard_map/pallas_call | solution.py:691
  27.4 0.0 collective-permute-done.6.refs_6_.refs_0_
  27.4 0.0 collective-permute-done.7.refs_7_.refs_1_
  27.4 0.0 collective-permute-done.8.refs_9_.refs_3_
  27.4 0.0 collective-permute-done.9.refs_10_.refs_4_
  27.4 0.7 %shard_map.127 = f32[46,8,128]{2,1,0:T(8,128)S(1)} custom-call(s32[3]{0:T(128)S(1)} %pad_add_fusion.pos, f32[16,32,256]{2,1,0:T(8,128)S(1)} %get-tuple-element.52.v.refs_4_.v0, f32[16,32,256]{2,1,0:T(8,128)S(1)} %get-tuple-element.53.rd.refs_5_, f32[8,128]{1,0:T(8,128)S(1)} %get-tuple-element.63.token, ...), custom_call_target="tpu_custom_call" | custom-call | flops 524288 | bytes 1929228 | tf_op jit(solution)/shard_map/pallas_call | solution.py:691
  28.1 0.1 collective-permute-start.10
  28.2 1.0 %shard_map.125 = (f32[3,2,32,256]{3,2,1,0:T(8,128)S(1)}, f32[3,2,32,256]{3,2,1,0:T(8,128)S(1)}, f32[22,40,256]{2,1,0:T(8,128)S(1)}, f32[22,40,256]{2,1,0:T(8,128)S(1)}) custom-call(s32[3]{0:T(128)S(1)} %pad_add_fusion.pos, f32[4,4]{1,0:T(4,128)S(1)} %pad_maximum_fusion.1.table, f32[3]{0:T(128)S(1)} %copy-done.6, ...), custom_call_target="tpu_custom_call" | custom-call | flops 1572864 | bytes 12583000 | tf_op jit(solution)/shard_map/pallas_call | solution.py:691
  29.2 0.4 collective-permute-done.10.z_got
  29.6 0.0 copy-start.4
  29.6 3.4 %shard_map.128 = (f32[3,16,32,256]{3,2,1,0:T(8,128)}, f32[3,16,32,256]{3,2,1,0:T(8,128)}, f32[16,32,256]{2,1,0:T(8,128)S(1)}, f32[16,32,256]{2,1,0:T(8,128)S(1)}, f32[16,1,128]{2,1,0:T(1,128)S(1)}) custom-call(s32[3]{0:T(128)S(1)} %pad_add_fusion.pos, f32[22,40,256]{2,1,0:T(8,128)S(1)} %get-tuple-element.58.main_v, ...), custom_call_target="tpu_custom_call" | custom-call | flops 7864320 | bytes 9998348 | tf_op jit(solution)/shard_map/pallas_call | solution.py:691
  33.0 11.6 %all_to_all.5.mom = f32[16,1,128]{2,1,0:T(1,128)S(1)} all-to-all(f32[16,1,128]{2,1,0:T(1,128)S(1)} %get-tuple-element.71), channel_id=1, replica_groups=mesh['case'=2,'gx'=4,'gy'=2,'gz'=2] {'gx','gy','gz'}, dimensions={0} | all-to-all | bytes 16384 | tf_op jit(solution)/shard_map/all_to_all | solution.py:836
  44.6 0.0 copy-done.4
  44.6 1.1 %shard_map.129 = f32[16,32,256]{2,1,0:T(8,128)} custom-call(f32[16,1,128]{2,1,0:T(1,128)S(1)} %all_to_all.5.mom, f32[16,32,256]{2,1,0:T(8,128)S(1)} %get-tuple-element.52.v.refs_4_.v0, f32[16,32,256]{2,1,0:T(8,128)S(1)} %get-tuple-element.72.v1, f32[16,32,256]{2,1,0:T(8,128)S(1)} %get-tuple-element.73.v2, f32[16,32,256]{2,1,0:T(8,128)S(1)} %copy-done.4), custom_call_target="tpu_custom_call" | custom-call | flops 1048576 | bytes 2629632 | tf_op jit(solution)/shard_map/pallas_call | solution.py:691
  (2 shorter events, 0.0 us)
Async XLA Ops:
  3.3 6.0 %copy-start.7 = (f32[4,4]{1,0:T(4,128)S(1)}, f32[4,4]{1,0:T(4,128)}, u32[]{:S(2)}) copy-start(f32[4,4]{1,0:T(4,128)} %param.16) | copy-start | bytes 196
  3.4 6.1 %copy-start = (s32[16,32,256]{2,1,0:T(8,128)S(1)}, s32[16,32,256]{2,1,0:T(8,128)}, u32[]{:S(2)}) copy-start(s32[16,32,256]{2,1,0:T(8,128)} %labels.7) | copy-start | bytes 1572868
  3.4 6.1 %copy-start.2 = (f32[16,32,256]{2,1,0:T(8,128)S(1)}, f32[16,32,256]{2,1,0:T(8,128)}, u32[]{:S(2)}) copy-start(f32[16,32,256]{2,1,0:T(8,128)} %history.3) | copy-start | bytes 1572868
  3.4 6.1 %copy-start.3 = (s32[16,32,256]{2,1,0:T(8,128)S(1)}, s32[16,32,256]{2,1,0:T(8,128)}, u32[]{:S(2)}) copy-start(s32[16,32,256]{2,1,0:T(8,128)} %notch.3) | copy-start | bytes 1572868
  3.4 6.0 %collective-permute-start.1 = (f32[16,32,128]{2,1,0:T(8,128)S(1)}, f32[16,32,128]{2,1,0:T(8,128)S(1)}, u32[]{:S(2)}, u32[]{:S(2)}) collective-permute-start(f32[16,32,128]{2,1,0:T(8,128)S(1)} %get-tuple-element.40.after), channel_id=1, source_target_pairs={{0,1},{1,0},{2,3},{3,2},{4,5},{5,4},{6,7},{7,6},{8,9},{9,8},{10,11... | collective-permute-start | bytes 786440 | tf_op jit(solution)/shard_map/ppermute | solution.py:656
  3.9 5.5 %collective-permute-start = (f32[4,16,256]{2,1,0:T(8,128)S(1)}, f32[4,16,256]{2,1,0:T(8,128)S(1)}, u32[]{:S(2)}, u32[]{:S(2)}) collective-permute-start(f32[4,16,256]{2,1,0:T(8,128)S(1)} %get-tuple-element.39), channel_id=1, source_target_pairs={{0,2},{2,0},{1,3},{3,1},{4,6},{6,4},{5,7},{7,5},{8,10},{10,8},{9,1... | collective-permute-start | bytes 196616 | tf_op jit(solution)/shard_map/ppermute | solution.py:656
  7.0 6.3 %collective-permute-start.2 = (f32[4,32,256]{2,1,0:T(8,128)S(1)}, f32[4,32,256]{2,1,0:T(8,128)S(1)}, u32[]{:S(2)}, u32[]{:S(2)}) collective-permute-start(f32[4,32,256]{2,1,0:T(8,128)S(1)} %get-tuple-element.41), channel_id=1, source_target_pairs={{0,4},{8,12},{4,0},{12,8},{1,5},{9,13},{5,1},{13,9},{2,6},{10,14},... | collective-permute-start | bytes 393224 | tf_op jit(solution)/shard_map/ppermute | solution.py:656
  8.7 4.7 %collective-permute-start.3 = (f32[4,32,256]{2,1,0:T(8,128)S(1)}, f32[4,32,256]{2,1,0:T(8,128)S(1)}, u32[]{:S(2)}, u32[]{:S(2)}) collective-permute-start(f32[4,32,256]{2,1,0:T(8,128)S(1)} %get-tuple-element.42), channel_id=1, source_target_pairs={{4,8},{8,4},{5,9},{9,5},{6,10},{10,6},{7,11},{11,7},{20,24},{24,20... | collective-permute-start | bytes 393224 | tf_op jit(solution)/shard_map/ppermute | solution.py:656
  13.4 11.9 %copy-start.1 = (f32[3,16,32,256]{3,2,1,0:T(8,128)S(1)}, f32[3,16,32,256]{3,2,1,0:T(8,128)}, u32[]{:S(2)}) copy-start(f32[3,16,32,256]{3,2,1,0:T(8,128)} %vel.3) | copy-start | bytes 4718596
  13.4 11.9 %copy-start.6 = (f32[3]{0:T(128)S(1)}, f32[3]{0:T(128)}, u32[]{:S(2)}) copy-start(f32[3]{0:T(128)} %impact.3) | copy-start | bytes 40
  14.5 10.9 %copy-start.5 = (s32[16,32,256]{2,1,0:T(8,128)S(1)}, s32[16,32,256]{2,1,0:T(8,128)}, u32[]{:S(2)}) copy-start(s32[16,32,256]{2,1,0:T(8,128)} %contact.3) | copy-start | bytes 1572868
  14.5 5.8 %collective-permute-start.5 = (f32[16,32,128]{2,1,0:T(8,128)S(1)}, f32[16,32,128]{2,1,0:T(8,128)S(1)}, u32[]{:S(2)}, u32[]{:S(2)}) collective-permute-start(f32[16,32,128]{2,1,0:T(8,128)S(1)} %get-tuple-element.49), channel_id=1, source_target_pairs={{0,1},{1,0},{2,3},{3,2},{4,5},{5,4},{6,7},{7,6},{8,9},{9,8},{10,11... | collective-permute-start | bytes 786440 | tf_op jit(solution)/shard_map/ppermute | solution.py:656
  14.5 12.9 %collective-permute-start.6 = (f32[8,32,256]{2,1,0:T(8,128)S(1)}, f32[8,32,256]{2,1,0:T(8,128)S(1)}, u32[]{:S(2)}, u32[]{:S(2)}) collective-permute-start(f32[8,32,256]{2,1,0:T(8,128)S(1)} %get-tuple-element.54), channel_id=1, source_target_pairs={{0,4},{8,12},{4,0},{12,8},{1,5},{9,13},{5,1},{13,9},{2,6},{10,14},... | collective-permute-start | bytes 786440 | tf_op jit(solution)/shard_map/ppermute | solution.py:656
  19.0 8.4 %collective-permute-start.7 = (f32[8,32,256]{2,1,0:T(8,128)S(1)}, f32[8,32,256]{2,1,0:T(8,128)S(1)}, u32[]{:S(2)}, u32[]{:S(2)}) collective-permute-start(f32[8,32,256]{2,1,0:T(8,128)S(1)} %get-tuple-element.55), channel_id=1, source_target_pairs={{4,8},{8,4},{5,9},{9,5},{6,10},{10,6},{7,11},{11,7},{20,24},{24,20... | collective-permute-start | bytes 786440 | tf_op jit(solution)/shard_map/ppermute | solution.py:656
  19.7 5.6 %collective-permute-start.4 = (f32[8,16,256]{2,1,0:T(8,128)S(1)}, f32[8,16,256]{2,1,0:T(8,128)S(1)}, u32[]{:S(2)}, u32[]{:S(2)}) collective-permute-start(f32[8,16,256]{2,1,0:T(8,128)S(1)} %get-tuple-element.48), channel_id=1, source_target_pairs={{0,2},{2,0},{1,3},{3,1},{4,6},{6,4},{5,7},{7,5},{8,10},{10,8},{9,1... | collective-permute-start | bytes 393224 | tf_op jit(solution)/shard_map/ppermute | solution.py:656
  20.8 6.6 %collective-permute-start.8 = (f32[2,8,256]{2,1,0:T(8,128)S(1)}, f32[2,8,256]{2,1,0:T(8,128)S(1)}, u32[]{:S(2)}, u32[]{:S(2)}) collective-permute-start(f32[2,8,256]{2,1,0:T(8,128)S(1)} %get-tuple-element.56), channel_id=1, source_target_pairs={{0,6},{2,4},{8,14},{10,12},{6,0},{4,2},{14,8},{12,10},{1,7},{3,5},... | collective-permute-start | bytes 49160 | tf_op jit(solution)/shard_map/ppermute | solution.py:656
  24.3 3.1 %collective-permute-start.9 = (f32[2,8,256]{2,1,0:T(8,128)S(1)}, f32[2,8,256]{2,1,0:T(8,128)S(1)}, u32[]{:S(2)}, u32[]{:S(2)}) collective-permute-start(f32[2,8,256]{2,1,0:T(8,128)S(1)} %get-tuple-element.57), channel_id=1, source_target_pairs={{4,10},{6,8},{10,4},{8,6},{5,11},{7,9},{11,5},{9,7},{20,26},{22,24... | collective-permute-start | bytes 49160 | tf_op jit(solution)/shard_map/ppermute | solution.py:656
  28.1 1.5 %collective-permute-start.10 = (f32[46,8,128]{2,1,0:T(8,128)S(1)}, f32[46,8,128]{2,1,0:T(8,128)S(1)}, u32[]{:S(2)}, u32[]{:S(2)}) collective-permute-start(f32[46,8,128]{2,1,0:T(8,128)S(1)} %shard_map.127), channel_id=1, source_target_pairs={{0,1},{1,0},{2,3},{3,2},{4,5},{5,4},{6,7},{7,6},{8,9},{9,8},{10,11... | collective-permute-start | bytes 565256 | tf_op jit(solution)/shard_map/ppermute | solution.py:656
  29.6 15.0 %copy-start.4 = (f32[16,32,256]{2,1,0:T(8,128)S(1)}, f32[16,32,256]{2,1,0:T(8,128)}, u32[]{:S(2)}) copy-start(f32[16,32,256]{2,1,0:T(8,128)} %damage.1) | copy-start | bytes 1572868

commit v14 on v13

--- a/solution.py
+++ b/solution.py
@@ -215,7 +215,7 @@
     )
     hist, rd_out, v_out, stress_out, mom_out = refs[n_y + 1 : n_y + 6]
     ys, zs = refs[n_y + 6 : 2 * n_y + 6], refs[2 * n_y + 6]
-    steps, many = inner_steps(damage.shape[0], 2)
+    steps, many = inner_steps(damage.shape[0], 7)
 
     def several(step, total):
         for at in range(many):

time: 45.9 us -> 45.9 us (level)
  transfers between devices with their start and end apart: 11 -> 11, of which waited for: 2 -> 2; matrix products, arithmetic and copies ran while one was open for 0% -> 0% of each run, Pallas kernels for 18% -> 17%
where the time goes in v14:
time: 45.9 us; the launch traced here: 45.7 us
  starting transfers between devices  15.6 us (34%)
  Pallas kernels  14.9 us (32%)
  blocking collectives  11.8 us (26%)
  other arithmetic  1.82 us (4%)
  between operations  0.93 us (2%)
  waiting for transfers between devices  0.59 us (1%)
    ppermute x11, starting transfers between devices, swap(): return lax.ppermute(array, axis, pairs + [(b, a) for a, b in pairs])  15.6 us
    pallas_call x10, Pallas kernels, call(): pl.pallas_call(kernel, out_shape=outs, in_specs=[spec_of(k, a) for k, a i...  14.9 us
    all_to_all x1, blocking collectives, per_device(): mom = lax.all_to_all(spread, ('gx', 'gy', 'gz'), 0, 0, tiled=True)  11.8 us
    concatenate x1, other arithmetic, per_device(): both = jnp.concatenate([displacement, damage[None]])  1.72 us
  transfers between devices with their start and end apart: 11, of which 2 were waited for; matrix products, arithmetic and copies ran while one was open for 0% of the time, Pallas kernels for 17%

profile of v14, /device:TPU:0, one launch (start us, length us, event | category | flops | bytes accessed | tf_op | source)
XLA Modules:
  0.0 45.7 jit_solution(16326935153472684053)
XLA Ops:
  0.6 1.7 %pad_maximum_fusion.disp = f32[4,16,32,256]{3,2,1,0:T(8,128)S(1)} fusion(f32[1,16,32,256]{3,2,1,0:T(8,128)} %bitcast.4, f32[3,16,32,256]{3,2,1,0:T(8,128)} %param.9), kind=kLoop, calls=%fused_computation | loop fusion | flops 524288 | bytes 4194304 | tf_op jit(solution)/shard_map/concatenate | solution.py:722
  2.4 0.1 pad_add_fusion.pos
  2.4 0.9 %shard_map.120 = (f32[4,16,256]{2,1,0:T(8,128)S(1)}, f32[16,32,128]{2,1,0:T(8,128)S(1)}) custom-call(s32[3]{0:T(128)S(1)} %pad_add_fusion.pos, f32[4,16,32,256]{3,2,1,0:T(8,128)S(1)} %pad_maximum_fusion.disp), custom_call_target="tpu_custom_call" | custom-call | flops 131072 | bytes 2424844 | tf_op jit(solution)/shard_map/pallas_call | solution.py:691
  3.3 0.0 copy-start.7
  3.4 0.0 copy-start
  3.4 0.0 copy-start.2
  3.4 0.0 copy-start.3
  3.4 0.5 %collective-permute-start.1 = (f32[16,32,128]{2,1,0:T(8,128)S(1)}, f32[16,32,128]{2,1,0:T(8,128)S(1)}, u32[]{:S(2)}, u32[]{:S(2)}) collective-permute-start(f32[16,32,128]{2,1,0:T(8,128)S(1)} %get-tuple-element.40.after), channel_id=1, source_target_pairs={{0,1},{1,0},{2,3},{3,2},{4,5},{5,4},{6,7},{7,6},{8,9},{9,8},{10,11... | collective-permute-start | bytes 786440 | tf_op jit(solution)/shard_map/ppermute | solution.py:656
  3.9 2.6 %collective-permute-start = (f32[4,16,256]{2,1,0:T(8,128)S(1)}, f32[4,16,256]{2,1,0:T(8,128)S(1)}, u32[]{:S(2)}, u32[]{:S(2)}) collective-permute-start(f32[4,16,256]{2,1,0:T(8,128)S(1)} %get-tuple-element.39), channel_id=1, source_target_pairs={{0,2},{2,0},{1,3},{3,1},{4,6},{6,4},{5,7},{7,5},{8,10},{10,8},{9,1... | collective-permute-start | bytes 196616 | tf_op jit(solution)/shard_map/ppermute | solution.py:656
  6.5 0.6 %shard_map.121 = (f32[4,32,256]{2,1,0:T(8,128)S(1)}, f32[4,32,256]{2,1,0:T(8,128)S(1)}) custom-call(s32[3]{0:T(128)S(1)} %pad_add_fusion.pos, f32[4,16,32,256]{3,2,1,0:T(8,128)S(1)} %pad_maximum_fusion.disp, f32[16,32,128]{2,1,0:T(8,128)S(1)} %get-tuple-element.40.after), custom_call_target="tpu_custom_call" | custom-call | flops 131072 | bytes 2621452 | tf_op jit(solution)/shard_map/pallas_call | solution.py:691
  7.0 1.6 %collective-permute-start.2 = (f32[4,32,256]{2,1,0:T(8,128)S(1)}, f32[4,32,256]{2,1,0:T(8,128)S(1)}, u32[]{:S(2)}, u32[]{:S(2)}) collective-permute-start(f32[4,32,256]{2,1,0:T(8,128)S(1)} %get-tuple-element.41), channel_id=1, source_target_pairs={{0,4},{8,12},{4,0},{12,8},{1,5},{9,13},{5,1},{13,9},{2,6},{10,14},... | collective-permute-start | bytes 393224 | tf_op jit(solution)/shard_map/ppermute | solution.py:656
  8.7 0.7 %collective-permute-start.3 = (f32[4,32,256]{2,1,0:T(8,128)S(1)}, f32[4,32,256]{2,1,0:T(8,128)S(1)}, u32[]{:S(2)}, u32[]{:S(2)}) collective-permute-start(f32[4,32,256]{2,1,0:T(8,128)S(1)} %get-tuple-element.42), channel_id=1, source_target_pairs={{4,8},{8,4},{5,9},{9,5},{6,10},{10,6},{7,11},{11,7},{20,24},{24,20... | collective-permute-start | bytes 393224 | tf_op jit(solution)/shard_map/ppermute | solution.py:656
  9.4 0.0 copy-done.7
  9.4 0.0 collective-permute-done.refs_0_
  9.4 0.0 collective-permute-done.1.refs_1_
  9.4 0.0 copy-done
  9.4 0.0 copy-done.2
  9.4 0.0 copy-done.3
  9.4 3.7 %shard_map.122 = (f32[16,32,256]{2,1,0:T(8,128)S(1)}, f32[16,32,256]{2,1,0:T(8,128)S(1)}, f32[16,32,256]{2,1,0:T(8,128)S(1)}, f32[6,16,32,256]{3,2,1,0:T(8,128)S...) custom-call(s32[3]{0:T(128)S(1)} %pad_add_fusion.pos, ...), custom_call_target="tpu_custom_call" | custom-call | flops 18350080 | bytes 9113676 | tf_op jit(solution)/shard_map/pallas_call | solution.py:691
  13.1 0.0 collective-permute-done.2.refs_2_
  13.2 0.0 collective-permute-done.3.refs_3_
  13.2 0.0 copy-start.1
  13.2 0.0 copy-start.6
  13.2 1.1 %shard_map.123 = (f32[2,32,256]{2,1,0:T(8,128)S(1)}, f32[16,32,256]{2,1,0:T(8,128)S(1)}, f32[16,32,256]{2,1,0:T(8,128)S(1)}, f32[6,2,32,256]{3,2,1,0:T(8,128)S(1...) custom-call(s32[3]{0:T(128)S(1)} %pad_add_fusion.pos, ...), custom_call_target="tpu_custom_call" | custom-call | flops 2621440 | bytes 8134732 | tf_op jit(solution)/shard_map/pallas_call | solution.py:691
  14.2 0.0 copy-start.5
  14.3 0.1 collective-permute-start.5
  14.3 4.5 %collective-permute-start.6 = (f32[8,32,256]{2,1,0:T(8,128)S(1)}, f32[8,32,256]{2,1,0:T(8,128)S(1)}, u32[]{:S(2)}, u32[]{:S(2)}) collective-permute-start(f32[8,32,256]{2,1,0:T(8,128)S(1)} %get-tuple-element.54), channel_id=1, source_target_pairs={{0,4},{8,12},{4,0},{12,8},{1,5},{9,13},{5,1},{13,9},{2,6},{10,14},... | collective-permute-start | bytes 786440 | tf_op jit(solution)/shard_map/ppermute | solution.py:656
  18.8 0.7 %collective-permute-start.7 = (f32[8,32,256]{2,1,0:T(8,128)S(1)}, f32[8,32,256]{2,1,0:T(8,128)S(1)}, u32[]{:S(2)}, u32[]{:S(2)}) collective-permute-start(f32[8,32,256]{2,1,0:T(8,128)S(1)} %get-tuple-element.55), channel_id=1, source_target_pairs={{4,8},{8,4},{5,9},{9,5},{6,10},{10,6},{7,11},{11,7},{20,24},{24,20... | collective-permute-start | bytes 786440 | tf_op jit(solution)/shard_map/ppermute | solution.py:656
  19.5 0.6 %collective-permute-start.4 = (f32[8,16,256]{2,1,0:T(8,128)S(1)}, f32[8,16,256]{2,1,0:T(8,128)S(1)}, u32[]{:S(2)}, u32[]{:S(2)}) collective-permute-start(f32[8,16,256]{2,1,0:T(8,128)S(1)} %get-tuple-element.48), channel_id=1, source_target_pairs={{0,2},{2,0},{1,3},{3,1},{4,6},{6,4},{5,7},{7,5},{8,10},{10,8},{9,1... | collective-permute-start | bytes 393224 | tf_op jit(solution)/shard_map/ppermute | solution.py:656
  20.1 0.0 collective-permute-done.5.after.refs_1_.z_own
  20.1 0.6 %shard_map.124 = (f32[2,8,256]{2,1,0:T(8,128)S(1)}, f32[2,8,256]{2,1,0:T(8,128)S(1)}) custom-call(s32[3]{0:T(128)S(1)} %pad_add_fusion.pos, f32[16,32,128]{2,1,0:T(8,128)S(1)} %collective-permute-done.5.after.refs_1_.z_own, f32[16,32,256]{2,1,0:T(8,128)S(1)} %get-tuple-element.52.v.refs_4_.v0, f32[16,32,256]{2,1,0:T(8,128)S(1)} %get-tuple-element.53.rd.refs_5_), custom_call_target="tpu_custom_call" | custom-call | flops 1024 | bytes 1343500 | tf_op jit(solution)/shard_map/pallas_call | solution.py:691
  20.6 3.7 %collective-permute-start.8 = (f32[2,8,256]{2,1,0:T(8,128)S(1)}, f32[2,8,256]{2,1,0:T(8,128)S(1)}, u32[]{:S(2)}, u32[]{:S(2)}) collective-permute-start(f32[2,8,256]{2,1,0:T(8,128)S(1)} %get-tuple-element.56), channel_id=1, source_target_pairs={{0,6},{2,4},{8,14},{10,12},{6,0},{4,2},{14,8},{12,10},{1,7},{3,5},... | collective-permute-start | bytes 49160 | tf_op jit(solution)/shard_map/ppermute | solution.py:656
  24.3 0.7 %collective-permute-start.9 = (f32[2,8,256]{2,1,0:T(8,128)S(1)}, f32[2,8,256]{2,1,0:T(8,128)S(1)}, u32[]{:S(2)}, u32[]{:S(2)}) collective-permute-start(f32[2,8,256]{2,1,0:T(8,128)S(1)} %get-tuple-element.57), channel_id=1, source_target_pairs={{4,10},{6,8},{10,4},{8,6},{5,11},{7,9},{11,5},{9,7},{20,26},{22,24... | collective-permute-start | bytes 49160 | tf_op jit(solution)/shard_map/ppermute | solution.py:656
  25.0 0.1 collective-permute-done.4.refs_0_.refs_8_.refs_2_
  25.1 0.0 copy-done.1
  25.1 0.0 copy-done.6
  25.1 0.0 copy-done.5
  25.1 2.1 %shard_map.126 = (f32[16,32,256]{2,1,0:T(8,128)}, f32[3,16,32,256]{3,2,1,0:T(8,128)S(1)}, f32[3,16,32,256]{3,2,1,0:T(8,128)S(1)}, f32[8,128]{1,0:T(8,128)S(1)}) custom-call(s32[3]{0:T(128)S(1)} %pad_add_fusion.pos, f32[4,4]{1,0:T(4,128)S(1)} %pad_maximum_fusion.1.table, f32[3]{0:T(128)S(1)} %copy-done.6, f32[4,16,32,256]{3,2,1,0:T(8,128)S(1)} %pad_maximum_fusion.disp, ...), custom_call_target="tpu_custom_call" | custom-call | flops 7208960 | bytes 12914776 | tf_op jit(solution)/shard_map/pallas_call | solution.py:691
  27.2 0.0 collective-permute-done.6.refs_6_.refs_0_
  27.2 0.0 collective-permute-done.7.refs_7_.refs_1_
  27.2 0.0 collective-permute-done.8.refs_9_.refs_3_
  27.2 0.0 collective-permute-done.9.refs_10_.refs_4_
  27.2 0.7 %shard_map.127 = f32[46,8,128]{2,1,0:T(8,128)S(1)} custom-call(s32[3]{0:T(128)S(1)} %pad_add_fusion.pos, f32[16,32,256]{2,1,0:T(8,128)S(1)} %get-tuple-element.52.v.refs_4_.v0, f32[16,32,256]{2,1,0:T(8,128)S(1)} %get-tuple-element.53.rd.refs_5_, f32[8,128]{1,0:T(8,128)S(1)} %get-tuple-element.63.token, ...), custom_call_target="tpu_custom_call" | custom-call | flops 524288 | bytes 1929228 | tf_op jit(solution)/shard_map/pallas_call | solution.py:691
  27.9 0.1 collective-permute-start.10
  28.0 1.0 %shard_map.125 = (f32[3,2,32,256]{3,2,1,0:T(8,128)S(1)}, f32[3,2,32,256]{3,2,1,0:T(8,128)S(1)}, f32[22,40,256]{2,1,0:T(8,128)S(1)}, f32[22,40,256]{2,1,0:T(8,128)S(1)}) custom-call(s32[3]{0:T(128)S(1)} %pad_add_fusion.pos, f32[4,4]{1,0:T(4,128)S(1)} %pad_maximum_fusion.1.table, f32[3]{0:T(128)S(1)} %copy-done.6, ...), custom_call_target="tpu_custom_call" | custom-call | flops 1572864 | bytes 12583000 | tf_op jit(solution)/shard_map/pallas_call | solution.py:691
  29.0 0.4 collective-permute-done.10.z_got
  29.4 0.0 copy-start.4
  29.4 3.4 %shard_map.128 = (f32[3,16,32,256]{3,2,1,0:T(8,128)}, f32[3,16,32,256]{3,2,1,0:T(8,128)}, f32[16,32,256]{2,1,0:T(8,128)S(1)}, f32[16,32,256]{2,1,0:T(8,128)S(1)}, f32[16,1,128]{2,1,0:T(1,128)S(1)}) custom-call(s32[3]{0:T(128)S(1)} %pad_add_fusion.pos, f32[22,40,256]{2,1,0:T(8,128)S(1)} %get-tuple-element.58.main_v, ...), custom_call_target="tpu_custom_call" | custom-call | flops 7864320 | bytes 9998348 | tf_op jit(solution)/shard_map/pallas_call | solution.py:691
  32.8 11.8 %all_to_all.5.mom = f32[16,1,128]{2,1,0:T(1,128)S(1)} all-to-all(f32[16,1,128]{2,1,0:T(1,128)S(1)} %get-tuple-element.71), channel_id=1, replica_groups=mesh['case'=2,'gx'=4,'gy'=2,'gz'=2] {'gx','gy','gz'}, dimensions={0} | all-to-all | bytes 16384 | tf_op jit(solution)/shard_map/all_to_all | solution.py:836
  44.6 0.0 copy-done.4
  44.6 1.1 %shard_map.129 = f32[16,32,256]{2,1,0:T(8,128)} custom-call(f32[16,1,128]{2,1,0:T(1,128)S(1)} %all_to_all.5.mom, f32[16,32,256]{2,1,0:T(8,128)S(1)} %get-tuple-element.52.v.refs_4_.v0, f32[16,32,256]{2,1,0:T(8,128)S(1)} %get-tuple-element.72.v1, f32[16,32,256]{2,1,0:T(8,128)S(1)} %get-tuple-element.73.v2, f32[16,32,256]{2,1,0:T(8,128)S(1)} %copy-done.4), custom_call_target="tpu_custom_call" | custom-call | flops 1048576 | bytes 2629632 | tf_op jit(solution)/shard_map/pallas_call | solution.py:691
  (2 shorter events, 0.0 us)
Async XLA Ops:
  3.3 6.0 %copy-start.7 = (f32[4,4]{1,0:T(4,128)S(1)}, f32[4,4]{1,0:T(4,128)}, u32[]{:S(2)}) copy-start(f32[4,4]{1,0:T(4,128)} %param.16) | copy-start | bytes 196
  3.4 6.1 %copy-start = (s32[16,32,256]{2,1,0:T(8,128)S(1)}, s32[16,32,256]{2,1,0:T(8,128)}, u32[]{:S(2)}) copy-start(s32[16,32,256]{2,1,0:T(8,128)} %labels.7) | copy-start | bytes 1572868
  3.4 6.1 %copy-start.2 = (f32[16,32,256]{2,1,0:T(8,128)S(1)}, f32[16,32,256]{2,1,0:T(8,128)}, u32[]{:S(2)}) copy-start(f32[16,32,256]{2,1,0:T(8,128)} %history.3) | copy-start | bytes 1572868
  3.4 6.1 %copy-start.3 = (s32[16,32,256]{2,1,0:T(8,128)S(1)}, s32[16,32,256]{2,1,0:T(8,128)}, u32[]{:S(2)}) copy-start(s32[16,32,256]{2,1,0:T(8,128)} %notch.3) | copy-start | bytes 1572868
  3.4 6.0 %collective-permute-start.1 = (f32[16,32,128]{2,1,0:T(8,128)S(1)}, f32[16,32,128]{2,1,0:T(8,128)S(1)}, u32[]{:S(2)}, u32[]{:S(2)}) collective-permute-start(f32[16,32,128]{2,1,0:T(8,128)S(1)} %get-tuple-element.40.after), channel_id=1, source_target_pairs={{0,1},{1,0},{2,3},{3,2},{4,5},{5,4},{6,7},{7,6},{8,9},{9,8},{10,11... | collective-permute-start | bytes 786440 | tf_op jit(solution)/shard_map/ppermute | solution.py:656
  3.9 5.5 %collective-permute-start = (f32[4,16,256]{2,1,0:T(8,128)S(1)}, f32[4,16,256]{2,1,0:T(8,128)S(1)}, u32[]{:S(2)}, u32[]{:S(2)}) collective-permute-start(f32[4,16,256]{2,1,0:T(8,128)S(1)} %get-tuple-element.39), channel_id=1, source_target_pairs={{0,2},{2,0},{1,3},{3,1},{4,6},{6,4},{5,7},{7,5},{8,10},{10,8},{9,1... | collective-permute-start | bytes 196616 | tf_op jit(solution)/shard_map/ppermute | solution.py:656
  7.0 6.1 %collective-permute-start.2 = (f32[4,32,256]{2,1,0:T(8,128)S(1)}, f32[4,32,256]{2,1,0:T(8,128)S(1)}, u32[]{:S(2)}, u32[]{:S(2)}) collective-permute-start(f32[4,32,256]{2,1,0:T(8,128)S(1)} %get-tuple-element.41), channel_id=1, source_target_pairs={{0,4},{8,12},{4,0},{12,8},{1,5},{9,13},{5,1},{13,9},{2,6},{10,14},... | collective-permute-start | bytes 393224 | tf_op jit(solution)/shard_map/ppermute | solution.py:656
  8.7 4.5 %collective-permute-start.3 = (f32[4,32,256]{2,1,0:T(8,128)S(1)}, f32[4,32,256]{2,1,0:T(8,128)S(1)}, u32[]{:S(2)}, u32[]{:S(2)}) collective-permute-start(f32[4,32,256]{2,1,0:T(8,128)S(1)} %get-tuple-element.42), channel_id=1, source_target_pairs={{4,8},{8,4},{5,9},{9,5},{6,10},{10,6},{7,11},{11,7},{20,24},{24,20... | collective-permute-start | bytes 393224 | tf_op jit(solution)/shard_map/ppermute | solution.py:656
  13.2 11.9 %copy-start.1 = (f32[3,16,32,256]{3,2,1,0:T(8,128)S(1)}, f32[3,16,32,256]{3,2,1,0:T(8,128)}, u32[]{:S(2)}) copy-start(f32[3,16,32,256]{3,2,1,0:T(8,128)} %vel.3) | copy-start | bytes 4718596
  13.2 11.9 %copy-start.6 = (f32[3]{0:T(128)S(1)}, f32[3]{0:T(128)}, u32[]{:S(2)}) copy-start(f32[3]{0:T(128)} %impact.3) | copy-start | bytes 40
  14.2 10.9 %copy-start.5 = (s32[16,32,256]{2,1,0:T(8,128)S(1)}, s32[16,32,256]{2,1,0:T(8,128)}, u32[]{:S(2)}) copy-start(s32[16,32,256]{2,1,0:T(8,128)} %contact.3) | copy-start | bytes 1572868
  14.3 5.8 %collective-permute-start.5 = (f32[16,32,128]{2,1,0:T(8,128)S(1)}, f32[16,32,128]{2,1,0:T(8,128)S(1)}, u32[]{:S(2)}, u32[]{:S(2)}) collective-permute-start(f32[16,32,128]{2,1,0:T(8,128)S(1)} %get-tuple-element.49), channel_id=1, source_target_pairs={{0,1},{1,0},{2,3},{3,2},{4,5},{5,4},{6,7},{7,6},{8,9},{9,8},{10,11... | collective-permute-start | bytes 786440 | tf_op jit(solution)/shard_map/ppermute | solution.py:656
  14.3 12.9 %collective-permute-start.6 = (f32[8,32,256]{2,1,0:T(8,128)S(1)}, f32[8,32,256]{2,1,0:T(8,128)S(1)}, u32[]{:S(2)}, u32[]{:S(2)}) collective-permute-start(f32[8,32,256]{2,1,0:T(8,128)S(1)} %get-tuple-element.54), channel_id=1, source_target_pairs={{0,4},{8,12},{4,0},{12,8},{1,5},{9,13},{5,1},{13,9},{2,6},{10,14},... | collective-permute-start | bytes 786440 | tf_op jit(solution)/shard_map/ppermute | solution.py:656
  18.8 8.4 %collective-permute-start.7 = (f32[8,32,256]{2,1,0:T(8,128)S(1)}, f32[8,32,256]{2,1,0:T(8,128)S(1)}, u32[]{:S(2)}, u32[]{:S(2)}) collective-permute-start(f32[8,32,256]{2,1,0:T(8,128)S(1)} %get-tuple-element.55), channel_id=1, source_target_pairs={{4,8},{8,4},{5,9},{9,5},{6,10},{10,6},{7,11},{11,7},{20,24},{24,20... | collective-permute-start | bytes 786440 | tf_op jit(solution)/shard_map/ppermute | solution.py:656
  19.5 5.6 %collective-permute-start.4 = (f32[8,16,256]{2,1,0:T(8,128)S(1)}, f32[8,16,256]{2,1,0:T(8,128)S(1)}, u32[]{:S(2)}, u32[]{:S(2)}) collective-permute-start(f32[8,16,256]{2,1,0:T(8,128)S(1)} %get-tuple-element.48), channel_id=1, source_target_pairs={{0,2},{2,0},{1,3},{3,1},{4,6},{6,4},{5,7},{7,5},{8,10},{10,8},{9,1... | collective-permute-start | bytes 393224 | tf_op jit(solution)/shard_map/ppermute | solution.py:656
  20.6 6.6 %collective-permute-start.8 = (f32[2,8,256]{2,1,0:T(8,128)S(1)}, f32[2,8,256]{2,1,0:T(8,128)S(1)}, u32[]{:S(2)}, u32[]{:S(2)}) collective-permute-start(f32[2,8,256]{2,1,0:T(8,128)S(1)} %get-tuple-element.56), channel_id=1, source_target_pairs={{0,6},{2,4},{8,14},{10,12},{6,0},{4,2},{14,8},{12,10},{1,7},{3,5},... | collective-permute-start | bytes 49160 | tf_op jit(solution)/shard_map/ppermute | solution.py:656
  24.3 2.9 %collective-permute-start.9 = (f32[2,8,256]{2,1,0:T(8,128)S(1)}, f32[2,8,256]{2,1,0:T(8,128)S(1)}, u32[]{:S(2)}, u32[]{:S(2)}) collective-permute-start(f32[2,8,256]{2,1,0:T(8,128)S(1)} %get-tuple-element.57), channel_id=1, source_target_pairs={{4,10},{6,8},{10,4},{8,6},{5,11},{7,9},{11,5},{9,7},{20,26},{22,24... | collective-permute-start | bytes 49160 | tf_op jit(solution)/shard_map/ppermute | solution.py:656
  27.9 1.5 %collective-permute-start.10 = (f32[46,8,128]{2,1,0:T(8,128)S(1)}, f32[46,8,128]{2,1,0:T(8,128)S(1)}, u32[]{:S(2)}, u32[]{:S(2)}) collective-permute-start(f32[46,8,128]{2,1,0:T(8,128)S(1)} %shard_map.127), channel_id=1, source_target_pairs={{0,1},{1,0},{2,3},{3,2},{4,5},{5,4},{6,7},{7,6},{8,9},{9,8},{10,11... | collective-permute-start | bytes 565256 | tf_op jit(solution)/shard_map/ppermute | solution.py:656
  29.4 15.2 %copy-start.4 = (f32[16,32,256]{2,1,0:T(8,128)S(1)}, f32[16,32,256]{2,1,0:T(8,128)}, u32[]{:S(2)}) copy-start(f32[16,32,256]{2,1,0:T(8,128)} %damage.1) | copy-start | bytes 1572868
